TPU v7x, 32 devices: a whole 2x2x4 slice. The times are simulated.
32 devices in a mesh: dap: 32 (over z, y, x, core).
Axes of the slice: x: 2, y: 2, z: 4, core: 2. Of those that a mesh axis runs over, the one named last changes fastest.
Arguments:
- alignment_embedding: bfloat16 [32, 320, 256], P('dap'), may hold values from -6 to 6
- couple_embedding: bfloat16 [320, 320, 128], P('dap'), may hold values from -6 to 6
- amino_strand: int32 [320], replicated, may hold values from 0 to 3, never falling along the last dimension, each value on 1 to 160 neighbouring positions
- amino_validity: int32 [320], replicated, may hold values from 0 to 1, as said below
- alignment_validity: int32 [32, 320], replicated, may hold values from 0 to 1, as said below
- separation_embedding: float32 [66, 128], replicated, may hold values from -3 to 3
- couple_shift_scaling: float32 [128], replicated, may hold values from 0.25 to 1.75
- couple_shift_factors: bfloat16 [128, 8], replicated, may hold values from -0.5 to 0.5
- horizontal_scaling_factor: float32 [256], replicated, may hold values from 0.25 to 1.75
- horizontal_entry_factors: bfloat16 [256, 4, 256], replicated, may hold values from -1 to 1
- horizontal_exit_factors: bfloat16 [256, 256], replicated, may hold values from -0.375 to 0.375
- vertical_scaling_factor: float32 [256], replicated, may hold values from 0.25 to 1.75
- vertical_entry_factors: bfloat16 [256, 4, 256], replicated, may hold values from -1 to 1
- vertical_exit_factors: bfloat16 [256, 256], replicated, may hold values from -0.375 to 0.375
- alignment_feedforward_scaling: float32 [256], replicated, may hold values from 0.25 to 1.75
- alignment_widen_factors: bfloat16 [256, 1024], replicated, may hold values from -0.375 to 0.375
- alignment_narrow_factors: bfloat16 [1024, 256], replicated, may hold values from -0.1875 to 0.1875
- product_scaling_factor: float32 [256], replicated, may hold values from 0.25 to 1.75
- product_twin_factors: bfloat16 [256, 64], replicated, may hold values from -0.375 to 0.375
- product_exit_factors: bfloat16 [1024, 128], replicated, may hold values from -0.75 to 0.75
- couple_feedforward_scaling: float32 [128], replicated, may hold values from 0.25 to 1.75
- couple_widen_factors: bfloat16 [128, 512], replicated, may hold values from -0.5 to 0.5
- couple_narrow_factors: bfloat16 [512, 128], replicated, may hold values from -0.25 to 0.25
Outputs:
- updated_sequences: bfloat16 [32, 320, 256], P(None, 'dap')
- updated_pairs: bfloat16 [320, 320, 128], P('dap')
Inputs may be any that keep to these rules, and one draw needn't show every extreme that they name: `amino_validity`: 1 on a leading run of 160 or more residues, 0 after it; the last residue is 0. `alignment_validity`: row 0 and residue 0 are 1 throughout.
All inputs are finite; a program needn't handle non-finite values.
Results may differ from a plain program's by a relative error of at most 0.013.
Values may be sent and summed in bfloat16 or wider, within the bound.
No kernel may reach another device: no remote copies, remote signals or barrier semaphores. Data moves between devices by JAX's collectives and lax.ppermute only.
A program may use at most 192 MiB of HBM per device.

v0:
```python
import jax
import jax.numpy as jnp
from jax import lax
from jax.sharding import PartitionSpec as P

FOCUS_COUNT = 8


EPS = 1e-05
OUTER_EPS = 0.001
MASKED = -1000000000.0
HIGH = lax.Precision.HIGHEST


def apply_layer_norm(input_tensor, gain):
    input_tensor = input_tensor.astype(jnp.float32)
    centred = input_tensor - jnp.mean(input_tensor, -1, keepdims=True)
    spread = jnp.mean(centred * centred, -1, keepdims=True)
    return centred * lax.rsqrt(spread + EPS) * gain


def accurate_product(former_factor, right):
    return jnp.einsum("...d,de->...e", former_factor, right, preferred_element_type=jnp.float32)


def linear_project(input_tensor, gain, weights):
    normed = apply_layer_norm(input_tensor, gain).astype(jnp.bfloat16)
    proj = jnp.einsum("rnd,dgc->grnc", normed, weights, preferred_element_type=jnp.float32)
    horizontal_lines, cols, inner = (input_tensor.shape[0], input_tensor.shape[1], weights.shape[2])

    def heads(t):
        return (
            t.reshape(horizontal_lines, cols, FOCUS_COUNT, inner // FOCUS_COUNT)
            .transpose(2, 0, 1, 3)
            .astype(jnp.bfloat16)
        )

    return (heads(proj[0]), heads(proj[1]), heads(proj[2]), jax.nn.sigmoid(proj[3]))


def gated_attention(
    query_vectors, key_vectors, content_arrays, gate_logits, lookup_validity_shift, bias
):
    scale = query_vectors.shape[-1] ** (-0.5)

    def one_head(args):
        qh, kh, vh, bh = args
        scores = jnp.einsum("ric,rjc->rij", qh, kh, preferred_element_type=jnp.float32) * scale
        scores = scores + bh[None].astype(jnp.float32)
        scores = jnp.where(lookup_validity_shift[:, None, :] > 0, scores, MASKED)
        top = jnp.max(scores, -1, keepdims=True)
        expo = jnp.exp(scores - top)
        weights = (expo / jnp.sum(expo, -1, keepdims=True)).astype(jnp.bfloat16)
        return jnp.einsum("rij,rjc->ric", weights, vh, preferred_element_type=jnp.float32)

    heads_out = lax.map(one_head, (query_vectors, key_vectors, content_arrays, bias))
    merged = heads_out.transpose(1, 2, 0, 3).reshape(gate_logits.shape)
    return (merged * gate_logits).astype(jnp.bfloat16)


def transition_block(input_tensor, gain, w_in, w_out):
    hidden = jax.nn.relu(
        accurate_product(apply_layer_norm(input_tensor, gain).astype(jnp.bfloat16), w_in)
    ).astype(jnp.bfloat16)
    return input_tensor + accurate_product(hidden, w_out)


def on_device(
    alignment_embedding,
    couple_embedding,
    amino_strand,
    amino_validity,
    alignment_validity,
    separation_embedding,
    couple_shift_scaling,
    couple_shift_factors,
    horizontal_scaling_factor,
    horizontal_entry_factors,
    horizontal_exit_factors,
    vertical_scaling_factor,
    vertical_entry_factors,
    vertical_exit_factors,
    alignment_feedforward_scaling,
    alignment_widen_factors,
    alignment_narrow_factors,
    product_scaling_factor,
    product_twin_factors,
    product_exit_factors,
    couple_feedforward_scaling,
    couple_widen_factors,
    couple_narrow_factors,
):
    residue_index = lax.axis_index("dap")
    residue_rows, length = (couple_embedding.shape[0], couple_embedding.shape[1])
    alignment_lines = alignment_embedding.shape[0]
    channel_depth = alignment_validity.shape[0]
    first_operand = residue_index * residue_rows
    positions = jnp.arange(length, dtype=jnp.int32)
    own_pos = first_operand + jnp.arange(residue_rows, dtype=jnp.int32)
    own_chain = lax.dynamic_slice_in_dim(amino_strand, first_operand, residue_rows)
    clip_offsets = (separation_embedding.shape[0] - 2) // 2
    same = own_chain[:, None] == amino_strand[None, :]
    bins = jnp.where(
        same,
        jnp.clip(own_pos[:, None] - positions[None, :] + clip_offsets, 0, 2 * clip_offsets),
        2 * clip_offsets + 1,
    )
    onehot = (
        bins[:, :, None]
        == jnp.arange(separation_embedding.shape[0], dtype=jnp.int32)[None, None, :]
    ).astype(jnp.float32)
    pair_one = couple_embedding.astype(jnp.float32) + jnp.einsum(
        "ijb,bz->ijz", onehot, separation_embedding, precision=HIGH
    )
    pair_normed = apply_layer_norm(pair_one, couple_shift_scaling).astype(jnp.bfloat16)
    bias_rows = jnp.einsum(
        "ijz,zh->hij", pair_normed, couple_shift_factors, preferred_element_type=jnp.float32
    ).astype(jnp.bfloat16)
    row_attention_first = residue_index * alignment_lines
    lookup_validity_shift = (
        lax.dynamic_slice_in_dim(
            alignment_validity, row_attention_first, alignment_lines, 0
        ).astype(jnp.float32)
        * amino_validity.astype(jnp.float32)[None, :]
    )
    query_vectors, key_vectors, content_arrays, gate_logits = linear_project(
        alignment_embedding, horizontal_scaling_factor, horizontal_entry_factors
    )
    full_bias = lax.all_gather(bias_rows, "dap", axis=1, tiled=True)
    sigmoid_scaled_result = gated_attention(
        query_vectors, key_vectors, content_arrays, gate_logits, lookup_validity_shift, full_bias
    )
    alignment_past_horizontal = (
        alignment_embedding.astype(jnp.float32)
        + accurate_product(sigmoid_scaled_result, horizontal_exit_factors)
    ).astype(jnp.bfloat16)
    column_slices = lax.all_to_all(
        alignment_past_horizontal, "dap", split_axis=1, concat_axis=0, tiled=True
    )
    column_major_rows = column_slices.transpose(1, 0, 2)
    vertical_validity_share = (
        lax.dynamic_slice_in_dim(alignment_validity, first_operand, residue_rows, 1)
        .astype(jnp.float32)
        .T
    )
    col_query, col_keys, col_values, col_gate = linear_project(
        column_major_rows, vertical_scaling_factor, vertical_entry_factors
    )
    empty_initialised = jnp.zeros((FOCUS_COUNT, channel_depth, channel_depth), jnp.bfloat16)
    sequence_after_columns = column_major_rows.astype(jnp.float32) + accurate_product(
        gated_attention(
            col_query, col_keys, col_values, col_gate, vertical_validity_share, empty_initialised
        ),
        vertical_exit_factors,
    )
    alignment_past_feedforward = transition_block(
        sequence_after_columns,
        alignment_feedforward_scaling,
        alignment_widen_factors,
        alignment_narrow_factors,
    )
    updated_sequences = alignment_past_feedforward.transpose(1, 0, 2).astype(jnp.bfloat16)
    projected_input = (
        accurate_product(
            apply_layer_norm(alignment_past_feedforward, product_scaling_factor).astype(
                jnp.bfloat16
            ),
            product_twin_factors,
        )
        * vertical_validity_share[:, :, None]
    ).astype(jnp.bfloat16)
    width = product_twin_factors.shape[1] // 2
    former_factor = projected_input[:, :, :width]
    right = projected_input[:, :, width:].reshape(residue_rows, channel_depth * width)
    own_mask = vertical_validity_share.astype(jnp.bfloat16)
    piece = lax.all_gather(right, "dap", axis=0, tiled=True)
    count = piece.shape[0]
    right_rows = piece.reshape(count, channel_depth, width)
    partner_mask = alignment_validity.astype(jnp.bfloat16)
    counts = jnp.dot(own_mask, partner_mask, preferred_element_type=jnp.float32) + OUTER_EPS

    def one_res(inner):
        left_row, count_row = inner
        outer = jnp.einsum("sc,jse->jce", left_row, right_rows, preferred_element_type=jnp.float32)
        outer = outer.reshape(count, width * width).astype(jnp.bfloat16)
        return (
            jnp.dot(outer, product_exit_factors, preferred_element_type=jnp.float32)
            / count_row[:, None]
        )

    update = lax.map(one_res, (former_factor, counts))
    pair_two = pair_one + update

    def one_pair_row(row):
        return transition_block(
            row, couple_feedforward_scaling, couple_widen_factors, couple_narrow_factors
        )

    updated_pairs = lax.map(one_pair_row, pair_two).astype(jnp.bfloat16)
    return (updated_sequences, updated_pairs)


def solution(mesh):
    placed = (
        P("dap", None, None),
        P("dap", None, None),
        P(),
        P(),
        P(),
        P(),
        P(),
        P(),
        P(),
        P(),
        P(),
        P(),
        P(),
        P(),
        P(),
        P(),
        P(),
        P(),
        P(),
        P(),
        P(),
        P(),
        P(),
    )
    return jax.shard_map(
        on_device,
        mesh=mesh,
        in_specs=placed,
        out_specs=(P(None, "dap", None), P("dap", None, None)),
        check_vma=False,
    )
```

profile of v0, /device:TPU:0, one launch (start us, length us, event | category | flops | bytes accessed | tf_op | source)
XLA Modules:
  0.0 277.8 jit_solution(423821582080786244)
XLA Ops:
  8.8 3.1 %fusion.157 = (f32[10,320]{1,0:T(8,128)S(1)}, f32[10,320,128]{2,1,0:T(8,128)S(1)}) fusion(f32[66,128]{1,0:T(8,128)} %param.36, s32[10,320]{1,0:T(8,128)S(1)} %clamp_select_fusion, bf16[10,320,128]{2,1,0:T(8,128)(2,1)} %param.32), kind=kOutput, calls=%fused_computation.183 | convolution fusion | flops 325840000 | bytes 2516992 | tf_op jit(solution)/shard_map/ijb,bz->ijz/dot_general | solution.py:112
  13.1 1.9 fusion.84
  15.4 1.5 fusion.156
  17.9 56.0 %all-gather.3.cloned.1.call-done = bf16[8,320,320]{2,0,1:T(8,128)(2,1)} async-done(((bf16[8,10,320]{2,0,1:T(8,128)(2,1)}), bf16[8,320,320]{2,0,1:T(8,128)(2,1)}) %all-gather.3.cloned.1.call-update) | async-done | bytes 1638416 | tf_op jit(solution)/shard_map/all_gather | solution.py:129
  73.9 4.1 %copy.70 = bf16[8,320,320]{1,2,0:T(8,128)(2,1)} copy(bf16[8,320,320]{2,0,1:T(8,128)(2,1)} %all-gather.3.cloned.1.call-done) | data formatting | bytes 3276800 | tf_op jit(solution)/shard_map/while | solution.py:56
  78.1 12.9 %while.44 = (s32[]{:T(128)}, f32[8,1,320,32]{2,3,1,0:T(8,128)S(1)}, f32[1,320]{1,0:T(1,128)S(1)}, bf16[8,1,320,32]{2,3,0,1:T(8,128)(2,1)S(1)}, bf16[8,1,320,32]{...) while((s32[]{:T(128)}, f32[8,1,320,32]{2,3,1,0:T(8,128)S(1)}, ...), condition=%wide.region_7.8_spmd.clone, body=%wide.region_4.7_spmd.sunk.clone | while | flops 14130882 | bytes 1692045 | solution.py:56
  79.7 1.3 fusion.211
  81.3 1.3 fusion.211
  82.9 1.3 fusion.211
  84.5 1.3 fusion.211
  87.8 1.3 fusion.211
  89.4 1.3 fusion.211
  93.1 1.6 reduce.11
  95.5 3.6 %all-to-all-start = ((bf16[32,2,1280]{2,1,0:T(2,128)(2,1)}), bf16[32,2,1280]{2,1,0:T(2,128)(2,1)S(1)}, u32[]{:S(2)}, u32[]{:S(2)}) async-start(bf16[32,2,1280]{2,1,0:T(2,128)(2,1)} %reshape.279), calls=%async_computation | async-start | bytes 327680 | tf_op jit(solution)/shard_map/all_to_all | solution.py:137
  100.3 7.2 %all-to-all-done = bf16[32,2,1280]{2,1,0:T(2,128)(2,1)S(1)} async-done(((bf16[32,2,1280]{2,1,0:T(2,128)(2,1)}), bf16[32,2,1280]{2,1,0:T(2,128)(2,1)S(1)}, u32[]{:S(2)}, u32[]{:S(2)}) %all-to-all-start) | async-done | bytes 163872 | tf_op jit(solution)/shard_map/all_to_all | solution.py:137
  109.1 2.5 fusion.158
  112.3 1.3 convert_element_type.176
  115.9 2.1 copy.107
  118.0 1.3 copy_bitcast_fusion
  119.3 25.3 %while.45 = (s32[]{:T(128)}, f32[8,10,32,32]{3,2,1,0:T(8,128)}, f32[10,32]{1,0:T(8,128)S(1)}, bf16[8,10,32,32]{3,2,1,0:T(8,128)(2,1)}, bf16[8,10,32,32]{3,2,1,0:T(8,128)(2,1)}, /*index=5*/bf16[8,10,32,32]{3,2,1,0:T(8,128)(2,1)}) while((s32[]{:T(128)}, f32[8,10,32,32]{3,2,1,0:T(8,128)}, f32[10,32]{1,0:T(8,128)S(1)}, ...), condition=%wide.region_13.14_spmd.clone, body=%wide.region_10.13_spmd.sunk.clone | while | flops 2058944 | bytes 581381 | solution.py:56
  120.5 2.0 fusion.220
  123.6 2.0 fusion.220
  126.8 2.0 fusion.220
  130.0 2.0 fusion.220
  133.2 2.0 fusion.220
  136.3 2.0 fusion.220
  139.5 2.0 fusion.220
  142.7 2.0 fusion.220
  144.7 3.2 %copy.80 = f32[10,32,8,32]{3,2,1,0:T(8,128)} copy(f32[10,32,8,32]{3,1,0,2:T(8,128)} %bitcast.309) | data formatting | bytes 655360 | tf_op jit(solution)/shard_map/transpose | solution.py:57
  147.9 1.7 reshape.257
  149.6 1.3 fusion.146
  151.2 2.5 fusion.110
  155.3 41.3 %all-gather = bf16[32,10,1024]{2,1,0:T(8,128)(2,1)S(1)} all-gather(bf16[1,10,1024]{2,1,0:T(8,128)(2,1)S(1)} %reshape.262), channel_id=1, replica_groups=mesh['dap'=32] {'dap'}, dimensions={0}, use_global_device_ids=true | all-gather | bytes 675840 | tf_op jit(solution)/shard_map/all_gather | solution.py:176
  196.7 3.1 %reshape.259 = bf16[320,32,32]{2,1,0:T(8,128)(2,1)} reshape(bf16[32,10,1024]{2,1,0:T(8,128)(2,1)S(1)} %all-gather) | data formatting | bytes 1310720 | tf_op jit(solution)/shard_map/reshape | solution.py:178
  199.8 5.5 %copy.83 = bf16[320,32,32]{0,1,2:T(8,128)(2,1)S(1)} copy(bf16[320,32,32]{2,1,0:T(8,128)(2,1)} %reshape.259) | data formatting | bytes 1310720 | tf_op jit(solution)/shard_map/while | solution.py:191
  205.3 20.1 %while.46 = (s32[]{:T(128)}, f32[10,320,128]{2,1,0:T(8,128)}, bf16[10,32,32]{2,1,0:T(8,128)(2,1)S(1)}, bf16[320,32,32]{0,1,2:T(8,128)(2,1)S(1)}, bf16[1024,128]{1,0:T(8,128)(2,1)}, /*index=5*/f32[10,320]{1,0:T(8,128)S(1)}) while((s32[]{:T(128)}, f32[10,320,128]{2,1,0:T(8,128)}, bf16[10,32,32]{2,1,0:T(8,128)(2,1)S(1)}, ...), condition=%wide.region_19.20_spmd.clone, body=%wide.region_18.19_spmd.sunk.clone | while | flops 105226240 | bytes 4895081 | solution.py:191
  225.3 2.8 %add.164 = f32[10,320,128]{2,1,0:T(8,128)} add(f32[10,320,128]{2,1,0:T(8,128)S(1)} %get-tuple-element.247, f32[10,320,128]{2,1,0:T(8,128)} %get-tuple-element.137) | non-fusion elementwise | flops 409600 | bytes 4915200 | tf_op jit(solution)/shard_map/add | solution.py:192
  228.2 42.7 %while.47 = (s32[]{:T(128)}, bf16[10,320,128]{2,1,0:T(8,128)(2,1)}, f32[10,320,128]{2,1,0:T(8,128)}, f32[128]{0:T(128)S(1)}, bf16[128,512]{1,0:T(8,128)(2,1)S(1)}, /*index=5*/bf16[512,128]{1,0:T(8,128)(2,1)S(1)}) while((s32[]{:T(128)}, bf16[10,320,128]{2,1,0:T(8,128)(2,1)}, f32[10,320,128]{2,1,0:T(8,128)}, f32[128]{0:T(128)S(1)}, ...), condition=%wide.region_23.24_spmd.clone, body=%wide.region_20.23_spmd.sunk.clone | while | flops 84582720 | bytes 1094477 | solution.py:199
  230.4 2.1 fusion.229
  234.7 2.1 fusion.229
  239.0 2.1 fusion.229
  243.2 2.1 fusion.229
  247.5 2.1 fusion.229
  251.8 2.1 fusion.229
  256.0 2.1 fusion.229
  260.3 2.1 fusion.229
  264.6 2.1 fusion.229
  268.9 2.1 fusion.229
  (223 shorter events, 70.7 us)
Async XLA Ops:
  7.2 8.2 %copy-start = (bf16[256,4,256]{2,1,0:T(4,128)(2,1)S(1)}, bf16[256,4,256]{2,1,0:T(4,128)(2,1)}, u32[]{:S(2)}) copy-start(bf16[256,4,256]{2,1,0:T(4,128)(2,1)} %param.40) | copy-start | bytes 1572868
  7.2 66.7 %all-gather.3.cloned.1.call-start = ((), (), s32[]{:S(2)}) async-start(), calls=%async_computation.1 | async-start | bytes 2027520 | tf_op jit(solution)/shard_map/all_gather | solution.py:129
  8.8 4.3 %copy-start.5 = (bf16[128,8]{0,1:T(8,128)(2,1)S(1)}, bf16[128,8]{0,1:T(8,128)(2,1)}, u32[]{:S(2)}) copy-start(bf16[128,8]{0,1:T(8,128)(2,1)} %param.38) | copy-start | bytes 6148
  8.8 4.3 %copy-start.10 = (f32[128]{0:T(128)S(1)}, f32[128]{0:T(128)}, u32[]{:S(2)}) copy-start(f32[128]{0:T(128)} %param.37) | copy-start | bytes 1540
  12.0 3.0 %copy-start.6 = (s32[320]{0:T(512)S(1)}, s32[320]{0:T(512)}, u32[]{:S(2)}) copy-start(s32[320]{0:T(512)} %param.34) | copy-start | bytes 3844
  12.0 3.0 %copy-start.2 = (bf16[1,320,256]{2,1,0:T(8,128)(2,1)S(1)}, bf16[1,320,256]{2,1,0:T(8,128)(2,1)}, u32[]{:S(2)}) copy-start(bf16[1,320,256]{2,1,0:T(8,128)(2,1)} %param.31) | copy-start | bytes 491524
  12.0 3.4 %copy-start.7 = (f32[256]{0:T(256)S(1)}, f32[256]{0:T(256)}, u32[]{:S(2)}) copy-start(f32[256]{0:T(256)} %param.39) | copy-start | bytes 3076
  16.9 0.8 copy-start.4
  17.9 60.2 %copy-start.3 = (f32[8,1,320,32]{2,3,1,0:T(8,128)S(1)}, f32[8,1,320,32]{2,3,1,0:T(8,128)}, u32[]{:S(2)}) copy-start(f32[8,1,320,32]{2,3,1,0:T(8,128)} %custom-call) | copy-start | bytes 983044
  95.5 12.0 %all-to-all-start = ((bf16[32,2,1280]{2,1,0:T(2,128)(2,1)}), bf16[32,2,1280]{2,1,0:T(2,128)(2,1)S(1)}, u32[]{:S(2)}, u32[]{:S(2)}) async-start(bf16[32,2,1280]{2,1,0:T(2,128)(2,1)} %reshape.279), calls=%async_computation | async-start | bytes 327680 | tf_op jit(solution)/shard_map/all_to_all | solution.py:137
  100.3 8.9 %copy-start.8 = (f32[256]{0:T(256)S(1)}, f32[256]{0:T(256)}, u32[]{:S(2)}) copy-start(f32[256]{0:T(256)} %param.42) | copy-start | bytes 3076
  115.9 2.1 copy-start.1
  147.9 3.3 %copy-start.9 = (f32[256]{0:T(256)S(1)}, f32[256]{0:T(256)}, u32[]{:S(2)}) copy-start(f32[256]{0:T(256)} %param.45) | copy-start | bytes 3076
  151.2 2.9 %copy-start.14 = (f32[256]{0:T(256)S(1)}, f32[256]{0:T(256)}, u32[]{:S(2)}) copy-start(f32[256]{0:T(256)} %param.48) | copy-start | bytes 3076
  205.3 1.0 copy-start.11
  207.3 0.9 copy-start.11
  209.3 0.9 copy-start.11
  211.3 0.9 copy-start.11
  213.3 0.9 copy-start.11
  215.3 0.9 copy-start.11
  217.3 0.9 copy-start.11
  219.3 0.9 copy-start.11
  221.3 0.9 copy-start.11
  223.3 0.9 copy-start.11
  225.3 2.8 %copy-start.12 = (bf16[128,512]{1,0:T(8,128)(2,1)S(1)}, bf16[128,512]{1,0:T(8,128)(2,1)}, u32[]{:S(2)}) copy-start(bf16[128,512]{1,0:T(8,128)(2,1)} %param.52) | copy-start | bytes 393220
  225.3 2.8 %copy-start.13 = (bf16[512,128]{1,0:T(8,128)(2,1)S(1)}, bf16[512,128]{1,0:T(8,128)(2,1)}, u32[]{:S(2)}) copy-start(bf16[512,128]{1,0:T(8,128)(2,1)} %param.53) | copy-start | bytes 393220
  225.3 2.8 %copy-start.15 = (f32[128]{0:T(128)S(1)}, f32[128]{0:T(128)}, u32[]{:S(2)}) copy-start(f32[128]{0:T(128)} %param.51) | copy-start | bytes 1540
Sparse Core Ops, SparseCore 0:
  15.1 58.7 all-gather.2
where the time goes:
time: 280 us; the launch traced here: 278 us
  matrix products  87.1 us (31%)
  waiting for transfers between devices  63.3 us (23%)
  blocking collectives  41.3 us (15%)
  local copies, waits for them, and re-layouts  34.6 us (12%)
  other arithmetic  32.8 us (12%)
  between operations  14.5 us (5%)
  starting transfers between devices  3.66 us (1%)
    all_gather x1, waiting for transfers between devices, on_device(): full_bias = lax.all_gather(bias_rows, 'dap', axis=1, tiled=True)  56 us
    all_gather x1, blocking collectives, on_device(): piece = lax.all_gather(right, 'dap', axis=0, tiled=True)  41.3 us
    dot_general x14, matrix products, accurate_product(): jnp.einsum('...d,de->...e', former_factor, right, preferred_element_type=...  26.7 us
    dot_general x16, matrix products, one_head(): jnp.einsum('rij,rjc->ric', weights, vh, preferred_element_type=jnp.float32)  17.7 us
    reduce_sum x15, other arithmetic, apply_layer_norm(): spread = jnp.mean(centred * centred, -1, keepdims=True)  13.2 us
    reduce_sum x13, other arithmetic, apply_layer_norm(): centred = input_tensor - jnp.mean(input_tensor, -1, keepdims=True)  11.1 us
    dot_general x10, matrix products, one_res(): jnp.dot(outer, product_exit_factors, preferred_element_type=jnp.float32)  10.5 us
    dot_general x8, matrix products, one_head(): jnp.einsum('ric,rjc->rij', qh, kh, preferred_element_type=jnp.float32)  10.1 us
  transfers between devices with their start and end apart: 2, of which 2 were waited for; matrix products, arithmetic and copies ran while one was open for 1% of the time, Pallas kernels for 0%

commit v1 on v0

v1 whole, which is shorter than its diff:
```python
import functools

import jax
import jax.numpy as jnp
from jax import lax
from jax.experimental import pallas as pl
from jax.experimental.pallas import tpu as pltpu
from jax.sharding import PartitionSpec as P

HEADS = 8
SUB = 8
EPS = 1e-05
OUTER_EPS = 0.001
MASKED = -1000000000.0
LOG2E = 1.4426950408889634
F32 = jnp.float32
BF16 = jnp.bfloat16
VMEM_LIMIT = 56 * 1024 * 1024


def dot(a, b):
    return jnp.dot(a, b, preferred_element_type=F32)


def dot_nt(a, b):
    return lax.dot_general(a, b, (((1,), (1,)), ((), ())), preferred_element_type=F32)


def dot_tn(a, b):
    return lax.dot_general(a, b, (((0,), (0,)), ((), ())), preferred_element_type=F32)


def layer_norm(x, gain):
    centred = x - jnp.mean(x, -1, keepdims=True)
    spread = jnp.mean(centred * centred, -1, keepdims=True)
    return centred * lax.rsqrt(spread + EPS) * gain


def iota(shape, dim):
    return lax.broadcasted_iota(jnp.int32, shape, dim)


def div_const(x, d, limit):
    m = 65536 // d + 1
    assert all((v * m) >> 16 == v // d for v in range(limit)) and limit * m < 2**31
    return (x * m) >> 16


def one_hot(match):
    return jnp.where(match, 1.0, 0.0).astype(BF16)


def chunks(total, step, body):
    if total == step:
        body(0)
    else:
        lax.fori_loop(0, total // step, lambda c, x: (body(pl.multiple_of(c * step, step)), x)[1], 0)


def pair_kernel(
    idx, chain, pair, chain_row, table, gain, factors, pair_one, bias, shifted, chain_wide, *, rows, length, bins
):
    step = pl.program_id(0)
    reach = (bins - 2) // 2

    @pl.when(step == 0)
    def _():
        k = iota((2 * length, bins), 0)
        wanted = jnp.clip(length - k + reach, 0, 2 * reach)
        pick = jnp.where(wanted == iota((2 * length, bins), 1), 1.0, 0.0)
        shifted[...] = jnp.dot(pick, table[...], precision=lax.Precision.HIGHEST, preferred_element_type=F32)
        eye = iota((length, length), 0) == iota((length, length), 1)
        column = jnp.sum(jnp.where(eye, chain_row[...].astype(F32), 0.0), axis=1, keepdims=True)
        chain_wide[...] = jnp.broadcast_to(column, chain_wide.shape)

    other = table[bins - 1 : bins, :]
    block = pair.shape[0]
    for r in range(block):
        i = idx[0] * rows + step * block + r
        near = shifted[pl.ds(length - i, length), :]
        same = chain_wide[...] == chain[i].astype(F32)
        x = pair[r].astype(F32) + jnp.where(same, near, other)
        pair_one[r] = x
        normed = layer_norm(x, gain[...]).astype(BF16)
        bias[r] = dot_nt(factors[...], normed).astype(BF16)


def pair_call(idx, chain, pair, table, gain, factors):
    rows, length, depth = pair.shape
    block = 5 if rows % 5 == 0 else 1
    bins = table.shape[0]
    smem = pl.BlockSpec(memory_space=pltpu.SMEM)
    whole = lambda *shape: pl.BlockSpec(shape, lambda s: (0,) * len(shape))
    return pl.pallas_call(
        functools.partial(pair_kernel, rows=rows, length=length, bins=bins),
        grid=(rows // block,),
        in_specs=[
            smem,
            smem,
            pl.BlockSpec((block, length, depth), lambda s: (s, 0, 0)),
            whole(1, length),
            whole(bins, depth),
            whole(1, depth),
            whole(HEADS, depth),
        ],
        out_specs=[
            pl.BlockSpec((block, length, depth), lambda s: (s, 0, 0)),
            pl.BlockSpec((block, HEADS, length), lambda s: (s, 0, 0)),
        ],
        out_shape=[
            jax.ShapeDtypeStruct((rows, length, depth), F32),
            jax.ShapeDtypeStruct((rows, HEADS, length), BF16),
        ],
        scratch_shapes=[pltpu.VMEM((2 * length, depth), F32), pltpu.VMEM((length, depth), F32)],
        compiler_params=pltpu.CompilerParams(vmem_limit_bytes=VMEM_LIMIT),
        cost_estimate=pl.CostEstimate(flops=4 * rows * length * depth * HEADS, bytes_accessed=4000000, transcendentals=0),
        name="pair_bias",
    )(idx, chain, pair, chain[None, :], table, gain[None, :], factors.T)


def row_kernel(idx, *refs, sub, far, rows, length, width):
    row_refs, refs = refs[:sub], refs[sub:]
    bias_refs, refs = refs[:far], refs[far:]
    validity, amino, gain, entry, exit_, out, keys, values, bias, own_normed, own_rows, query, gate, gated = refs
    me = idx[0]
    z, p = me // sub, me % sub
    own = far * rows
    scale = (width // HEADS) ** -0.5 * LOG2E

    r = iota((own, length), 0)
    block = div_const(r, rows, own)
    residue = ((z ^ block) * sub + p) * rows + r - block * rows
    pick = one_hot(residue == iota((own, length), 1))

    step = min(length, 320)
    for k in range(sub):

        def project(start, k=k):
            normed = layer_norm(row_refs[k][0, pl.ds(start, step), :].astype(F32), gain[...]).astype(BF16)
            both = dot(normed, entry[:, width : 3 * width])
            keys[k, pl.ds(start, step), :] = both[:, :width].astype(BF16)
            values[k, pl.ds(start, step), :] = both[:, width:].astype(BF16)
            part = pick if length == step else one_hot(residue[:, :step] == iota((own, step), 1) + start)
            q_rows, a_rows = dot(part, normed), dot(part, row_refs[k][0, pl.ds(start, step), :])
            here = pl.ds(k * own, own)
            if length == step:
                own_normed[here, :] = q_rows
                own_rows[here, :] = a_rows
            else:
                fresh = start == 0
                own_normed[here, :] = q_rows + jnp.where(fresh, 0.0, own_normed[here, :])
                own_rows[here, :] = a_rows + jnp.where(fresh, 0.0, own_rows[here, :])

        chunks(length, step, project)

    total = sub * own
    part = min(total, 320)

    def queries(start):
        here = pl.ds(start, part)
        normed = own_normed[here, :].astype(BF16)
        query[here, :] = dot(normed, entry[:, :width]) * scale
        gate[here, :] = jax.nn.sigmoid(dot(normed, entry[:, 3 * width :]))

    chunks(total, part, queries)

    for b in range(far):
        bias[b * rows : (b + 1) * rows] = bias_refs[b][...].astype(F32) * LOG2E

    head_of = iota((HEADS, width), 1) // (width // HEADS)
    head_mask = jnp.where(head_of == iota((HEADS, width), 0), 1.0, 0.0)
    take = 40 if own % 40 == 0 else rows

    def attend(n, k, start):
        s = z * sub + (p ^ k)
        valid = validity[pl.ds(s, 1), :] * amino[...]
        masked = jnp.where(valid > 0, 0.0, MASKED)
        here = pl.ds(pl.multiple_of(n * take, take), take) if not isinstance(n, int) else pl.ds(n * take, take)
        q = (query[here, :][:, None, :] * head_mask[None]).reshape(take * HEADS, width).astype(BF16)
        scores = dot_nt(q, keys[k]) + bias[pl.ds(start, take)].reshape(take * HEADS, length) + masked
        expo = jnp.exp2(scores - jnp.max(scores, -1, keepdims=True))
        total_ = jnp.sum(expo, -1, keepdims=True)
        mixed = dot(expo.astype(BF16), values[k]) / total_
        merged = jnp.sum(mixed.reshape(take, HEADS, width) * head_mask[None], axis=1)
        gated[here, :] = merged * gate[here, :]

    parts = own // take
    if parts == 1:
        for k in range(sub):
            attend(k, k, 0)
    else:
        lax.fori_loop(0, sub * parts, lambda n, x: (attend(n, n // parts, (n % parts) * take), x)[1], 0)

    def leave(start):
        q = iota((part, total), 0) + start
        residue_, row = div_const(q, sub, total), q & (sub - 1)
        swap = one_hot((row ^ p) * own + residue_ == iota((part, total), 1))
        gated_rows = dot(swap, gated[...].astype(BF16)).astype(BF16)
        x = dot(swap, own_rows[...].astype(BF16)) + dot(gated_rows, exit_[...])
        out[pl.ds(start, part), :] = x.astype(BF16)

    chunks(total, part, leave)


def row_call(idx, msa_rows, bias_blocks, validity, amino, gain, entry, exit_):
    sub, far = len(msa_rows), len(bias_blocks)
    _, length, width = msa_rows[0].shape
    rows = bias_blocks[0].shape[0]
    own = far * rows
    vmem = pl.BlockSpec(memory_space=pltpu.VMEM)
    return pl.pallas_call(
        functools.partial(row_kernel, sub=sub, far=far, rows=rows, length=length, width=width),
        in_specs=[pl.BlockSpec(memory_space=pltpu.SMEM)] + [vmem] * (sub + far + 5),
        out_specs=vmem,
        out_shape=jax.ShapeDtypeStruct((own * sub, width), BF16),
        scratch_shapes=[
            pltpu.VMEM((sub, length, width), BF16),
            pltpu.VMEM((sub, length, width), BF16),
            pltpu.VMEM((own, HEADS, length), F32),
            pltpu.VMEM((sub * own, width), F32),
            pltpu.VMEM((sub * own, width), F32),
            pltpu.VMEM((sub * own, width), F32),
            pltpu.VMEM((sub * own, width), F32),
            pltpu.VMEM((sub * own, width), F32),
        ],
        compiler_params=pltpu.CompilerParams(vmem_limit_bytes=VMEM_LIMIT),
        cost_estimate=pl.CostEstimate(flops=10**10, bytes_accessed=4000000, transcendentals=10**6),
        name="row_attention",
    )(idx, *msa_rows, *bias_blocks, validity, amino[None, :], gain[None, :], entry, exit_)


def column_kernel(idx, *refs, sub, far, rows, block, depth, width):
    piece_refs, refs = refs[:far], refs[far:]
    (
        validity,
        col_gain,
        entry,
        exit_,
        ff_gain,
        widen,
        narrow,
        product_gain,
        twin,
        updated,
        left,
        right,
        start_rows,
        gated,
    ) = refs
    me = idx[0]
    z = me // sub
    first = me * rows + pl.program_id(0) * block
    scale = (width // HEADS) ** -0.5 * LOG2E
    total = block * depth
    for b in range(far):
        here = pl.ds(pl.multiple_of((z ^ b) * sub, sub), sub)
        start_rows[:, here, :] = piece_refs[b][...].astype(F32)
    x = start_rows[...].reshape(total, width)
    normed = layer_norm(x, col_gain[...]).astype(BF16)
    proj = dot(normed, entry[...])
    query = proj[:, :width] * scale
    keys = proj[:, width : 2 * width].astype(BF16)
    values = proj[:, 2 * width : 3 * width].astype(BF16)
    gate = jax.nn.sigmoid(proj[:, 3 * width :])

    length = validity.shape[1]
    lanes = 128
    pick = one_hot(iota((length, lanes), 0) == first + iota((length, lanes), 1))
    valid = dot(validity[...].astype(F32).astype(BF16), pick)
    head_of = iota((HEADS, width), 1) // (width // HEADS)
    head_mask = jnp.where(head_of == iota((HEADS, width), 0), 1.0, 0.0)
    for i in range(block):
        here = slice(i * depth, (i + 1) * depth)
        q = (query[here][:, None, :] * head_mask[None]).reshape(depth * HEADS, width).astype(BF16)
        masked = jnp.where(valid[:, i : i + 1] > 0, 0.0, MASKED)
        scores = dot_nt(keys[here], q) + masked
        expo = jnp.exp2(scores - jnp.max(scores, 0, keepdims=True))
        weights = (expo / jnp.sum(expo, 0, keepdims=True)).astype(BF16)
        mixed = dot_tn(weights, values[here])
        merged = jnp.sum(mixed.reshape(depth, HEADS, width) * head_mask[None], axis=1)
        gated[here, :] = merged * gate[here]
    x = x + dot(gated[...].astype(BF16), exit_[...])
    hidden = jnp.maximum(dot(layer_norm(x, ff_gain[...]).astype(BF16), widen[...]), 0.0).astype(BF16)
    x = x + dot(hidden, narrow[...])
    updated[...] = x.astype(BF16).reshape(block, depth, width)
    outer = layer_norm(x, product_gain[...]).astype(BF16)
    both = dot(outer, twin[...])
    channels = twin.shape[1] // 2
    spread = iota((depth, channels * depth), 1)
    channel = spread // depth
    repeat = one_hot(
        iota((2 * channels, channels * depth), 0) - channels == iota((2 * channels, channels * depth), 1) // depth
    )
    mine = jnp.where(spread - channel * depth == iota((depth, channels * depth), 0), 1.0, 0.0)
    for i in range(block):
        here = slice(i * depth, (i + 1) * depth)
        part = (both[here] * valid[:, i : i + 1]).astype(BF16)
        left[here, :] = part[:, :channels]
        right[i : i + 1, :] = jnp.sum(dot(part, repeat) * mine, axis=0, keepdims=True).astype(BF16)


def column_call(idx, pieces, validity, col_gain, entry, exit_, ff_gain, widen, narrow, product_gain, twin):
    far = len(pieces)
    rows, sub, width = pieces[0].shape
    depth, length = validity.shape
    block = rows
    while block * depth > 320 and block % 2 == 0:
        block //= 2
    channels = twin.shape[1] // 2
    vmem = lambda a: pl.BlockSpec(a.shape, lambda s: (0,) * a.ndim)
    rest = [
        validity,
        col_gain[None, :],
        entry,
        exit_,
        ff_gain[None, :],
        widen,
        narrow,
        product_gain[None, :],
        twin,
    ]
    return pl.pallas_call(
        functools.partial(column_kernel, sub=sub, far=far, rows=rows, block=block, depth=depth, width=width),
        grid=(rows // block,),
        in_specs=[pl.BlockSpec(memory_space=pltpu.SMEM)]
        + [pl.BlockSpec((block, sub, width), lambda s: (s, 0, 0))] * far
        + [vmem(a) for a in rest],
        out_specs=[
            pl.BlockSpec((block, depth, width), lambda s: (s, 0, 0)),
            pl.BlockSpec((block * depth, channels), lambda s: (s, 0)),
            pl.BlockSpec((None, block, channels * depth), lambda s: (s, 0, 0)),
        ],
        out_shape=[
            jax.ShapeDtypeStruct((rows, depth, width), BF16),
            jax.ShapeDtypeStruct((rows * depth, channels), BF16),
            jax.ShapeDtypeStruct((rows // block, block, channels * depth), BF16),
        ],
        scratch_shapes=[pltpu.VMEM((block, depth, width), F32), pltpu.VMEM((block * depth, width), F32)],
        compiler_params=pltpu.CompilerParams(vmem_limit_bytes=VMEM_LIMIT),
        cost_estimate=pl.CostEstimate(flops=10**10, bytes_accessed=4000000, transcendentals=10**6),
        name="column_attention",
    )(idx, *pieces, *rest)


def mix_kernel(left, factors, out, *, rows, depth):
    lanes = factors.shape[2]
    for e in range(factors.shape[0]):
        y = dot(left[...], factors[e]).astype(BF16)
        for i in range(rows):
            out[e * depth : (e + 1) * depth, i * lanes : (i + 1) * lanes] = y[i * depth : (i + 1) * depth]


def mix_call(left, factors, rows):
    total, channels = left.shape
    depth = total // rows
    lanes = factors.shape[2]
    block = 8
    return pl.pallas_call(
        functools.partial(mix_kernel, rows=rows, depth=depth),
        grid=(channels // block,),
        in_specs=[
            pl.BlockSpec((total, channels), lambda s: (0, 0)),
            pl.BlockSpec((block, channels, lanes), lambda s: (s, 0, 0)),
        ],
        out_specs=pl.BlockSpec((block * depth, rows * lanes), lambda s: (s, 0)),
        out_shape=jax.ShapeDtypeStruct((channels * depth, rows * lanes), BF16),
        compiler_params=pltpu.CompilerParams(vmem_limit_bytes=VMEM_LIMIT),
        cost_estimate=pl.CostEstimate(flops=10**9, bytes_accessed=4000000, transcendentals=0),
        name="left_mix",
    )(left, factors)


def finish_kernel(
    idx, near, across, mixed, pair_one, validity, gain, widen, narrow, out, right, turned, *, sub, far, rows, length, block
):
    me = idx[0]
    z, p = me // sub, me % sub
    step = pl.program_id(0)
    half = near.shape[0]
    lanes = pair_one.shape[2]
    part = min(length, 320)

    @pl.when(step == 0)
    def _():
        r = iota((part, half), 1)
        b = div_const(r, rows, half)
        i = r - b * rows
        across_sub, across_far = (b // far) * 2, b % far
        home = ((z ^ across_far) * sub + (p ^ across_sub)) * rows + i
        away = ((z ^ across_far) * sub + (p ^ 1 ^ across_sub)) * rows + i

        def arrange(start):
            j = iota((part, half), 0) + start
            here = pl.ds(start, part)
            right[here, :] = (dot(one_hot(j == home), near[...]) + dot(one_hot(j == away), across[...])).astype(BF16)

        chunks(length, part, arrange)
        turned[...] = validity[...].astype(F32).T.astype(BF16)

    i0 = me * rows + step * block
    target = i0 + iota((length, block * lanes), 1) // lanes
    mine = one_hot(iota((length, block * lanes), 0) == target)
    mine = dot(validity[...].astype(F32).astype(BF16), mine).astype(BF16)

    def finish(start):
        here = pl.ds(start, part)
        counts = dot(turned[here, :], mine) + OUTER_EPS
        update = dot(right[here, :], mixed[...]) / counts
        for r in range(block):
            x = pair_one[r, here, :] + update[:, r * lanes : (r + 1) * lanes]
            normed = layer_norm(x, gain[...]).astype(BF16)
            hidden = jnp.maximum(dot(normed, widen[...]), 0.0).astype(BF16)
            out[r, here, :] = (x + dot(hidden, narrow[...])).astype(BF16)

    chunks(length, part, finish)


def finish_call(idx, near, across, mixed, pair_one, validity, gain, widen, narrow, sub, far):
    rows, length, lanes = pair_one.shape
    depth = validity.shape[0]
    block = 2 if rows % 2 == 0 else 1
    product = mixed.shape[0]
    vmem = lambda a: pl.BlockSpec(a.shape, lambda s: (0,) * a.ndim)
    gain = gain[None, :]
    return pl.pallas_call(
        functools.partial(finish_kernel, sub=sub, far=far, rows=rows, length=length, block=block),
        grid=(rows // block,),
        in_specs=[
            pl.BlockSpec(memory_space=pltpu.SMEM),
            vmem(near),
            vmem(across),
            pl.BlockSpec((product, block * lanes), lambda s: (0, s)),
            pl.BlockSpec((block, length, lanes), lambda s: (s, 0, 0)),
            vmem(validity),
            vmem(gain),
            vmem(widen),
            vmem(narrow),
        ],
        out_specs=pl.BlockSpec((block, length, lanes), lambda s: (s, 0, 0)),
        out_shape=jax.ShapeDtypeStruct((rows, length, lanes), BF16),
        scratch_shapes=[pltpu.VMEM((length, product), BF16), pltpu.VMEM((length, depth), BF16)],
        compiler_params=pltpu.CompilerParams(vmem_limit_bytes=VMEM_LIMIT),
        cost_estimate=pl.CostEstimate(flops=10**10, bytes_accessed=4000000, transcendentals=0),
        name="pair_update",
    )(idx, near, across, mixed, pair_one, validity, gain, widen, narrow)


def on_device(
    devices,
    alignment_embedding,
    couple_embedding,
    amino_strand,
    amino_validity,
    alignment_validity,
    separation_embedding,
    couple_shift_scaling,
    couple_shift_factors,
    horizontal_scaling_factor,
    horizontal_entry_factors,
    horizontal_exit_factors,
    vertical_scaling_factor,
    vertical_entry_factors,
    vertical_exit_factors,
    alignment_feedforward_scaling,
    alignment_widen_factors,
    alignment_narrow_factors,
    product_scaling_factor,
    product_twin_factors,
    product_exit_factors,
    couple_feedforward_scaling,
    couple_widen_factors,
    couple_narrow_factors,
):
    far = devices // SUB
    idx = lax.axis_index("dap").astype(jnp.int32).reshape(1)

    def swap(x, distance):
        return lax.ppermute(x, "dap", [(d, d ^ distance) for d in range(devices)])

    width = alignment_embedding.shape[2]
    rows = couple_embedding.shape[0]
    depth = alignment_validity.shape[0]

    msa_rows = [alignment_embedding] * SUB
    for k in range(2, SUB, 2):
        msa_rows[k] = swap(alignment_embedding, k)
    for k in range(0, SUB, 2):
        msa_rows[k + 1] = swap(msa_rows[k], 1)

    pair_one, bias = pair_call(
        idx, amino_strand, couple_embedding, separation_embedding, couple_shift_scaling, couple_shift_factors
    )
    bias_blocks = [bias] + [swap(bias, SUB * k) for k in range(1, far)]
    sent = row_call(
        idx,
        msa_rows,
        bias_blocks,
        alignment_validity,
        amino_validity,
        horizontal_scaling_factor,
        horizontal_entry_factors.reshape(width, 4 * width),
        horizontal_exit_factors,
    ).reshape(far, rows, SUB, width)
    pieces = [sent[0]] + [swap(sent[k], SUB * k) for k in range(1, far)]
    updated, left, right = column_call(
        idx,
        pieces,
        alignment_validity,
        vertical_scaling_factor,
        vertical_entry_factors.reshape(width, 4 * width),
        vertical_exit_factors,
        alignment_feedforward_scaling,
        alignment_widen_factors,
        alignment_narrow_factors,
        product_scaling_factor,
        product_twin_factors,
    )
    channels = left.shape[1]
    right = right.reshape(rows, channels * depth)
    column = jnp.concatenate([right] + [swap(right, SUB * k) for k in range(1, far)], 0)
    near = jnp.concatenate([column] + [swap(column, k) for k in range(2, SUB, 2)], 0)
    across = swap(near, 1)
    factors = product_exit_factors.reshape(channels, channels, -1).transpose(1, 0, 2)
    mixed = mix_call(left, factors, rows)
    updated_pairs = finish_call(
        idx,
        near,
        across,
        mixed,
        pair_one,
        alignment_validity,
        couple_feedforward_scaling,
        couple_widen_factors,
        couple_narrow_factors,
        SUB,
        far,
    )
    return updated.transpose(1, 0, 2), updated_pairs


def solution(mesh):
    split = P("dap", None, None)
    return jax.shard_map(
        functools.partial(on_device, mesh.shape["dap"]),
        mesh=mesh,
        in_specs=(split, split) + (P(),) * 21,
        out_specs=(P(None, "dap", None), split),
        check_vma=False,
    )
```

time: 280 us -> 91.3 us (0.33)
  matrix products: 87.1 us -> 0 us
  blocking collectives: 41.3 us -> 0 us
  waiting for transfers between devices: 63.3 us -> 25.4 us
  other arithmetic: 32.8 us -> 0.8 us
  Pallas kernels: 0 us -> 30.3 us
  local copies, waits for them, and re-layouts: 34.6 us -> 11.6 us
  starting transfers between devices: 3.66 us -> 21.6 us
  between operations: 14.5 us -> 0.79 us
    dot_general x63 -> x0, matrix products: 78 us -> none  [the longest x14 26.7 us: accurate_product(): jnp.einsum('...d,de->...e', former_factor, right, preferred_element_type=...]
    all_gather x1 -> x0, waiting for transfers between devices: 56 us -> none  [on_device(): full_bias = lax.all_gather(bias_rows, 'dap', axis=1, tiled=True)]
    all_gather x1 -> x0, blocking collectives: 41.3 us -> none  [on_device(): piece = lax.all_gather(right, 'dap', axis=0, tiled=True)]
    pallas_call x0 -> x5, Pallas kernels: none -> 30.3 us  [the longest x1 9.46 us: finish_call(): pl.pallas_call(functools.partial(finish_kernel, sub=sub, far=far, rows=ro...]
    ppermute x0 -> x20, waiting for transfers between devices: none -> 25.4 us  [swap(): return lax.ppermute(x, 'dap', [(d, d ^ distance) for d in range(devices)])]
    reduce_sum x36 -> x0, other arithmetic: 25.2 us -> none  [the longest x15 13.2 us: apply_layer_norm(): spread = jnp.mean(centred * centred, -1, keepdims=True)]
    ppermute x0 -> x20, starting transfers between devices: none -> 21.6 us  [swap(): return lax.ppermute(x, 'dap', [(d, d ^ distance) for d in range(devices)])]
    while x22 -> x0, local copies, waits for them, and re-layouts: 12.2 us -> none  [the longest x1 5.5 us: on_device(): update = lax.map(one_res, (former_factor, counts))]
  transfers between devices with their start and end apart: 2 -> 20, of which waited for: 2 -> 12; matrix products, arithmetic and copies ran while one was open for 1% -> 8% of each run, Pallas kernels for 0% -> 8%
where the time goes in v1:
time: 91.3 us; the launch traced here: 90.5 us
  Pallas kernels  30.3 us (33%)
  waiting for transfers between devices  25.4 us (28%)
  starting transfers between devices  21.6 us (24%)
  local copies, waits for them, and re-layouts  11.6 us (13%)
    ppermute x20, waiting for transfers between devices, swap(): return lax.ppermute(x, 'dap', [(d, d ^ distance) for d in range(devices)])  25.4 us
    ppermute x20, starting transfers between devices, swap(): return lax.ppermute(x, 'dap', [(d, d ^ distance) for d in range(devices)])  21.6 us
    pallas_call x1, Pallas kernels, finish_call(): pl.pallas_call(functools.partial(finish_kernel, sub=sub, far=far, rows=ro...  9.46 us
    pallas_call x1, Pallas kernels, row_call(): pl.pallas_call(functools.partial(row_kernel, sub=sub, far=far, rows=rows,...  7.54 us
    pallas_call x1, Pallas kernels, column_call(): pl.pallas_call(functools.partial(column_kernel, sub=sub, far=far, rows=ro...  5.71 us
    unnamed x39, local copies, waits for them, and re-layouts  5.67 us
    pallas_call x1, Pallas kernels, mix_call(): pl.pallas_call(functools.partial(mix_kernel, rows=rows, depth=depth), gri...  4.07 us
    pallas_call x1, Pallas kernels, pair_call(): pl.pallas_call(functools.partial(pair_kernel, rows=rows, length=length, b...  3.5 us
  transfers between devices with their start and end apart: 20, of which 12 were waited for; matrix products, arithmetic and copies ran while one was open for 8% of the time, Pallas kernels for 8%

profile of v1, /device:TPU:0, one launch (start us, length us, event | category | flops | bytes accessed | tf_op | source)
XLA Modules:
  0.0 90.5 jit_solution(3866946766160703958)
XLA Ops:
  0.6 3.0 %collective-permute-start.3 = (bf16[1,320,256]{2,1,0:T(8,128)(2,1)}, bf16[1,320,256]{2,1,0:T(8,128)(2,1)S(1)}, u32[]{:S(2)}, u32[]{:S(2)}) collective-permute-start(bf16[1,320,256]{2,1,0:T(8,128)(2,1)} %refs_0_.1), channel_id=1, source_target_pairs={{0,4},{1,5},{2,6},{3,7},{4,0},{5,1},{6,2},{7,3},{8,12},{9,13},{10,... | collective-permute-start | bytes 491528 | tf_op jit(solution)/shard_map/ppermute | solution.py:478
  3.7 1.5 %collective-permute-start.1 = (bf16[1,320,256]{2,1,0:T(8,128)(2,1)}, bf16[1,320,256]{2,1,0:T(8,128)(2,1)S(1)}, u32[]{:S(2)}, u32[]{:S(2)}) collective-permute-start(bf16[1,320,256]{2,1,0:T(8,128)(2,1)} %refs_0_.1), channel_id=1, source_target_pairs={{0,2},{1,3},{2,0},{3,1},{4,6},{5,7},{6,4},{7,5},{8,10},{9,11},{10,... | collective-permute-start | bytes 491528 | tf_op jit(solution)/shard_map/ppermute | solution.py:478
  5.2 0.1 collective-permute-start.5
  5.2 2.9 %collective-permute-done.3.refs_4_ = bf16[1,320,256]{2,1,0:T(8,128)(2,1)S(1)} collective-permute-done((bf16[1,320,256]{2,1,0:T(8,128)(2,1)}, bf16[1,320,256]{2,1,0:T(8,128)(2,1)S(1)}, u32[]{:S(2)}, u32[]{:S(2)}) %collective-permute-start.3) | collective-permute-done | bytes 163872 | tf_op jit(solution)/shard_map/ppermute | solution.py:478
  8.1 2.9 %collective-permute-done.1.refs_2_ = bf16[1,320,256]{2,1,0:T(8,128)(2,1)S(1)} collective-permute-done((bf16[1,320,256]{2,1,0:T(8,128)(2,1)}, bf16[1,320,256]{2,1,0:T(8,128)(2,1)S(1)}, u32[]{:S(2)}, u32[]{:S(2)}) %collective-permute-start.1) | collective-permute-done | bytes 163872 | tf_op jit(solution)/shard_map/ppermute | solution.py:478
  11.0 1.8 %collective-permute-done.5.refs_6_ = bf16[1,320,256]{2,1,0:T(8,128)(2,1)S(1)} collective-permute-done((bf16[1,320,256]{2,1,0:T(8,128)(2,1)}, bf16[1,320,256]{2,1,0:T(8,128)(2,1)S(1)}, u32[]{:S(2)}, u32[]{:S(2)}) %collective-permute-start.5) | collective-permute-done | bytes 163872 | tf_op jit(solution)/shard_map/ppermute | solution.py:478
  12.8 1.3 %broadcast_in_dim.24.chain_row = s32[1,320]{1,0:T(1,128)} reshape(s32[320]{0:T(512)} %chain.1) | data formatting | bytes 2560 | tf_op jit(solution)/shard_map/broadcast_in_dim | solution.py:118
  14.1 3.5 %pair_bias.1 = (f32[10,320,128]{2,1,0:T(8,128)}, bf16[10,8,320]{2,1,0:T(8,128)(2,1)}) custom-call(s32[1]{0:T(128)} %bitcast.idx, s32[320]{0:T(512)} %chain.1, bf16[10,320,128]{2,1,0:T(8,128)(2,1)} %pair.1, s32[1,320]{1,0:T(1,128)} %broadcast_in_dim.24.chain_row, f32[66,128]{1,0:T(8,128)} %table.1, f32[1,128]{1,0:T(1,128)} %bitcast.38, bf16[8,128]{1,0:T(8,128)(2,1)} %bitcast.37), custom_call_target="tpu_custom_call" | custom-call | flops 13107200 | bytes 4000000 | tf_op jit(solution)/shard_map/pair_bias/pallas_call | solution.py:94
  17.6 3.8 %collective-permute-start.9 = (bf16[10,8,320]{2,1,0:T(8,128)(2,1)}, bf16[10,8,320]{2,1,0:T(8,128)(2,1)S(1)}, u32[]{:S(2)}, u32[]{:S(2)}) collective-permute-start(bf16[10,8,320]{2,1,0:T(8,128)(2,1)} %get-tuple-element.7.refs_8_), channel_id=1, source_target_pairs={{0,24},{1,25},{2,26},{3,27},{4,28},{5,29},{6,30},{7,31},{8,16},{9,... | collective-permute-start | bytes 153608 | tf_op jit(solution)/shard_map/ppermute | solution.py:478
  21.4 3.0 %collective-permute-done.9.refs_11_ = bf16[10,8,320]{2,1,0:T(8,128)(2,1)S(1)} collective-permute-done((bf16[10,8,320]{2,1,0:T(8,128)(2,1)}, bf16[10,8,320]{2,1,0:T(8,128)(2,1)S(1)}, u32[]{:S(2)}, u32[]{:S(2)}) %collective-permute-start.9) | collective-permute-done | bytes 51232 | tf_op jit(solution)/shard_map/ppermute | solution.py:478
  24.3 0.6 collective-permute-start.8
  25.0 5.5 %collective-permute-done.8.refs_10_ = bf16[10,8,320]{2,1,0:T(8,128)(2,1)S(1)} collective-permute-done((bf16[10,8,320]{2,1,0:T(8,128)(2,1)}, bf16[10,8,320]{2,1,0:T(8,128)(2,1)S(1)}, u32[]{:S(2)}, u32[]{:S(2)}) %collective-permute-start.8) | collective-permute-done | bytes 51232 | tf_op jit(solution)/shard_map/ppermute | solution.py:478
  30.5 0.3 collective-permute-start.7
  30.8 1.3 %broadcast_in_dim.26.refs_13_ = s32[1,320]{1,0:T(1,128)} reshape(s32[320]{0:T(512)} %param.26) | data formatting | bytes 2560 | tf_op jit(solution)/shard_map/broadcast_in_dim | solution.py:229
  32.0 1.9 %copy.28 = bf16[32,8,4,256]{3,1,2,0:T(8,128)(2,1)} copy(bf16[32,8,4,256]{3,2,1,0:T(4,128)(2,1)} %bitcast.26) | data formatting | bytes 1048576
  34.0 1.0 %collective-permute-done.7.refs_9_ = bf16[10,8,320]{2,1,0:T(8,128)(2,1)S(1)} collective-permute-done((bf16[10,8,320]{2,1,0:T(8,128)(2,1)}, bf16[10,8,320]{2,1,0:T(8,128)(2,1)S(1)}, u32[]{:S(2)}, u32[]{:S(2)}) %collective-permute-start.7) | collective-permute-done | bytes 51232 | tf_op jit(solution)/shard_map/ppermute | solution.py:478
  35.0 0.5 copy-done.14
  35.5 0.1 copy-done.8
  35.6 0.0 copy-done.9
  35.7 0.1 copy-done.10
  35.7 0.0 copy-done.11
  35.8 7.5 %row_attention.1 = bf16[320,256]{1,0:T(8,128)(2,1)} custom-call(s32[1]{0:T(128)} %bitcast.idx, bf16[1,320,256]{2,1,0:T(8,128)(2,1)} %refs_0_.1, bf16[1,320,256]{2,1,0:T(8,128)(2,1)} %copy-done.8, bf16[1,320,256]{2,1,0:T(8,128)(2,1)} %copy-done.6, bf16[1,320,256]{2,1,0:T(8,128)(2,1)} %copy-done.10, bf16[1,320,256]{2,1,0:T(8,128)(2,1)} %copy-done.5, ...), custom_call_target="tpu_custom_call" | custom-call | flops 10000000000 | bytes 4000000 | tf_op jit(solution)/shard_map/row_attention/pallas_call | solution.py:211
  43.3 1.5 %slice_bitcast_fusion = (bf16[10,8,256]{2,1,0:T(8,128)(2,1)S(1)}, bf16[10,8,256]{2,1,0:T(8,128)(2,1)S(1)}, bf16[10,8,256]{2,1,0:T(8,128)(2,1)S(1)}, bf16[10,8,256]{2,1,0:T(8,128)(2,1)}) fusion(bf16[320,256]{1,0:T(8,128)(2,1)} %row_attention.1), kind=kLoop, calls=%fused_computation.2 | loop fusion | bytes 327680 | tf_op jit(solution)/shard_map/squeeze | solution.py:504
  44.8 2.6 %collective-permute-start.12 = (bf16[10,8,256]{2,1,0:T(8,128)(2,1)S(1)}, bf16[10,8,256]{2,1,0:T(8,128)(2,1)S(1)}, u32[]{:S(2)}, u32[]{:S(2)}) collective-permute-start(bf16[10,8,256]{2,1,0:T(8,128)(2,1)S(1)} %get-tuple-element.12), channel_id=1, source_target_pairs={{0,24},{1,25},{2,26},{3,27},{4,28},{5,29},{6,30},{7,31},{8,16},{9,... | collective-permute-start | bytes 122888 | tf_op jit(solution)/shard_map/ppermute | solution.py:478
  47.4 1.8 %collective-permute-start.10 = (bf16[10,8,256]{2,1,0:T(8,128)(2,1)S(1)}, bf16[10,8,256]{2,1,0:T(8,128)(2,1)S(1)}, u32[]{:S(2)}, u32[]{:S(2)}) collective-permute-start(bf16[10,8,256]{2,1,0:T(8,128)(2,1)S(1)} %get-tuple-element.14), channel_id=1, source_target_pairs={{0,8},{1,9},{2,10},{3,11},{4,12},{5,13},{6,14},{7,15},{8,0},{9,1},... | collective-permute-start | bytes 122888 | tf_op jit(solution)/shard_map/ppermute | solution.py:478
  49.2 0.7 copy.26.refs_12_
  49.9 0.9 copy.29
  50.8 1.5 %collective-permute-done.11.refs_2_ = bf16[10,8,256]{2,1,0:T(8,128)(2,1)S(1)} collective-permute-done((bf16[10,8,256]{2,1,0:T(8,128)(2,1)S(1)}, bf16[10,8,256]{2,1,0:T(8,128)(2,1)S(1)}, u32[]{:S(2)}, u32[]{:S(2)}) %collective-permute-start.11) | collective-permute-done | bytes 40992 | tf_op jit(solution)/shard_map/ppermute | solution.py:478
  52.3 0.6 copy-done.16
  52.9 5.7 %column_attention.1 = (bf16[10,32,256]{2,1,0:T(8,128)(2,1)}, bf16[320,32]{1,0:T(8,128)(2,1)}, bf16[1,10,1024]{2,1,0:T(8,128)(2,1)}) custom-call(s32[1]{0:T(128)} %bitcast.idx, bf16[10,8,256]{2,1,0:T(8,128)(2,1)} %get-tuple-element.15.refs_0_, bf16[10,8,256]{2,1,0:T(8,128)(2,1)} %copy-done.17, bf16[10,8,256]{2,1,0:T(8,128)(2,1)} %copy-done.16, ...), custom_call_target="tpu_custom_call" | custom-call | flops 10000000000 | bytes 4000000 | tf_op jit(solution)/shard_map/column_attention/pallas_call | solution.py:322
  58.6 1.9 %collective-permute-start.15 = (bf16[10,1024]{1,0:T(8,128)(2,1)}, bf16[10,1024]{1,0:T(8,128)(2,1)S(1)}, u32[]{:S(2)}, u32[]{:S(2)}) collective-permute-start(bf16[10,1024]{1,0:T(8,128)(2,1)} %bitcast.32), channel_id=1, source_target_pairs={{0,24},{1,25},{2,26},{3,27},{4,28},{5,29},{6,30},{7,31},{8,16},{9,... | collective-permute-start | bytes 61448 | tf_op jit(solution)/shard_map/ppermute | solution.py:478
  60.5 0.4 collective-permute-start.14
  61.0 2.1 %collective-permute-start.13 = (bf16[10,1024]{1,0:T(8,128)(2,1)}, bf16[10,1024]{1,0:T(8,128)(2,1)S(1)}, u32[]{:S(2)}, u32[]{:S(2)}) collective-permute-start(bf16[10,1024]{1,0:T(8,128)(2,1)} %bitcast.34), channel_id=1, source_target_pairs={{0,8},{1,9},{2,10},{3,11},{4,12},{5,13},{6,14},{7,15},{8,0},{9,1},... | collective-permute-start | bytes 61448 | tf_op jit(solution)/shard_map/ppermute | solution.py:478
  63.0 1.5 %collective-permute-done.15 = bf16[10,1024]{1,0:T(8,128)(2,1)S(1)} collective-permute-done((bf16[10,1024]{1,0:T(8,128)(2,1)}, bf16[10,1024]{1,0:T(8,128)(2,1)S(1)}, u32[]{:S(2)}, u32[]{:S(2)}) %collective-permute-start.15) | collective-permute-done | bytes 20512 | tf_op jit(solution)/shard_map/ppermute | solution.py:478
  64.6 1.3 %collective-permute-done.14 = bf16[10,1024]{1,0:T(8,128)(2,1)S(1)} collective-permute-done((bf16[10,1024]{1,0:T(8,128)(2,1)}, bf16[10,1024]{1,0:T(8,128)(2,1)S(1)}, u32[]{:S(2)}, u32[]{:S(2)}) %collective-permute-start.14) | collective-permute-done | bytes 20512 | tf_op jit(solution)/shard_map/ppermute | solution.py:478
  65.9 0.8 pad_maximum_fusion
  66.7 2.5 %collective-permute-start.18 = (bf16[40,1024]{1,0:T(8,128)(2,1)S(1)}, bf16[40,1024]{1,0:T(8,128)(2,1)S(1)}, u32[]{:S(2)}, u32[]{:S(2)}) collective-permute-start(bf16[40,1024]{1,0:T(8,128)(2,1)S(1)} %pad_maximum_fusion), channel_id=1, source_target_pairs={{0,6},{1,7},{2,4},{3,5},{4,2},{5,3},{6,0},{7,1},{8,14},{9,15},{10,... | collective-permute-start | bytes 245768 | tf_op jit(solution)/shard_map/ppermute | solution.py:478
  69.2 0.5 collective-permute-start.17
  69.8 0.5 collective-permute-start.16
  70.3 1.9 %collective-permute-done.18 = bf16[40,1024]{1,0:T(8,128)(2,1)S(1)} collective-permute-done((bf16[40,1024]{1,0:T(8,128)(2,1)S(1)}, bf16[40,1024]{1,0:T(8,128)(2,1)S(1)}, u32[]{:S(2)}, u32[]{:S(2)}) %collective-permute-start.18) | collective-permute-done | bytes 81952 | tf_op jit(solution)/shard_map/ppermute | solution.py:478
  72.1 1.6 %collective-permute-done.17 = bf16[40,1024]{1,0:T(8,128)(2,1)S(1)} collective-permute-done((bf16[40,1024]{1,0:T(8,128)(2,1)S(1)}, bf16[40,1024]{1,0:T(8,128)(2,1)S(1)}, u32[]{:S(2)}, u32[]{:S(2)}) %collective-permute-start.17) | collective-permute-done | bytes 81952 | tf_op jit(solution)/shard_map/ppermute | solution.py:478
  73.7 0.5 collective-permute-done.16
  74.2 1.2 %concatenate.8.near = bf16[160,1024]{1,0:T(8,128)(2,1)S(1)} concatenate(bf16[10,1024]{1,0:T(8,128)(2,1)} %bitcast.36, bf16[10,1024]{1,0:T(8,128)(2,1)S(1)} %collective-permute-done.13, bf16[10,1024]{1,0:T(8,128)(2,1)S(1)} %collective-permute-done.14, bf16[10,1024]{1,0:T(8,128)(2,1)S(1)} %collective-permute-done.15, bf16[40,1024]{1,0:T(8,128)(2,1)S(1)} %collective-permute-done.16, ...), dimensions={0} | concatenate | bytes 655360 | tf_op jit(solution)/shard_map/concatenate | solution.py:521
  75.4 0.1 collective-permute-start.19
  75.5 0.8 copy.31
  76.3 4.1 %left_mix.1.mixed = bf16[1024,1280]{1,0:T(8,128)(2,1)} custom-call(bf16[320,32]{1,0:T(8,128)(2,1)} %get-tuple-element.10.left, bf16[32,32,128]{2,1,0:T(8,128)(2,1)} %bitcast.31), custom_call_target="tpu_custom_call" | custom-call | flops 1000000000 | bytes 4000000 | tf_op jit(solution)/shard_map/left_mix/pallas_call | solution.py:358
  80.3 0.7 copy-done.4
  81.1 9.5 %pair_update.1 = bf16[10,320,128]{2,1,0:T(8,128)(2,1)} custom-call(s32[1]{0:T(128)} %bitcast.idx, bf16[160,1024]{1,0:T(8,128)(2,1)} %copy-done.1, bf16[160,1024]{1,0:T(8,128)(2,1)} %copy-done.4, bf16[1024,1280]{1,0:T(8,128)(2,1)} %left_mix.1.mixed, f32[10,320,128]{2,1,0:T(8,128)} %get-tuple-element.11.pair_one, s32[32,320]{1,0:T(8,128)} %validity.1, ...), custom_call_target="tpu_custom_call" | custom-call | flops 10000000000 | bytes 4000000 | tf_op jit(solution)/shard_map/pair_update/pallas_call | solution.py:425
  (42 shorter events, 0.1 us)
Async XLA Ops:
  0.6 7.4 %collective-permute-start.3 = (bf16[1,320,256]{2,1,0:T(8,128)(2,1)}, bf16[1,320,256]{2,1,0:T(8,128)(2,1)S(1)}, u32[]{:S(2)}, u32[]{:S(2)}) collective-permute-start(bf16[1,320,256]{2,1,0:T(8,128)(2,1)} %refs_0_.1), channel_id=1, source_target_pairs={{0,4},{1,5},{2,6},{3,7},{4,0},{5,1},{6,2},{7,3},{8,12},{9,13},{10,... | collective-permute-start | bytes 491528 | tf_op jit(solution)/shard_map/ppermute | solution.py:478
  3.7 7.3 %collective-permute-start.1 = (bf16[1,320,256]{2,1,0:T(8,128)(2,1)}, bf16[1,320,256]{2,1,0:T(8,128)(2,1)S(1)}, u32[]{:S(2)}, u32[]{:S(2)}) collective-permute-start(bf16[1,320,256]{2,1,0:T(8,128)(2,1)} %refs_0_.1), channel_id=1, source_target_pairs={{0,2},{1,3},{2,0},{3,1},{4,6},{5,7},{6,4},{7,5},{8,10},{9,11},{10,... | collective-permute-start | bytes 491528 | tf_op jit(solution)/shard_map/ppermute | solution.py:478
  5.2 7.7 %collective-permute-start.5 = (bf16[1,320,256]{2,1,0:T(8,128)(2,1)}, bf16[1,320,256]{2,1,0:T(8,128)(2,1)S(1)}, u32[]{:S(2)}, u32[]{:S(2)}) collective-permute-start(bf16[1,320,256]{2,1,0:T(8,128)(2,1)} %refs_0_.1), channel_id=1, source_target_pairs={{0,6},{1,7},{2,4},{3,5},{4,2},{5,3},{6,0},{7,1},{8,14},{9,15},{10,... | collective-permute-start | bytes 491528 | tf_op jit(solution)/shard_map/ppermute | solution.py:478
  5.2 29.7 %collective-permute-start = (bf16[1,320,256]{2,1,0:T(8,128)(2,1)}, bf16[1,320,256]{2,1,0:T(8,128)(2,1)S(1)}, u32[]{:S(2)}, u32[]{:S(2)}) collective-permute-start(bf16[1,320,256]{2,1,0:T(8,128)(2,1)} %refs_0_.1), channel_id=1, source_target_pairs={{0,1},{1,0},{2,3},{3,2},{4,5},{5,4},{6,7},{7,6},{8,9},{9,8},{10,11... | collective-permute-start | bytes 491528 | tf_op jit(solution)/shard_map/ppermute | solution.py:478
  8.1 26.9 %copy-start.5 = (bf16[1,320,256]{2,1,0:T(8,128)(2,1)}, bf16[1,320,256]{2,1,0:T(8,128)(2,1)S(1)}, u32[]{:S(2)}) copy-start(bf16[1,320,256]{2,1,0:T(8,128)(2,1)S(1)} %collective-permute-done.3.refs_4_) | copy-start | bytes 491524
  8.1 26.9 %collective-permute-start.4 = (bf16[1,320,256]{2,1,0:T(8,128)(2,1)S(1)}, bf16[1,320,256]{2,1,0:T(8,128)(2,1)S(1)}, u32[]{:S(2)}, u32[]{:S(2)}) collective-permute-start(bf16[1,320,256]{2,1,0:T(8,128)(2,1)S(1)} %collective-permute-done.3.refs_4_), channel_id=1, source_target_pairs={{0,1},{1,0},{2,3},{3,2},{4,5},{5,4},{6,7},{7,6},{8,9},{9,8},{10,11... | collective-permute-start | bytes 491528 | tf_op jit(solution)/shard_map/ppermute | solution.py:478
  11.0 24.0 %copy-start.6 = (bf16[1,320,256]{2,1,0:T(8,128)(2,1)}, bf16[1,320,256]{2,1,0:T(8,128)(2,1)S(1)}, u32[]{:S(2)}) copy-start(bf16[1,320,256]{2,1,0:T(8,128)(2,1)S(1)} %collective-permute-done.1.refs_2_) | copy-start | bytes 491524
  11.0 24.0 %collective-permute-start.2 = (bf16[1,320,256]{2,1,0:T(8,128)(2,1)S(1)}, bf16[1,320,256]{2,1,0:T(8,128)(2,1)S(1)}, u32[]{:S(2)}, u32[]{:S(2)}) collective-permute-start(bf16[1,320,256]{2,1,0:T(8,128)(2,1)S(1)} %collective-permute-done.1.refs_2_), channel_id=1, source_target_pairs={{0,1},{1,0},{2,3},{3,2},{4,5},{5,4},{6,7},{7,6},{8,9},{9,8},{10,11... | collective-permute-start | bytes 491528 | tf_op jit(solution)/shard_map/ppermute | solution.py:478
  12.8 22.2 %copy-start.7 = (bf16[1,320,256]{2,1,0:T(8,128)(2,1)}, bf16[1,320,256]{2,1,0:T(8,128)(2,1)S(1)}, u32[]{:S(2)}) copy-start(bf16[1,320,256]{2,1,0:T(8,128)(2,1)S(1)} %collective-permute-done.5.refs_6_) | copy-start | bytes 491524
  12.8 22.1 %collective-permute-start.6 = (bf16[1,320,256]{2,1,0:T(8,128)(2,1)S(1)}, bf16[1,320,256]{2,1,0:T(8,128)(2,1)S(1)}, u32[]{:S(2)}, u32[]{:S(2)}) collective-permute-start(bf16[1,320,256]{2,1,0:T(8,128)(2,1)S(1)} %collective-permute-done.5.refs_6_), channel_id=1, source_target_pairs={{0,1},{1,0},{2,3},{3,2},{4,5},{5,4},{6,7},{7,6},{8,9},{9,8},{10,11... | collective-permute-start | bytes 491528 | tf_op jit(solution)/shard_map/ppermute | solution.py:478
  17.6 6.7 %collective-permute-start.9 = (bf16[10,8,320]{2,1,0:T(8,128)(2,1)}, bf16[10,8,320]{2,1,0:T(8,128)(2,1)S(1)}, u32[]{:S(2)}, u32[]{:S(2)}) collective-permute-start(bf16[10,8,320]{2,1,0:T(8,128)(2,1)} %get-tuple-element.7.refs_8_), channel_id=1, source_target_pairs={{0,24},{1,25},{2,26},{3,27},{4,28},{5,29},{6,30},{7,31},{8,16},{9,... | collective-permute-start | bytes 153608 | tf_op jit(solution)/shard_map/ppermute | solution.py:478
  24.3 10.7 %copy-start.12 = (bf16[10,8,320]{2,1,0:T(8,128)(2,1)}, bf16[10,8,320]{2,1,0:T(8,128)(2,1)S(1)}, u32[]{:S(2)}) copy-start(bf16[10,8,320]{2,1,0:T(8,128)(2,1)S(1)} %collective-permute-done.9.refs_11_) | copy-start | bytes 153604
  24.3 6.2 %collective-permute-start.8 = (bf16[10,8,320]{2,1,0:T(8,128)(2,1)}, bf16[10,8,320]{2,1,0:T(8,128)(2,1)S(1)}, u32[]{:S(2)}, u32[]{:S(2)}) collective-permute-start(bf16[10,8,320]{2,1,0:T(8,128)(2,1)} %get-tuple-element.7.refs_8_), channel_id=1, source_target_pairs={{0,16},{1,17},{2,18},{3,19},{4,20},{5,21},{6,22},{7,23},{8,24},{9,... | collective-permute-start | bytes 153608 | tf_op jit(solution)/shard_map/ppermute | solution.py:478
  30.5 4.5 %copy-start.13 = (bf16[10,8,320]{2,1,0:T(8,128)(2,1)}, bf16[10,8,320]{2,1,0:T(8,128)(2,1)S(1)}, u32[]{:S(2)}) copy-start(bf16[10,8,320]{2,1,0:T(8,128)(2,1)S(1)} %collective-permute-done.8.refs_10_) | copy-start | bytes 153604
  30.5 4.4 %collective-permute-start.7 = (bf16[10,8,320]{2,1,0:T(8,128)(2,1)}, bf16[10,8,320]{2,1,0:T(8,128)(2,1)S(1)}, u32[]{:S(2)}, u32[]{:S(2)}) collective-permute-start(bf16[10,8,320]{2,1,0:T(8,128)(2,1)} %get-tuple-element.7.refs_8_), channel_id=1, source_target_pairs={{0,8},{1,9},{2,10},{3,11},{4,12},{5,13},{6,14},{7,15},{8,0},{9,1},... | collective-permute-start | bytes 153608 | tf_op jit(solution)/shard_map/ppermute | solution.py:478
  34.9 0.6 copy-start.14
  34.9 0.7 copy-start.8
  34.9 0.7 copy-start.9
  35.0 0.8 copy-start.10
  35.0 0.8 copy-start.11
  35.8 13.4 %copy-start.3 = (bf16[256,64]{0,1:T(8,128)(2,1)S(1)}, bf16[256,64]{0,1:T(8,128)(2,1)}, u32[]{:S(2)}) copy-start(bf16[256,64]{0,1:T(8,128)(2,1)} %param.41) | copy-start | bytes 98308
  35.8 14.1 %copy-start = (bf16[256,4,256]{2,1,0:T(4,128)(2,1)S(1)}, bf16[256,4,256]{2,1,0:T(4,128)(2,1)}, u32[]{:S(2)}) copy-start(bf16[256,4,256]{2,1,0:T(4,128)(2,1)} %param.35) | copy-start | bytes 1572868
  44.8 6.0 %collective-permute-start.12 = (bf16[10,8,256]{2,1,0:T(8,128)(2,1)S(1)}, bf16[10,8,256]{2,1,0:T(8,128)(2,1)S(1)}, u32[]{:S(2)}, u32[]{:S(2)}) collective-permute-start(bf16[10,8,256]{2,1,0:T(8,128)(2,1)S(1)} %get-tuple-element.12), channel_id=1, source_target_pairs={{0,24},{1,25},{2,26},{3,27},{4,28},{5,29},{6,30},{7,31},{8,16},{9,... | collective-permute-start | bytes 122888 | tf_op jit(solution)/shard_map/ppermute | solution.py:478
  47.4 4.9 %collective-permute-start.11 = (bf16[10,8,256]{2,1,0:T(8,128)(2,1)S(1)}, bf16[10,8,256]{2,1,0:T(8,128)(2,1)S(1)}, u32[]{:S(2)}, u32[]{:S(2)}) collective-permute-start(bf16[10,8,256]{2,1,0:T(8,128)(2,1)S(1)} %get-tuple-element.13), channel_id=1, source_target_pairs={{0,16},{1,17},{2,18},{3,19},{4,20},{5,21},{6,22},{7,23},{8,24},{9,... | collective-permute-start | bytes 122888 | tf_op jit(solution)/shard_map/ppermute | solution.py:478
  47.4 4.9 %collective-permute-start.10 = (bf16[10,8,256]{2,1,0:T(8,128)(2,1)S(1)}, bf16[10,8,256]{2,1,0:T(8,128)(2,1)S(1)}, u32[]{:S(2)}, u32[]{:S(2)}) collective-permute-start(bf16[10,8,256]{2,1,0:T(8,128)(2,1)S(1)} %get-tuple-element.14), channel_id=1, source_target_pairs={{0,8},{1,9},{2,10},{3,11},{4,12},{5,13},{6,14},{7,15},{8,0},{9,1},... | collective-permute-start | bytes 122888 | tf_op jit(solution)/shard_map/ppermute | solution.py:478
  50.8 1.5 %copy-start.15 = (bf16[10,8,256]{2,1,0:T(8,128)(2,1)}, bf16[10,8,256]{2,1,0:T(8,128)(2,1)S(1)}, u32[]{:S(2)}) copy-start(bf16[10,8,256]{2,1,0:T(8,128)(2,1)S(1)} %collective-permute-done.12.refs_3_) | copy-start | bytes 122884
  52.3 0.6 copy-start.16
  52.3 0.6 copy-start.17
  52.9 22.5 %copy-start.2 = (bf16[1024,128]{1,0:T(8,128)(2,1)S(1)}, bf16[1024,128]{1,0:T(8,128)(2,1)}, u32[]{:S(2)}) copy-start(bf16[1024,128]{1,0:T(8,128)(2,1)} %param.42) | copy-start | bytes 786436
  58.6 5.9 %collective-permute-start.15 = (bf16[10,1024]{1,0:T(8,128)(2,1)}, bf16[10,1024]{1,0:T(8,128)(2,1)S(1)}, u32[]{:S(2)}, u32[]{:S(2)}) collective-permute-start(bf16[10,1024]{1,0:T(8,128)(2,1)} %bitcast.32), channel_id=1, source_target_pairs={{0,24},{1,25},{2,26},{3,27},{4,28},{5,29},{6,30},{7,31},{8,16},{9,... | collective-permute-start | bytes 61448 | tf_op jit(solution)/shard_map/ppermute | solution.py:478
  60.5 5.4 %collective-permute-start.14 = (bf16[10,1024]{1,0:T(8,128)(2,1)}, bf16[10,1024]{1,0:T(8,128)(2,1)S(1)}, u32[]{:S(2)}, u32[]{:S(2)}) collective-permute-start(bf16[10,1024]{1,0:T(8,128)(2,1)} %bitcast.33), channel_id=1, source_target_pairs={{0,16},{1,17},{2,18},{3,19},{4,20},{5,21},{6,22},{7,23},{8,24},{9,... | collective-permute-start | bytes 61448 | tf_op jit(solution)/shard_map/ppermute | solution.py:478
  61.0 4.9 %collective-permute-start.13 = (bf16[10,1024]{1,0:T(8,128)(2,1)}, bf16[10,1024]{1,0:T(8,128)(2,1)S(1)}, u32[]{:S(2)}, u32[]{:S(2)}) collective-permute-start(bf16[10,1024]{1,0:T(8,128)(2,1)} %bitcast.34), channel_id=1, source_target_pairs={{0,8},{1,9},{2,10},{3,11},{4,12},{5,13},{6,14},{7,15},{8,0},{9,1},... | collective-permute-start | bytes 61448 | tf_op jit(solution)/shard_map/ppermute | solution.py:478
  66.7 5.4 %collective-permute-start.18 = (bf16[40,1024]{1,0:T(8,128)(2,1)S(1)}, bf16[40,1024]{1,0:T(8,128)(2,1)S(1)}, u32[]{:S(2)}, u32[]{:S(2)}) collective-permute-start(bf16[40,1024]{1,0:T(8,128)(2,1)S(1)} %pad_maximum_fusion), channel_id=1, source_target_pairs={{0,6},{1,7},{2,4},{3,5},{4,2},{5,3},{6,0},{7,1},{8,14},{9,15},{10,... | collective-permute-start | bytes 245768 | tf_op jit(solution)/shard_map/ppermute | solution.py:478
  69.2 4.4 %collective-permute-start.17 = (bf16[40,1024]{1,0:T(8,128)(2,1)S(1)}, bf16[40,1024]{1,0:T(8,128)(2,1)S(1)}, u32[]{:S(2)}, u32[]{:S(2)}) collective-permute-start(bf16[40,1024]{1,0:T(8,128)(2,1)S(1)} %pad_maximum_fusion), channel_id=1, source_target_pairs={{0,4},{1,5},{2,6},{3,7},{4,0},{5,1},{6,2},{7,3},{8,12},{9,13},{10,... | collective-permute-start | bytes 245768 | tf_op jit(solution)/shard_map/ppermute | solution.py:478
  69.8 4.4 %collective-permute-start.16 = (bf16[40,1024]{1,0:T(8,128)(2,1)S(1)}, bf16[40,1024]{1,0:T(8,128)(2,1)S(1)}, u32[]{:S(2)}, u32[]{:S(2)}) collective-permute-start(bf16[40,1024]{1,0:T(8,128)(2,1)S(1)} %pad_maximum_fusion), channel_id=1, source_target_pairs={{0,2},{1,3},{2,0},{3,1},{4,6},{5,7},{6,4},{7,5},{8,10},{9,11},{10,... | collective-permute-start | bytes 245768 | tf_op jit(solution)/shard_map/ppermute | solution.py:478
  75.4 5.0 %copy-start.1 = (bf16[160,1024]{1,0:T(8,128)(2,1)}, bf16[160,1024]{1,0:T(8,128)(2,1)S(1)}, u32[]{:S(2)}) copy-start(bf16[160,1024]{1,0:T(8,128)(2,1)S(1)} %concatenate.8.near) | copy-start | bytes 983044
  75.4 5.0 %collective-permute-start.19 = (bf16[160,1024]{1,0:T(8,128)(2,1)S(1)}, bf16[160,1024]{1,0:T(8,128)(2,1)S(1)}, u32[]{:S(2)}, u32[]{:S(2)}) collective-permute-start(bf16[160,1024]{1,0:T(8,128)(2,1)S(1)} %concatenate.8.near), channel_id=1, source_target_pairs={{0,1},{1,0},{2,3},{3,2},{4,5},{5,4},{6,7},{7,6},{8,9},{9,8},{10,11... | collective-permute-start | bytes 983048 | tf_op jit(solution)/shard_map/ppermute | solution.py:478
  80.3 0.7 copy-start.4

commit v2 on v1

--- a/solution.py
+++ b/solution.py
@@ -70,7 +70,7 @@
         pick = jnp.where(wanted == iota((2 * length, bins), 1), 1.0, 0.0)
         shifted[...] = jnp.dot(pick, table[...], precision=lax.Precision.HIGHEST, preferred_element_type=F32)
         eye = iota((length, length), 0) == iota((length, length), 1)
-        column = jnp.sum(jnp.where(eye, chain_row[...].astype(F32), 0.0), axis=1, keepdims=True)
+        column = jnp.sum(jnp.where(eye, chain_row[...].astype(F32).reshape(1, length), 0.0), axis=1, keepdims=True)
         chain_wide[...] = jnp.broadcast_to(column, chain_wide.shape)
 
     other = table[bins - 1 : bins, :]
@@ -98,7 +98,7 @@
             smem,
             smem,
             pl.BlockSpec((block, length, depth), lambda s: (s, 0, 0)),
-            whole(1, length),
+            whole(length),
             whole(bins, depth),
             whole(1, depth),
             whole(HEADS, depth),
@@ -115,13 +115,12 @@
         compiler_params=pltpu.CompilerParams(vmem_limit_bytes=VMEM_LIMIT),
         cost_estimate=pl.CostEstimate(flops=4 * rows * length * depth * HEADS, bytes_accessed=4000000, transcendentals=0),
         name="pair_bias",
-    )(idx, chain, pair, chain[None, :], table, gain[None, :], factors.T)
-
-
-def row_kernel(idx, *refs, sub, far, rows, length, width):
-    row_refs, refs = refs[:sub], refs[sub:]
-    bias_refs, refs = refs[:far], refs[far:]
-    validity, amino, gain, entry, exit_, out, keys, values, bias, own_normed, own_rows, query, gate, gated = refs
+    )(idx, chain, pair, chain, table, gain[None, :], factors.T)
+
+
+def project_kernel(idx, *refs, sub, far, rows, length, width):
+    row_refs, refs = refs[:4], refs[4:]
+    gain, entry, keys, values, query, gate, own_rows, own_normed = refs
     me = idx[0]
     z, p = me // sub, me % sub
     own = far * rows
@@ -134,14 +133,17 @@
 
     step = min(length, 320)
     for k in range(sub):
-
-        def project(start, k=k):
-            normed = layer_norm(row_refs[k][0, pl.ds(start, step), :].astype(F32), gain[...]).astype(BF16)
+        source = row_refs[k] if k < 2 else row_refs[2 + k % 2]
+        place = 0 if k < 2 else k // 2 - 1
+
+        def project(start, k=k, source=source, place=place):
+            x = source[place, pl.ds(start, step), :]
+            normed = layer_norm(x.astype(F32), gain[...]).astype(BF16)
             both = dot(normed, entry[:, width : 3 * width])
             keys[k, pl.ds(start, step), :] = both[:, :width].astype(BF16)
             values[k, pl.ds(start, step), :] = both[:, width:].astype(BF16)
             part = pick if length == step else one_hot(residue[:, :step] == iota((own, step), 1) + start)
-            q_rows, a_rows = dot(part, normed), dot(part, row_refs[k][0, pl.ds(start, step), :])
+            q_rows, a_rows = dot(part, normed), dot(part, x)
             here = pl.ds(k * own, own)
             if length == step:
                 own_normed[here, :] = q_rows
@@ -164,6 +166,35 @@
 
     chunks(total, part, queries)
 
+
+def project_call(idx, msa_rows, gain, entry, far, rows):
+    sub = SUB
+    _, length, width = msa_rows[0].shape
+    own = far * rows
+    vmem = pl.BlockSpec(memory_space=pltpu.VMEM)
+    wide = jax.ShapeDtypeStruct((sub, length, width), BF16)
+    narrow = jax.ShapeDtypeStruct((sub * own, width), F32)
+    return pl.pallas_call(
+        functools.partial(project_kernel, sub=sub, far=far, rows=rows, length=length, width=width),
+        in_specs=[pl.BlockSpec(memory_space=pltpu.SMEM)] + [vmem] * 6,
+        out_specs=[vmem] * 5,
+        out_shape=[wide, wide, narrow, narrow, narrow],
+        scratch_shapes=[pltpu.VMEM((sub * own, width), F32)],
+        compiler_params=pltpu.CompilerParams(vmem_limit_bytes=VMEM_LIMIT),
+        cost_estimate=pl.CostEstimate(flops=10**9, bytes_accessed=4000000, transcendentals=10**5),
+        name="row_project",
+    )(idx, *msa_rows, gain[None, :], entry)
+
+
+def row_kernel(idx, *refs, sub, far, rows, length, width):
+    bias_refs, refs = refs[:far], refs[far:]
+    keys, values, query, gate, own_rows, validity, amino, exit_ = refs[:8]
+    outs, refs = refs[8 : 8 + far], refs[8 + far :]
+    bias, gated = refs
+    me = idx[0]
+    z, p = me // sub, me % sub
+    own = far * rows
+    total = sub * own
     for b in range(far):
         bias[b * rows : (b + 1) * rows] = bias_refs[b][...].astype(F32) * LOG2E
 
@@ -173,7 +204,7 @@
 
     def attend(n, k, start):
         s = z * sub + (p ^ k)
-        valid = validity[pl.ds(s, 1), :] * amino[...]
+        valid = validity[pl.ds(s, 1), :] * amino[...].reshape(1, length)
         masked = jnp.where(valid > 0, 0.0, MASKED)
         here = pl.ds(pl.multiple_of(n * take, take), take) if not isinstance(n, int) else pl.ds(n * take, take)
         q = (query[here, :][:, None, :] * head_mask[None]).reshape(take * HEADS, width).astype(BF16)
@@ -191,42 +222,36 @@
     else:
         lax.fori_loop(0, sub * parts, lambda n, x: (attend(n, n // parts, (n % parts) * take), x)[1], 0)
 
-    def leave(start):
-        q = iota((part, total), 0) + start
+    piece = rows * sub
+    for b in range(far):
+        q = iota((piece, total), 0) + b * piece
         residue_, row = div_const(q, sub, total), q & (sub - 1)
-        swap = one_hot((row ^ p) * own + residue_ == iota((part, total), 1))
+        swap = one_hot((row ^ p) * own + residue_ == iota((piece, total), 1))
         gated_rows = dot(swap, gated[...].astype(BF16)).astype(BF16)
         x = dot(swap, own_rows[...].astype(BF16)) + dot(gated_rows, exit_[...])
-        out[pl.ds(start, part), :] = x.astype(BF16)
-
-    chunks(total, part, leave)
-
-
-def row_call(idx, msa_rows, bias_blocks, validity, amino, gain, entry, exit_):
-    sub, far = len(msa_rows), len(bias_blocks)
-    _, length, width = msa_rows[0].shape
+        outs[b][...] = x.astype(BF16).reshape(rows, sub, width)
+
+
+def row_call(idx, bias_blocks, projected, validity, amino, exit_):
+    keys, values, query, gate, own_rows = projected
+    sub, far = keys.shape[0], len(bias_blocks)
+    _, length, width = keys.shape
     rows = bias_blocks[0].shape[0]
     own = far * rows
     vmem = pl.BlockSpec(memory_space=pltpu.VMEM)
     return pl.pallas_call(
         functools.partial(row_kernel, sub=sub, far=far, rows=rows, length=length, width=width),
-        in_specs=[pl.BlockSpec(memory_space=pltpu.SMEM)] + [vmem] * (sub + far + 5),
-        out_specs=vmem,
-        out_shape=jax.ShapeDtypeStruct((own * sub, width), BF16),
+        in_specs=[pl.BlockSpec(memory_space=pltpu.SMEM)] + [vmem] * (far + 8),
+        out_specs=[vmem] * far,
+        out_shape=[jax.ShapeDtypeStruct((rows, sub, width), BF16)] * far,
         scratch_shapes=[
-            pltpu.VMEM((sub, length, width), BF16),
-            pltpu.VMEM((sub, length, width), BF16),
             pltpu.VMEM((own, HEADS, length), F32),
-            pltpu.VMEM((sub * own, width), F32),
-            pltpu.VMEM((sub * own, width), F32),
-            pltpu.VMEM((sub * own, width), F32),
-            pltpu.VMEM((sub * own, width), F32),
             pltpu.VMEM((sub * own, width), F32),
         ],
         compiler_params=pltpu.CompilerParams(vmem_limit_bytes=VMEM_LIMIT),
         cost_estimate=pl.CostEstimate(flops=10**10, bytes_accessed=4000000, transcendentals=10**6),
         name="row_attention",
-    )(idx, *msa_rows, *bias_blocks, validity, amino[None, :], gain[None, :], entry, exit_)
+    )(idx, *bias_blocks, keys, values, query, gate, own_rows, validity, amino, exit_)
 
 
 def column_kernel(idx, *refs, sub, far, rows, block, depth, width):
@@ -343,24 +368,26 @@
 
 
 def mix_kernel(left, factors, out, *, rows, depth):
-    lanes = factors.shape[2]
-    for e in range(factors.shape[0]):
-        y = dot(left[...], factors[e]).astype(BF16)
+    lanes = out.shape[1] // rows
+    for e in range(0, out.shape[0] // depth, 2):
+        y = dot(left[...], factors[:, e * lanes : (e + 2) * lanes]).astype(BF16)
         for i in range(rows):
-            out[e * depth : (e + 1) * depth, i * lanes : (i + 1) * lanes] = y[i * depth : (i + 1) * depth]
+            for f in range(2):
+                block = y[i * depth : (i + 1) * depth, f * lanes : (f + 1) * lanes]
+                out[(e + f) * depth : (e + f + 1) * depth, i * lanes : (i + 1) * lanes] = block
 
 
 def mix_call(left, factors, rows):
     total, channels = left.shape
     depth = total // rows
-    lanes = factors.shape[2]
+    lanes = factors.shape[1] // channels
     block = 8
     return pl.pallas_call(
         functools.partial(mix_kernel, rows=rows, depth=depth),
         grid=(channels // block,),
         in_specs=[
             pl.BlockSpec((total, channels), lambda s: (0, 0)),
-            pl.BlockSpec((block, channels, lanes), lambda s: (s, 0, 0)),
+            pl.BlockSpec((channels, block * lanes), lambda s: (0, s)),
         ],
         out_specs=pl.BlockSpec((block * depth, rows * lanes), lambda s: (s, 0)),
         out_shape=jax.ShapeDtypeStruct((channels * depth, rows * lanes), BF16),
@@ -371,12 +398,14 @@
 
 
 def finish_kernel(
-    idx, near, across, mixed, pair_one, validity, gain, widen, narrow, out, right, turned, *, sub, far, rows, length, block
+    idx, *refs, sub, far, rows, length, block
 ):
+    near_refs, across_refs, refs = refs[: sub // 2], refs[sub // 2 : sub], refs[sub:]
+    mixed, pair_one, validity, gain, widen, narrow, out, right, turned = refs
     me = idx[0]
     z, p = me // sub, me % sub
     step = pl.program_id(0)
-    half = near.shape[0]
+    half = far * rows * sub // 2
     lanes = pair_one.shape[2]
     part = min(length, 320)
 
@@ -385,14 +414,18 @@
         r = iota((part, half), 1)
         b = div_const(r, rows, half)
         i = r - b * rows
-        across_sub, across_far = (b // far) * 2, b % far
+        across_sub = 2 * div_const(b, far, half // rows)
+        across_far = b - far * (across_sub >> 1)
         home = ((z ^ across_far) * sub + (p ^ across_sub)) * rows + i
         away = ((z ^ across_far) * sub + (p ^ 1 ^ across_sub)) * rows + i
+
+        near = jnp.concatenate([ref[...].astype(F32) for ref in near_refs], 0).astype(BF16)
+        across = jnp.concatenate([ref[...].astype(F32) for ref in across_refs], 0).astype(BF16)
 
         def arrange(start):
             j = iota((part, half), 0) + start
             here = pl.ds(start, part)
-            right[here, :] = (dot(one_hot(j == home), near[...]) + dot(one_hot(j == away), across[...])).astype(BF16)
+            right[here, :] = (dot(one_hot(j == home), near) + dot(one_hot(j == away), across)).astype(BF16)
 
         chunks(length, part, arrange)
         turned[...] = validity[...].astype(F32).T.astype(BF16)
@@ -427,8 +460,7 @@
         grid=(rows // block,),
         in_specs=[
             pl.BlockSpec(memory_space=pltpu.SMEM),
-            vmem(near),
-            vmem(across),
+            *[vmem(a) for a in near + across],
             pl.BlockSpec((product, block * lanes), lambda s: (0, s)),
             pl.BlockSpec((block, length, lanes), lambda s: (s, 0, 0)),
             vmem(validity),
@@ -442,7 +474,7 @@
         compiler_params=pltpu.CompilerParams(vmem_limit_bytes=VMEM_LIMIT),
         cost_estimate=pl.CostEstimate(flops=10**10, bytes_accessed=4000000, transcendentals=0),
         name="pair_update",
-    )(idx, near, across, mixed, pair_one, validity, gain, widen, narrow)
+    )(idx, *near, *across, mixed, pair_one, validity, gain, widen, narrow)
 
 
 def on_device(
@@ -481,26 +513,20 @@
     rows = couple_embedding.shape[0]
     depth = alignment_validity.shape[0]
 
-    msa_rows = [alignment_embedding] * SUB
-    for k in range(2, SUB, 2):
-        msa_rows[k] = swap(alignment_embedding, k)
-    for k in range(0, SUB, 2):
-        msa_rows[k + 1] = swap(msa_rows[k], 1)
-
+    beside = swap(alignment_embedding, 1)
+    near = [swap(alignment_embedding, k) for k in range(2, SUB, 2)]
     pair_one, bias = pair_call(
         idx, amino_strand, couple_embedding, separation_embedding, couple_shift_scaling, couple_shift_factors
     )
+    entry = horizontal_entry_factors.reshape(width, 4 * width)
+    bias, entry, beside, *near = lax.optimization_barrier((bias, entry, beside, *near))
     bias_blocks = [bias] + [swap(bias, SUB * k) for k in range(1, far)]
-    sent = row_call(
-        idx,
-        msa_rows,
-        bias_blocks,
-        alignment_validity,
-        amino_validity,
-        horizontal_scaling_factor,
-        horizontal_entry_factors.reshape(width, 4 * width),
-        horizontal_exit_factors,
-    ).reshape(far, rows, SUB, width)
+    near = jnp.concatenate(near, 0)
+    across = swap(near, 1)
+    projected = project_call(
+        idx, [alignment_embedding, beside, near, across], horizontal_scaling_factor, entry, far, rows
+    )
+    sent = row_call(idx, bias_blocks, projected, alignment_validity, amino_validity, horizontal_exit_factors)
     pieces = [sent[0]] + [swap(sent[k], SUB * k) for k in range(1, far)]
     updated, left, right = column_call(
         idx,
@@ -517,11 +543,14 @@
     )
     channels = left.shape[1]
     right = right.reshape(rows, channels * depth)
-    column = jnp.concatenate([right] + [swap(right, SUB * k) for k in range(1, far)], 0)
-    near = jnp.concatenate([column] + [swap(column, k) for k in range(2, SUB, 2)], 0)
-    across = swap(near, 1)
-    factors = product_exit_factors.reshape(channels, channels, -1).transpose(1, 0, 2)
+    factors = product_exit_factors.reshape(channels, -1)
     mixed = mix_call(left, factors, rows)
+    parts = [right] + [swap(right, SUB * k) for k in range(1, far)]
+    parts = lax.optimization_barrier((mixed, *parts))
+    mixed, parts = parts[0], parts[1:]
+    column = jnp.concatenate(parts, 0)
+    near = [column] + [swap(column, k) for k in range(2, SUB, 2)]
+    across = [swap(a, 1) for a in near]
     updated_pairs = finish_call(
         idx,
         near,

time: 91.3 us -> 74.1 us (0.81)
  waiting for transfers between devices: 25.4 us -> 10 us
  local copies, waits for them, and re-layouts: 11.6 us -> 7.09 us
  Pallas kernels: 30.3 us -> 34.1 us
    ppermute x20 -> x21, waiting for transfers between devices: 25.4 us -> 10 us  [swap(): return lax.ppermute(x, 'dap', [(d, d ^ distance) for d in range(devices)])]
    pallas_call x0 -> x1, Pallas kernels: none -> 5.4 us  [project_call(): pl.pallas_call(functools.partial(project_kernel, sub=sub, far=far, rows=r...]
    broadcast_in_dim x2 -> x0, local copies, waits for them, and re-layouts: 2.54 us -> none  [the longest x1 1.27 us: pair_call(): chain[None, :]]
    pallas_call x1, Pallas kernels: 7.54 us -> 5.95 us  [row_call(): pl.pallas_call(functools.partial(row_kernel, sub=sub, far=far, rows=rows,...]
    squeeze x1 -> x0, local copies, waits for them, and re-layouts: 1.46 us -> none  [on_device(): pieces = [sent[0]] + [swap(sent[k], SUB * k) for k in range(1, far)]]
    concatenate x1, local copies, waits for them, and re-layouts: 1.17 us -> 0.01 us  [on_device(): near = jnp.concatenate(near, 0)]
    unnamed x39 -> x47, local copies, waits for them, and re-layouts: 5.67 us -> 6.26 us
    ppermute x20 -> x21, starting transfers between devices: 21.6 us -> 21.5 us  [swap(): return lax.ppermute(x, 'dap', [(d, d ^ distance) for d in range(devices)])]
  transfers between devices with their start and end apart: 20 -> 21, of which waited for: 12 -> 7; matrix products, arithmetic and copies ran while one was open for 8% -> 6% of each run, Pallas kernels for 8% -> 18%
where the time goes in v2:
time: 74.1 us; the launch traced here: 73.6 us
  Pallas kernels  34.1 us (46%)
  starting transfers between devices  21.5 us (29%)
  waiting for transfers between devices  10 us (13%)
  local copies, waits for them, and re-layouts  7.09 us (10%)
  between operations  0.86 us (1%)
    ppermute x21, starting transfers between devices, swap(): return lax.ppermute(x, 'dap', [(d, d ^ distance) for d in range(devices)])  21.5 us
    ppermute x21, waiting for transfers between devices, swap(): return lax.ppermute(x, 'dap', [(d, d ^ distance) for d in range(devices)])  10 us
    pallas_call x1, Pallas kernels, finish_call(): pl.pallas_call(functools.partial(finish_kernel, sub=sub, far=far, rows=ro...  9.53 us
    unnamed x47, local copies, waits for them, and re-layouts  6.26 us
    pallas_call x1, Pallas kernels, row_call(): pl.pallas_call(functools.partial(row_kernel, sub=sub, far=far, rows=rows,...  5.95 us
    pallas_call x1, Pallas kernels, column_call(): pl.pallas_call(functools.partial(column_kernel, sub=sub, far=far, rows=ro...  5.66 us
    pallas_call x1, Pallas kernels, project_call(): pl.pallas_call(functools.partial(project_kernel, sub=sub, far=far, rows=r...  5.4 us
    pallas_call x1, Pallas kernels, mix_call(): pl.pallas_call(functools.partial(mix_kernel, rows=rows, depth=depth), gri...  4.07 us
  transfers between devices with their start and end apart: 21, of which 7 were waited for; matrix products, arithmetic and copies ran while one was open for 6% of the time, Pallas kernels for 18%

profile of v2, /device:TPU:0, one launch (start us, length us, event | category | flops | bytes accessed | tf_op | source)
XLA Modules:
  0.0 73.6 jit_solution(312956708987214536)
XLA Ops:
  0.6 0.5 collective-permute-start
  1.1 2.6 %collective-permute-start.1 = (bf16[1,320,256]{2,1,0:T(8,128)(2,1)}, bf16[1,320,256]{2,1,0:T(8,128)(2,1)S(1)}, u32[]{:S(2)}, u32[]{:S(2)}) collective-permute-start(bf16[1,320,256]{2,1,0:T(8,128)(2,1)} %refs_0_.1), channel_id=1, source_target_pairs={{0,2},{1,3},{2,0},{3,1},{4,6},{5,7},{6,4},{7,5},{8,10},{9,11},{10,... | collective-permute-start | bytes 491528 | tf_op jit(solution)/shard_map/ppermute | solution.py:510
  3.7 1.5 %collective-permute-start.2 = (bf16[1,320,256]{2,1,0:T(8,128)(2,1)}, bf16[1,320,256]{2,1,0:T(8,128)(2,1)S(1)}, u32[]{:S(2)}, u32[]{:S(2)}) collective-permute-start(bf16[1,320,256]{2,1,0:T(8,128)(2,1)} %refs_0_.1), channel_id=1, source_target_pairs={{0,4},{1,5},{2,6},{3,7},{4,0},{5,1},{6,2},{7,3},{8,12},{9,13},{10,... | collective-permute-start | bytes 491528 | tf_op jit(solution)/shard_map/ppermute | solution.py:510
  5.2 0.0 collective-permute-start.3
  5.3 1.9 %copy.26 = bf16[32,8,4,256]{3,1,2,0:T(8,128)(2,1)} copy(bf16[32,8,4,256]{3,2,1,0:T(4,128)(2,1)} %bitcast.14) | data formatting | bytes 1048576
  7.2 3.5 %pair_bias.1 = (f32[10,320,128]{2,1,0:T(8,128)}, bf16[10,8,320]{2,1,0:T(8,128)(2,1)}) custom-call(s32[1]{0:T(128)} %bitcast.idx, s32[320]{0:T(512)} %chain_row.1, bf16[10,320,128]{2,1,0:T(8,128)(2,1)} %pair.1, s32[320]{0:T(512)} %chain_row.1, f32[66,128]{1,0:T(8,128)} %table.1, f32[1,128]{1,0:T(1,128)} %bitcast.23, bf16[8,128]{1,0:T(8,128)(2,1)} %bitcast.22), custom_call_target="tpu_custom_call" | custom-call | flops 13107200 | bytes 4000000 | tf_op jit(solution)/shard_map/pair_bias/pallas_call | solution.py:94
  10.7 0.0 collective-permute-done.refs_1_
  10.7 0.0 collective-permute-done.1
  10.7 3.0 %collective-permute-done.2 = bf16[1,320,256]{2,1,0:T(8,128)(2,1)S(1)} collective-permute-done((bf16[1,320,256]{2,1,0:T(8,128)(2,1)}, bf16[1,320,256]{2,1,0:T(8,128)(2,1)S(1)}, u32[]{:S(2)}, u32[]{:S(2)}) %collective-permute-start.2) | collective-permute-done | bytes 163872 | tf_op jit(solution)/shard_map/ppermute | solution.py:510
  13.8 0.1 collective-permute-start.7
  13.9 1.6 %collective-permute-start.4 = (bf16[10,8,320]{2,1,0:T(8,128)(2,1)}, bf16[10,8,320]{2,1,0:T(8,128)(2,1)S(1)}, u32[]{:S(2)}, u32[]{:S(2)}) collective-permute-start(bf16[10,8,320]{2,1,0:T(8,128)(2,1)} %get-tuple-element.28.refs_0_), channel_id=1, source_target_pairs={{0,8},{1,9},{2,10},{3,11},{4,12},{5,13},{6,14},{7,15},{8,0},{9,1},... | collective-permute-start | bytes 153608 | tf_op jit(solution)/shard_map/ppermute | solution.py:510
  15.5 2.6 %collective-permute-start.5 = (bf16[10,8,320]{2,1,0:T(8,128)(2,1)}, bf16[10,8,320]{2,1,0:T(8,128)(2,1)S(1)}, u32[]{:S(2)}, u32[]{:S(2)}) collective-permute-start(bf16[10,8,320]{2,1,0:T(8,128)(2,1)} %get-tuple-element.28.refs_0_), channel_id=1, source_target_pairs={{0,16},{1,17},{2,18},{3,19},{4,20},{5,21},{6,22},{7,23},{8,24},{9,... | collective-permute-start | bytes 153608 | tf_op jit(solution)/shard_map/ppermute | solution.py:510
  18.1 0.2 collective-permute-start.6
  18.3 0.0 collective-permute-done.7.refs_3_
  18.3 0.8 %copy-done.6 = bf16[3,320,256]{2,1,0:T(8,128)(2,1)} copy-done((bf16[3,320,256]{2,1,0:T(8,128)(2,1)}, bf16[3,320,256]{2,1,0:T(8,128)(2,1)S(1)}, u32[]{:S(2)}) %copy-start.6) | copy-done | bytes 491544
  19.1 5.4 %row_project.1 = (bf16[8,320,256]{2,1,0:T(8,128)(2,1)}, bf16[8,320,256]{2,1,0:T(8,128)(2,1)}, f32[320,256]{1,0:T(8,128)}, f32[320,256]{1,0:T(8,128)}, f32[320,256]{1,0:T(8,128)}) custom-call(s32[1]{0:T(128)} %bitcast.idx, bf16[1,320,256]{2,1,0:T(8,128)(2,1)} %refs_0_.1, bf16[1,320,256]{2,1,0:T(8,128)(2,1)} %copy-done.7, bf16[3,320,256]{2,1,0:T(8,128)(2,1)} %copy-done.3, ...), custom_call_target="tpu_custom_call" | custom-call | flops 1000000000 | bytes 4000000 | tf_op jit(solution)/shard_map/row_project/pallas_call | solution.py:177
  24.5 0.0 collective-permute-done.4.refs_1_
  24.6 0.0 collective-permute-done.5.refs_2_
  24.6 0.0 copy-start.16
  24.6 0.6 copy-done.15
  25.2 0.0 copy-done.16
  25.2 0.0 copy-done.17
  25.2 5.9 %row_attention.1 = (bf16[10,8,256]{2,1,0:T(8,128)(2,1)}, bf16[10,8,256]{2,1,0:T(8,128)(2,1)}, bf16[10,8,256]{2,1,0:T(8,128)(2,1)}, bf16[10,8,256]{2,1,0:T(8,128)(2,1)}) custom-call(s32[1]{0:T(128)} %bitcast.idx, bf16[10,8,320]{2,1,0:T(8,128)(2,1)} %get-tuple-element.28.refs_0_, bf16[10,8,320]{2,1,0:T(8,128)(2,1)} %copy-done.15, ...), custom_call_target="tpu_custom_call" | custom-call | flops 10000000000 | bytes 4000000 | tf_op jit(solution)/shard_map/row_attention/pallas_call | solution.py:242
  31.2 3.6 %collective-permute-start.10 = (bf16[10,8,256]{2,1,0:T(8,128)(2,1)}, bf16[10,8,256]{2,1,0:T(8,128)(2,1)S(1)}, u32[]{:S(2)}, u32[]{:S(2)}) collective-permute-start(bf16[10,8,256]{2,1,0:T(8,128)(2,1)} %get-tuple-element.42), channel_id=1, source_target_pairs={{0,24},{1,25},{2,26},{3,27},{4,28},{5,29},{6,30},{7,31},{8,16},{9,... | collective-permute-start | bytes 122888 | tf_op jit(solution)/shard_map/ppermute | solution.py:510
  34.8 0.0 collective-permute-start.8
  34.8 0.8 %collective-permute-start.9 = (bf16[10,8,256]{2,1,0:T(8,128)(2,1)}, bf16[10,8,256]{2,1,0:T(8,128)(2,1)S(1)}, u32[]{:S(2)}, u32[]{:S(2)}) collective-permute-start(bf16[10,8,256]{2,1,0:T(8,128)(2,1)} %get-tuple-element.41), channel_id=1, source_target_pairs={{0,16},{1,17},{2,18},{3,19},{4,20},{5,21},{6,22},{7,23},{8,24},{9,... | collective-permute-start | bytes 122888 | tf_op jit(solution)/shard_map/ppermute | solution.py:510
  35.6 0.9 %copy.27 = bf16[32,8,4,256]{3,1,2,0:T(8,128)(2,1)} copy(bf16[32,8,4,256]{3,2,1,0:T(4,128)(2,1)S(1)} %bitcast.15) | data formatting | bytes 1048576
  36.4 0.7 copy.25.refs_12_
  37.2 0.8 %reshape.22.factors = bf16[32,4096]{1,0:T(8,128)(2,1)} reshape(bf16[1024,128]{1,0:T(8,128)(2,1)S(1)} %copy-done.1) | data formatting | bytes 524288 | tf_op jit(solution)/shard_map/reshape | solution.py:546
  38.0 1.0 %collective-permute-done.8.refs_1_ = bf16[10,8,256]{2,1,0:T(8,128)(2,1)S(1)} collective-permute-done((bf16[10,8,256]{2,1,0:T(8,128)(2,1)}, bf16[10,8,256]{2,1,0:T(8,128)(2,1)S(1)}, u32[]{:S(2)}, u32[]{:S(2)}) %collective-permute-start.8) | collective-permute-done | bytes 40992 | tf_op jit(solution)/shard_map/ppermute | solution.py:510
  39.0 0.9 %collective-permute-done.9.refs_2_ = bf16[10,8,256]{2,1,0:T(8,128)(2,1)S(1)} collective-permute-done((bf16[10,8,256]{2,1,0:T(8,128)(2,1)}, bf16[10,8,256]{2,1,0:T(8,128)(2,1)S(1)}, u32[]{:S(2)}, u32[]{:S(2)}) %collective-permute-start.9) | collective-permute-done | bytes 40992 | tf_op jit(solution)/shard_map/ppermute | solution.py:510
  39.9 0.6 copy-done.20
  40.5 5.7 %column_attention.1 = (bf16[10,32,256]{2,1,0:T(8,128)(2,1)}, bf16[320,32]{1,0:T(8,128)(2,1)}, bf16[1,10,1024]{2,1,0:T(8,128)(2,1)}) custom-call(s32[1]{0:T(128)} %bitcast.idx, bf16[10,8,256]{2,1,0:T(8,128)(2,1)} %get-tuple-element.39.refs_0_, bf16[10,8,256]{2,1,0:T(8,128)(2,1)} %copy-done.19, bf16[10,8,256]{2,1,0:T(8,128)(2,1)} %copy-done.20, ...), custom_call_target="tpu_custom_call" | custom-call | flops 10000000000 | bytes 4000000 | tf_op jit(solution)/shard_map/column_attention/pallas_call | solution.py:347
  46.1 2.0 %collective-permute-start.11 = (bf16[10,1024]{1,0:T(8,128)(2,1)}, bf16[10,1024]{1,0:T(8,128)(2,1)S(1)}, u32[]{:S(2)}, u32[]{:S(2)}) collective-permute-start(bf16[10,1024]{1,0:T(8,128)(2,1)} %bitcast.18), channel_id=1, source_target_pairs={{0,8},{1,9},{2,10},{3,11},{4,12},{5,13},{6,14},{7,15},{8,0},{9,1},... | collective-permute-start | bytes 61448 | tf_op jit(solution)/shard_map/ppermute | solution.py:510
  48.2 0.4 collective-permute-start.12
  48.6 1.9 %collective-permute-start.13 = (bf16[10,1024]{1,0:T(8,128)(2,1)}, bf16[10,1024]{1,0:T(8,128)(2,1)S(1)}, u32[]{:S(2)}, u32[]{:S(2)}) collective-permute-start(bf16[10,1024]{1,0:T(8,128)(2,1)} %bitcast.20), channel_id=1, source_target_pairs={{0,24},{1,25},{2,26},{3,27},{4,28},{5,29},{6,30},{7,31},{8,16},{9,... | collective-permute-start | bytes 61448 | tf_op jit(solution)/shard_map/ppermute | solution.py:510
  50.5 4.1 %left_mix.1.refs_8_ = bf16[1024,1280]{1,0:T(8,128)(2,1)} custom-call(bf16[320,32]{1,0:T(8,128)(2,1)} %get-tuple-element.44.left, bf16[32,4096]{1,0:T(8,128)(2,1)} %reshape.22.factors), custom_call_target="tpu_custom_call" | custom-call | flops 1000000000 | bytes 4000000 | tf_op jit(solution)/shard_map/left_mix/pallas_call | solution.py:385
  54.6 0.0 collective-permute-done.11
  54.6 0.0 collective-permute-done.12
  54.7 1.3 %collective-permute-start.14 = (bf16[40,1024]{1,0:T(8,128)(2,1)S(1)}, bf16[40,1024]{1,0:T(8,128)(2,1)S(1)}, u32[]{:S(2)}, u32[]{:S(2)}) collective-permute-start(bf16[40,1024]{1,0:T(8,128)(2,1)S(1)} %pad_maximum_fusion.refs_0_), channel_id=1, source_target_pairs={{0,2},{1,3},{2,0},{3,1},{4,6},{5,7},{6,4},{7,5},{8,10},{9,11},{10,... | collective-permute-start | bytes 245768 | tf_op jit(solution)/shard_map/ppermute | solution.py:510
  56.0 0.8 %collective-permute-start.15 = (bf16[40,1024]{1,0:T(8,128)(2,1)S(1)}, bf16[40,1024]{1,0:T(8,128)(2,1)S(1)}, u32[]{:S(2)}, u32[]{:S(2)}) collective-permute-start(bf16[40,1024]{1,0:T(8,128)(2,1)S(1)} %pad_maximum_fusion.refs_0_), channel_id=1, source_target_pairs={{0,4},{1,5},{2,6},{3,7},{4,0},{5,1},{6,2},{7,3},{8,12},{9,13},{10,... | collective-permute-start | bytes 245768 | tf_op jit(solution)/shard_map/ppermute | solution.py:510
  56.8 1.4 %collective-permute-start.16 = (bf16[40,1024]{1,0:T(8,128)(2,1)S(1)}, bf16[40,1024]{1,0:T(8,128)(2,1)S(1)}, u32[]{:S(2)}, u32[]{:S(2)}) collective-permute-start(bf16[40,1024]{1,0:T(8,128)(2,1)S(1)} %pad_maximum_fusion.refs_0_), channel_id=1, source_target_pairs={{0,6},{1,7},{2,4},{3,5},{4,2},{5,3},{6,0},{7,1},{8,14},{9,15},{10,... | collective-permute-start | bytes 245768 | tf_op jit(solution)/shard_map/ppermute | solution.py:510
  58.3 0.9 %collective-permute-done.14.refs_1_ = bf16[40,1024]{1,0:T(8,128)(2,1)S(1)} collective-permute-done((bf16[40,1024]{1,0:T(8,128)(2,1)S(1)}, bf16[40,1024]{1,0:T(8,128)(2,1)S(1)}, u32[]{:S(2)}, u32[]{:S(2)}) %collective-permute-start.14) | collective-permute-done | bytes 81952 | tf_op jit(solution)/shard_map/ppermute | solution.py:510
  59.2 1.2 %collective-permute-done.15.refs_2_ = bf16[40,1024]{1,0:T(8,128)(2,1)S(1)} collective-permute-done((bf16[40,1024]{1,0:T(8,128)(2,1)S(1)}, bf16[40,1024]{1,0:T(8,128)(2,1)S(1)}, u32[]{:S(2)}, u32[]{:S(2)}) %collective-permute-start.15) | collective-permute-done | bytes 81952 | tf_op jit(solution)/shard_map/ppermute | solution.py:510
  60.4 1.7 %collective-permute-done.16.refs_3_ = bf16[40,1024]{1,0:T(8,128)(2,1)S(1)} collective-permute-done((bf16[40,1024]{1,0:T(8,128)(2,1)S(1)}, bf16[40,1024]{1,0:T(8,128)(2,1)S(1)}, u32[]{:S(2)}, u32[]{:S(2)}) %collective-permute-start.16) | collective-permute-done | bytes 81952 | tf_op jit(solution)/shard_map/ppermute | solution.py:510
  62.2 1.2 %collective-permute-done.20.refs_7_ = bf16[40,1024]{1,0:T(8,128)(2,1)S(1)} collective-permute-done((bf16[40,1024]{1,0:T(8,128)(2,1)S(1)}, bf16[40,1024]{1,0:T(8,128)(2,1)S(1)}, u32[]{:S(2)}, u32[]{:S(2)}) %collective-permute-start.20) | collective-permute-done | bytes 81952 | tf_op jit(solution)/shard_map/ppermute | solution.py:510
  63.5 0.6 copy-done.14
  64.1 9.5 %pair_update.1 = bf16[10,320,128]{2,1,0:T(8,128)(2,1)} custom-call(s32[1]{0:T(128)} %bitcast.idx, bf16[40,1024]{1,0:T(8,128)(2,1)} %copy-done.2, bf16[40,1024]{1,0:T(8,128)(2,1)} %copy-done.8, bf16[40,1024]{1,0:T(8,128)(2,1)} %copy-done.9, bf16[40,1024]{1,0:T(8,128)(2,1)} %copy-done.10, bf16[40,1024]{1,0:T(8,128)(2,1)} %copy-done.11, ...), custom_call_target="tpu_custom_call" | custom-call | flops 10000000000 | bytes 4000000 | tf_op jit(solution)/shard_map/pair_update/pallas_call | solution.py:458
  (50 shorter events, 0.2 us)
Async XLA Ops:
  0.6 10.1 %collective-permute-start = (bf16[1,320,256]{2,1,0:T(8,128)(2,1)}, bf16[1,320,256]{2,1,0:T(8,128)(2,1)S(1)}, u32[]{:S(2)}, u32[]{:S(2)}) collective-permute-start(bf16[1,320,256]{2,1,0:T(8,128)(2,1)} %refs_0_.1), channel_id=1, source_target_pairs={{0,1},{1,0},{2,3},{3,2},{4,5},{5,4},{6,7},{7,6},{8,9},{9,8},{10,11... | collective-permute-start | bytes 491528 | tf_op jit(solution)/shard_map/ppermute | solution.py:510
  1.1 9.5 %collective-permute-start.1 = (bf16[1,320,256]{2,1,0:T(8,128)(2,1)}, bf16[1,320,256]{2,1,0:T(8,128)(2,1)S(1)}, u32[]{:S(2)}, u32[]{:S(2)}) collective-permute-start(bf16[1,320,256]{2,1,0:T(8,128)(2,1)} %refs_0_.1), channel_id=1, source_target_pairs={{0,2},{1,3},{2,0},{3,1},{4,6},{5,7},{6,4},{7,5},{8,10},{9,11},{10,... | collective-permute-start | bytes 491528 | tf_op jit(solution)/shard_map/ppermute | solution.py:510
  3.7 10.0 %collective-permute-start.2 = (bf16[1,320,256]{2,1,0:T(8,128)(2,1)}, bf16[1,320,256]{2,1,0:T(8,128)(2,1)S(1)}, u32[]{:S(2)}, u32[]{:S(2)}) collective-permute-start(bf16[1,320,256]{2,1,0:T(8,128)(2,1)} %refs_0_.1), channel_id=1, source_target_pairs={{0,4},{1,5},{2,6},{3,7},{4,0},{5,1},{6,2},{7,3},{8,12},{9,13},{10,... | collective-permute-start | bytes 491528 | tf_op jit(solution)/shard_map/ppermute | solution.py:510
  5.2 8.5 %collective-permute-start.3 = (bf16[1,320,256]{2,1,0:T(8,128)(2,1)}, bf16[1,320,256]{2,1,0:T(8,128)(2,1)S(1)}, u32[]{:S(2)}, u32[]{:S(2)}) collective-permute-start(bf16[1,320,256]{2,1,0:T(8,128)(2,1)} %refs_0_.1), channel_id=1, source_target_pairs={{0,6},{1,7},{2,4},{3,5},{4,2},{5,3},{6,0},{7,1},{8,14},{9,15},{10,... | collective-permute-start | bytes 491528 | tf_op jit(solution)/shard_map/ppermute | solution.py:510
  10.7 7.6 %copy-start.7 = (bf16[1,320,256]{2,1,0:T(8,128)(2,1)}, bf16[1,320,256]{2,1,0:T(8,128)(2,1)S(1)}, u32[]{:S(2)}) copy-start(bf16[1,320,256]{2,1,0:T(8,128)(2,1)S(1)} %collective-permute-done.refs_1_) | copy-start | bytes 491524
  13.8 4.6 %copy-start.3 = (bf16[3,320,256]{2,1,0:T(8,128)(2,1)}, bf16[3,320,256]{2,1,0:T(8,128)(2,1)S(1)}, u32[]{:S(2)}) copy-start(bf16[3,320,256]{2,1,0:T(8,128)(2,1)S(1)} %constant_dynamic-update-slice_fusion.refs_2_) | copy-start | bytes 1474564
  13.8 4.5 %collective-permute-start.7 = (bf16[3,320,256]{2,1,0:T(8,128)(2,1)S(1)}, bf16[3,320,256]{2,1,0:T(8,128)(2,1)S(1)}, u32[]{:S(2)}, u32[]{:S(2)}) collective-permute-start(bf16[3,320,256]{2,1,0:T(8,128)(2,1)S(1)} %constant_dynamic-update-slice_fusion.refs_2_), channel_id=1, source_target_pairs={{0,1},{1,0},{2,3},{3,2},{4,5},{5,4},{6,7},{7,6},{8,9},{9,8},{10,11... | collective-permute-start | bytes 1474568 | tf_op jit(solution)/shard_map/ppermute | solution.py:510
  13.9 10.7 %collective-permute-start.4 = (bf16[10,8,320]{2,1,0:T(8,128)(2,1)}, bf16[10,8,320]{2,1,0:T(8,128)(2,1)S(1)}, u32[]{:S(2)}, u32[]{:S(2)}) collective-permute-start(bf16[10,8,320]{2,1,0:T(8,128)(2,1)} %get-tuple-element.28.refs_0_), channel_id=1, source_target_pairs={{0,8},{1,9},{2,10},{3,11},{4,12},{5,13},{6,14},{7,15},{8,0},{9,1},... | collective-permute-start | bytes 153608 | tf_op jit(solution)/shard_map/ppermute | solution.py:510
  15.5 9.1 %collective-permute-start.5 = (bf16[10,8,320]{2,1,0:T(8,128)(2,1)}, bf16[10,8,320]{2,1,0:T(8,128)(2,1)S(1)}, u32[]{:S(2)}, u32[]{:S(2)}) collective-permute-start(bf16[10,8,320]{2,1,0:T(8,128)(2,1)} %get-tuple-element.28.refs_0_), channel_id=1, source_target_pairs={{0,16},{1,17},{2,18},{3,19},{4,20},{5,21},{6,22},{7,23},{8,24},{9,... | collective-permute-start | bytes 153608 | tf_op jit(solution)/shard_map/ppermute | solution.py:510
  18.1 6.5 %collective-permute-start.6 = (bf16[10,8,320]{2,1,0:T(8,128)(2,1)}, bf16[10,8,320]{2,1,0:T(8,128)(2,1)S(1)}, u32[]{:S(2)}, u32[]{:S(2)}) collective-permute-start(bf16[10,8,320]{2,1,0:T(8,128)(2,1)} %get-tuple-element.28.refs_0_), channel_id=1, source_target_pairs={{0,24},{1,25},{2,26},{3,27},{4,28},{5,29},{6,30},{7,31},{8,16},{9,... | collective-permute-start | bytes 153608 | tf_op jit(solution)/shard_map/ppermute | solution.py:510
  18.3 0.8 %copy-start.6 = (bf16[3,320,256]{2,1,0:T(8,128)(2,1)}, bf16[3,320,256]{2,1,0:T(8,128)(2,1)S(1)}, u32[]{:S(2)}) copy-start(bf16[3,320,256]{2,1,0:T(8,128)(2,1)S(1)} %collective-permute-done.7.refs_3_) | copy-start | bytes 1474564
  24.5 0.6 copy-start.15
  24.6 0.6 copy-start.16
  24.6 0.6 copy-start.17
  25.2 10.3 %copy-start = (bf16[256,4,256]{2,1,0:T(4,128)(2,1)S(1)}, bf16[256,4,256]{2,1,0:T(4,128)(2,1)}, u32[]{:S(2)}) copy-start(bf16[256,4,256]{2,1,0:T(4,128)(2,1)} %param.35) | copy-start | bytes 1572868
  25.2 11.2 %copy-start.4 = (bf16[256,64]{0,1:T(8,128)(2,1)S(1)}, bf16[256,64]{0,1:T(8,128)(2,1)}, u32[]{:S(2)}) copy-start(bf16[256,64]{0,1:T(8,128)(2,1)} %param.41) | copy-start | bytes 98308
  25.2 12.0 %copy-start.1 = (bf16[1024,128]{1,0:T(8,128)(2,1)S(1)}, bf16[1024,128]{1,0:T(8,128)(2,1)}, u32[]{:S(2)}) copy-start(bf16[1024,128]{1,0:T(8,128)(2,1)} %param.42) | copy-start | bytes 786436
  31.2 6.8 %collective-permute-start.10 = (bf16[10,8,256]{2,1,0:T(8,128)(2,1)}, bf16[10,8,256]{2,1,0:T(8,128)(2,1)S(1)}, u32[]{:S(2)}, u32[]{:S(2)}) collective-permute-start(bf16[10,8,256]{2,1,0:T(8,128)(2,1)} %get-tuple-element.42), channel_id=1, source_target_pairs={{0,24},{1,25},{2,26},{3,27},{4,28},{5,29},{6,30},{7,31},{8,16},{9,... | collective-permute-start | bytes 122888 | tf_op jit(solution)/shard_map/ppermute | solution.py:510
  34.8 4.2 %collective-permute-start.8 = (bf16[10,8,256]{2,1,0:T(8,128)(2,1)}, bf16[10,8,256]{2,1,0:T(8,128)(2,1)S(1)}, u32[]{:S(2)}, u32[]{:S(2)}) collective-permute-start(bf16[10,8,256]{2,1,0:T(8,128)(2,1)} %get-tuple-element.40), channel_id=1, source_target_pairs={{0,8},{1,9},{2,10},{3,11},{4,12},{5,13},{6,14},{7,15},{8,0},{9,1},... | collective-permute-start | bytes 122888 | tf_op jit(solution)/shard_map/ppermute | solution.py:510
  34.8 5.1 %collective-permute-start.9 = (bf16[10,8,256]{2,1,0:T(8,128)(2,1)}, bf16[10,8,256]{2,1,0:T(8,128)(2,1)S(1)}, u32[]{:S(2)}, u32[]{:S(2)}) collective-permute-start(bf16[10,8,256]{2,1,0:T(8,128)(2,1)} %get-tuple-element.41), channel_id=1, source_target_pairs={{0,16},{1,17},{2,18},{3,19},{4,20},{5,21},{6,22},{7,23},{8,24},{9,... | collective-permute-start | bytes 122888 | tf_op jit(solution)/shard_map/ppermute | solution.py:510
  38.0 1.9 %copy-start.18 = (bf16[10,8,256]{2,1,0:T(8,128)(2,1)}, bf16[10,8,256]{2,1,0:T(8,128)(2,1)S(1)}, u32[]{:S(2)}) copy-start(bf16[10,8,256]{2,1,0:T(8,128)(2,1)S(1)} %collective-permute-done.10.refs_3_) | copy-start | bytes 122884
  39.0 0.9 %copy-start.19 = (bf16[10,8,256]{2,1,0:T(8,128)(2,1)}, bf16[10,8,256]{2,1,0:T(8,128)(2,1)S(1)}, u32[]{:S(2)}) copy-start(bf16[10,8,256]{2,1,0:T(8,128)(2,1)S(1)} %collective-permute-done.8.refs_1_) | copy-start | bytes 122884
  39.9 0.6 copy-start.20
  46.1 8.5 %collective-permute-start.11 = (bf16[10,1024]{1,0:T(8,128)(2,1)}, bf16[10,1024]{1,0:T(8,128)(2,1)S(1)}, u32[]{:S(2)}, u32[]{:S(2)}) collective-permute-start(bf16[10,1024]{1,0:T(8,128)(2,1)} %bitcast.18), channel_id=1, source_target_pairs={{0,8},{1,9},{2,10},{3,11},{4,12},{5,13},{6,14},{7,15},{8,0},{9,1},... | collective-permute-start | bytes 61448 | tf_op jit(solution)/shard_map/ppermute | solution.py:510
  48.2 6.5 %collective-permute-start.12 = (bf16[10,1024]{1,0:T(8,128)(2,1)}, bf16[10,1024]{1,0:T(8,128)(2,1)S(1)}, u32[]{:S(2)}, u32[]{:S(2)}) collective-permute-start(bf16[10,1024]{1,0:T(8,128)(2,1)} %bitcast.19), channel_id=1, source_target_pairs={{0,16},{1,17},{2,18},{3,19},{4,20},{5,21},{6,22},{7,23},{8,24},{9,... | collective-permute-start | bytes 61448 | tf_op jit(solution)/shard_map/ppermute | solution.py:510
  48.6 6.0 %collective-permute-start.13 = (bf16[10,1024]{1,0:T(8,128)(2,1)}, bf16[10,1024]{1,0:T(8,128)(2,1)S(1)}, u32[]{:S(2)}, u32[]{:S(2)}) collective-permute-start(bf16[10,1024]{1,0:T(8,128)(2,1)} %bitcast.20), channel_id=1, source_target_pairs={{0,24},{1,25},{2,26},{3,27},{4,28},{5,29},{6,30},{7,31},{8,16},{9,... | collective-permute-start | bytes 61448 | tf_op jit(solution)/shard_map/ppermute | solution.py:510
  50.5 4.1 %copy-start.5 = (bf16[1,10,1024]{2,1,0:T(8,128)(2,1)S(1)}, bf16[1,10,1024]{2,1,0:T(8,128)(2,1)}, u32[]{:S(2)}) copy-start(bf16[1,10,1024]{2,1,0:T(8,128)(2,1)} %get-tuple-element.45) | copy-start | bytes 61444
  54.7 8.8 %copy-start.2 = (bf16[40,1024]{1,0:T(8,128)(2,1)}, bf16[40,1024]{1,0:T(8,128)(2,1)S(1)}, u32[]{:S(2)}) copy-start(bf16[40,1024]{1,0:T(8,128)(2,1)S(1)} %pad_maximum_fusion.refs_0_) | copy-start | bytes 245764
  54.7 4.5 %collective-permute-start.14 = (bf16[40,1024]{1,0:T(8,128)(2,1)S(1)}, bf16[40,1024]{1,0:T(8,128)(2,1)S(1)}, u32[]{:S(2)}, u32[]{:S(2)}) collective-permute-start(bf16[40,1024]{1,0:T(8,128)(2,1)S(1)} %pad_maximum_fusion.refs_0_), channel_id=1, source_target_pairs={{0,2},{1,3},{2,0},{3,1},{4,6},{5,7},{6,4},{7,5},{8,10},{9,11},{10,... | collective-permute-start | bytes 245768 | tf_op jit(solution)/shard_map/ppermute | solution.py:510
  56.0 4.4 %collective-permute-start.15 = (bf16[40,1024]{1,0:T(8,128)(2,1)S(1)}, bf16[40,1024]{1,0:T(8,128)(2,1)S(1)}, u32[]{:S(2)}, u32[]{:S(2)}) collective-permute-start(bf16[40,1024]{1,0:T(8,128)(2,1)S(1)} %pad_maximum_fusion.refs_0_), channel_id=1, source_target_pairs={{0,4},{1,5},{2,6},{3,7},{4,0},{5,1},{6,2},{7,3},{8,12},{9,13},{10,... | collective-permute-start | bytes 245768 | tf_op jit(solution)/shard_map/ppermute | solution.py:510
  56.8 5.3 %collective-permute-start.16 = (bf16[40,1024]{1,0:T(8,128)(2,1)S(1)}, bf16[40,1024]{1,0:T(8,128)(2,1)S(1)}, u32[]{:S(2)}, u32[]{:S(2)}) collective-permute-start(bf16[40,1024]{1,0:T(8,128)(2,1)S(1)} %pad_maximum_fusion.refs_0_), channel_id=1, source_target_pairs={{0,6},{1,7},{2,4},{3,5},{4,2},{5,3},{6,0},{7,1},{8,14},{9,15},{10,... | collective-permute-start | bytes 245768 | tf_op jit(solution)/shard_map/ppermute | solution.py:510
  58.3 3.9 %collective-permute-start.17 = (bf16[40,1024]{1,0:T(8,128)(2,1)S(1)}, bf16[40,1024]{1,0:T(8,128)(2,1)S(1)}, u32[]{:S(2)}, u32[]{:S(2)}) collective-permute-start(bf16[40,1024]{1,0:T(8,128)(2,1)S(1)} %pad_maximum_fusion.refs_0_), channel_id=1, source_target_pairs={{0,1},{1,0},{2,3},{3,2},{4,5},{5,4},{6,7},{7,6},{8,9},{9,8},{10,11... | collective-permute-start | bytes 245768 | tf_op jit(solution)/shard_map/ppermute | solution.py:510
  59.2 4.2 %copy-start.8 = (bf16[40,1024]{1,0:T(8,128)(2,1)}, bf16[40,1024]{1,0:T(8,128)(2,1)S(1)}, u32[]{:S(2)}) copy-start(bf16[40,1024]{1,0:T(8,128)(2,1)S(1)} %collective-permute-done.14.refs_1_) | copy-start | bytes 245764
  59.2 3.0 %collective-permute-start.18 = (bf16[40,1024]{1,0:T(8,128)(2,1)S(1)}, bf16[40,1024]{1,0:T(8,128)(2,1)S(1)}, u32[]{:S(2)}, u32[]{:S(2)}) collective-permute-start(bf16[40,1024]{1,0:T(8,128)(2,1)S(1)} %collective-permute-done.14.refs_1_), channel_id=1, source_target_pairs={{0,1},{1,0},{2,3},{3,2},{4,5},{5,4},{6,7},{7,6},{8,9},{9,8},{10,11... | collective-permute-start | bytes 245768 | tf_op jit(solution)/shard_map/ppermute | solution.py:510
  60.4 3.0 %copy-start.9 = (bf16[40,1024]{1,0:T(8,128)(2,1)}, bf16[40,1024]{1,0:T(8,128)(2,1)S(1)}, u32[]{:S(2)}) copy-start(bf16[40,1024]{1,0:T(8,128)(2,1)S(1)} %collective-permute-done.15.refs_2_) | copy-start | bytes 245764
  60.4 1.8 %collective-permute-start.19 = (bf16[40,1024]{1,0:T(8,128)(2,1)S(1)}, bf16[40,1024]{1,0:T(8,128)(2,1)S(1)}, u32[]{:S(2)}, u32[]{:S(2)}) collective-permute-start(bf16[40,1024]{1,0:T(8,128)(2,1)S(1)} %collective-permute-done.15.refs_2_), channel_id=1, source_target_pairs={{0,1},{1,0},{2,3},{3,2},{4,5},{5,4},{6,7},{7,6},{8,9},{9,8},{10,11... | collective-permute-start | bytes 245768 | tf_op jit(solution)/shard_map/ppermute | solution.py:510
  62.2 1.3 %copy-start.10 = (bf16[40,1024]{1,0:T(8,128)(2,1)}, bf16[40,1024]{1,0:T(8,128)(2,1)S(1)}, u32[]{:S(2)}) copy-start(bf16[40,1024]{1,0:T(8,128)(2,1)S(1)} %collective-permute-done.16.refs_3_) | copy-start | bytes 245764
  62.2 1.3 %collective-permute-start.20 = (bf16[40,1024]{1,0:T(8,128)(2,1)S(1)}, bf16[40,1024]{1,0:T(8,128)(2,1)S(1)}, u32[]{:S(2)}, u32[]{:S(2)}) collective-permute-start(bf16[40,1024]{1,0:T(8,128)(2,1)S(1)} %collective-permute-done.16.refs_3_), channel_id=1, source_target_pairs={{0,1},{1,0},{2,3},{3,2},{4,5},{5,4},{6,7},{7,6},{8,9},{9,8},{10,11... | collective-permute-start | bytes 245768 | tf_op jit(solution)/shard_map/ppermute | solution.py:510
  62.2 1.3 %copy-start.11 = (bf16[40,1024]{1,0:T(8,128)(2,1)}, bf16[40,1024]{1,0:T(8,128)(2,1)S(1)}, u32[]{:S(2)}) copy-start(bf16[40,1024]{1,0:T(8,128)(2,1)S(1)} %collective-permute-done.17.refs_4_) | copy-start | bytes 245764
  62.2 1.3 %copy-start.12 = (bf16[40,1024]{1,0:T(8,128)(2,1)}, bf16[40,1024]{1,0:T(8,128)(2,1)S(1)}, u32[]{:S(2)}) copy-start(bf16[40,1024]{1,0:T(8,128)(2,1)S(1)} %collective-permute-done.18.refs_5_) | copy-start | bytes 245764
  62.2 1.3 %copy-start.13 = (bf16[40,1024]{1,0:T(8,128)(2,1)}, bf16[40,1024]{1,0:T(8,128)(2,1)S(1)}, u32[]{:S(2)}) copy-start(bf16[40,1024]{1,0:T(8,128)(2,1)S(1)} %collective-permute-done.19.refs_6_) | copy-start | bytes 245764
  63.4 0.6 copy-start.14

commit v3 on v2

--- a/solution.py
+++ b/solution.py
@@ -15,7 +15,10 @@
 LOG2E = 1.4426950408889634
 F32 = jnp.float32
 BF16 = jnp.bfloat16
-VMEM_LIMIT = 56 * 1024 * 1024
+
+
+def vmem_limit(length):
+    return (16 if length is not None and length <= 320 else 56) * 1024 * 1024
 
 
 def dot(a, b):
@@ -112,8 +115,8 @@
             jax.ShapeDtypeStruct((rows, HEADS, length), BF16),
         ],
         scratch_shapes=[pltpu.VMEM((2 * length, depth), F32), pltpu.VMEM((length, depth), F32)],
-        compiler_params=pltpu.CompilerParams(vmem_limit_bytes=VMEM_LIMIT),
-        cost_estimate=pl.CostEstimate(flops=4 * rows * length * depth * HEADS, bytes_accessed=4000000, transcendentals=0),
+        compiler_params=pltpu.CompilerParams(vmem_limit_bytes=vmem_limit(None)),
+        cost_estimate=pl.CostEstimate(flops=4 * 10**9, bytes_accessed=4000000, transcendentals=10**5),
         name="pair_bias",
     )(idx, chain, pair, chain, table, gain[None, :], factors.T)
 
@@ -180,8 +183,8 @@
         out_specs=[vmem] * 5,
         out_shape=[wide, wide, narrow, narrow, narrow],
         scratch_shapes=[pltpu.VMEM((sub * own, width), F32)],
-        compiler_params=pltpu.CompilerParams(vmem_limit_bytes=VMEM_LIMIT),
-        cost_estimate=pl.CostEstimate(flops=10**9, bytes_accessed=4000000, transcendentals=10**5),
+        compiler_params=pltpu.CompilerParams(vmem_limit_bytes=vmem_limit(length)),
+        cost_estimate=pl.CostEstimate(flops=3 * 10**9, bytes_accessed=4000000, transcendentals=10**5),
         name="row_project",
     )(idx, *msa_rows, gain[None, :], entry)
 
@@ -248,50 +251,61 @@
             pltpu.VMEM((own, HEADS, length), F32),
             pltpu.VMEM((sub * own, width), F32),
         ],
-        compiler_params=pltpu.CompilerParams(vmem_limit_bytes=VMEM_LIMIT),
-        cost_estimate=pl.CostEstimate(flops=10**10, bytes_accessed=4000000, transcendentals=10**6),
+        compiler_params=pltpu.CompilerParams(vmem_limit_bytes=vmem_limit(length)),
+        cost_estimate=pl.CostEstimate(flops=4 * 10**9, bytes_accessed=4000000, transcendentals=10**5),
         name="row_attention",
     )(idx, *bias_blocks, keys, values, query, gate, own_rows, validity, amino, exit_)
 
 
 def column_kernel(idx, *refs, sub, far, rows, block, depth, width):
     piece_refs, refs = refs[:far], refs[far:]
-    (
-        validity,
-        col_gain,
-        entry,
-        exit_,
-        ff_gain,
-        widen,
-        narrow,
-        product_gain,
-        twin,
-        updated,
-        left,
-        right,
-        start_rows,
-        gated,
-    ) = refs
+    entry, twin, *sources = refs[:9]
+    updated, left, right, start_rows, gated, *held = refs[9:-1]
+    sems = refs[-1]
+    copies = [pltpu.make_async_copy(src, dst, sems.at[n]) for n, (src, dst) in enumerate(zip(sources, held))]
+    steps = rows // block
+
+    def begin():
+        for copy in copies:
+            copy.start()
+
+    def arrived(*which):
+        def wait():
+            for n in which:
+                copies[n].wait()
+
+        if steps == 1:
+            wait()
+        else:
+            pl.when(pl.program_id(0) == 0)(wait)
+        return [held[n][...] for n in which]
+
+    if steps == 1:
+        begin()
+    else:
+        pl.when(pl.program_id(0) == 0)(begin)
     me = idx[0]
     z = me // sub
-    first = me * rows + pl.program_id(0) * block
+    first = me * rows + (0 if steps == 1 else pl.program_id(0) * block)
     scale = (width // HEADS) ** -0.5 * LOG2E
     total = block * depth
     for b in range(far):
         here = pl.ds(pl.multiple_of((z ^ b) * sub, sub), sub)
         start_rows[:, here, :] = piece_refs[b][...].astype(F32)
     x = start_rows[...].reshape(total, width)
-    normed = layer_norm(x, col_gain[...]).astype(BF16)
+    (col_gain,) = arrived(0)
+    normed = layer_norm(x, col_gain).astype(BF16)
     proj = dot(normed, entry[...])
     query = proj[:, :width] * scale
     keys = proj[:, width : 2 * width].astype(BF16)
     values = proj[:, 2 * width : 3 * width].astype(BF16)
     gate = jax.nn.sigmoid(proj[:, 3 * width :])
 
+    (validity,) = arrived(1)
     length = validity.shape[1]
     lanes = 128
     pick = one_hot(iota((length, lanes), 0) == first + iota((length, lanes), 1))
-    valid = dot(validity[...].astype(F32).astype(BF16), pick)
+    valid = dot(validity.astype(F32).astype(BF16), pick)
     head_of = iota((HEADS, width), 1) // (width // HEADS)
     head_mask = jnp.where(head_of == iota((HEADS, width), 0), 1.0, 0.0)
     for i in range(block):
@@ -304,11 +318,12 @@
         mixed = dot_tn(weights, values[here])
         merged = jnp.sum(mixed.reshape(depth, HEADS, width) * head_mask[None], axis=1)
         gated[here, :] = merged * gate[here]
-    x = x + dot(gated[...].astype(BF16), exit_[...])
-    hidden = jnp.maximum(dot(layer_norm(x, ff_gain[...]).astype(BF16), widen[...]), 0.0).astype(BF16)
-    x = x + dot(hidden, narrow[...])
+    exit_, ff_gain, widen, narrow, product_gain = arrived(2, 3, 4, 5, 6)
+    x = x + dot(gated[...].astype(BF16), exit_)
+    hidden = jnp.maximum(dot(layer_norm(x, ff_gain).astype(BF16), widen), 0.0).astype(BF16)
+    x = x + dot(hidden, narrow)
     updated[...] = x.astype(BF16).reshape(block, depth, width)
-    outer = layer_norm(x, product_gain[...]).astype(BF16)
+    outer = layer_norm(x, product_gain).astype(BF16)
     both = dot(outer, twin[...])
     channels = twin.shape[1] // 2
     spread = iota((depth, channels * depth), 1)
@@ -321,7 +336,7 @@
         here = slice(i * depth, (i + 1) * depth)
         part = (both[here] * valid[:, i : i + 1]).astype(BF16)
         left[here, :] = part[:, :channels]
-        right[i : i + 1, :] = jnp.sum(dot(part, repeat) * mine, axis=0, keepdims=True).astype(BF16)
+        right[0, i : i + 1, :] = jnp.sum(dot(part, repeat) * mine, axis=0, keepdims=True).astype(BF16)
 
 
 def column_call(idx, pieces, validity, col_gain, entry, exit_, ff_gain, widen, narrow, product_gain, twin):
@@ -332,39 +347,45 @@
     while block * depth > 320 and block % 2 == 0:
         block //= 2
     channels = twin.shape[1] // 2
-    vmem = lambda a: pl.BlockSpec(a.shape, lambda s: (0,) * a.ndim)
-    rest = [
+    steps = rows // block
+    here = [entry, twin]
+    sources = [
+        col_gain[None, :],
         validity,
-        col_gain[None, :],
-        entry,
         exit_,
         ff_gain[None, :],
         widen,
         narrow,
         product_gain[None, :],
-        twin,
     ]
+    if steps == 1:
+        grid, spec = {}, lambda shape, index: pl.BlockSpec(memory_space=pltpu.VMEM)
+    else:
+        grid, spec = {"grid": (steps,)}, pl.BlockSpec
     return pl.pallas_call(
         functools.partial(column_kernel, sub=sub, far=far, rows=rows, block=block, depth=depth, width=width),
-        grid=(rows // block,),
+        **grid,
         in_specs=[pl.BlockSpec(memory_space=pltpu.SMEM)]
-        + [pl.BlockSpec((block, sub, width), lambda s: (s, 0, 0))] * far
-        + [vmem(a) for a in rest],
+        + [spec((block, sub, width), lambda s: (s, 0, 0))] * far
+        + [spec(a.shape, lambda s: (0, 0)) for a in here]
+        + [pl.BlockSpec(memory_space=pltpu.HBM)] * len(sources),
         out_specs=[
-            pl.BlockSpec((block, depth, width), lambda s: (s, 0, 0)),
-            pl.BlockSpec((block * depth, channels), lambda s: (s, 0)),
-            pl.BlockSpec((None, block, channels * depth), lambda s: (s, 0, 0)),
+            spec((block, depth, width), lambda s: (s, 0, 0)),
+            spec((block * depth, channels), lambda s: (s, 0)),
+            spec((1, block, channels * depth), lambda s: (s, 0, 0)),
         ],
         out_shape=[
             jax.ShapeDtypeStruct((rows, depth, width), BF16),
             jax.ShapeDtypeStruct((rows * depth, channels), BF16),
-            jax.ShapeDtypeStruct((rows // block, block, channels * depth), BF16),
-        ],
-        scratch_shapes=[pltpu.VMEM((block, depth, width), F32), pltpu.VMEM((block * depth, width), F32)],
-        compiler_params=pltpu.CompilerParams(vmem_limit_bytes=VMEM_LIMIT),
-        cost_estimate=pl.CostEstimate(flops=10**10, bytes_accessed=4000000, transcendentals=10**6),
+            jax.ShapeDtypeStruct((steps, block, channels * depth), BF16),
+        ],
+        scratch_shapes=[pltpu.VMEM((block, depth, width), F32), pltpu.VMEM((block * depth, width), F32)]
+        + [pltpu.VMEM(a.shape, a.dtype) for a in sources]
+        + [pltpu.SemaphoreType.DMA((len(sources),))],
+        compiler_params=pltpu.CompilerParams(vmem_limit_bytes=vmem_limit(length)),
+        cost_estimate=pl.CostEstimate(flops=5 * 10**9, bytes_accessed=4000000, transcendentals=10**5),
         name="column_attention",
-    )(idx, *pieces, *rest)
+    )(idx, *pieces, *here, *sources)
 
 
 def mix_kernel(left, factors, out, *, rows, depth):
@@ -377,7 +398,7 @@
                 out[(e + f) * depth : (e + f + 1) * depth, i * lanes : (i + 1) * lanes] = block
 
 
-def mix_call(left, factors, rows):
+def mix_call(left, factors, rows, length):
     total, channels = left.shape
     depth = total // rows
     lanes = factors.shape[1] // channels
@@ -391,8 +412,8 @@
         ],
         out_specs=pl.BlockSpec((block * depth, rows * lanes), lambda s: (s, 0)),
         out_shape=jax.ShapeDtypeStruct((channels * depth, rows * lanes), BF16),
-        compiler_params=pltpu.CompilerParams(vmem_limit_bytes=VMEM_LIMIT),
-        cost_estimate=pl.CostEstimate(flops=10**9, bytes_accessed=4000000, transcendentals=0),
+        compiler_params=pltpu.CompilerParams(vmem_limit_bytes=vmem_limit(length)),
+        cost_estimate=pl.CostEstimate(flops=2 * 10**9, bytes_accessed=4000000, transcendentals=10**5),
         name="left_mix",
     )(left, factors)
 
@@ -404,13 +425,12 @@
     mixed, pair_one, validity, gain, widen, narrow, out, right, turned = refs
     me = idx[0]
     z, p = me // sub, me % sub
-    step = pl.program_id(0)
+    step = 0 if block == rows else pl.program_id(0)
     half = far * rows * sub // 2
     lanes = pair_one.shape[2]
     part = min(length, 320)
 
-    @pl.when(step == 0)
-    def _():
+    def first():
         r = iota((part, half), 1)
         b = div_const(r, rows, half)
         i = r - b * rows
@@ -430,6 +450,10 @@
         chunks(length, part, arrange)
         turned[...] = validity[...].astype(F32).T.astype(BF16)
 
+    if block == rows:
+        first()
+    else:
+        pl.when(step == 0)(first)
     i0 = me * rows + step * block
     target = i0 + iota((length, block * lanes), 1) // lanes
     mine = one_hot(iota((length, block * lanes), 0) == target)
@@ -451,28 +475,34 @@
 def finish_call(idx, near, across, mixed, pair_one, validity, gain, widen, narrow, sub, far):
     rows, length, lanes = pair_one.shape
     depth = validity.shape[0]
-    block = 2 if rows % 2 == 0 else 1
+    block = rows if length <= 320 else 2 if rows % 2 == 0 else 1
     product = mixed.shape[0]
-    vmem = lambda a: pl.BlockSpec(a.shape, lambda s: (0,) * a.ndim)
     gain = gain[None, :]
+    if block == rows:
+        grid, vmem = {}, lambda a: pl.BlockSpec(memory_space=pltpu.VMEM)
+        mixed_spec = pair_spec = vmem(mixed)
+    else:
+        grid, vmem = {"grid": (rows // block,)}, lambda a: pl.BlockSpec(a.shape, lambda s: (0,) * a.ndim)
+        mixed_spec = pl.BlockSpec((product, block * lanes), lambda s: (0, s))
+        pair_spec = pl.BlockSpec((block, length, lanes), lambda s: (s, 0, 0))
     return pl.pallas_call(
         functools.partial(finish_kernel, sub=sub, far=far, rows=rows, length=length, block=block),
-        grid=(rows // block,),
+        **grid,
         in_specs=[
             pl.BlockSpec(memory_space=pltpu.SMEM),
             *[vmem(a) for a in near + across],
-            pl.BlockSpec((product, block * lanes), lambda s: (0, s)),
-            pl.BlockSpec((block, length, lanes), lambda s: (s, 0, 0)),
+            mixed_spec,
+            pair_spec,
             vmem(validity),
             vmem(gain),
             vmem(widen),
             vmem(narrow),
         ],
-        out_specs=pl.BlockSpec((block, length, lanes), lambda s: (s, 0, 0)),
+        out_specs=pair_spec,
         out_shape=jax.ShapeDtypeStruct((rows, length, lanes), BF16),
         scratch_shapes=[pltpu.VMEM((length, product), BF16), pltpu.VMEM((length, depth), BF16)],
-        compiler_params=pltpu.CompilerParams(vmem_limit_bytes=VMEM_LIMIT),
-        cost_estimate=pl.CostEstimate(flops=10**10, bytes_accessed=4000000, transcendentals=0),
+        compiler_params=pltpu.CompilerParams(vmem_limit_bytes=vmem_limit(length)),
+        cost_estimate=pl.CostEstimate(flops=5 * 10**9, bytes_accessed=4000000, transcendentals=10**5),
         name="pair_update",
     )(idx, *near, *across, mixed, pair_one, validity, gain, widen, narrow)
 
@@ -519,8 +549,11 @@
         idx, amino_strand, couple_embedding, separation_embedding, couple_shift_scaling, couple_shift_factors
     )
     entry = horizontal_entry_factors.reshape(width, 4 * width)
-    bias, entry, beside, *near = lax.optimization_barrier((bias, entry, beside, *near))
-    bias_blocks = [bias] + [swap(bias, SUB * k) for k in range(1, far)]
+    bias_blocks = [swap(bias, SUB)]
+    later, entry, beside, *first = lax.optimization_barrier((bias, entry, beside, *near[:-1]))
+    bias_blocks += [swap(later, SUB * k) for k in range(2, far)]
+    bias_blocks = [bias] + bias_blocks
+    near = first + near[-1:]
     near = jnp.concatenate(near, 0)
     across = swap(near, 1)
     projected = project_call(
@@ -544,7 +577,7 @@
     channels = left.shape[1]
     right = right.reshape(rows, channels * depth)
     factors = product_exit_factors.reshape(channels, -1)
-    mixed = mix_call(left, factors, rows)
+    mixed = mix_call(left, factors, rows, alignment_validity.shape[1])
     parts = [right] + [swap(right, SUB * k) for k in range(1, far)]
     parts = lax.optimization_barrier((mixed, *parts))
     mixed, parts = parts[0], parts[1:]

time: 74.1 us -> 60.8 us (0.82)
  Pallas kernels: 34.1 us -> 19.6 us
  waiting for transfers between devices: 10 us -> 17.8 us
  local copies, waits for them, and re-layouts: 7.09 us -> 0.56 us
    ppermute x21, waiting for transfers between devices: 10 us -> 17.8 us  [swap(): return lax.ppermute(x, 'dap', [(d, d ^ distance) for d in range(devices)])]
    unnamed x47 -> x45, local copies, waits for them, and re-layouts: 6.26 us -> 0.43 us
    pallas_call x1, Pallas kernels: 9.53 us -> 4.82 us  [finish_call(): pl.pallas_call(functools.partial(finish_kernel, sub=sub, far=far, rows=ro...]
    pallas_call x1, Pallas kernels: 5.4 us -> 2.31 us  [project_call(): pl.pallas_call(functools.partial(project_kernel, sub=sub, far=far, rows=r...]
    pallas_call x1, Pallas kernels: 5.95 us -> 3.25 us  [row_call(): pl.pallas_call(functools.partial(row_kernel, sub=sub, far=far, rows=rows,...]
    pallas_call x1, Pallas kernels: 4.07 us -> 1.48 us  [mix_call(): pl.pallas_call(functools.partial(mix_kernel, rows=rows, depth=depth), gri...]
    pallas_call x1, Pallas kernels: 5.66 us -> 4.21 us  [column_call(): pl.pallas_call(functools.partial(column_kernel, sub=sub, far=far, rows=ro...]
  transfers between devices with their start and end apart: 21 -> 21, of which waited for: 7 -> 12; matrix products, arithmetic and copies ran while one was open for 6% -> 1% of each run, Pallas kernels for 18% -> 12%
where the time goes in v3:
time: 60.8 us; the launch traced here: 60.7 us
  starting transfers between devices  21.6 us (36%)
  Pallas kernels  19.6 us (32%)
  waiting for transfers between devices  17.8 us (29%)
  between operations  0.97 us (2%)
    ppermute x21, starting transfers between devices, swap(): return lax.ppermute(x, 'dap', [(d, d ^ distance) for d in range(devices)])  21.6 us
    ppermute x21, waiting for transfers between devices, swap(): return lax.ppermute(x, 'dap', [(d, d ^ distance) for d in range(devices)])  17.8 us
    pallas_call x1, Pallas kernels, finish_call(): pl.pallas_call(functools.partial(finish_kernel, sub=sub, far=far, rows=ro...  4.82 us
    pallas_call x1, Pallas kernels, column_call(): pl.pallas_call(functools.partial(column_kernel, sub=sub, far=far, rows=ro...  4.21 us
    pallas_call x1, Pallas kernels, pair_call(): pl.pallas_call(functools.partial(pair_kernel, rows=rows, length=length, b...  3.57 us
    pallas_call x1, Pallas kernels, row_call(): pl.pallas_call(functools.partial(row_kernel, sub=sub, far=far, rows=rows,...  3.25 us
    pallas_call x1, Pallas kernels, project_call(): pl.pallas_call(functools.partial(project_kernel, sub=sub, far=far, rows=r...  2.31 us
    pallas_call x1, Pallas kernels, mix_call(): pl.pallas_call(functools.partial(mix_kernel, rows=rows, depth=depth), gri...  1.48 us
  transfers between devices with their start and end apart: 21, of which 12 were waited for; matrix products, arithmetic and copies ran while one was open for 1% of the time, Pallas kernels for 12%

profile of v3, /device:TPU:0, one launch (start us, length us, event | category | flops | bytes accessed | tf_op | source)
XLA Modules:
  0.0 60.7 jit_solution(3352279763169527215)
XLA Ops:
  0.6 0.5 collective-permute-start.1
  1.1 2.6 %collective-permute-start.2 = (bf16[1,320,256]{2,1,0:T(8,128)(2,1)}, bf16[1,320,256]{2,1,0:T(8,128)(2,1)S(1)}, u32[]{:S(2)}, u32[]{:S(2)}) collective-permute-start(bf16[1,320,256]{2,1,0:T(8,128)(2,1)} %refs_0_.1), channel_id=1, source_target_pairs={{0,2},{1,3},{2,0},{3,1},{4,6},{5,7},{6,4},{7,5},{8,10},{9,11},{10,... | collective-permute-start | bytes 491528 | tf_op jit(solution)/shard_map/ppermute | solution.py:540
  3.7 1.5 %collective-permute-start.3 = (bf16[1,320,256]{2,1,0:T(8,128)(2,1)}, bf16[1,320,256]{2,1,0:T(8,128)(2,1)S(1)}, u32[]{:S(2)}, u32[]{:S(2)}) collective-permute-start(bf16[1,320,256]{2,1,0:T(8,128)(2,1)} %refs_0_.1), channel_id=1, source_target_pairs={{0,4},{1,5},{2,6},{3,7},{4,0},{5,1},{6,2},{7,3},{8,12},{9,13},{10,... | collective-permute-start | bytes 491528 | tf_op jit(solution)/shard_map/ppermute | solution.py:540
  5.2 0.0 collective-permute-start.6
  5.3 3.6 %pair_bias.1 = (f32[10,320,128]{2,1,0:T(8,128)}, bf16[10,8,320]{2,1,0:T(8,128)(2,1)}) custom-call(s32[1]{0:T(128)} %bitcast.idx, s32[320]{0:T(512)} %chain_row.1, bf16[10,320,128]{2,1,0:T(8,128)(2,1)} %pair.1, s32[320]{0:T(512)} %chain_row.1, f32[66,128]{1,0:T(8,128)} %table.1, f32[1,128]{1,0:T(1,128)} %bitcast.28, bf16[8,128]{1,0:T(8,128)(2,1)} %bitcast.27), custom_call_target="tpu_custom_call" | custom-call | flops 4000000000 | bytes 4000000 | tf_op jit(solution)/shard_map/pair_bias/pallas_call | solution.py:97
  8.8 0.0 copy-start.10
  8.9 0.1 copy.26
  9.0 0.0 collective-permute-done.2
  9.0 4.7 %collective-permute-done.3 = bf16[1,320,256]{2,1,0:T(8,128)(2,1)S(1)} collective-permute-done((bf16[1,320,256]{2,1,0:T(8,128)(2,1)}, bf16[1,320,256]{2,1,0:T(8,128)(2,1)S(1)}, u32[]{:S(2)}, u32[]{:S(2)}) %collective-permute-start.3) | collective-permute-done | bytes 163872 | tf_op jit(solution)/shard_map/ppermute | solution.py:540
  13.8 0.1 collective-permute-start.7
  13.9 1.6 %collective-permute-start = (bf16[10,8,320]{2,1,0:T(8,128)(2,1)S(1)}, bf16[10,8,320]{2,1,0:T(8,128)(2,1)S(1)}, u32[]{:S(2)}, u32[]{:S(2)}) collective-permute-start(bf16[10,8,320]{2,1,0:T(8,128)(2,1)S(1)} %copy-done.7), channel_id=1, source_target_pairs={{0,8},{1,9},{2,10},{3,11},{4,12},{5,13},{6,14},{7,15},{8,0},{9,1},... | collective-permute-start | bytes 153608 | tf_op jit(solution)/shard_map/ppermute | solution.py:540
  15.5 2.6 %collective-permute-start.4 = (bf16[10,8,320]{2,1,0:T(8,128)(2,1)S(1)}, bf16[10,8,320]{2,1,0:T(8,128)(2,1)S(1)}, u32[]{:S(2)}, u32[]{:S(2)}) collective-permute-start(bf16[10,8,320]{2,1,0:T(8,128)(2,1)S(1)} %copy-done.7), channel_id=1, source_target_pairs={{0,16},{1,17},{2,18},{3,19},{4,20},{5,21},{6,22},{7,23},{8,24},{9,... | collective-permute-start | bytes 153608 | tf_op jit(solution)/shard_map/ppermute | solution.py:540
  18.1 0.2 collective-permute-start.5
  18.3 0.0 copy-start.3
  18.3 0.0 copy-start.8
  18.4 0.0 copy-start.9
  18.4 2.3 %row_project.1 = (bf16[8,320,256]{2,1,0:T(8,128)(2,1)S(1)}, bf16[8,320,256]{2,1,0:T(8,128)(2,1)S(1)}, f32[320,256]{1,0:T(8,128)S(1)}, f32[320,256]{1,0:T(8,128)S(1)}, f32[320,256]{1,0:T(8,128)S(1)}) custom-call(s32[1]{0:T(128)} %bitcast.idx, bf16[1,320,256]{2,1,0:T(8,128)(2,1)S(1)} %copy-done.2, bf16[1,320,256]{2,1,0:T(8,128)(2,1)S(1)} %collective-permute-done.1.refs_1_, ...), custom_call_target="tpu_custom_call" | custom-call | flops 3000000000 | bytes 4000000 | tf_op jit(solution)/shard_map/row_project/pallas_call | solution.py:180
  20.7 1.6 %collective-permute-done.4.refs_2_ = bf16[10,8,320]{2,1,0:T(8,128)(2,1)S(1)} collective-permute-done((bf16[10,8,320]{2,1,0:T(8,128)(2,1)S(1)}, bf16[10,8,320]{2,1,0:T(8,128)(2,1)S(1)}, u32[]{:S(2)}, u32[]{:S(2)}) %collective-permute-start.4) | collective-permute-done | bytes 51232 | tf_op jit(solution)/shard_map/ppermute | solution.py:540
  22.3 1.9 %collective-permute-done.5.refs_3_ = bf16[10,8,320]{2,1,0:T(8,128)(2,1)S(1)} collective-permute-done((bf16[10,8,320]{2,1,0:T(8,128)(2,1)S(1)}, bf16[10,8,320]{2,1,0:T(8,128)(2,1)S(1)}, u32[]{:S(2)}, u32[]{:S(2)}) %collective-permute-start.5) | collective-permute-done | bytes 51232 | tf_op jit(solution)/shard_map/ppermute | solution.py:540
  24.2 0.0 copy-start.17
  24.2 3.3 %row_attention.1 = (bf16[10,8,256]{2,1,0:T(8,128)(2,1)S(1)}, bf16[10,8,256]{2,1,0:T(8,128)(2,1)S(1)}, bf16[10,8,256]{2,1,0:T(8,128)(2,1)S(1)}, bf16[10,8,256]{2,1,0:T(8,128)(2,1)S(1)}) custom-call(s32[1]{0:T(128)} %bitcast.idx, bf16[10,8,320]{2,1,0:T(8,128)(2,1)S(1)} %copy-done.7, bf16[10,8,320]{2,1,0:T(8,128)(2,1)S(1)} %collective-permute-done.refs_1_, ...), custom_call_target="tpu_custom_call" | custom-call | flops 4000000000 | bytes 4000000 | tf_op jit(solution)/shard_map/row_attention/pallas_call | solution.py:245
  27.5 0.0 copy-start
  27.5 0.0 copy-start.11
  27.5 0.0 copy-start.12
  27.6 2.1 %collective-permute-start.10 = (bf16[10,8,256]{2,1,0:T(8,128)(2,1)S(1)}, bf16[10,8,256]{2,1,0:T(8,128)(2,1)S(1)}, u32[]{:S(2)}, u32[]{:S(2)}) collective-permute-start(bf16[10,8,256]{2,1,0:T(8,128)(2,1)S(1)} %get-tuple-element.40), channel_id=1, source_target_pairs={{0,24},{1,25},{2,26},{3,27},{4,28},{5,29},{6,30},{7,31},{8,16},{9,... | collective-permute-start | bytes 122888 | tf_op jit(solution)/shard_map/ppermute | solution.py:540
  29.7 0.3 collective-permute-start.8
  30.0 2.0 %collective-permute-start.9 = (bf16[10,8,256]{2,1,0:T(8,128)(2,1)S(1)}, bf16[10,8,256]{2,1,0:T(8,128)(2,1)S(1)}, u32[]{:S(2)}, u32[]{:S(2)}) collective-permute-start(bf16[10,8,256]{2,1,0:T(8,128)(2,1)S(1)} %get-tuple-element.39), channel_id=1, source_target_pairs={{0,16},{1,17},{2,18},{3,19},{4,20},{5,21},{6,22},{7,23},{8,24},{9,... | collective-permute-start | bytes 122888 | tf_op jit(solution)/shard_map/ppermute | solution.py:540
  32.0 0.1 copy.27
  32.1 0.1 copy.25.refs_5_
  32.2 0.1 reshape.22.factors
  32.4 1.1 %collective-permute-done.10.refs_3_ = bf16[10,8,256]{2,1,0:T(8,128)(2,1)S(1)} collective-permute-done((bf16[10,8,256]{2,1,0:T(8,128)(2,1)S(1)}, bf16[10,8,256]{2,1,0:T(8,128)(2,1)S(1)}, u32[]{:S(2)}, u32[]{:S(2)}) %collective-permute-start.10) | collective-permute-done | bytes 40992 | tf_op jit(solution)/shard_map/ppermute | solution.py:540
  33.4 0.4 collective-permute-done.8.refs_1_
  33.9 1.1 %collective-permute-done.9.refs_2_ = bf16[10,8,256]{2,1,0:T(8,128)(2,1)S(1)} collective-permute-done((bf16[10,8,256]{2,1,0:T(8,128)(2,1)S(1)}, bf16[10,8,256]{2,1,0:T(8,128)(2,1)S(1)}, u32[]{:S(2)}, u32[]{:S(2)}) %collective-permute-start.9) | collective-permute-done | bytes 40992 | tf_op jit(solution)/shard_map/ppermute | solution.py:540
  35.0 4.2 %column_attention.1 = (bf16[10,32,256]{2,1,0:T(8,128)(2,1)}, bf16[320,32]{1,0:T(8,128)(2,1)S(1)}, bf16[1,10,1024]{2,1,0:T(8,128)(2,1)S(1)}) custom-call(s32[1]{0:T(128)} %bitcast.idx, bf16[10,8,256]{2,1,0:T(8,128)(2,1)S(1)} %get-tuple-element.37.refs_0_, bf16[10,8,256]{2,1,0:T(8,128)(2,1)S(1)} %collective-permute-done.8.refs_1_, ...), custom_call_target="tpu_custom_call" | custom-call | flops 5000000000 | bytes 4000000 | tf_op jit(solution)/shard_map/column_attention/pallas_call | solution.py:365
  39.2 1.8 %collective-permute-start.11 = (bf16[10,1024]{1,0:T(8,128)(2,1)S(1)}, bf16[10,1024]{1,0:T(8,128)(2,1)S(1)}, u32[]{:S(2)}, u32[]{:S(2)}) collective-permute-start(bf16[10,1024]{1,0:T(8,128)(2,1)S(1)} %bitcast.16), channel_id=1, source_target_pairs={{0,8},{1,9},{2,10},{3,11},{4,12},{5,13},{6,14},{7,15},{8,0},{9,1},... | collective-permute-start | bytes 61448 | tf_op jit(solution)/shard_map/ppermute | solution.py:540
  41.0 0.4 collective-permute-start.12
  41.3 2.3 %collective-permute-start.13 = (bf16[10,1024]{1,0:T(8,128)(2,1)S(1)}, bf16[10,1024]{1,0:T(8,128)(2,1)S(1)}, u32[]{:S(2)}, u32[]{:S(2)}) collective-permute-start(bf16[10,1024]{1,0:T(8,128)(2,1)S(1)} %bitcast.18), channel_id=1, source_target_pairs={{0,24},{1,25},{2,26},{3,27},{4,28},{5,29},{6,30},{7,31},{8,16},{9,... | collective-permute-start | bytes 61448 | tf_op jit(solution)/shard_map/ppermute | solution.py:540
  43.6 1.5 %left_mix.1.refs_8_ = bf16[1024,1280]{1,0:T(8,128)(2,1)S(1)} custom-call(bf16[320,32]{1,0:T(8,128)(2,1)S(1)} %get-tuple-element.42.left, bf16[32,4096]{1,0:T(8,128)(2,1)S(1)} %reshape.22.factors), custom_call_target="tpu_custom_call" | custom-call | flops 2000000000 | bytes 4000000 | tf_op jit(solution)/shard_map/left_mix/pallas_call | solution.py:406
  45.1 0.7 %collective-permute-done.12 = bf16[10,1024]{1,0:T(8,128)(2,1)S(1)} collective-permute-done((bf16[10,1024]{1,0:T(8,128)(2,1)S(1)}, bf16[10,1024]{1,0:T(8,128)(2,1)S(1)}, u32[]{:S(2)}, u32[]{:S(2)}) %collective-permute-start.12) | collective-permute-done | bytes 20512 | tf_op jit(solution)/shard_map/ppermute | solution.py:540
  45.9 1.2 %collective-permute-done.13 = bf16[10,1024]{1,0:T(8,128)(2,1)S(1)} collective-permute-done((bf16[10,1024]{1,0:T(8,128)(2,1)S(1)}, bf16[10,1024]{1,0:T(8,128)(2,1)S(1)}, u32[]{:S(2)}, u32[]{:S(2)}) %collective-permute-start.13) | collective-permute-done | bytes 20512 | tf_op jit(solution)/shard_map/ppermute | solution.py:540
  47.1 1.2 %collective-permute-start.14 = (bf16[40,1024]{1,0:T(8,128)(2,1)S(1)}, bf16[40,1024]{1,0:T(8,128)(2,1)S(1)}, u32[]{:S(2)}, u32[]{:S(2)}) collective-permute-start(bf16[40,1024]{1,0:T(8,128)(2,1)S(1)} %pad_maximum_fusion.refs_0_), channel_id=1, source_target_pairs={{0,2},{1,3},{2,0},{3,1},{4,6},{5,7},{6,4},{7,5},{8,10},{9,11},{10,... | collective-permute-start | bytes 245768 | tf_op jit(solution)/shard_map/ppermute | solution.py:540
  48.3 0.9 %collective-permute-start.15 = (bf16[40,1024]{1,0:T(8,128)(2,1)S(1)}, bf16[40,1024]{1,0:T(8,128)(2,1)S(1)}, u32[]{:S(2)}, u32[]{:S(2)}) collective-permute-start(bf16[40,1024]{1,0:T(8,128)(2,1)S(1)} %pad_maximum_fusion.refs_0_), channel_id=1, source_target_pairs={{0,4},{1,5},{2,6},{3,7},{4,0},{5,1},{6,2},{7,3},{8,12},{9,13},{10,... | collective-permute-start | bytes 245768 | tf_op jit(solution)/shard_map/ppermute | solution.py:540
  49.2 1.4 %collective-permute-start.16 = (bf16[40,1024]{1,0:T(8,128)(2,1)S(1)}, bf16[40,1024]{1,0:T(8,128)(2,1)S(1)}, u32[]{:S(2)}, u32[]{:S(2)}) collective-permute-start(bf16[40,1024]{1,0:T(8,128)(2,1)S(1)} %pad_maximum_fusion.refs_0_), channel_id=1, source_target_pairs={{0,6},{1,7},{2,4},{3,5},{4,2},{5,3},{6,0},{7,1},{8,14},{9,15},{10,... | collective-permute-start | bytes 245768 | tf_op jit(solution)/shard_map/ppermute | solution.py:540
  50.6 0.9 %collective-permute-done.14.refs_1_ = bf16[40,1024]{1,0:T(8,128)(2,1)S(1)} collective-permute-done((bf16[40,1024]{1,0:T(8,128)(2,1)S(1)}, bf16[40,1024]{1,0:T(8,128)(2,1)S(1)}, u32[]{:S(2)}, u32[]{:S(2)}) %collective-permute-start.14) | collective-permute-done | bytes 81952 | tf_op jit(solution)/shard_map/ppermute | solution.py:540
  51.6 1.2 %collective-permute-done.15.refs_2_ = bf16[40,1024]{1,0:T(8,128)(2,1)S(1)} collective-permute-done((bf16[40,1024]{1,0:T(8,128)(2,1)S(1)}, bf16[40,1024]{1,0:T(8,128)(2,1)S(1)}, u32[]{:S(2)}, u32[]{:S(2)}) %collective-permute-start.15) | collective-permute-done | bytes 81952 | tf_op jit(solution)/shard_map/ppermute | solution.py:540
  52.8 1.8 %collective-permute-done.16.refs_3_ = bf16[40,1024]{1,0:T(8,128)(2,1)S(1)} collective-permute-done((bf16[40,1024]{1,0:T(8,128)(2,1)S(1)}, bf16[40,1024]{1,0:T(8,128)(2,1)S(1)}, u32[]{:S(2)}, u32[]{:S(2)}) %collective-permute-start.16) | collective-permute-done | bytes 81952 | tf_op jit(solution)/shard_map/ppermute | solution.py:540
  54.6 1.3 %collective-permute-done.20.refs_7_ = bf16[40,1024]{1,0:T(8,128)(2,1)S(1)} collective-permute-done((bf16[40,1024]{1,0:T(8,128)(2,1)S(1)}, bf16[40,1024]{1,0:T(8,128)(2,1)S(1)}, u32[]{:S(2)}, u32[]{:S(2)}) %collective-permute-start.20) | collective-permute-done | bytes 81952 | tf_op jit(solution)/shard_map/ppermute | solution.py:540
  55.8 4.8 %pair_update.1 = bf16[10,320,128]{2,1,0:T(8,128)(2,1)} custom-call(s32[1]{0:T(128)} %bitcast.idx, bf16[40,1024]{1,0:T(8,128)(2,1)S(1)} %pad_maximum_fusion.refs_0_, bf16[40,1024]{1,0:T(8,128)(2,1)S(1)} %collective-permute-done.14.refs_1_, bf16[40,1024]{1,0:T(8,128)(2,1)S(1)} %collective-permute-done.15.refs_2_, ...), custom_call_target="tpu_custom_call" | custom-call | flops 5000000000 | bytes 4000000 | tf_op jit(solution)/shard_map/pair_update/pallas_call | solution.py:488
  (48 shorter events, 0.2 us)
Async XLA Ops:
  0.6 8.3 %collective-permute-start.1 = (bf16[1,320,256]{2,1,0:T(8,128)(2,1)}, bf16[1,320,256]{2,1,0:T(8,128)(2,1)S(1)}, u32[]{:S(2)}, u32[]{:S(2)}) collective-permute-start(bf16[1,320,256]{2,1,0:T(8,128)(2,1)} %refs_0_.1), channel_id=1, source_target_pairs={{0,1},{1,0},{2,3},{3,2},{4,5},{5,4},{6,7},{7,6},{8,9},{9,8},{10,11... | collective-permute-start | bytes 491528 | tf_op jit(solution)/shard_map/ppermute | solution.py:540
  1.1 7.8 %collective-permute-start.2 = (bf16[1,320,256]{2,1,0:T(8,128)(2,1)}, bf16[1,320,256]{2,1,0:T(8,128)(2,1)S(1)}, u32[]{:S(2)}, u32[]{:S(2)}) collective-permute-start(bf16[1,320,256]{2,1,0:T(8,128)(2,1)} %refs_0_.1), channel_id=1, source_target_pairs={{0,2},{1,3},{2,0},{3,1},{4,6},{5,7},{6,4},{7,5},{8,10},{9,11},{10,... | collective-permute-start | bytes 491528 | tf_op jit(solution)/shard_map/ppermute | solution.py:540
  3.7 10.0 %collective-permute-start.3 = (bf16[1,320,256]{2,1,0:T(8,128)(2,1)}, bf16[1,320,256]{2,1,0:T(8,128)(2,1)S(1)}, u32[]{:S(2)}, u32[]{:S(2)}) collective-permute-start(bf16[1,320,256]{2,1,0:T(8,128)(2,1)} %refs_0_.1), channel_id=1, source_target_pairs={{0,4},{1,5},{2,6},{3,7},{4,0},{5,1},{6,2},{7,3},{8,12},{9,13},{10,... | collective-permute-start | bytes 491528 | tf_op jit(solution)/shard_map/ppermute | solution.py:540
  5.2 8.5 %collective-permute-start.6 = (bf16[1,320,256]{2,1,0:T(8,128)(2,1)}, bf16[1,320,256]{2,1,0:T(8,128)(2,1)S(1)}, u32[]{:S(2)}, u32[]{:S(2)}) collective-permute-start(bf16[1,320,256]{2,1,0:T(8,128)(2,1)} %refs_0_.1), channel_id=1, source_target_pairs={{0,6},{1,7},{2,4},{3,5},{4,2},{5,3},{6,0},{7,1},{8,14},{9,15},{10,... | collective-permute-start | bytes 491528 | tf_op jit(solution)/shard_map/ppermute | solution.py:540
  5.3 3.6 %copy-start.16 = (bf16[256,4,256]{2,1,0:T(4,128)(2,1)S(1)}, bf16[256,4,256]{2,1,0:T(4,128)(2,1)}, u32[]{:S(2)}) copy-start(bf16[256,4,256]{2,1,0:T(4,128)(2,1)} %param.32) | copy-start | bytes 1572868
  8.8 5.0 %copy-start.7 = (bf16[10,8,320]{2,1,0:T(8,128)(2,1)S(1)}, bf16[10,8,320]{2,1,0:T(8,128)(2,1)}, u32[]{:S(2)}) copy-start(bf16[10,8,320]{2,1,0:T(8,128)(2,1)} %get-tuple-element.27.refs_0_) | copy-start | bytes 153604
  8.8 9.5 %copy-start.2 = (bf16[1,320,256]{2,1,0:T(8,128)(2,1)S(1)}, bf16[1,320,256]{2,1,0:T(8,128)(2,1)}, u32[]{:S(2)}) copy-start(bf16[1,320,256]{2,1,0:T(8,128)(2,1)} %refs_0_.1) | copy-start | bytes 491524
  8.8 9.5 %copy-start.10 = (f32[256]{0:T(256)S(1)}, f32[256]{0:T(256)}, u32[]{:S(2)}) copy-start(f32[256]{0:T(256)} %param.31) | copy-start | bytes 3076
  13.8 4.5 %collective-permute-start.7 = (bf16[3,320,256]{2,1,0:T(8,128)(2,1)S(1)}, bf16[3,320,256]{2,1,0:T(8,128)(2,1)S(1)}, u32[]{:S(2)}, u32[]{:S(2)}) collective-permute-start(bf16[3,320,256]{2,1,0:T(8,128)(2,1)S(1)} %constant_dynamic-update-slice_fusion.refs_2_), channel_id=1, source_target_pairs={{0,1},{1,0},{2,3},{3,2},{4,5},{5,4},{6,7},{7,6},{8,9},{9,8},{10,11... | collective-permute-start | bytes 1474568 | tf_op jit(solution)/shard_map/ppermute | solution.py:540
  13.9 6.8 %collective-permute-start = (bf16[10,8,320]{2,1,0:T(8,128)(2,1)S(1)}, bf16[10,8,320]{2,1,0:T(8,128)(2,1)S(1)}, u32[]{:S(2)}, u32[]{:S(2)}) collective-permute-start(bf16[10,8,320]{2,1,0:T(8,128)(2,1)S(1)} %copy-done.7), channel_id=1, source_target_pairs={{0,8},{1,9},{2,10},{3,11},{4,12},{5,13},{6,14},{7,15},{8,0},{9,1},... | collective-permute-start | bytes 153608 | tf_op jit(solution)/shard_map/ppermute | solution.py:540
  15.5 6.8 %collective-permute-start.4 = (bf16[10,8,320]{2,1,0:T(8,128)(2,1)S(1)}, bf16[10,8,320]{2,1,0:T(8,128)(2,1)S(1)}, u32[]{:S(2)}, u32[]{:S(2)}) collective-permute-start(bf16[10,8,320]{2,1,0:T(8,128)(2,1)S(1)} %copy-done.7), channel_id=1, source_target_pairs={{0,16},{1,17},{2,18},{3,19},{4,20},{5,21},{6,22},{7,23},{8,24},{9,... | collective-permute-start | bytes 153608 | tf_op jit(solution)/shard_map/ppermute | solution.py:540
  18.1 6.1 %collective-permute-start.5 = (bf16[10,8,320]{2,1,0:T(8,128)(2,1)S(1)}, bf16[10,8,320]{2,1,0:T(8,128)(2,1)S(1)}, u32[]{:S(2)}, u32[]{:S(2)}) collective-permute-start(bf16[10,8,320]{2,1,0:T(8,128)(2,1)S(1)} %copy-done.7), channel_id=1, source_target_pairs={{0,24},{1,25},{2,26},{3,27},{4,28},{5,29},{6,30},{7,31},{8,16},{9,... | collective-permute-start | bytes 153608 | tf_op jit(solution)/shard_map/ppermute | solution.py:540
  18.3 5.8 %copy-start.3 = (bf16[256,256]{1,0:T(8,128)(2,1)S(1)}, bf16[256,256]{1,0:T(8,128)(2,1)}, u32[]{:S(2)}) copy-start(bf16[256,256]{1,0:T(8,128)(2,1)} %refs_11_.2) | copy-start | bytes 393220
  18.3 5.8 %copy-start.8 = (s32[32,320]{1,0:T(8,128)S(1)}, s32[32,320]{1,0:T(8,128)}, u32[]{:S(2)}) copy-start(s32[32,320]{1,0:T(8,128)} %refs_10_.5) | copy-start | bytes 122884
  18.4 5.8 %copy-start.9 = (s32[320]{0:T(512)S(1)}, s32[320]{0:T(512)}, u32[]{:S(2)}) copy-start(s32[320]{0:T(512)} %refs_10_.3) | copy-start | bytes 3844
  24.2 7.8 %copy-start.17 = (bf16[256,4,256]{2,1,0:T(4,128)(2,1)S(1)}, bf16[256,4,256]{2,1,0:T(4,128)(2,1)}, u32[]{:S(2)}) copy-start(bf16[256,4,256]{2,1,0:T(4,128)(2,1)} %param.35) | copy-start | bytes 1572868
  24.2 7.9 %copy-start.19 = (bf16[256,64]{0,1:T(8,128)(2,1)S(1)}, bf16[256,64]{0,1:T(8,128)(2,1)}, u32[]{:S(2)}) copy-start(bf16[256,64]{0,1:T(8,128)(2,1)} %param.41) | copy-start | bytes 98308
  24.2 8.0 %copy-start.18 = (bf16[1024,128]{1,0:T(8,128)(2,1)S(1)}, bf16[1024,128]{1,0:T(8,128)(2,1)}, u32[]{:S(2)}) copy-start(bf16[1024,128]{1,0:T(8,128)(2,1)} %param.42) | copy-start | bytes 786436
  27.5 7.4 %copy-start = (bf16[256,1024]{1,0:T(8,128)(2,1)S(1)}, bf16[256,1024]{1,0:T(8,128)(2,1)}, u32[]{:S(2)}) copy-start(bf16[256,1024]{1,0:T(8,128)(2,1)} %refs_10_.4) | copy-start | bytes 1572868
  27.5 7.4 %copy-start.1 = (bf16[1024,256]{1,0:T(8,128)(2,1)S(1)}, bf16[1024,256]{1,0:T(8,128)(2,1)}, u32[]{:S(2)}) copy-start(bf16[1024,256]{1,0:T(8,128)(2,1)} %refs_11_.3) | copy-start | bytes 1572868
  27.5 7.4 %copy-start.4 = (bf16[256,256]{1,0:T(8,128)(2,1)S(1)}, bf16[256,256]{1,0:T(8,128)(2,1)}, u32[]{:S(2)}) copy-start(bf16[256,256]{1,0:T(8,128)(2,1)} %refs_8_.1) | copy-start | bytes 393220
  27.5 7.4 %copy-start.11 = (f32[256]{0:T(256)S(1)}, f32[256]{0:T(256)}, u32[]{:S(2)}) copy-start(f32[256]{0:T(256)} %param.34) | copy-start | bytes 3076
  27.5 7.4 %copy-start.12 = (f32[256]{0:T(256)S(1)}, f32[256]{0:T(256)}, u32[]{:S(2)}) copy-start(f32[256]{0:T(256)} %param.37) | copy-start | bytes 3076
  27.5 7.4 %copy-start.13 = (f32[256]{0:T(256)S(1)}, f32[256]{0:T(256)}, u32[]{:S(2)}) copy-start(f32[256]{0:T(256)} %param.40) | copy-start | bytes 3076
  27.6 5.9 %collective-permute-start.10 = (bf16[10,8,256]{2,1,0:T(8,128)(2,1)S(1)}, bf16[10,8,256]{2,1,0:T(8,128)(2,1)S(1)}, u32[]{:S(2)}, u32[]{:S(2)}) collective-permute-start(bf16[10,8,256]{2,1,0:T(8,128)(2,1)S(1)} %get-tuple-element.40), channel_id=1, source_target_pairs={{0,24},{1,25},{2,26},{3,27},{4,28},{5,29},{6,30},{7,31},{8,16},{9,... | collective-permute-start | bytes 122888 | tf_op jit(solution)/shard_map/ppermute | solution.py:540
  29.7 4.2 %collective-permute-start.8 = (bf16[10,8,256]{2,1,0:T(8,128)(2,1)S(1)}, bf16[10,8,256]{2,1,0:T(8,128)(2,1)S(1)}, u32[]{:S(2)}, u32[]{:S(2)}) collective-permute-start(bf16[10,8,256]{2,1,0:T(8,128)(2,1)S(1)} %get-tuple-element.38), channel_id=1, source_target_pairs={{0,8},{1,9},{2,10},{3,11},{4,12},{5,13},{6,14},{7,15},{8,0},{9,1},... | collective-permute-start | bytes 122888 | tf_op jit(solution)/shard_map/ppermute | solution.py:540
  30.0 4.9 %collective-permute-start.9 = (bf16[10,8,256]{2,1,0:T(8,128)(2,1)S(1)}, bf16[10,8,256]{2,1,0:T(8,128)(2,1)S(1)}, u32[]{:S(2)}, u32[]{:S(2)}) collective-permute-start(bf16[10,8,256]{2,1,0:T(8,128)(2,1)S(1)} %get-tuple-element.39), channel_id=1, source_target_pairs={{0,16},{1,17},{2,18},{3,19},{4,20},{5,21},{6,22},{7,23},{8,24},{9,... | collective-permute-start | bytes 122888 | tf_op jit(solution)/shard_map/ppermute | solution.py:540
  39.2 6.0 %collective-permute-start.11 = (bf16[10,1024]{1,0:T(8,128)(2,1)S(1)}, bf16[10,1024]{1,0:T(8,128)(2,1)S(1)}, u32[]{:S(2)}, u32[]{:S(2)}) collective-permute-start(bf16[10,1024]{1,0:T(8,128)(2,1)S(1)} %bitcast.16), channel_id=1, source_target_pairs={{0,8},{1,9},{2,10},{3,11},{4,12},{5,13},{6,14},{7,15},{8,0},{9,1},... | collective-permute-start | bytes 61448 | tf_op jit(solution)/shard_map/ppermute | solution.py:540
  41.0 4.9 %collective-permute-start.12 = (bf16[10,1024]{1,0:T(8,128)(2,1)S(1)}, bf16[10,1024]{1,0:T(8,128)(2,1)S(1)}, u32[]{:S(2)}, u32[]{:S(2)}) collective-permute-start(bf16[10,1024]{1,0:T(8,128)(2,1)S(1)} %bitcast.17), channel_id=1, source_target_pairs={{0,16},{1,17},{2,18},{3,19},{4,20},{5,21},{6,22},{7,23},{8,24},{9,... | collective-permute-start | bytes 61448 | tf_op jit(solution)/shard_map/ppermute | solution.py:540
  41.3 5.7 %collective-permute-start.13 = (bf16[10,1024]{1,0:T(8,128)(2,1)S(1)}, bf16[10,1024]{1,0:T(8,128)(2,1)S(1)}, u32[]{:S(2)}, u32[]{:S(2)}) collective-permute-start(bf16[10,1024]{1,0:T(8,128)(2,1)S(1)} %bitcast.18), channel_id=1, source_target_pairs={{0,24},{1,25},{2,26},{3,27},{4,28},{5,29},{6,30},{7,31},{8,16},{9,... | collective-permute-start | bytes 61448 | tf_op jit(solution)/shard_map/ppermute | solution.py:540
  43.6 12.2 %copy-start.5 = (bf16[128,512]{1,0:T(8,128)(2,1)S(1)}, bf16[128,512]{1,0:T(8,128)(2,1)}, u32[]{:S(2)}) copy-start(bf16[128,512]{1,0:T(8,128)(2,1)} %refs_12_.1) | copy-start | bytes 393220
  43.6 12.2 %copy-start.6 = (bf16[512,128]{1,0:T(8,128)(2,1)S(1)}, bf16[512,128]{1,0:T(8,128)(2,1)}, u32[]{:S(2)}) copy-start(bf16[512,128]{1,0:T(8,128)(2,1)} %refs_13_.1) | copy-start | bytes 393220
  43.6 12.2 %copy-start.14 = (f32[128]{0:T(128)S(1)}, f32[128]{0:T(128)}, u32[]{:S(2)}) copy-start(f32[128]{0:T(128)} %param.43) | copy-start | bytes 1540
  43.6 12.2 %copy-start.15 = (f32[10,320,128]{2,1,0:T(8,128)S(1)}, f32[10,320,128]{2,1,0:T(8,128)}, u32[]{:S(2)}) copy-start(f32[10,320,128]{2,1,0:T(8,128)} %get-tuple-element.49.refs_9_) | copy-start | bytes 4915204
  47.1 4.5 %collective-permute-start.14 = (bf16[40,1024]{1,0:T(8,128)(2,1)S(1)}, bf16[40,1024]{1,0:T(8,128)(2,1)S(1)}, u32[]{:S(2)}, u32[]{:S(2)}) collective-permute-start(bf16[40,1024]{1,0:T(8,128)(2,1)S(1)} %pad_maximum_fusion.refs_0_), channel_id=1, source_target_pairs={{0,2},{1,3},{2,0},{3,1},{4,6},{5,7},{6,4},{7,5},{8,10},{9,11},{10,... | collective-permute-start | bytes 245768 | tf_op jit(solution)/shard_map/ppermute | solution.py:540
  48.3 4.4 %collective-permute-start.15 = (bf16[40,1024]{1,0:T(8,128)(2,1)S(1)}, bf16[40,1024]{1,0:T(8,128)(2,1)S(1)}, u32[]{:S(2)}, u32[]{:S(2)}) collective-permute-start(bf16[40,1024]{1,0:T(8,128)(2,1)S(1)} %pad_maximum_fusion.refs_0_), channel_id=1, source_target_pairs={{0,4},{1,5},{2,6},{3,7},{4,0},{5,1},{6,2},{7,3},{8,12},{9,13},{10,... | collective-permute-start | bytes 245768 | tf_op jit(solution)/shard_map/ppermute | solution.py:540
  49.2 5.3 %collective-permute-start.16 = (bf16[40,1024]{1,0:T(8,128)(2,1)S(1)}, bf16[40,1024]{1,0:T(8,128)(2,1)S(1)}, u32[]{:S(2)}, u32[]{:S(2)}) collective-permute-start(bf16[40,1024]{1,0:T(8,128)(2,1)S(1)} %pad_maximum_fusion.refs_0_), channel_id=1, source_target_pairs={{0,6},{1,7},{2,4},{3,5},{4,2},{5,3},{6,0},{7,1},{8,14},{9,15},{10,... | collective-permute-start | bytes 245768 | tf_op jit(solution)/shard_map/ppermute | solution.py:540
  50.6 3.9 %collective-permute-start.17 = (bf16[40,1024]{1,0:T(8,128)(2,1)S(1)}, bf16[40,1024]{1,0:T(8,128)(2,1)S(1)}, u32[]{:S(2)}, u32[]{:S(2)}) collective-permute-start(bf16[40,1024]{1,0:T(8,128)(2,1)S(1)} %pad_maximum_fusion.refs_0_), channel_id=1, source_target_pairs={{0,1},{1,0},{2,3},{3,2},{4,5},{5,4},{6,7},{7,6},{8,9},{9,8},{10,11... | collective-permute-start | bytes 245768 | tf_op jit(solution)/shard_map/ppermute | solution.py:540
  51.6 3.0 %collective-permute-start.18 = (bf16[40,1024]{1,0:T(8,128)(2,1)S(1)}, bf16[40,1024]{1,0:T(8,128)(2,1)S(1)}, u32[]{:S(2)}, u32[]{:S(2)}) collective-permute-start(bf16[40,1024]{1,0:T(8,128)(2,1)S(1)} %collective-permute-done.14.refs_1_), channel_id=1, source_target_pairs={{0,1},{1,0},{2,3},{3,2},{4,5},{5,4},{6,7},{7,6},{8,9},{9,8},{10,11... | collective-permute-start | bytes 245768 | tf_op jit(solution)/shard_map/ppermute | solution.py:540
  52.8 1.8 %collective-permute-start.19 = (bf16[40,1024]{1,0:T(8,128)(2,1)S(1)}, bf16[40,1024]{1,0:T(8,128)(2,1)S(1)}, u32[]{:S(2)}, u32[]{:S(2)}) collective-permute-start(bf16[40,1024]{1,0:T(8,128)(2,1)S(1)} %collective-permute-done.15.refs_2_), channel_id=1, source_target_pairs={{0,1},{1,0},{2,3},{3,2},{4,5},{5,4},{6,7},{7,6},{8,9},{9,8},{10,11... | collective-permute-start | bytes 245768 | tf_op jit(solution)/shard_map/ppermute | solution.py:540
  54.5 1.3 %collective-permute-start.20 = (bf16[40,1024]{1,0:T(8,128)(2,1)S(1)}, bf16[40,1024]{1,0:T(8,128)(2,1)S(1)}, u32[]{:S(2)}, u32[]{:S(2)}) collective-permute-start(bf16[40,1024]{1,0:T(8,128)(2,1)S(1)} %collective-permute-done.16.refs_3_), channel_id=1, source_target_pairs={{0,1},{1,0},{2,3},{3,2},{4,5},{5,4},{6,7},{7,6},{8,9},{9,8},{10,11... | collective-permute-start | bytes 245768 | tf_op jit(solution)/shard_map/ppermute | solution.py:540

commit v4 on v3

--- a/solution.py
+++ b/solution.py
@@ -122,7 +122,7 @@
 
 
 def project_kernel(idx, *refs, sub, far, rows, length, width):
-    row_refs, refs = refs[:4], refs[4:]
+    row_refs, refs = refs[:2], refs[2:]
     gain, entry, keys, values, query, gate, own_rows, own_normed = refs
     me = idx[0]
     z, p = me // sub, me % sub
@@ -136,8 +136,7 @@
 
     step = min(length, 320)
     for k in range(sub):
-        source = row_refs[k] if k < 2 else row_refs[2 + k % 2]
-        place = 0 if k < 2 else k // 2 - 1
+        source, place = row_refs[k % 2], k // 2
 
         def project(start, k=k, source=source, place=place):
             x = source[place, pl.ds(start, step), :]
@@ -179,7 +178,7 @@
     narrow = jax.ShapeDtypeStruct((sub * own, width), F32)
     return pl.pallas_call(
         functools.partial(project_kernel, sub=sub, far=far, rows=rows, length=length, width=width),
-        in_specs=[pl.BlockSpec(memory_space=pltpu.SMEM)] + [vmem] * 6,
+        in_specs=[pl.BlockSpec(memory_space=pltpu.SMEM)] + [vmem] * 4,
         out_specs=[vmem] * 5,
         out_shape=[wide, wide, narrow, narrow, narrow],
         scratch_shapes=[pltpu.VMEM((sub * own, width), F32)],
@@ -189,20 +188,25 @@
     )(idx, *msa_rows, gain[None, :], entry)
 
 
-def row_kernel(idx, *refs, sub, far, rows, length, width):
-    bias_refs, refs = refs[:far], refs[far:]
+def row_kernel(idx, *refs, order, sub, far, rows, length, width):
+    bias_refs, refs = refs[:2], refs[2:]
     keys, values, query, gate, own_rows, validity, amino, exit_ = refs[:8]
     outs, refs = refs[8 : 8 + far], refs[8 + far :]
-    bias, gated = refs
+    by_residue, bias, gated = refs
     me = idx[0]
     z, p = me // sub, me % sub
     own = far * rows
     total = sub * own
-    for b in range(far):
-        bias[b * rows : (b + 1) * rows] = bias_refs[b][...].astype(F32) * LOG2E
-
-    head_of = iota((HEADS, width), 1) // (width // HEADS)
-    head_mask = jnp.where(head_of == iota((HEADS, width), 0), 1.0, 0.0)
+    half = far // 2
+    for n, b in enumerate(order):
+        block = bias_refs[n // half][n % half * rows : (n % half + 1) * rows]
+        by_residue[b * rows : (b + 1) * rows] = block.astype(F32) * LOG2E
+    for h in range(HEADS):
+        bias[h] = by_residue[:, h, :]
+
+    channel = width // HEADS
+    head_of = iota((1, width), 1) // channel
+    head_mask = [jnp.where(head_of == h, 1.0, 0.0) for h in range(HEADS)]
     take = 40 if own % 40 == 0 else rows
 
     def attend(n, k, start):
@@ -210,12 +214,15 @@
         valid = validity[pl.ds(s, 1), :] * amino[...].reshape(1, length)
         masked = jnp.where(valid > 0, 0.0, MASKED)
         here = pl.ds(pl.multiple_of(n * take, take), take) if not isinstance(n, int) else pl.ds(n * take, take)
-        q = (query[here, :][:, None, :] * head_mask[None]).reshape(take * HEADS, width).astype(BF16)
-        scores = dot_nt(q, keys[k]) + bias[pl.ds(start, take)].reshape(take * HEADS, length) + masked
+        q = query[here, :]
+        q = jnp.concatenate([q * mask for mask in head_mask], 0).astype(BF16)
+        scores = dot_nt(q, keys[k]) + bias[:, pl.ds(start, take), :].reshape(HEADS * take, length) + masked
         expo = jnp.exp2(scores - jnp.max(scores, -1, keepdims=True))
-        total_ = jnp.sum(expo, -1, keepdims=True)
-        mixed = dot(expo.astype(BF16), values[k]) / total_
-        merged = jnp.sum(mixed.reshape(take, HEADS, width) * head_mask[None], axis=1)
+        share = 1.0 / jnp.sum(expo, -1, keepdims=True)
+        mixed = dot(expo.astype(BF16), values[k]) * share
+        merged = mixed[:take] * head_mask[0]
+        for h in range(1, HEADS):
+            merged += mixed[h * take : (h + 1) * take] * head_mask[h]
         gated[here, :] = merged * gate[here, :]
 
     parts = own // take
@@ -235,26 +242,27 @@
         outs[b][...] = x.astype(BF16).reshape(rows, sub, width)
 
 
-def row_call(idx, bias_blocks, projected, validity, amino, exit_):
+def row_call(idx, bias_halves, order, projected, validity, amino, exit_):
     keys, values, query, gate, own_rows = projected
-    sub, far = keys.shape[0], len(bias_blocks)
+    sub, far = keys.shape[0], len(order)
     _, length, width = keys.shape
-    rows = bias_blocks[0].shape[0]
+    rows = 2 * bias_halves[0].shape[0] // far
     own = far * rows
     vmem = pl.BlockSpec(memory_space=pltpu.VMEM)
     return pl.pallas_call(
-        functools.partial(row_kernel, sub=sub, far=far, rows=rows, length=length, width=width),
-        in_specs=[pl.BlockSpec(memory_space=pltpu.SMEM)] + [vmem] * (far + 8),
+        functools.partial(row_kernel, order=order, sub=sub, far=far, rows=rows, length=length, width=width),
+        in_specs=[pl.BlockSpec(memory_space=pltpu.SMEM)] + [vmem] * 10,
         out_specs=[vmem] * far,
         out_shape=[jax.ShapeDtypeStruct((rows, sub, width), BF16)] * far,
         scratch_shapes=[
             pltpu.VMEM((own, HEADS, length), F32),
+            pltpu.VMEM((HEADS, own, length), F32),
             pltpu.VMEM((sub * own, width), F32),
         ],
         compiler_params=pltpu.CompilerParams(vmem_limit_bytes=vmem_limit(length)),
         cost_estimate=pl.CostEstimate(flops=4 * 10**9, bytes_accessed=4000000, transcendentals=10**5),
         name="row_attention",
-    )(idx, *bias_blocks, keys, values, query, gate, own_rows, validity, amino, exit_)
+    )(idx, *bias_halves, keys, values, query, gate, own_rows, validity, amino, exit_)
 
 
 def column_kernel(idx, *refs, sub, far, rows, block, depth, width):
@@ -306,21 +314,23 @@
     lanes = 128
     pick = one_hot(iota((length, lanes), 0) == first + iota((length, lanes), 1))
     valid = dot(validity.astype(F32).astype(BF16), pick)
-    head_of = iota((HEADS, width), 1) // (width // HEADS)
-    head_mask = jnp.where(head_of == iota((HEADS, width), 0), 1.0, 0.0)
+    head_of = iota((1, width), 1) // (width // HEADS)
+    head_mask = [jnp.where(head_of == h, 1.0, 0.0) for h in range(HEADS)]
     for i in range(block):
         here = slice(i * depth, (i + 1) * depth)
-        q = (query[here][:, None, :] * head_mask[None]).reshape(depth * HEADS, width).astype(BF16)
+        q = jnp.concatenate([query[here] * mask for mask in head_mask], 0).astype(BF16)
         masked = jnp.where(valid[:, i : i + 1] > 0, 0.0, MASKED)
         scores = dot_nt(keys[here], q) + masked
         expo = jnp.exp2(scores - jnp.max(scores, 0, keepdims=True))
-        weights = (expo / jnp.sum(expo, 0, keepdims=True)).astype(BF16)
+        weights = (expo * (1.0 / jnp.sum(expo, 0, keepdims=True))).astype(BF16)
         mixed = dot_tn(weights, values[here])
-        merged = jnp.sum(mixed.reshape(depth, HEADS, width) * head_mask[None], axis=1)
+        merged = mixed[:depth] * head_mask[0]
+        for h in range(1, HEADS):
+            merged += mixed[h * depth : (h + 1) * depth] * head_mask[h]
         gated[here, :] = merged * gate[here]
     exit_, ff_gain, widen, narrow, product_gain = arrived(2, 3, 4, 5, 6)
     x = x + dot(gated[...].astype(BF16), exit_)
-    hidden = jnp.maximum(dot(layer_norm(x, ff_gain).astype(BF16), widen), 0.0).astype(BF16)
+    hidden = jnp.maximum(dot(layer_norm(x, ff_gain).astype(BF16), widen).astype(BF16), 0.0)
     x = x + dot(hidden, narrow)
     updated[...] = x.astype(BF16).reshape(block, depth, width)
     outer = layer_norm(x, product_gain).astype(BF16)
@@ -466,7 +476,7 @@
         for r in range(block):
             x = pair_one[r, here, :] + update[:, r * lanes : (r + 1) * lanes]
             normed = layer_norm(x, gain[...]).astype(BF16)
-            hidden = jnp.maximum(dot(normed, widen[...]), 0.0).astype(BF16)
+            hidden = jnp.maximum(dot(normed, widen[...]).astype(BF16), 0.0)
             out[r, here, :] = (x + dot(hidden, narrow[...])).astype(BF16)
 
     chunks(length, part, finish)
@@ -543,23 +553,26 @@
     rows = couple_embedding.shape[0]
     depth = alignment_validity.shape[0]
 
-    beside = swap(alignment_embedding, 1)
     near = [swap(alignment_embedding, k) for k in range(2, SUB, 2)]
     pair_one, bias = pair_call(
         idx, amino_strand, couple_embedding, separation_embedding, couple_shift_scaling, couple_shift_factors
     )
     entry = horizontal_entry_factors.reshape(width, 4 * width)
-    bias_blocks = [swap(bias, SUB)]
-    later, entry, beside, *first = lax.optimization_barrier((bias, entry, beside, *near[:-1]))
-    bias_blocks += [swap(later, SUB * k) for k in range(2, far)]
-    bias_blocks = [bias] + bias_blocks
-    near = first + near[-1:]
-    near = jnp.concatenate(near, 0)
+    order, distance = [0], far // 2
+    mine, theirs = bias, swap(bias, SUB * distance)
+    order += [b ^ distance for b in order]
+    while distance > 1:
+        distance //= 2
+        mine = jnp.concatenate([mine, theirs], 0)
+        theirs = swap(mine, SUB * distance)
+        order += [b ^ distance for b in order]
+    near = jnp.concatenate([alignment_embedding, *near], 0)
+    entry, mine, near = lax.optimization_barrier((entry, mine, near))
     across = swap(near, 1)
-    projected = project_call(
-        idx, [alignment_embedding, beside, near, across], horizontal_scaling_factor, entry, far, rows
+    projected = project_call(idx, [near, across], horizontal_scaling_factor, entry, far, rows)
+    sent = row_call(
+        idx, [mine, theirs], order, projected, alignment_validity, amino_validity, horizontal_exit_factors
     )
-    sent = row_call(idx, bias_blocks, projected, alignment_validity, amino_validity, horizontal_exit_factors)
     pieces = [sent[0]] + [swap(sent[k], SUB * k) for k in range(1, far)]
     updated, left, right = column_call(
         idx,

time: 60.8 us -> 58.9 us (0.969)
  waiting for transfers between devices: 17.8 us -> 15.4 us
  local copies, waits for them, and re-layouts: 0.56 us -> 1.39 us
    ppermute x21 -> x19, waiting for transfers between devices: 17.8 us -> 15.4 us  [swap(): return lax.ppermute(x, 'dap', [(d, d ^ distance) for d in range(devices)])]
    unnamed x45 -> x42, local copies, waits for them, and re-layouts: 0.43 us -> 1.26 us
    ppermute x21 -> x19, starting transfers between devices: 21.6 us -> 21.7 us  [swap(): return lax.ppermute(x, 'dap', [(d, d ^ distance) for d in range(devices)])]
  transfers between devices with their start and end apart: 21 -> 19, of which waited for: 12 -> 10; matrix products, arithmetic and copies ran while one was open for 1% -> 2% of each run, Pallas kernels for 12% -> 12%
where the time goes in v4:
time: 58.9 us; the launch traced here: 58.7 us
  starting transfers between devices  21.7 us (37%)
  Pallas kernels  19.1 us (32%)
  waiting for transfers between devices  15.4 us (26%)
  local copies, waits for them, and re-layouts  1.39 us (2%)
  between operations  0.94 us (2%)
    ppermute x19, starting transfers between devices, swap(): return lax.ppermute(x, 'dap', [(d, d ^ distance) for d in range(devices)])  21.7 us
    ppermute x19, waiting for transfers between devices, swap(): return lax.ppermute(x, 'dap', [(d, d ^ distance) for d in range(devices)])  15.4 us
    pallas_call x1, Pallas kernels, finish_call(): pl.pallas_call(functools.partial(finish_kernel, sub=sub, far=far, rows=ro...  4.81 us
    pallas_call x1, Pallas kernels, column_call(): pl.pallas_call(functools.partial(column_kernel, sub=sub, far=far, rows=ro...  4.07 us
    pallas_call x1, Pallas kernels, pair_call(): pl.pallas_call(functools.partial(pair_kernel, rows=rows, length=length, b...  3.58 us
    pallas_call x1, Pallas kernels, row_call(): pl.pallas_call(functools.partial(row_kernel, order=order, sub=sub, far=fa...  2.87 us
    pallas_call x1, Pallas kernels, project_call(): pl.pallas_call(functools.partial(project_kernel, sub=sub, far=far, rows=r...  2.28 us
    pallas_call x1, Pallas kernels, mix_call(): pl.pallas_call(functools.partial(mix_kernel, rows=rows, depth=depth), gri...  1.47 us
  transfers between devices with their start and end apart: 19, of which 10 were waited for; matrix products, arithmetic and copies ran while one was open for 2% of the time, Pallas kernels for 12%

profile of v4, /device:TPU:0, one launch (start us, length us, event | category | flops | bytes accessed | tf_op | source)
XLA Modules:
  0.0 58.7 jit_solution(14842644813603218754)
XLA Ops:
  0.6 3.0 %collective-permute-start.1 = (bf16[1,320,256]{2,1,0:T(8,128)(2,1)}, bf16[1,320,256]{2,1,0:T(8,128)(2,1)S(1)}, u32[]{:S(2)}, u32[]{:S(2)}) collective-permute-start(bf16[1,320,256]{2,1,0:T(8,128)(2,1)} %param.23), channel_id=1, source_target_pairs={{0,2},{1,3},{2,0},{3,1},{4,6},{5,7},{6,4},{7,5},{8,10},{9,11},{10,... | collective-permute-start | bytes 491528 | tf_op jit(solution)/shard_map/ppermute | solution.py:550
  3.6 1.5 %collective-permute-start.2 = (bf16[1,320,256]{2,1,0:T(8,128)(2,1)}, bf16[1,320,256]{2,1,0:T(8,128)(2,1)S(1)}, u32[]{:S(2)}, u32[]{:S(2)}) collective-permute-start(bf16[1,320,256]{2,1,0:T(8,128)(2,1)} %param.23), channel_id=1, source_target_pairs={{0,4},{1,5},{2,6},{3,7},{4,0},{5,1},{6,2},{7,3},{8,12},{9,13},{10,... | collective-permute-start | bytes 491528 | tf_op jit(solution)/shard_map/ppermute | solution.py:550
  5.2 0.0 collective-permute-start.3
  5.2 3.6 %pair_bias.1 = (f32[10,320,128]{2,1,0:T(8,128)}, bf16[10,8,320]{2,1,0:T(8,128)(2,1)}) custom-call(s32[1]{0:T(128)} %bitcast.idx, s32[320]{0:T(512)} %chain_row.1, bf16[10,320,128]{2,1,0:T(8,128)(2,1)} %pair.1, s32[320]{0:T(512)} %chain_row.1, f32[66,128]{1,0:T(8,128)} %table.1, f32[1,128]{1,0:T(1,128)} %bitcast.28, bf16[8,128]{1,0:T(8,128)(2,1)} %bitcast.27), custom_call_target="tpu_custom_call" | custom-call | flops 4000000000 | bytes 4000000 | tf_op jit(solution)/shard_map/pair_bias/pallas_call | solution.py:97
  8.8 3.1 %collective-permute-start = (bf16[10,8,320]{2,1,0:T(8,128)(2,1)}, bf16[10,8,320]{2,1,0:T(8,128)(2,1)S(1)}, u32[]{:S(2)}, u32[]{:S(2)}) collective-permute-start(bf16[10,8,320]{2,1,0:T(8,128)(2,1)} %get-tuple-element.24), channel_id=1, source_target_pairs={{0,16},{1,17},{2,18},{3,19},{4,20},{5,21},{6,22},{7,23},{8,24},{9,... | collective-permute-start | bytes 153608 | tf_op jit(solution)/shard_map/ppermute | solution.py:550
  11.8 0.9 %constant_dynamic-update-slice_fusion.1 = bf16[20,8,320]{2,1,0:T(8,128)(2,1)S(1)} fusion(bf16[10,8,320]{2,1,0:T(8,128)(2,1)} %get-tuple-element.24), kind=kLoop, calls=%fused_computation.3 | loop fusion | bytes 112640
  12.7 0.1 copy.26
  12.8 1.5 %collective-permute-done = bf16[10,8,320]{2,1,0:T(8,128)(2,1)S(1)} collective-permute-done((bf16[10,8,320]{2,1,0:T(8,128)(2,1)}, bf16[10,8,320]{2,1,0:T(8,128)(2,1)S(1)}, u32[]{:S(2)}, u32[]{:S(2)}) %collective-permute-start) | collective-permute-done | bytes 51232 | tf_op jit(solution)/shard_map/ppermute | solution.py:550
  14.3 0.0 collective-permute-done.1
  14.3 0.1 pad_maximum_fusion.refs_0_
  14.4 0.1 collective-permute-start.5
  14.5 2.0 %collective-permute-start.4 = (bf16[20,8,320]{2,1,0:T(8,128)(2,1)S(1)}, bf16[20,8,320]{2,1,0:T(8,128)(2,1)S(1)}, u32[]{:S(2)}, u32[]{:S(2)}) collective-permute-start(bf16[20,8,320]{2,1,0:T(8,128)(2,1)S(1)} %constant_dynamic-update-slice_fusion.refs_0_), channel_id=1, source_target_pairs={{0,8},{1,9},{2,10},{3,11},{4,12},{5,13},{6,14},{7,15},{8,0},{9,1},... | collective-permute-start | bytes 307208 | tf_op jit(solution)/shard_map/ppermute | solution.py:550
  16.5 0.1 collective-permute-done.5.refs_1_
  16.6 2.3 %row_project.1 = (bf16[8,320,256]{2,1,0:T(8,128)(2,1)S(1)}, bf16[8,320,256]{2,1,0:T(8,128)(2,1)S(1)}, f32[320,256]{1,0:T(8,128)S(1)}, f32[320,256]{1,0:T(8,128)S(1)}, f32[320,256]{1,0:T(8,128)S(1)}) custom-call(s32[1]{0:T(128)} %bitcast.idx, bf16[4,320,256]{2,1,0:T(8,128)(2,1)S(1)} %pad_maximum_fusion.refs_0_, ...), custom_call_target="tpu_custom_call" | custom-call | flops 3000000000 | bytes 4000000 | tf_op jit(solution)/shard_map/row_project/pallas_call | solution.py:179
  18.9 1.5 %collective-permute-done.4.refs_1_ = bf16[20,8,320]{2,1,0:T(8,128)(2,1)S(1)} collective-permute-done((bf16[20,8,320]{2,1,0:T(8,128)(2,1)S(1)}, bf16[20,8,320]{2,1,0:T(8,128)(2,1)S(1)}, u32[]{:S(2)}, u32[]{:S(2)}) %collective-permute-start.4) | collective-permute-done | bytes 102432 | tf_op jit(solution)/shard_map/ppermute | solution.py:550
  20.4 0.0 copy-start.15
  20.4 0.0 copy-start.18
  20.4 0.0 copy-start.16
  20.4 2.9 %row_attention.1 = (bf16[10,8,256]{2,1,0:T(8,128)(2,1)S(1)}, bf16[10,8,256]{2,1,0:T(8,128)(2,1)S(1)}, bf16[10,8,256]{2,1,0:T(8,128)(2,1)S(1)}, bf16[10,8,256]{2,1,0:T(8,128)(2,1)S(1)}) custom-call(s32[1]{0:T(128)} %bitcast.idx, bf16[20,8,320]{2,1,0:T(8,128)(2,1)S(1)} %constant_dynamic-update-slice_fusion.refs_0_, ...), custom_call_target="tpu_custom_call" | custom-call | flops 4000000000 | bytes 4000000 | tf_op jit(solution)/shard_map/row_attention/pallas_call | solution.py:252
  23.3 0.0 copy-start
  23.3 0.0 copy-start.1
  23.3 0.0 copy-start.3
  23.3 0.0 copy-start.9
  23.4 0.0 copy-start.10
  23.4 0.0 copy-start.11
  23.4 1.8 %collective-permute-start.6 = (bf16[10,8,256]{2,1,0:T(8,128)(2,1)S(1)}, bf16[10,8,256]{2,1,0:T(8,128)(2,1)S(1)}, u32[]{:S(2)}, u32[]{:S(2)}) collective-permute-start(bf16[10,8,256]{2,1,0:T(8,128)(2,1)S(1)} %get-tuple-element.34), channel_id=1, source_target_pairs={{0,8},{1,9},{2,10},{3,11},{4,12},{5,13},{6,14},{7,15},{8,0},{9,1},... | collective-permute-start | bytes 122888 | tf_op jit(solution)/shard_map/ppermute | solution.py:550
  25.2 3.1 %collective-permute-start.7 = (bf16[10,8,256]{2,1,0:T(8,128)(2,1)S(1)}, bf16[10,8,256]{2,1,0:T(8,128)(2,1)S(1)}, u32[]{:S(2)}, u32[]{:S(2)}) collective-permute-start(bf16[10,8,256]{2,1,0:T(8,128)(2,1)S(1)} %get-tuple-element.35), channel_id=1, source_target_pairs={{0,16},{1,17},{2,18},{3,19},{4,20},{5,21},{6,22},{7,23},{8,24},{9,... | collective-permute-start | bytes 122888 | tf_op jit(solution)/shard_map/ppermute | solution.py:550
  28.3 0.0 collective-permute-start.8
  28.3 0.1 copy.27
  28.4 0.1 copy.25.refs_5_
  28.6 0.1 reshape.22.factors
  28.7 2.4 %collective-permute-done.7.refs_2_ = bf16[10,8,256]{2,1,0:T(8,128)(2,1)S(1)} collective-permute-done((bf16[10,8,256]{2,1,0:T(8,128)(2,1)S(1)}, bf16[10,8,256]{2,1,0:T(8,128)(2,1)S(1)}, u32[]{:S(2)}, u32[]{:S(2)}) %collective-permute-start.7) | collective-permute-done | bytes 40992 | tf_op jit(solution)/shard_map/ppermute | solution.py:550
  31.1 3.0 %collective-permute-done.8.refs_3_ = bf16[10,8,256]{2,1,0:T(8,128)(2,1)S(1)} collective-permute-done((bf16[10,8,256]{2,1,0:T(8,128)(2,1)S(1)}, bf16[10,8,256]{2,1,0:T(8,128)(2,1)S(1)}, u32[]{:S(2)}, u32[]{:S(2)}) %collective-permute-start.8) | collective-permute-done | bytes 40992 | tf_op jit(solution)/shard_map/ppermute | solution.py:550
  34.2 4.1 %column_attention.1 = (bf16[10,32,256]{2,1,0:T(8,128)(2,1)}, bf16[320,32]{1,0:T(8,128)(2,1)S(1)}, bf16[1,10,1024]{2,1,0:T(8,128)(2,1)S(1)}) custom-call(s32[1]{0:T(128)} %bitcast.idx, bf16[10,8,256]{2,1,0:T(8,128)(2,1)S(1)} %get-tuple-element.33.refs_0_, bf16[10,8,256]{2,1,0:T(8,128)(2,1)S(1)} %collective-permute-done.6.refs_1_, ...), custom_call_target="tpu_custom_call" | custom-call | flops 5000000000 | bytes 4000000 | tf_op jit(solution)/shard_map/column_attention/pallas_call | solution.py:375
  38.2 0.1 collective-permute-start.10
  38.3 1.3 %collective-permute-start.11 = (bf16[10,1024]{1,0:T(8,128)(2,1)S(1)}, bf16[10,1024]{1,0:T(8,128)(2,1)S(1)}, u32[]{:S(2)}, u32[]{:S(2)}) collective-permute-start(bf16[10,1024]{1,0:T(8,128)(2,1)S(1)} %bitcast.17), channel_id=1, source_target_pairs={{0,24},{1,25},{2,26},{3,27},{4,28},{5,29},{6,30},{7,31},{8,16},{9,... | collective-permute-start | bytes 61448 | tf_op jit(solution)/shard_map/ppermute | solution.py:550
  39.6 2.2 %collective-permute-start.9 = (bf16[10,1024]{1,0:T(8,128)(2,1)S(1)}, bf16[10,1024]{1,0:T(8,128)(2,1)S(1)}, u32[]{:S(2)}, u32[]{:S(2)}) collective-permute-start(bf16[10,1024]{1,0:T(8,128)(2,1)S(1)} %bitcast.18), channel_id=1, source_target_pairs={{0,8},{1,9},{2,10},{3,11},{4,12},{5,13},{6,14},{7,15},{8,0},{9,1},... | collective-permute-start | bytes 61448 | tf_op jit(solution)/shard_map/ppermute | solution.py:550
  41.8 1.5 %left_mix.1.refs_8_ = bf16[1024,1280]{1,0:T(8,128)(2,1)S(1)} custom-call(bf16[320,32]{1,0:T(8,128)(2,1)S(1)} %get-tuple-element.38.left, bf16[32,4096]{1,0:T(8,128)(2,1)S(1)} %reshape.22.factors), custom_call_target="tpu_custom_call" | custom-call | flops 2000000000 | bytes 4000000 | tf_op jit(solution)/shard_map/left_mix/pallas_call | solution.py:416
  43.3 0.0 collective-permute-done.10
  43.3 0.8 %collective-permute-done.11 = bf16[10,1024]{1,0:T(8,128)(2,1)S(1)} collective-permute-done((bf16[10,1024]{1,0:T(8,128)(2,1)S(1)}, bf16[10,1024]{1,0:T(8,128)(2,1)S(1)}, u32[]{:S(2)}, u32[]{:S(2)}) %collective-permute-start.11) | collective-permute-done | bytes 20512 | tf_op jit(solution)/shard_map/ppermute | solution.py:550
  44.1 1.6 %collective-permute-start.12 = (bf16[40,1024]{1,0:T(8,128)(2,1)S(1)}, bf16[40,1024]{1,0:T(8,128)(2,1)S(1)}, u32[]{:S(2)}, u32[]{:S(2)}) collective-permute-start(bf16[40,1024]{1,0:T(8,128)(2,1)S(1)} %pad_maximum_fusion.1.refs_0_), channel_id=1, source_target_pairs={{0,2},{1,3},{2,0},{3,1},{4,6},{5,7},{6,4},{7,5},{8,10},{9,11},{10,... | collective-permute-start | bytes 245768 | tf_op jit(solution)/shard_map/ppermute | solution.py:550
  45.7 1.5 %collective-permute-start.13 = (bf16[40,1024]{1,0:T(8,128)(2,1)S(1)}, bf16[40,1024]{1,0:T(8,128)(2,1)S(1)}, u32[]{:S(2)}, u32[]{:S(2)}) collective-permute-start(bf16[40,1024]{1,0:T(8,128)(2,1)S(1)} %pad_maximum_fusion.1.refs_0_), channel_id=1, source_target_pairs={{0,4},{1,5},{2,6},{3,7},{4,0},{5,1},{6,2},{7,3},{8,12},{9,13},{10,... | collective-permute-start | bytes 245768 | tf_op jit(solution)/shard_map/ppermute | solution.py:550
  47.2 0.5 collective-permute-start.14
  47.7 0.9 %collective-permute-done.12.refs_1_ = bf16[40,1024]{1,0:T(8,128)(2,1)S(1)} collective-permute-done((bf16[40,1024]{1,0:T(8,128)(2,1)S(1)}, bf16[40,1024]{1,0:T(8,128)(2,1)S(1)}, u32[]{:S(2)}, u32[]{:S(2)}) %collective-permute-start.12) | collective-permute-done | bytes 81952 | tf_op jit(solution)/shard_map/ppermute | solution.py:550
  48.7 1.5 %collective-permute-done.13.refs_2_ = bf16[40,1024]{1,0:T(8,128)(2,1)S(1)} collective-permute-done((bf16[40,1024]{1,0:T(8,128)(2,1)S(1)}, bf16[40,1024]{1,0:T(8,128)(2,1)S(1)}, u32[]{:S(2)}, u32[]{:S(2)}) %collective-permute-start.13) | collective-permute-done | bytes 81952 | tf_op jit(solution)/shard_map/ppermute | solution.py:550
  50.2 2.4 %collective-permute-done.14.refs_3_ = bf16[40,1024]{1,0:T(8,128)(2,1)S(1)} collective-permute-done((bf16[40,1024]{1,0:T(8,128)(2,1)S(1)}, bf16[40,1024]{1,0:T(8,128)(2,1)S(1)}, u32[]{:S(2)}, u32[]{:S(2)}) %collective-permute-start.14) | collective-permute-done | bytes 81952 | tf_op jit(solution)/shard_map/ppermute | solution.py:550
  52.6 1.3 %collective-permute-done.18.refs_7_ = bf16[40,1024]{1,0:T(8,128)(2,1)S(1)} collective-permute-done((bf16[40,1024]{1,0:T(8,128)(2,1)S(1)}, bf16[40,1024]{1,0:T(8,128)(2,1)S(1)}, u32[]{:S(2)}, u32[]{:S(2)}) %collective-permute-start.18) | collective-permute-done | bytes 81952 | tf_op jit(solution)/shard_map/ppermute | solution.py:550
  53.9 4.8 %pair_update.1 = bf16[10,320,128]{2,1,0:T(8,128)(2,1)} custom-call(s32[1]{0:T(128)} %bitcast.idx, bf16[40,1024]{1,0:T(8,128)(2,1)S(1)} %pad_maximum_fusion.1.refs_0_, bf16[40,1024]{1,0:T(8,128)(2,1)S(1)} %collective-permute-done.12.refs_1_, bf16[40,1024]{1,0:T(8,128)(2,1)S(1)} %collective-permute-done.13.refs_2_, ...), custom_call_target="tpu_custom_call" | custom-call | flops 5000000000 | bytes 4000000 | tf_op jit(solution)/shard_map/pair_update/pallas_call | solution.py:498
  (42 shorter events, 0.1 us)
Async XLA Ops:
  0.6 13.7 %collective-permute-start.1 = (bf16[1,320,256]{2,1,0:T(8,128)(2,1)}, bf16[1,320,256]{2,1,0:T(8,128)(2,1)S(1)}, u32[]{:S(2)}, u32[]{:S(2)}) collective-permute-start(bf16[1,320,256]{2,1,0:T(8,128)(2,1)} %param.23), channel_id=1, source_target_pairs={{0,2},{1,3},{2,0},{3,1},{4,6},{5,7},{6,4},{7,5},{8,10},{9,11},{10,... | collective-permute-start | bytes 491528 | tf_op jit(solution)/shard_map/ppermute | solution.py:550
  3.6 10.7 %collective-permute-start.2 = (bf16[1,320,256]{2,1,0:T(8,128)(2,1)}, bf16[1,320,256]{2,1,0:T(8,128)(2,1)S(1)}, u32[]{:S(2)}, u32[]{:S(2)}) collective-permute-start(bf16[1,320,256]{2,1,0:T(8,128)(2,1)} %param.23), channel_id=1, source_target_pairs={{0,4},{1,5},{2,6},{3,7},{4,0},{5,1},{6,2},{7,3},{8,12},{9,13},{10,... | collective-permute-start | bytes 491528 | tf_op jit(solution)/shard_map/ppermute | solution.py:550
  5.2 9.2 %collective-permute-start.3 = (bf16[1,320,256]{2,1,0:T(8,128)(2,1)}, bf16[1,320,256]{2,1,0:T(8,128)(2,1)S(1)}, u32[]{:S(2)}, u32[]{:S(2)}) collective-permute-start(bf16[1,320,256]{2,1,0:T(8,128)(2,1)} %param.23), channel_id=1, source_target_pairs={{0,6},{1,7},{2,4},{3,5},{4,2},{5,3},{6,0},{7,1},{8,14},{9,15},{10,... | collective-permute-start | bytes 491528 | tf_op jit(solution)/shard_map/ppermute | solution.py:550
  5.2 7.5 %copy-start.14 = (bf16[256,4,256]{2,1,0:T(4,128)(2,1)S(1)}, bf16[256,4,256]{2,1,0:T(4,128)(2,1)}, u32[]{:S(2)}) copy-start(bf16[256,4,256]{2,1,0:T(4,128)(2,1)} %param.32) | copy-start | bytes 1572868
  5.2 9.1 %copy-start.17 = (bf16[1,320,256]{2,1,0:T(8,128)(2,1)S(1)}, bf16[1,320,256]{2,1,0:T(8,128)(2,1)}, u32[]{:S(2)}) copy-start(bf16[1,320,256]{2,1,0:T(8,128)(2,1)} %param.23) | copy-start | bytes 491524
  8.8 7.8 %copy-start.8 = (f32[256]{0:T(256)S(1)}, f32[256]{0:T(256)}, u32[]{:S(2)}) copy-start(f32[256]{0:T(256)} %param.31) | copy-start | bytes 3076
  8.8 5.5 %collective-permute-start = (bf16[10,8,320]{2,1,0:T(8,128)(2,1)}, bf16[10,8,320]{2,1,0:T(8,128)(2,1)S(1)}, u32[]{:S(2)}, u32[]{:S(2)}) collective-permute-start(bf16[10,8,320]{2,1,0:T(8,128)(2,1)} %get-tuple-element.24), channel_id=1, source_target_pairs={{0,16},{1,17},{2,18},{3,19},{4,20},{5,21},{6,22},{7,23},{8,24},{9,... | collective-permute-start | bytes 153608 | tf_op jit(solution)/shard_map/ppermute | solution.py:550
  14.4 2.2 %collective-permute-start.5 = (bf16[4,320,256]{2,1,0:T(8,128)(2,1)S(1)}, bf16[4,320,256]{2,1,0:T(8,128)(2,1)S(1)}, u32[]{:S(2)}, u32[]{:S(2)}) collective-permute-start(bf16[4,320,256]{2,1,0:T(8,128)(2,1)S(1)} %pad_maximum_fusion.refs_0_), channel_id=1, source_target_pairs={{0,1},{1,0},{2,3},{3,2},{4,5},{5,4},{6,7},{7,6},{8,9},{9,8},{10,11... | collective-permute-start | bytes 1966088 | tf_op jit(solution)/shard_map/ppermute | solution.py:550
  14.5 5.9 %collective-permute-start.4 = (bf16[20,8,320]{2,1,0:T(8,128)(2,1)S(1)}, bf16[20,8,320]{2,1,0:T(8,128)(2,1)S(1)}, u32[]{:S(2)}, u32[]{:S(2)}) collective-permute-start(bf16[20,8,320]{2,1,0:T(8,128)(2,1)S(1)} %constant_dynamic-update-slice_fusion.refs_0_), channel_id=1, source_target_pairs={{0,8},{1,9},{2,10},{3,11},{4,12},{5,13},{6,14},{7,15},{8,0},{9,1},... | collective-permute-start | bytes 307208 | tf_op jit(solution)/shard_map/ppermute | solution.py:550
  16.6 3.8 %copy-start.2 = (bf16[256,256]{1,0:T(8,128)(2,1)S(1)}, bf16[256,256]{1,0:T(8,128)(2,1)}, u32[]{:S(2)}) copy-start(bf16[256,256]{1,0:T(8,128)(2,1)} %refs_9_.1) | copy-start | bytes 393220
  16.6 3.8 %copy-start.6 = (s32[32,320]{1,0:T(8,128)S(1)}, s32[32,320]{1,0:T(8,128)}, u32[]{:S(2)}) copy-start(s32[32,320]{1,0:T(8,128)} %refs_10_.3) | copy-start | bytes 122884
  16.6 3.8 %copy-start.7 = (s32[320]{0:T(512)S(1)}, s32[320]{0:T(512)}, u32[]{:S(2)}) copy-start(s32[320]{0:T(512)} %refs_8_.2) | copy-start | bytes 3844
  20.4 7.9 %copy-start.15 = (bf16[256,4,256]{2,1,0:T(4,128)(2,1)S(1)}, bf16[256,4,256]{2,1,0:T(4,128)(2,1)}, u32[]{:S(2)}) copy-start(bf16[256,4,256]{2,1,0:T(4,128)(2,1)} %param.35) | copy-start | bytes 1572868
  20.4 8.0 %copy-start.18 = (bf16[256,64]{0,1:T(8,128)(2,1)S(1)}, bf16[256,64]{0,1:T(8,128)(2,1)}, u32[]{:S(2)}) copy-start(bf16[256,64]{0,1:T(8,128)(2,1)} %param.41) | copy-start | bytes 98308
  20.4 8.1 %copy-start.16 = (bf16[1024,128]{1,0:T(8,128)(2,1)S(1)}, bf16[1024,128]{1,0:T(8,128)(2,1)}, u32[]{:S(2)}) copy-start(bf16[1024,128]{1,0:T(8,128)(2,1)} %param.42) | copy-start | bytes 786436
  23.3 10.8 %copy-start = (bf16[256,1024]{1,0:T(8,128)(2,1)S(1)}, bf16[256,1024]{1,0:T(8,128)(2,1)}, u32[]{:S(2)}) copy-start(bf16[256,1024]{1,0:T(8,128)(2,1)} %refs_10_.2) | copy-start | bytes 1572868
  23.3 10.8 %copy-start.1 = (bf16[1024,256]{1,0:T(8,128)(2,1)S(1)}, bf16[1024,256]{1,0:T(8,128)(2,1)}, u32[]{:S(2)}) copy-start(bf16[1024,256]{1,0:T(8,128)(2,1)} %refs_11_.1) | copy-start | bytes 1572868
  23.3 10.8 %copy-start.3 = (bf16[256,256]{1,0:T(8,128)(2,1)S(1)}, bf16[256,256]{1,0:T(8,128)(2,1)}, u32[]{:S(2)}) copy-start(bf16[256,256]{1,0:T(8,128)(2,1)} %refs_8_.3) | copy-start | bytes 393220
  23.3 10.8 %copy-start.9 = (f32[256]{0:T(256)S(1)}, f32[256]{0:T(256)}, u32[]{:S(2)}) copy-start(f32[256]{0:T(256)} %param.34) | copy-start | bytes 3076
  23.4 10.8 %copy-start.10 = (f32[256]{0:T(256)S(1)}, f32[256]{0:T(256)}, u32[]{:S(2)}) copy-start(f32[256]{0:T(256)} %param.37) | copy-start | bytes 3076
  23.4 10.8 %copy-start.11 = (f32[256]{0:T(256)S(1)}, f32[256]{0:T(256)}, u32[]{:S(2)}) copy-start(f32[256]{0:T(256)} %param.40) | copy-start | bytes 3076
  23.4 5.3 %collective-permute-start.6 = (bf16[10,8,256]{2,1,0:T(8,128)(2,1)S(1)}, bf16[10,8,256]{2,1,0:T(8,128)(2,1)S(1)}, u32[]{:S(2)}, u32[]{:S(2)}) collective-permute-start(bf16[10,8,256]{2,1,0:T(8,128)(2,1)S(1)} %get-tuple-element.34), channel_id=1, source_target_pairs={{0,8},{1,9},{2,10},{3,11},{4,12},{5,13},{6,14},{7,15},{8,0},{9,1},... | collective-permute-start | bytes 122888 | tf_op jit(solution)/shard_map/ppermute | solution.py:550
  25.2 5.9 %collective-permute-start.7 = (bf16[10,8,256]{2,1,0:T(8,128)(2,1)S(1)}, bf16[10,8,256]{2,1,0:T(8,128)(2,1)S(1)}, u32[]{:S(2)}, u32[]{:S(2)}) collective-permute-start(bf16[10,8,256]{2,1,0:T(8,128)(2,1)S(1)} %get-tuple-element.35), channel_id=1, source_target_pairs={{0,16},{1,17},{2,18},{3,19},{4,20},{5,21},{6,22},{7,23},{8,24},{9,... | collective-permute-start | bytes 122888 | tf_op jit(solution)/shard_map/ppermute | solution.py:550
  28.3 5.8 %collective-permute-start.8 = (bf16[10,8,256]{2,1,0:T(8,128)(2,1)S(1)}, bf16[10,8,256]{2,1,0:T(8,128)(2,1)S(1)}, u32[]{:S(2)}, u32[]{:S(2)}) collective-permute-start(bf16[10,8,256]{2,1,0:T(8,128)(2,1)S(1)} %get-tuple-element.36), channel_id=1, source_target_pairs={{0,24},{1,25},{2,26},{3,27},{4,28},{5,29},{6,30},{7,31},{8,16},{9,... | collective-permute-start | bytes 122888 | tf_op jit(solution)/shard_map/ppermute | solution.py:550
  38.2 5.0 %collective-permute-start.10 = (bf16[10,1024]{1,0:T(8,128)(2,1)S(1)}, bf16[10,1024]{1,0:T(8,128)(2,1)S(1)}, u32[]{:S(2)}, u32[]{:S(2)}) collective-permute-start(bf16[10,1024]{1,0:T(8,128)(2,1)S(1)} %bitcast.16), channel_id=1, source_target_pairs={{0,16},{1,17},{2,18},{3,19},{4,20},{5,21},{6,22},{7,23},{8,24},{9,... | collective-permute-start | bytes 61448 | tf_op jit(solution)/shard_map/ppermute | solution.py:550
  38.3 5.8 %collective-permute-start.11 = (bf16[10,1024]{1,0:T(8,128)(2,1)S(1)}, bf16[10,1024]{1,0:T(8,128)(2,1)S(1)}, u32[]{:S(2)}, u32[]{:S(2)}) collective-permute-start(bf16[10,1024]{1,0:T(8,128)(2,1)S(1)} %bitcast.17), channel_id=1, source_target_pairs={{0,24},{1,25},{2,26},{3,27},{4,28},{5,29},{6,30},{7,31},{8,16},{9,... | collective-permute-start | bytes 61448 | tf_op jit(solution)/shard_map/ppermute | solution.py:550
  39.6 4.5 %collective-permute-start.9 = (bf16[10,1024]{1,0:T(8,128)(2,1)S(1)}, bf16[10,1024]{1,0:T(8,128)(2,1)S(1)}, u32[]{:S(2)}, u32[]{:S(2)}) collective-permute-start(bf16[10,1024]{1,0:T(8,128)(2,1)S(1)} %bitcast.18), channel_id=1, source_target_pairs={{0,8},{1,9},{2,10},{3,11},{4,12},{5,13},{6,14},{7,15},{8,0},{9,1},... | collective-permute-start | bytes 61448 | tf_op jit(solution)/shard_map/ppermute | solution.py:550
  41.8 12.0 %copy-start.4 = (bf16[128,512]{1,0:T(8,128)(2,1)S(1)}, bf16[128,512]{1,0:T(8,128)(2,1)}, u32[]{:S(2)}) copy-start(bf16[128,512]{1,0:T(8,128)(2,1)} %refs_12_.1) | copy-start | bytes 393220
  41.8 12.0 %copy-start.5 = (bf16[512,128]{1,0:T(8,128)(2,1)S(1)}, bf16[512,128]{1,0:T(8,128)(2,1)}, u32[]{:S(2)}) copy-start(bf16[512,128]{1,0:T(8,128)(2,1)} %refs_13_.1) | copy-start | bytes 393220
  41.8 12.0 %copy-start.12 = (f32[128]{0:T(128)S(1)}, f32[128]{0:T(128)}, u32[]{:S(2)}) copy-start(f32[128]{0:T(128)} %param.43) | copy-start | bytes 1540
  41.8 12.0 %copy-start.13 = (f32[10,320,128]{2,1,0:T(8,128)S(1)}, f32[10,320,128]{2,1,0:T(8,128)}, u32[]{:S(2)}) copy-start(f32[10,320,128]{2,1,0:T(8,128)} %get-tuple-element.45.refs_9_) | copy-start | bytes 4915204
  44.1 4.5 %collective-permute-start.12 = (bf16[40,1024]{1,0:T(8,128)(2,1)S(1)}, bf16[40,1024]{1,0:T(8,128)(2,1)S(1)}, u32[]{:S(2)}, u32[]{:S(2)}) collective-permute-start(bf16[40,1024]{1,0:T(8,128)(2,1)S(1)} %pad_maximum_fusion.1.refs_0_), channel_id=1, source_target_pairs={{0,2},{1,3},{2,0},{3,1},{4,6},{5,7},{6,4},{7,5},{8,10},{9,11},{10,... | collective-permute-start | bytes 245768 | tf_op jit(solution)/shard_map/ppermute | solution.py:550
  45.7 4.4 %collective-permute-start.13 = (bf16[40,1024]{1,0:T(8,128)(2,1)S(1)}, bf16[40,1024]{1,0:T(8,128)(2,1)S(1)}, u32[]{:S(2)}, u32[]{:S(2)}) collective-permute-start(bf16[40,1024]{1,0:T(8,128)(2,1)S(1)} %pad_maximum_fusion.1.refs_0_), channel_id=1, source_target_pairs={{0,4},{1,5},{2,6},{3,7},{4,0},{5,1},{6,2},{7,3},{8,12},{9,13},{10,... | collective-permute-start | bytes 245768 | tf_op jit(solution)/shard_map/ppermute | solution.py:550
  47.2 5.3 %collective-permute-start.14 = (bf16[40,1024]{1,0:T(8,128)(2,1)S(1)}, bf16[40,1024]{1,0:T(8,128)(2,1)S(1)}, u32[]{:S(2)}, u32[]{:S(2)}) collective-permute-start(bf16[40,1024]{1,0:T(8,128)(2,1)S(1)} %pad_maximum_fusion.1.refs_0_), channel_id=1, source_target_pairs={{0,6},{1,7},{2,4},{3,5},{4,2},{5,3},{6,0},{7,1},{8,14},{9,15},{10,... | collective-permute-start | bytes 245768 | tf_op jit(solution)/shard_map/ppermute | solution.py:550
  47.7 4.9 %collective-permute-start.15 = (bf16[40,1024]{1,0:T(8,128)(2,1)S(1)}, bf16[40,1024]{1,0:T(8,128)(2,1)S(1)}, u32[]{:S(2)}, u32[]{:S(2)}) collective-permute-start(bf16[40,1024]{1,0:T(8,128)(2,1)S(1)} %pad_maximum_fusion.1.refs_0_), channel_id=1, source_target_pairs={{0,1},{1,0},{2,3},{3,2},{4,5},{5,4},{6,7},{7,6},{8,9},{9,8},{10,11... | collective-permute-start | bytes 245768 | tf_op jit(solution)/shard_map/ppermute | solution.py:550
  48.7 3.9 %collective-permute-start.16 = (bf16[40,1024]{1,0:T(8,128)(2,1)S(1)}, bf16[40,1024]{1,0:T(8,128)(2,1)S(1)}, u32[]{:S(2)}, u32[]{:S(2)}) collective-permute-start(bf16[40,1024]{1,0:T(8,128)(2,1)S(1)} %collective-permute-done.12.refs_1_), channel_id=1, source_target_pairs={{0,1},{1,0},{2,3},{3,2},{4,5},{5,4},{6,7},{7,6},{8,9},{9,8},{10,11... | collective-permute-start | bytes 245768 | tf_op jit(solution)/shard_map/ppermute | solution.py:550
  50.2 2.4 %collective-permute-start.17 = (bf16[40,1024]{1,0:T(8,128)(2,1)S(1)}, bf16[40,1024]{1,0:T(8,128)(2,1)S(1)}, u32[]{:S(2)}, u32[]{:S(2)}) collective-permute-start(bf16[40,1024]{1,0:T(8,128)(2,1)S(1)} %collective-permute-done.13.refs_2_), channel_id=1, source_target_pairs={{0,1},{1,0},{2,3},{3,2},{4,5},{5,4},{6,7},{7,6},{8,9},{9,8},{10,11... | collective-permute-start | bytes 245768 | tf_op jit(solution)/shard_map/ppermute | solution.py:550
  52.6 1.3 %collective-permute-start.18 = (bf16[40,1024]{1,0:T(8,128)(2,1)S(1)}, bf16[40,1024]{1,0:T(8,128)(2,1)S(1)}, u32[]{:S(2)}, u32[]{:S(2)}) collective-permute-start(bf16[40,1024]{1,0:T(8,128)(2,1)S(1)} %collective-permute-done.14.refs_3_), channel_id=1, source_target_pairs={{0,1},{1,0},{2,3},{3,2},{4,5},{5,4},{6,7},{7,6},{8,9},{9,8},{10,11... | collective-permute-start | bytes 245768 | tf_op jit(solution)/shard_map/ppermute | solution.py:550

commit v5 on v4

--- a/solution.py
+++ b/solution.py
@@ -70,8 +70,13 @@
     def _():
         k = iota((2 * length, bins), 0)
         wanted = jnp.clip(length - k + reach, 0, 2 * reach)
-        pick = jnp.where(wanted == iota((2 * length, bins), 1), 1.0, 0.0)
-        shifted[...] = jnp.dot(pick, table[...], precision=lax.Precision.HIGHEST, preferred_element_type=F32)
+        pick = one_hot(wanted == iota((2 * length, bins), 1))
+        rest, total = table[...], 0.0
+        for _ in range(3):
+            part = rest.astype(BF16)
+            total += dot(pick, part)
+            rest = rest - part.astype(F32)
+        shifted[...] = total
         eye = iota((length, length), 0) == iota((length, length), 1)
         column = jnp.sum(jnp.where(eye, chain_row[...].astype(F32).reshape(1, length), 0.0), axis=1, keepdims=True)
         chain_wide[...] = jnp.broadcast_to(column, chain_wide.shape)
@@ -398,7 +403,7 @@
     )(idx, *pieces, *here, *sources)
 
 
-def mix_kernel(left, factors, out, *, rows, depth):
+def mix_kernel(idx, left, factors, validity, out, inverse, *, rows, depth, steps):
     lanes = out.shape[1] // rows
     for e in range(0, out.shape[0] // depth, 2):
         y = dot(left[...], factors[:, e * lanes : (e + 2) * lanes]).astype(BF16)
@@ -407,38 +412,64 @@
                 block = y[i * depth : (i + 1) * depth, f * lanes : (f + 1) * lanes]
                 out[(e + f) * depth : (e + f + 1) * depth, i * lanes : (i + 1) * lanes] = block
 
-
-def mix_call(left, factors, rows, length):
+    def count():
+        length = validity.shape[1]
+        valid = validity[...].astype(F32)
+        target = idx[0] * rows + iota((length, rows * lanes), 1) // lanes
+        mine = dot(valid.astype(BF16), one_hot(iota((length, rows * lanes), 0) == target))
+        mine, turned = mine.astype(BF16), valid.T.astype(BF16)
+        part = min(length, 320)
+        for start in range(0, length, part):
+            inverse[start : start + part, :] = 1.0 / (dot(turned[start : start + part], mine) + OUTER_EPS)
+
+    if steps == 1:
+        count()
+    else:
+        pl.when(pl.program_id(0) == 0)(count)
+
+
+def mix_call(idx, left, factors, validity, rows):
     total, channels = left.shape
-    depth = total // rows
+    depth, length = validity.shape
     lanes = factors.shape[1] // channels
-    block = 8
+    steps = 1 if length <= 320 else 4
+    block = channels // steps
+    if steps == 1:
+        grid, spec = {}, lambda shape, index: pl.BlockSpec(memory_space=pltpu.VMEM)
+    else:
+        grid, spec = {"grid": (steps,)}, pl.BlockSpec
     return pl.pallas_call(
-        functools.partial(mix_kernel, rows=rows, depth=depth),
-        grid=(channels // block,),
+        functools.partial(mix_kernel, rows=rows, depth=depth, steps=steps),
+        **grid,
         in_specs=[
-            pl.BlockSpec((total, channels), lambda s: (0, 0)),
-            pl.BlockSpec((channels, block * lanes), lambda s: (0, s)),
-        ],
-        out_specs=pl.BlockSpec((block * depth, rows * lanes), lambda s: (s, 0)),
-        out_shape=jax.ShapeDtypeStruct((channels * depth, rows * lanes), BF16),
+            pl.BlockSpec(memory_space=pltpu.SMEM),
+            spec((total, channels), lambda s: (0, 0)),
+            spec((channels, block * lanes), lambda s: (0, s)),
+            spec((depth, length), lambda s: (0, 0)),
+        ],
+        out_specs=[
+            spec((block * depth, rows * lanes), lambda s: (s, 0)),
+            spec((length, rows * lanes), lambda s: (0, 0)),
+        ],
+        out_shape=[
+            jax.ShapeDtypeStruct((channels * depth, rows * lanes), BF16),
+            jax.ShapeDtypeStruct((length, rows * lanes), F32),
+        ],
         compiler_params=pltpu.CompilerParams(vmem_limit_bytes=vmem_limit(length)),
         cost_estimate=pl.CostEstimate(flops=2 * 10**9, bytes_accessed=4000000, transcendentals=10**5),
         name="left_mix",
-    )(left, factors)
-
-
-def finish_kernel(
-    idx, *refs, sub, far, rows, length, block
-):
-    near_refs, across_refs, refs = refs[: sub // 2], refs[sub // 2 : sub], refs[sub:]
-    mixed, pair_one, validity, gain, widen, narrow, out, right, turned = refs
+    )(idx, left, factors, validity)
+
+
+def finish_kernel(idx, *refs, pieces, sub, far, rows, length, block):
+    near_refs, across_refs, refs = refs[:pieces], refs[pieces : 2 * pieces], refs[2 * pieces :]
+    mixed, inverse, pair_one, gain, widen, narrow, out, right, held, sems = refs
     me = idx[0]
     z, p = me // sub, me % sub
-    step = 0 if block == rows else pl.program_id(0)
     half = far * rows * sub // 2
     lanes = pair_one.shape[2]
     part = min(length, 320)
+    alone = block == rows
 
     def first():
         r = iota((part, half), 1)
@@ -448,7 +479,6 @@
         across_far = b - far * (across_sub >> 1)
         home = ((z ^ across_far) * sub + (p ^ across_sub)) * rows + i
         away = ((z ^ across_far) * sub + (p ^ 1 ^ across_sub)) * rows + i
-
         near = jnp.concatenate([ref[...].astype(F32) for ref in near_refs], 0).astype(BF16)
         across = jnp.concatenate([ref[...].astype(F32) for ref in across_refs], 0).astype(BF16)
 
@@ -458,63 +488,77 @@
             right[here, :] = (dot(one_hot(j == home), near) + dot(one_hot(j == away), across)).astype(BF16)
 
         chunks(length, part, arrange)
-        turned[...] = validity[...].astype(F32).T.astype(BF16)
-
-    if block == rows:
+
+    if alone:
         first()
     else:
-        pl.when(step == 0)(first)
-    i0 = me * rows + step * block
-    target = i0 + iota((length, block * lanes), 1) // lanes
-    mine = one_hot(iota((length, block * lanes), 0) == target)
-    mine = dot(validity[...].astype(F32).astype(BF16), mine).astype(BF16)
+        pl.when(pl.program_id(0) == 0)(first)
+
+    together = 2 if block % 2 == 0 else 1
+    copies = []
 
     def finish(start):
         here = pl.ds(start, part)
-        counts = dot(turned[here, :], mine) + OUTER_EPS
-        update = dot(right[here, :], mixed[...]) / counts
-        for r in range(block):
-            x = pair_one[r, here, :] + update[:, r * lanes : (r + 1) * lanes]
+        update = dot(right[here, :], mixed[...])
+        for n, r in enumerate(range(0, block, together)):
+            x = []
+            for q in range(r, r + together):
+                columns = slice(q * lanes, (q + 1) * lanes)
+                x.append(pair_one[q, here, :] + update[:, columns] * inverse[here, columns])
+            x = jnp.concatenate(x, 0)
             normed = layer_norm(x, gain[...]).astype(BF16)
             hidden = jnp.maximum(dot(normed, widen[...]).astype(BF16), 0.0)
-            out[r, here, :] = (x + dot(hidden, narrow[...])).astype(BF16)
+            x = (x + dot(hidden, narrow[...])).astype(BF16)
+            for q in range(together):
+                (held if alone else out)[r + q, here, :] = x[q * part : (q + 1) * part]
+            if alone:
+                done = pl.ds(r, together)
+                copies.append(pltpu.make_async_copy(held.at[done], out.at[done], sems.at[n]))
+                copies[-1].start()
 
     chunks(length, part, finish)
-
-
-def finish_call(idx, near, across, mixed, pair_one, validity, gain, widen, narrow, sub, far):
+    for copy in copies:
+        copy.wait()
+
+
+def finish_call(idx, near, across, mixed, inverse, pair_one, gain, widen, narrow, sub, far):
     rows, length, lanes = pair_one.shape
-    depth = validity.shape[0]
     block = rows if length <= 320 else 2 if rows % 2 == 0 else 1
     product = mixed.shape[0]
     gain = gain[None, :]
     if block == rows:
-        grid, vmem = {}, lambda a: pl.BlockSpec(memory_space=pltpu.VMEM)
-        mixed_spec = pair_spec = vmem(mixed)
-    else:
-        grid, vmem = {"grid": (rows // block,)}, lambda a: pl.BlockSpec(a.shape, lambda s: (0,) * a.ndim)
-        mixed_spec = pl.BlockSpec((product, block * lanes), lambda s: (0, s))
-        pair_spec = pl.BlockSpec((block, length, lanes), lambda s: (s, 0, 0))
+        grid, spec = {}, lambda shape, index: pl.BlockSpec(memory_space=pltpu.VMEM)
+        out_spec = pl.BlockSpec(memory_space=pl.ANY)
+    else:
+        grid, spec = {"grid": (rows // block,)}, pl.BlockSpec
+        out_spec = spec((block, length, lanes), lambda s: (s, 0, 0))
+    whole = lambda a: spec(a.shape, lambda s: (0,) * a.ndim)
     return pl.pallas_call(
-        functools.partial(finish_kernel, sub=sub, far=far, rows=rows, length=length, block=block),
+        functools.partial(
+            finish_kernel, pieces=len(near), sub=sub, far=far, rows=rows, length=length, block=block
+        ),
         **grid,
         in_specs=[
             pl.BlockSpec(memory_space=pltpu.SMEM),
-            *[vmem(a) for a in near + across],
-            mixed_spec,
-            pair_spec,
-            vmem(validity),
-            vmem(gain),
-            vmem(widen),
-            vmem(narrow),
-        ],
-        out_specs=pair_spec,
+            *[whole(a) for a in near + across],
+            spec((product, block * lanes), lambda s: (0, s)),
+            spec((length, block * lanes), lambda s: (0, s)),
+            spec((block, length, lanes), lambda s: (s, 0, 0)),
+            whole(gain),
+            whole(widen),
+            whole(narrow),
+        ],
+        out_specs=out_spec,
         out_shape=jax.ShapeDtypeStruct((rows, length, lanes), BF16),
-        scratch_shapes=[pltpu.VMEM((length, product), BF16), pltpu.VMEM((length, depth), BF16)],
+        scratch_shapes=[
+            pltpu.VMEM((length, product), BF16),
+            pltpu.VMEM((rows, length, lanes) if block == rows else (1, 16, 128), BF16),
+            pltpu.SemaphoreType.DMA((rows,)),
+        ],
         compiler_params=pltpu.CompilerParams(vmem_limit_bytes=vmem_limit(length)),
-        cost_estimate=pl.CostEstimate(flops=5 * 10**9, bytes_accessed=4000000, transcendentals=10**5),
+        cost_estimate=pl.CostEstimate(flops=4 * 10**9, bytes_accessed=4000000, transcendentals=10**5),
         name="pair_update",
-    )(idx, *near, *across, mixed, pair_one, validity, gain, widen, narrow)
+    )(idx, *near, *across, mixed, inverse, pair_one, gain, widen, narrow)
 
 
 def on_device(
@@ -573,7 +617,9 @@
     sent = row_call(
         idx, [mine, theirs], order, projected, alignment_validity, amino_validity, horizontal_exit_factors
     )
-    pieces = [sent[0]] + [swap(sent[k], SUB * k) for k in range(1, far)]
+    pieces = [swap(sent[k], SUB * k) for k in [*range(2, far), 1]]
+    pieces = lax.optimization_barrier(pieces)
+    pieces = [sent[0]] + [part for _, part in sorted(zip([*range(2, far), 1], pieces), key=lambda pair: pair[0])]
     updated, left, right = column_call(
         idx,
         pieces,
@@ -590,20 +636,23 @@
     channels = left.shape[1]
     right = right.reshape(rows, channels * depth)
     factors = product_exit_factors.reshape(channels, -1)
-    mixed = mix_call(left, factors, rows, alignment_validity.shape[1])
-    parts = [right] + [swap(right, SUB * k) for k in range(1, far)]
-    parts = lax.optimization_barrier((mixed, *parts))
-    mixed, parts = parts[0], parts[1:]
+    mixed, inverse = mix_call(idx, left, factors, alignment_validity, rows)
+    parts = [swap(right, SUB * k) for k in [1, *range(far - 1, 1, -1)]]
+    mixed, right, *parts = lax.optimization_barrier((mixed, right, *parts))
+    parts = [right] + [part for _, part in sorted(zip([1, *range(far - 1, 1, -1)], parts), key=lambda pair: pair[0])]
     column = jnp.concatenate(parts, 0)
-    near = [column] + [swap(column, k) for k in range(2, SUB, 2)]
+    near = [swap(column, k) for k in [6, 2, 4]]
+    near = lax.optimization_barrier(near)
+    near = [part for _, part in sorted(zip([6, 2, 4], near), key=lambda pair: pair[0])]
+    near = [column, jnp.concatenate(near, 0)]
     across = [swap(a, 1) for a in near]
     updated_pairs = finish_call(
         idx,
         near,
         across,
         mixed,
+        inverse,
         pair_one,
-        alignment_validity,
         couple_feedforward_scaling,
         couple_widen_factors,
         couple_narrow_factors,

time: 58.9 us -> 58 us (0.985)
  Pallas kernels: 19.1 us -> 18 us
  starting transfers between devices: 21.7 us -> 22.3 us
  waiting for transfers between devices: 15.4 us -> 14.8 us
    pallas_call x2, Pallas kernels: 6.29 us -> 5.17 us  [the longest x1 3.93 us: finish_call(): pl.pallas_call(functools.partial(finish_kernel, pieces=len(near), sub=sub...]
    ppermute x19 -> x17, waiting for transfers between devices: 15.4 us -> 14.8 us  [swap(): return lax.ppermute(x, 'dap', [(d, d ^ distance) for d in range(devices)])]
    ppermute x19 -> x17, starting transfers between devices: 21.7 us -> 22.3 us  [swap(): return lax.ppermute(x, 'dap', [(d, d ^ distance) for d in range(devices)])]
    unnamed x42 -> x44, local copies, waits for them, and re-layouts: 1.26 us -> 1.27 us
  transfers between devices with their start and end apart: 19 -> 17, of which waited for: 10 -> 11; matrix products, arithmetic and copies ran while one was open for 2% -> 2% of each run, Pallas kernels for 12% -> 12%
where the time goes in v5:
time: 58 us; the launch traced here: 57.8 us
  starting transfers between devices  22.3 us (38%)
  Pallas kernels  18 us (31%)
  waiting for transfers between devices  14.8 us (26%)
  local copies, waits for them, and re-layouts  1.41 us (2%)
  between operations  1.11 us (2%)
    ppermute x17, starting transfers between devices, swap(): return lax.ppermute(x, 'dap', [(d, d ^ distance) for d in range(devices)])  22.3 us
    ppermute x17, waiting for transfers between devices, swap(): return lax.ppermute(x, 'dap', [(d, d ^ distance) for d in range(devices)])  14.8 us
    pallas_call x1, Pallas kernels, column_call(): pl.pallas_call(functools.partial(column_kernel, sub=sub, far=far, rows=ro...  4.25 us
    pallas_call x1, Pallas kernels, finish_call(): pl.pallas_call(functools.partial(finish_kernel, pieces=len(near), sub=sub...  3.93 us
    pallas_call x1, Pallas kernels, pair_call(): pl.pallas_call(functools.partial(pair_kernel, rows=rows, length=length, b...  3.45 us
    pallas_call x1, Pallas kernels, row_call(): pl.pallas_call(functools.partial(row_kernel, order=order, sub=sub, far=fa...  2.87 us
    pallas_call x1, Pallas kernels, project_call(): pl.pallas_call(functools.partial(project_kernel, sub=sub, far=far, rows=r...  2.29 us
    unnamed x44, local copies, waits for them, and re-layouts  1.27 us
  transfers between devices with their start and end apart: 17, of which 11 were waited for; matrix products, arithmetic and copies ran while one was open for 2% of the time, Pallas kernels for 12%

profile of v5, /device:TPU:0, one launch (start us, length us, event | category | flops | bytes accessed | tf_op | source)
XLA Modules:
  0.0 57.8 jit_solution(4604864049877808301)
XLA Ops:
  0.6 4.0 %collective-permute-start.3 = (bf16[1,320,256]{2,1,0:T(8,128)(2,1)}, bf16[1,320,256]{2,1,0:T(8,128)(2,1)S(1)}, u32[]{:S(2)}, u32[]{:S(2)}) collective-permute-start(bf16[1,320,256]{2,1,0:T(8,128)(2,1)} %param.23), channel_id=1, source_target_pairs={{0,6},{1,7},{2,4},{3,5},{4,2},{5,3},{6,0},{7,1},{8,14},{9,15},{10,... | collective-permute-start | bytes 491528 | tf_op jit(solution)/shard_map/ppermute | solution.py:594
  4.6 0.5 collective-permute-start.2
  5.1 0.1 collective-permute-start.1
  5.2 3.4 %pair_bias.1 = (f32[10,320,128]{2,1,0:T(8,128)}, bf16[10,8,320]{2,1,0:T(8,128)(2,1)}) custom-call(s32[1]{0:T(128)} %bitcast.idx, s32[320]{0:T(512)} %chain_row.1, bf16[10,320,128]{2,1,0:T(8,128)(2,1)} %pair.1, s32[320]{0:T(512)} %chain_row.1, f32[66,128]{1,0:T(8,128)} %table.1, f32[1,128]{1,0:T(1,128)} %bitcast.28, bf16[8,128]{1,0:T(8,128)(2,1)} %bitcast.27), custom_call_target="tpu_custom_call" | custom-call | flops 4000000000 | bytes 4000000 | tf_op jit(solution)/shard_map/pair_bias/pallas_call | solution.py:102
  8.7 3.0 %collective-permute-start = (bf16[10,8,320]{2,1,0:T(8,128)(2,1)}, bf16[10,8,320]{2,1,0:T(8,128)(2,1)S(1)}, u32[]{:S(2)}, u32[]{:S(2)}) collective-permute-start(bf16[10,8,320]{2,1,0:T(8,128)(2,1)} %get-tuple-element.32), channel_id=1, source_target_pairs={{0,16},{1,17},{2,18},{3,19},{4,20},{5,21},{6,22},{7,23},{8,24},{9,... | collective-permute-start | bytes 153608 | tf_op jit(solution)/shard_map/ppermute | solution.py:594
  11.7 0.9 %constant_dynamic-update-slice_fusion.1 = bf16[20,8,320]{2,1,0:T(8,128)(2,1)S(1)} fusion(bf16[10,8,320]{2,1,0:T(8,128)(2,1)} %get-tuple-element.32), kind=kLoop, calls=%fused_computation.3 | loop fusion | bytes 112640
  12.6 0.1 copy.26
  12.7 1.5 %collective-permute-done = bf16[10,8,320]{2,1,0:T(8,128)(2,1)S(1)} collective-permute-done((bf16[10,8,320]{2,1,0:T(8,128)(2,1)}, bf16[10,8,320]{2,1,0:T(8,128)(2,1)S(1)}, u32[]{:S(2)}, u32[]{:S(2)}) %collective-permute-start) | collective-permute-done | bytes 51232 | tf_op jit(solution)/shard_map/ppermute | solution.py:594
  14.2 0.1 pad_maximum_fusion.refs_0_
  14.3 0.1 collective-permute-start.5
  14.4 2.0 %collective-permute-start.4 = (bf16[20,8,320]{2,1,0:T(8,128)(2,1)S(1)}, bf16[20,8,320]{2,1,0:T(8,128)(2,1)S(1)}, u32[]{:S(2)}, u32[]{:S(2)}) collective-permute-start(bf16[20,8,320]{2,1,0:T(8,128)(2,1)S(1)} %constant_dynamic-update-slice_fusion.refs_0_), channel_id=1, source_target_pairs={{0,8},{1,9},{2,10},{3,11},{4,12},{5,13},{6,14},{7,15},{8,0},{9,1},... | collective-permute-start | bytes 307208 | tf_op jit(solution)/shard_map/ppermute | solution.py:594
  16.3 0.1 collective-permute-done.5.refs_1_
  16.5 2.3 %row_project.1 = (bf16[8,320,256]{2,1,0:T(8,128)(2,1)S(1)}, bf16[8,320,256]{2,1,0:T(8,128)(2,1)S(1)}, f32[320,256]{1,0:T(8,128)S(1)}, f32[320,256]{1,0:T(8,128)S(1)}, f32[320,256]{1,0:T(8,128)S(1)}) custom-call(s32[1]{0:T(128)} %bitcast.idx, bf16[4,320,256]{2,1,0:T(8,128)(2,1)S(1)} %pad_maximum_fusion.refs_0_, ...), custom_call_target="tpu_custom_call" | custom-call | flops 3000000000 | bytes 4000000 | tf_op jit(solution)/shard_map/row_project/pallas_call | solution.py:184
  18.8 1.5 %collective-permute-done.4.refs_1_ = bf16[20,8,320]{2,1,0:T(8,128)(2,1)S(1)} collective-permute-done((bf16[20,8,320]{2,1,0:T(8,128)(2,1)S(1)}, bf16[20,8,320]{2,1,0:T(8,128)(2,1)S(1)}, u32[]{:S(2)}, u32[]{:S(2)}) %collective-permute-start.4) | collective-permute-done | bytes 102432 | tf_op jit(solution)/shard_map/ppermute | solution.py:594
  20.3 0.0 copy-start.15
  20.3 0.0 copy-start.18
  20.3 0.0 copy-start.16
  20.3 2.9 %row_attention.1 = (bf16[10,8,256]{2,1,0:T(8,128)(2,1)S(1)}, bf16[10,8,256]{2,1,0:T(8,128)(2,1)S(1)}, bf16[10,8,256]{2,1,0:T(8,128)(2,1)S(1)}, bf16[10,8,256]{2,1,0:T(8,128)(2,1)S(1)}) custom-call(s32[1]{0:T(128)} %bitcast.idx, bf16[20,8,320]{2,1,0:T(8,128)(2,1)S(1)} %constant_dynamic-update-slice_fusion.refs_0_, ...), custom_call_target="tpu_custom_call" | custom-call | flops 4000000000 | bytes 4000000 | tf_op jit(solution)/shard_map/row_attention/pallas_call | solution.py:257
  23.2 0.0 copy-start
  23.2 0.0 copy-start.1
  23.2 0.0 copy-start.3
  23.2 0.0 copy-start.10
  23.2 0.0 copy-start.11
  23.3 3.2 %collective-permute-start.6 = (bf16[10,8,256]{2,1,0:T(8,128)(2,1)S(1)}, bf16[10,8,256]{2,1,0:T(8,128)(2,1)S(1)}, u32[]{:S(2)}, u32[]{:S(2)}) collective-permute-start(bf16[10,8,256]{2,1,0:T(8,128)(2,1)S(1)} %get-tuple-element.42), channel_id=1, source_target_pairs={{0,16},{1,17},{2,18},{3,19},{4,20},{5,21},{6,22},{7,23},{8,24},{9,... | collective-permute-start | bytes 122888 | tf_op jit(solution)/shard_map/ppermute | solution.py:594
  26.4 1.3 %collective-permute-start.7 = (bf16[10,8,256]{2,1,0:T(8,128)(2,1)S(1)}, bf16[10,8,256]{2,1,0:T(8,128)(2,1)S(1)}, u32[]{:S(2)}, u32[]{:S(2)}) collective-permute-start(bf16[10,8,256]{2,1,0:T(8,128)(2,1)S(1)} %get-tuple-element.43), channel_id=1, source_target_pairs={{0,24},{1,25},{2,26},{3,27},{4,28},{5,29},{6,30},{7,31},{8,16},{9,... | collective-permute-start | bytes 122888 | tf_op jit(solution)/shard_map/ppermute | solution.py:594
  27.7 0.5 collective-permute-start.8
  28.2 0.1 copy.27
  28.3 0.1 copy.25.refs_5_
  28.4 0.1 reshape.22.factors
  28.6 0.3 collective-permute-done.6.refs_2_
  28.8 3.4 %collective-permute-done.7.refs_3_ = bf16[10,8,256]{2,1,0:T(8,128)(2,1)S(1)} collective-permute-done((bf16[10,8,256]{2,1,0:T(8,128)(2,1)S(1)}, bf16[10,8,256]{2,1,0:T(8,128)(2,1)S(1)}, u32[]{:S(2)}, u32[]{:S(2)}) %collective-permute-start.7) | collective-permute-done | bytes 40992 | tf_op jit(solution)/shard_map/ppermute | solution.py:594
  32.3 4.2 %column_attention.1 = (bf16[10,32,256]{2,1,0:T(8,128)(2,1)}, bf16[320,32]{1,0:T(8,128)(2,1)S(1)}, bf16[1,10,1024]{2,1,0:T(8,128)(2,1)S(1)}) custom-call(s32[1]{0:T(128)} %bitcast.idx, bf16[10,8,256]{2,1,0:T(8,128)(2,1)S(1)} %get-tuple-element.41.refs_0_, bf16[10,8,256]{2,1,0:T(8,128)(2,1)S(1)} %collective-permute-done.8.refs_1_, ...), custom_call_target="tpu_custom_call" | custom-call | flops 5000000000 | bytes 4000000 | tf_op jit(solution)/shard_map/column_attention/pallas_call | solution.py:380
  36.5 0.1 collective-permute-start.9
  36.6 2.9 %collective-permute-start.10 = (bf16[10,1024]{1,0:T(8,128)(2,1)S(1)}, bf16[10,1024]{1,0:T(8,128)(2,1)S(1)}, u32[]{:S(2)}, u32[]{:S(2)}) collective-permute-start(bf16[10,1024]{1,0:T(8,128)(2,1)S(1)} %bitcast.17), channel_id=1, source_target_pairs={{0,24},{1,25},{2,26},{3,27},{4,28},{5,29},{6,30},{7,31},{8,16},{9,... | collective-permute-start | bytes 61448 | tf_op jit(solution)/shard_map/ppermute | solution.py:594
  39.5 0.6 %collective-permute-start.11 = (bf16[10,1024]{1,0:T(8,128)(2,1)S(1)}, bf16[10,1024]{1,0:T(8,128)(2,1)S(1)}, u32[]{:S(2)}, u32[]{:S(2)}) collective-permute-start(bf16[10,1024]{1,0:T(8,128)(2,1)S(1)} %bitcast.18), channel_id=1, source_target_pairs={{0,16},{1,17},{2,18},{3,19},{4,20},{5,21},{6,22},{7,23},{8,24},{9,... | collective-permute-start | bytes 61448 | tf_op jit(solution)/shard_map/ppermute | solution.py:594
  40.1 1.2 %left_mix.1 = (bf16[1024,1280]{1,0:T(8,128)(2,1)S(1)}, f32[320,1280]{1,0:T(8,128)S(1)}) custom-call(s32[1]{0:T(128)} %bitcast.idx, bf16[320,32]{1,0:T(8,128)(2,1)S(1)} %get-tuple-element.49.left, bf16[32,4096]{1,0:T(8,128)(2,1)S(1)} %reshape.22.factors, s32[32,320]{1,0:T(8,128)S(1)} %copy-done.6), custom_call_target="tpu_custom_call" | custom-call | flops 2000000000 | bytes 4000000 | tf_op jit(solution)/shard_map/left_mix/pallas_call | solution.py:441
  41.4 1.0 %collective-permute-done.10 = bf16[10,1024]{1,0:T(8,128)(2,1)S(1)} collective-permute-done((bf16[10,1024]{1,0:T(8,128)(2,1)S(1)}, bf16[10,1024]{1,0:T(8,128)(2,1)S(1)}, u32[]{:S(2)}, u32[]{:S(2)}) %collective-permute-start.10) | collective-permute-done | bytes 20512 | tf_op jit(solution)/shard_map/ppermute | solution.py:594
  42.4 2.0 %collective-permute-done.11 = bf16[10,1024]{1,0:T(8,128)(2,1)S(1)} collective-permute-done((bf16[10,1024]{1,0:T(8,128)(2,1)S(1)}, bf16[10,1024]{1,0:T(8,128)(2,1)S(1)}, u32[]{:S(2)}, u32[]{:S(2)}) %collective-permute-start.11) | collective-permute-done | bytes 20512 | tf_op jit(solution)/shard_map/ppermute | solution.py:594
  44.4 2.5 %collective-permute-start.12 = (bf16[40,1024]{1,0:T(8,128)(2,1)S(1)}, bf16[40,1024]{1,0:T(8,128)(2,1)S(1)}, u32[]{:S(2)}, u32[]{:S(2)}) collective-permute-start(bf16[40,1024]{1,0:T(8,128)(2,1)S(1)} %pad_maximum_fusion.1.refs_0_), channel_id=1, source_target_pairs={{0,6},{1,7},{2,4},{3,5},{4,2},{5,3},{6,0},{7,1},{8,14},{9,15},{10,... | collective-permute-start | bytes 245768 | tf_op jit(solution)/shard_map/ppermute | solution.py:594
  46.9 0.6 collective-permute-start.13
  47.5 0.5 collective-permute-start.14
  48.0 1.9 %collective-permute-done.12 = bf16[40,1024]{1,0:T(8,128)(2,1)S(1)} collective-permute-done((bf16[40,1024]{1,0:T(8,128)(2,1)S(1)}, bf16[40,1024]{1,0:T(8,128)(2,1)S(1)}, u32[]{:S(2)}, u32[]{:S(2)}) %collective-permute-start.12) | collective-permute-done | bytes 81952 | tf_op jit(solution)/shard_map/ppermute | solution.py:594
  49.8 1.5 %collective-permute-done.13 = bf16[40,1024]{1,0:T(8,128)(2,1)S(1)} collective-permute-done((bf16[40,1024]{1,0:T(8,128)(2,1)S(1)}, bf16[40,1024]{1,0:T(8,128)(2,1)S(1)}, u32[]{:S(2)}, u32[]{:S(2)}) %collective-permute-start.13) | collective-permute-done | bytes 81952 | tf_op jit(solution)/shard_map/ppermute | solution.py:594
  51.3 0.6 collective-permute-done.14
  51.9 0.1 collective-permute-start.16
  52.0 0.5 collective-permute-start.15
  52.5 1.1 %collective-permute-done.15.refs_2_ = bf16[40,1024]{1,0:T(8,128)(2,1)S(1)} collective-permute-done((bf16[40,1024]{1,0:T(8,128)(2,1)S(1)}, bf16[40,1024]{1,0:T(8,128)(2,1)S(1)}, u32[]{:S(2)}, u32[]{:S(2)}) %collective-permute-start.15) | collective-permute-done | bytes 81952 | tf_op jit(solution)/shard_map/ppermute | solution.py:594
  53.7 3.9 %pair_update.1 = bf16[10,320,128]{2,1,0:T(8,128)(2,1)} custom-call(s32[1]{0:T(128)} %bitcast.idx, bf16[40,1024]{1,0:T(8,128)(2,1)S(1)} %pad_maximum_fusion.1.refs_0_, bf16[120,1024]{1,0:T(8,128)(2,1)S(1)} %constant_dynamic-update-slice_fusion.2.refs_1_, bf16[40,1024]{1,0:T(8,128)(2,1)S(1)} %collective-permute-done.15.refs_2_, ...), custom_call_target="tpu_custom_call" | custom-call | flops 4000000000 | bytes 4000000 | tf_op jit(solution)/shard_map/pair_update/pallas_call | solution.py:536
  (41 shorter events, 0.2 us)
Async XLA Ops:
  0.6 13.5 %collective-permute-start.3 = (bf16[1,320,256]{2,1,0:T(8,128)(2,1)}, bf16[1,320,256]{2,1,0:T(8,128)(2,1)S(1)}, u32[]{:S(2)}, u32[]{:S(2)}) collective-permute-start(bf16[1,320,256]{2,1,0:T(8,128)(2,1)} %param.23), channel_id=1, source_target_pairs={{0,6},{1,7},{2,4},{3,5},{4,2},{5,3},{6,0},{7,1},{8,14},{9,15},{10,... | collective-permute-start | bytes 491528 | tf_op jit(solution)/shard_map/ppermute | solution.py:594
  4.6 9.6 %collective-permute-start.2 = (bf16[1,320,256]{2,1,0:T(8,128)(2,1)}, bf16[1,320,256]{2,1,0:T(8,128)(2,1)S(1)}, u32[]{:S(2)}, u32[]{:S(2)}) collective-permute-start(bf16[1,320,256]{2,1,0:T(8,128)(2,1)} %param.23), channel_id=1, source_target_pairs={{0,4},{1,5},{2,6},{3,7},{4,0},{5,1},{6,2},{7,3},{8,12},{9,13},{10,... | collective-permute-start | bytes 491528 | tf_op jit(solution)/shard_map/ppermute | solution.py:594
  5.1 9.1 %collective-permute-start.1 = (bf16[1,320,256]{2,1,0:T(8,128)(2,1)}, bf16[1,320,256]{2,1,0:T(8,128)(2,1)S(1)}, u32[]{:S(2)}, u32[]{:S(2)}) collective-permute-start(bf16[1,320,256]{2,1,0:T(8,128)(2,1)} %param.23), channel_id=1, source_target_pairs={{0,2},{1,3},{2,0},{3,1},{4,6},{5,7},{6,4},{7,5},{8,10},{9,11},{10,... | collective-permute-start | bytes 491528 | tf_op jit(solution)/shard_map/ppermute | solution.py:594
  5.2 7.3 %copy-start.14 = (bf16[256,4,256]{2,1,0:T(4,128)(2,1)S(1)}, bf16[256,4,256]{2,1,0:T(4,128)(2,1)}, u32[]{:S(2)}) copy-start(bf16[256,4,256]{2,1,0:T(4,128)(2,1)} %param.32) | copy-start | bytes 1572868
  5.2 9.0 %copy-start.17 = (bf16[1,320,256]{2,1,0:T(8,128)(2,1)S(1)}, bf16[1,320,256]{2,1,0:T(8,128)(2,1)}, u32[]{:S(2)}) copy-start(bf16[1,320,256]{2,1,0:T(8,128)(2,1)} %param.23) | copy-start | bytes 491524
  8.7 7.8 %copy-start.8 = (f32[256]{0:T(256)S(1)}, f32[256]{0:T(256)}, u32[]{:S(2)}) copy-start(f32[256]{0:T(256)} %param.31) | copy-start | bytes 3076
  8.7 5.5 %collective-permute-start = (bf16[10,8,320]{2,1,0:T(8,128)(2,1)}, bf16[10,8,320]{2,1,0:T(8,128)(2,1)S(1)}, u32[]{:S(2)}, u32[]{:S(2)}) collective-permute-start(bf16[10,8,320]{2,1,0:T(8,128)(2,1)} %get-tuple-element.32), channel_id=1, source_target_pairs={{0,16},{1,17},{2,18},{3,19},{4,20},{5,21},{6,22},{7,23},{8,24},{9,... | collective-permute-start | bytes 153608 | tf_op jit(solution)/shard_map/ppermute | solution.py:594
  14.3 2.2 %collective-permute-start.5 = (bf16[4,320,256]{2,1,0:T(8,128)(2,1)S(1)}, bf16[4,320,256]{2,1,0:T(8,128)(2,1)S(1)}, u32[]{:S(2)}, u32[]{:S(2)}) collective-permute-start(bf16[4,320,256]{2,1,0:T(8,128)(2,1)S(1)} %pad_maximum_fusion.refs_0_), channel_id=1, source_target_pairs={{0,1},{1,0},{2,3},{3,2},{4,5},{5,4},{6,7},{7,6},{8,9},{9,8},{10,11... | collective-permute-start | bytes 1966088 | tf_op jit(solution)/shard_map/ppermute | solution.py:594
  14.4 5.9 %collective-permute-start.4 = (bf16[20,8,320]{2,1,0:T(8,128)(2,1)S(1)}, bf16[20,8,320]{2,1,0:T(8,128)(2,1)S(1)}, u32[]{:S(2)}, u32[]{:S(2)}) collective-permute-start(bf16[20,8,320]{2,1,0:T(8,128)(2,1)S(1)} %constant_dynamic-update-slice_fusion.refs_0_), channel_id=1, source_target_pairs={{0,8},{1,9},{2,10},{3,11},{4,12},{5,13},{6,14},{7,15},{8,0},{9,1},... | collective-permute-start | bytes 307208 | tf_op jit(solution)/shard_map/ppermute | solution.py:594
  16.5 3.8 %copy-start.2 = (bf16[256,256]{1,0:T(8,128)(2,1)S(1)}, bf16[256,256]{1,0:T(8,128)(2,1)}, u32[]{:S(2)}) copy-start(bf16[256,256]{1,0:T(8,128)(2,1)} %refs_9_.2) | copy-start | bytes 393220
  16.5 3.8 %copy-start.6 = (s32[32,320]{1,0:T(8,128)S(1)}, s32[32,320]{1,0:T(8,128)}, u32[]{:S(2)}) copy-start(s32[32,320]{1,0:T(8,128)} %validity.1) | copy-start | bytes 122884
  16.5 3.8 %copy-start.7 = (s32[320]{0:T(512)S(1)}, s32[320]{0:T(512)}, u32[]{:S(2)}) copy-start(s32[320]{0:T(512)} %refs_8_.3) | copy-start | bytes 3844
  20.3 7.9 %copy-start.15 = (bf16[256,4,256]{2,1,0:T(4,128)(2,1)S(1)}, bf16[256,4,256]{2,1,0:T(4,128)(2,1)}, u32[]{:S(2)}) copy-start(bf16[256,4,256]{2,1,0:T(4,128)(2,1)} %param.35) | copy-start | bytes 1572868
  20.3 8.0 %copy-start.18 = (bf16[256,64]{0,1:T(8,128)(2,1)S(1)}, bf16[256,64]{0,1:T(8,128)(2,1)}, u32[]{:S(2)}) copy-start(bf16[256,64]{0,1:T(8,128)(2,1)} %param.41) | copy-start | bytes 98308
  20.3 8.1 %copy-start.16 = (bf16[1024,128]{1,0:T(8,128)(2,1)S(1)}, bf16[1024,128]{1,0:T(8,128)(2,1)}, u32[]{:S(2)}) copy-start(bf16[1024,128]{1,0:T(8,128)(2,1)} %param.42) | copy-start | bytes 786436
  23.2 9.1 %copy-start = (bf16[256,1024]{1,0:T(8,128)(2,1)S(1)}, bf16[256,1024]{1,0:T(8,128)(2,1)}, u32[]{:S(2)}) copy-start(bf16[256,1024]{1,0:T(8,128)(2,1)} %refs_10_.1) | copy-start | bytes 1572868
  23.2 9.0 %copy-start.1 = (bf16[1024,256]{1,0:T(8,128)(2,1)S(1)}, bf16[1024,256]{1,0:T(8,128)(2,1)}, u32[]{:S(2)}) copy-start(bf16[1024,256]{1,0:T(8,128)(2,1)} %refs_11_.1) | copy-start | bytes 1572868
  23.2 9.0 %copy-start.3 = (bf16[256,256]{1,0:T(8,128)(2,1)S(1)}, bf16[256,256]{1,0:T(8,128)(2,1)}, u32[]{:S(2)}) copy-start(bf16[256,256]{1,0:T(8,128)(2,1)} %refs_8_.4) | copy-start | bytes 393220
  23.2 9.0 %copy-start.9 = (f32[256]{0:T(256)S(1)}, f32[256]{0:T(256)}, u32[]{:S(2)}) copy-start(f32[256]{0:T(256)} %param.34) | copy-start | bytes 3076
  23.2 9.0 %copy-start.10 = (f32[256]{0:T(256)S(1)}, f32[256]{0:T(256)}, u32[]{:S(2)}) copy-start(f32[256]{0:T(256)} %param.37) | copy-start | bytes 3076
  23.2 9.0 %copy-start.11 = (f32[256]{0:T(256)S(1)}, f32[256]{0:T(256)}, u32[]{:S(2)}) copy-start(f32[256]{0:T(256)} %param.40) | copy-start | bytes 3076
  23.3 5.6 %collective-permute-start.6 = (bf16[10,8,256]{2,1,0:T(8,128)(2,1)S(1)}, bf16[10,8,256]{2,1,0:T(8,128)(2,1)S(1)}, u32[]{:S(2)}, u32[]{:S(2)}) collective-permute-start(bf16[10,8,256]{2,1,0:T(8,128)(2,1)S(1)} %get-tuple-element.42), channel_id=1, source_target_pairs={{0,16},{1,17},{2,18},{3,19},{4,20},{5,21},{6,22},{7,23},{8,24},{9,... | collective-permute-start | bytes 122888 | tf_op jit(solution)/shard_map/ppermute | solution.py:594
  26.4 5.8 %collective-permute-start.7 = (bf16[10,8,256]{2,1,0:T(8,128)(2,1)S(1)}, bf16[10,8,256]{2,1,0:T(8,128)(2,1)S(1)}, u32[]{:S(2)}, u32[]{:S(2)}) collective-permute-start(bf16[10,8,256]{2,1,0:T(8,128)(2,1)S(1)} %get-tuple-element.43), channel_id=1, source_target_pairs={{0,24},{1,25},{2,26},{3,27},{4,28},{5,29},{6,30},{7,31},{8,16},{9,... | collective-permute-start | bytes 122888 | tf_op jit(solution)/shard_map/ppermute | solution.py:594
  27.7 4.5 %collective-permute-start.8 = (bf16[10,8,256]{2,1,0:T(8,128)(2,1)S(1)}, bf16[10,8,256]{2,1,0:T(8,128)(2,1)S(1)}, u32[]{:S(2)}, u32[]{:S(2)}) collective-permute-start(bf16[10,8,256]{2,1,0:T(8,128)(2,1)S(1)} %get-tuple-element.44), channel_id=1, source_target_pairs={{0,8},{1,9},{2,10},{3,11},{4,12},{5,13},{6,14},{7,15},{8,0},{9,1},... | collective-permute-start | bytes 122888 | tf_op jit(solution)/shard_map/ppermute | solution.py:594
  36.5 4.8 %collective-permute-start.9 = (bf16[10,1024]{1,0:T(8,128)(2,1)S(1)}, bf16[10,1024]{1,0:T(8,128)(2,1)S(1)}, u32[]{:S(2)}, u32[]{:S(2)}) collective-permute-start(bf16[10,1024]{1,0:T(8,128)(2,1)S(1)} %bitcast.16), channel_id=1, source_target_pairs={{0,8},{1,9},{2,10},{3,11},{4,12},{5,13},{6,14},{7,15},{8,0},{9,1},... | collective-permute-start | bytes 61448 | tf_op jit(solution)/shard_map/ppermute | solution.py:594
  36.6 5.8 %collective-permute-start.10 = (bf16[10,1024]{1,0:T(8,128)(2,1)S(1)}, bf16[10,1024]{1,0:T(8,128)(2,1)S(1)}, u32[]{:S(2)}, u32[]{:S(2)}) collective-permute-start(bf16[10,1024]{1,0:T(8,128)(2,1)S(1)} %bitcast.17), channel_id=1, source_target_pairs={{0,24},{1,25},{2,26},{3,27},{4,28},{5,29},{6,30},{7,31},{8,16},{9,... | collective-permute-start | bytes 61448 | tf_op jit(solution)/shard_map/ppermute | solution.py:594
  39.5 4.9 %collective-permute-start.11 = (bf16[10,1024]{1,0:T(8,128)(2,1)S(1)}, bf16[10,1024]{1,0:T(8,128)(2,1)S(1)}, u32[]{:S(2)}, u32[]{:S(2)}) collective-permute-start(bf16[10,1024]{1,0:T(8,128)(2,1)S(1)} %bitcast.18), channel_id=1, source_target_pairs={{0,16},{1,17},{2,18},{3,19},{4,20},{5,21},{6,22},{7,23},{8,24},{9,... | collective-permute-start | bytes 61448 | tf_op jit(solution)/shard_map/ppermute | solution.py:594
  40.1 13.6 %copy-start.4 = (bf16[128,512]{1,0:T(8,128)(2,1)S(1)}, bf16[128,512]{1,0:T(8,128)(2,1)}, u32[]{:S(2)}) copy-start(bf16[128,512]{1,0:T(8,128)(2,1)} %refs_8_.5) | copy-start | bytes 393220
  40.1 13.6 %copy-start.5 = (bf16[512,128]{1,0:T(8,128)(2,1)S(1)}, bf16[512,128]{1,0:T(8,128)(2,1)}, u32[]{:S(2)}) copy-start(bf16[512,128]{1,0:T(8,128)(2,1)} %refs_9_.3) | copy-start | bytes 393220
  40.1 13.6 %copy-start.12 = (f32[128]{0:T(128)S(1)}, f32[128]{0:T(128)}, u32[]{:S(2)}) copy-start(f32[128]{0:T(128)} %param.43) | copy-start | bytes 1540
  40.1 13.6 %copy-start.13 = (f32[10,320,128]{2,1,0:T(8,128)S(1)}, f32[10,320,128]{2,1,0:T(8,128)}, u32[]{:S(2)}) copy-start(f32[10,320,128]{2,1,0:T(8,128)} %get-tuple-element.61.refs_6_) | copy-start | bytes 4915204
  44.4 5.4 %collective-permute-start.12 = (bf16[40,1024]{1,0:T(8,128)(2,1)S(1)}, bf16[40,1024]{1,0:T(8,128)(2,1)S(1)}, u32[]{:S(2)}, u32[]{:S(2)}) collective-permute-start(bf16[40,1024]{1,0:T(8,128)(2,1)S(1)} %pad_maximum_fusion.1.refs_0_), channel_id=1, source_target_pairs={{0,6},{1,7},{2,4},{3,5},{4,2},{5,3},{6,0},{7,1},{8,14},{9,15},{10,... | collective-permute-start | bytes 245768 | tf_op jit(solution)/shard_map/ppermute | solution.py:594
  46.9 4.4 %collective-permute-start.13 = (bf16[40,1024]{1,0:T(8,128)(2,1)S(1)}, bf16[40,1024]{1,0:T(8,128)(2,1)S(1)}, u32[]{:S(2)}, u32[]{:S(2)}) collective-permute-start(bf16[40,1024]{1,0:T(8,128)(2,1)S(1)} %pad_maximum_fusion.1.refs_0_), channel_id=1, source_target_pairs={{0,2},{1,3},{2,0},{3,1},{4,6},{5,7},{6,4},{7,5},{8,10},{9,11},{10,... | collective-permute-start | bytes 245768 | tf_op jit(solution)/shard_map/ppermute | solution.py:594
  47.5 4.4 %collective-permute-start.14 = (bf16[40,1024]{1,0:T(8,128)(2,1)S(1)}, bf16[40,1024]{1,0:T(8,128)(2,1)S(1)}, u32[]{:S(2)}, u32[]{:S(2)}) collective-permute-start(bf16[40,1024]{1,0:T(8,128)(2,1)S(1)} %pad_maximum_fusion.1.refs_0_), channel_id=1, source_target_pairs={{0,4},{1,5},{2,6},{3,7},{4,0},{5,1},{6,2},{7,3},{8,12},{9,13},{10,... | collective-permute-start | bytes 245768 | tf_op jit(solution)/shard_map/ppermute | solution.py:594
  51.9 1.7 %collective-permute-start.16 = (bf16[120,1024]{1,0:T(8,128)(2,1)S(1)}, bf16[120,1024]{1,0:T(8,128)(2,1)S(1)}, u32[]{:S(2)}, u32[]{:S(2)}) collective-permute-start(bf16[120,1024]{1,0:T(8,128)(2,1)S(1)} %constant_dynamic-update-slice_fusion.2.refs_1_), channel_id=1, source_target_pairs={{0,1},{1,0},{2,3},{3,2},{4,5},{5,4},{6,7},{7,6},{8,9},{9,8},{10,11... | collective-permute-start | bytes 737288 | tf_op jit(solution)/shard_map/ppermute | solution.py:594
  52.0 1.6 %collective-permute-start.15 = (bf16[40,1024]{1,0:T(8,128)(2,1)S(1)}, bf16[40,1024]{1,0:T(8,128)(2,1)S(1)}, u32[]{:S(2)}, u32[]{:S(2)}) collective-permute-start(bf16[40,1024]{1,0:T(8,128)(2,1)S(1)} %pad_maximum_fusion.1.refs_0_), channel_id=1, source_target_pairs={{0,1},{1,0},{2,3},{3,2},{4,5},{5,4},{6,7},{7,6},{8,9},{9,8},{10,11... | collective-permute-start | bytes 245768 | tf_op jit(solution)/shard_map/ppermute | solution.py:594

commit v6 on v5

--- a/solution.py
+++ b/solution.py
@@ -477,8 +477,9 @@
         i = r - b * rows
         across_sub = 2 * div_const(b, far, half // rows)
         across_far = b - far * (across_sub >> 1)
-        home = ((z ^ across_far) * sub + (p ^ across_sub)) * rows + i
-        away = ((z ^ across_far) * sub + (p ^ 1 ^ across_sub)) * rows + i
+        core = jnp.where(across_sub > 0, 1, 0) ^ jnp.where(across_far > 0, 1, 0)
+        home = ((z ^ across_far) * sub + (p ^ across_sub ^ core)) * rows + i
+        away = ((z ^ across_far) * sub + (p ^ 1 ^ across_sub ^ core)) * rows + i
         near = jnp.concatenate([ref[...].astype(F32) for ref in near_refs], 0).astype(BF16)
         across = jnp.concatenate([ref[...].astype(F32) for ref in across_refs], 0).astype(BF16)
 
@@ -637,11 +638,11 @@
     right = right.reshape(rows, channels * depth)
     factors = product_exit_factors.reshape(channels, -1)
     mixed, inverse = mix_call(idx, left, factors, alignment_validity, rows)
-    parts = [swap(right, SUB * k) for k in [1, *range(far - 1, 1, -1)]]
+    parts = [swap(right, SUB * k ^ 1) for k in [*range(2, far), 1]]
     mixed, right, *parts = lax.optimization_barrier((mixed, right, *parts))
-    parts = [right] + [part for _, part in sorted(zip([1, *range(far - 1, 1, -1)], parts), key=lambda pair: pair[0])]
+    parts = [right] + [part for _, part in sorted(zip([*range(2, far), 1], parts), key=lambda pair: pair[0])]
     column = jnp.concatenate(parts, 0)
-    near = [swap(column, k) for k in [6, 2, 4]]
+    near = [swap(column, k ^ 1) for k in [6, 2, 4]]
     near = lax.optimization_barrier(near)
     near = [part for _, part in sorted(zip([6, 2, 4], near), key=lambda pair: pair[0])]
     near = [column, jnp.concatenate(near, 0)]

time: 58 us -> 56.3 us (0.971)
  starting transfers between devices: 22.3 us -> 21.4 us
  waiting for transfers between devices: 14.8 us -> 14 us
    ppermute x17, starting transfers between devices: 22.3 us -> 21.4 us  [swap(): return lax.ppermute(x, 'dap', [(d, d ^ distance) for d in range(devices)])]
    ppermute x17, waiting for transfers between devices: 14.8 us -> 14 us  [swap(): return lax.ppermute(x, 'dap', [(d, d ^ distance) for d in range(devices)])]
where the time goes in v6:
time: 56.3 us; the launch traced here: 56.1 us
  starting transfers between devices  21.4 us (38%)
  Pallas kernels  18 us (32%)
  waiting for transfers between devices  14 us (25%)
  local copies, waits for them, and re-layouts  1.41 us (3%)
  between operations  1.11 us (2%)
    ppermute x17, starting transfers between devices, swap(): return lax.ppermute(x, 'dap', [(d, d ^ distance) for d in range(devices)])  21.4 us
    ppermute x17, waiting for transfers between devices, swap(): return lax.ppermute(x, 'dap', [(d, d ^ distance) for d in range(devices)])  14 us
    pallas_call x1, Pallas kernels, column_call(): pl.pallas_call(functools.partial(column_kernel, sub=sub, far=far, rows=ro...  4.25 us
    pallas_call x1, Pallas kernels, finish_call(): pl.pallas_call(functools.partial(finish_kernel, pieces=len(near), sub=sub...  3.94 us
    pallas_call x1, Pallas kernels, pair_call(): pl.pallas_call(functools.partial(pair_kernel, rows=rows, length=length, b...  3.45 us
    pallas_call x1, Pallas kernels, row_call(): pl.pallas_call(functools.partial(row_kernel, order=order, sub=sub, far=fa...  2.87 us
    pallas_call x1, Pallas kernels, project_call(): pl.pallas_call(functools.partial(project_kernel, sub=sub, far=far, rows=r...  2.29 us
    unnamed x44, local copies, waits for them, and re-layouts  1.28 us
  transfers between devices with their start and end apart: 17, of which 11 were waited for; matrix products, arithmetic and copies ran while one was open for 2% of the time, Pallas kernels for 12%

profile of v6, /device:TPU:0, one launch (start us, length us, event | category | flops | bytes accessed | tf_op | source)
XLA Modules:
  0.0 56.1 jit_solution(16572307064760400143)
XLA Ops:
  0.6 4.0 %collective-permute-start.3 = (bf16[1,320,256]{2,1,0:T(8,128)(2,1)}, bf16[1,320,256]{2,1,0:T(8,128)(2,1)S(1)}, u32[]{:S(2)}, u32[]{:S(2)}) collective-permute-start(bf16[1,320,256]{2,1,0:T(8,128)(2,1)} %param.23), channel_id=1, source_target_pairs={{0,6},{1,7},{2,4},{3,5},{4,2},{5,3},{6,0},{7,1},{8,14},{9,15},{10,... | collective-permute-start | bytes 491528 | tf_op jit(solution)/shard_map/ppermute | solution.py:595
  4.6 0.5 collective-permute-start.2
  5.1 0.1 collective-permute-start.1
  5.2 3.4 %pair_bias.1 = (f32[10,320,128]{2,1,0:T(8,128)}, bf16[10,8,320]{2,1,0:T(8,128)(2,1)}) custom-call(s32[1]{0:T(128)} %bitcast.idx, s32[320]{0:T(512)} %chain_row.1, bf16[10,320,128]{2,1,0:T(8,128)(2,1)} %pair.1, s32[320]{0:T(512)} %chain_row.1, f32[66,128]{1,0:T(8,128)} %table.1, f32[1,128]{1,0:T(1,128)} %bitcast.28, bf16[8,128]{1,0:T(8,128)(2,1)} %bitcast.27), custom_call_target="tpu_custom_call" | custom-call | flops 4000000000 | bytes 4000000 | tf_op jit(solution)/shard_map/pair_bias/pallas_call | solution.py:102
  8.7 3.0 %collective-permute-start = (bf16[10,8,320]{2,1,0:T(8,128)(2,1)}, bf16[10,8,320]{2,1,0:T(8,128)(2,1)S(1)}, u32[]{:S(2)}, u32[]{:S(2)}) collective-permute-start(bf16[10,8,320]{2,1,0:T(8,128)(2,1)} %get-tuple-element.32), channel_id=1, source_target_pairs={{0,16},{1,17},{2,18},{3,19},{4,20},{5,21},{6,22},{7,23},{8,24},{9,... | collective-permute-start | bytes 153608 | tf_op jit(solution)/shard_map/ppermute | solution.py:595
  11.7 0.9 %constant_dynamic-update-slice_fusion.1 = bf16[20,8,320]{2,1,0:T(8,128)(2,1)S(1)} fusion(bf16[10,8,320]{2,1,0:T(8,128)(2,1)} %get-tuple-element.32), kind=kLoop, calls=%fused_computation.3 | loop fusion | bytes 112640
  12.6 0.1 copy.26
  12.7 1.5 %collective-permute-done = bf16[10,8,320]{2,1,0:T(8,128)(2,1)S(1)} collective-permute-done((bf16[10,8,320]{2,1,0:T(8,128)(2,1)}, bf16[10,8,320]{2,1,0:T(8,128)(2,1)S(1)}, u32[]{:S(2)}, u32[]{:S(2)}) %collective-permute-start) | collective-permute-done | bytes 51232 | tf_op jit(solution)/shard_map/ppermute | solution.py:595
  14.2 0.1 pad_maximum_fusion.refs_0_
  14.3 0.1 collective-permute-start.5
  14.4 2.0 %collective-permute-start.4 = (bf16[20,8,320]{2,1,0:T(8,128)(2,1)S(1)}, bf16[20,8,320]{2,1,0:T(8,128)(2,1)S(1)}, u32[]{:S(2)}, u32[]{:S(2)}) collective-permute-start(bf16[20,8,320]{2,1,0:T(8,128)(2,1)S(1)} %constant_dynamic-update-slice_fusion.refs_0_), channel_id=1, source_target_pairs={{0,8},{1,9},{2,10},{3,11},{4,12},{5,13},{6,14},{7,15},{8,0},{9,1},... | collective-permute-start | bytes 307208 | tf_op jit(solution)/shard_map/ppermute | solution.py:595
  16.3 0.1 collective-permute-done.5.refs_1_
  16.5 2.3 %row_project.1 = (bf16[8,320,256]{2,1,0:T(8,128)(2,1)S(1)}, bf16[8,320,256]{2,1,0:T(8,128)(2,1)S(1)}, f32[320,256]{1,0:T(8,128)S(1)}, f32[320,256]{1,0:T(8,128)S(1)}, f32[320,256]{1,0:T(8,128)S(1)}) custom-call(s32[1]{0:T(128)} %bitcast.idx, bf16[4,320,256]{2,1,0:T(8,128)(2,1)S(1)} %pad_maximum_fusion.refs_0_, ...), custom_call_target="tpu_custom_call" | custom-call | flops 3000000000 | bytes 4000000 | tf_op jit(solution)/shard_map/row_project/pallas_call | solution.py:184
  18.8 1.5 %collective-permute-done.4.refs_1_ = bf16[20,8,320]{2,1,0:T(8,128)(2,1)S(1)} collective-permute-done((bf16[20,8,320]{2,1,0:T(8,128)(2,1)S(1)}, bf16[20,8,320]{2,1,0:T(8,128)(2,1)S(1)}, u32[]{:S(2)}, u32[]{:S(2)}) %collective-permute-start.4) | collective-permute-done | bytes 102432 | tf_op jit(solution)/shard_map/ppermute | solution.py:595
  20.3 0.0 copy-start.15
  20.3 0.0 copy-start.18
  20.3 0.0 copy-start.16
  20.3 2.9 %row_attention.1 = (bf16[10,8,256]{2,1,0:T(8,128)(2,1)S(1)}, bf16[10,8,256]{2,1,0:T(8,128)(2,1)S(1)}, bf16[10,8,256]{2,1,0:T(8,128)(2,1)S(1)}, bf16[10,8,256]{2,1,0:T(8,128)(2,1)S(1)}) custom-call(s32[1]{0:T(128)} %bitcast.idx, bf16[20,8,320]{2,1,0:T(8,128)(2,1)S(1)} %constant_dynamic-update-slice_fusion.refs_0_, ...), custom_call_target="tpu_custom_call" | custom-call | flops 4000000000 | bytes 4000000 | tf_op jit(solution)/shard_map/row_attention/pallas_call | solution.py:257
  23.2 0.0 copy-start
  23.2 0.0 copy-start.1
  23.2 0.0 copy-start.3
  23.2 0.0 copy-start.9
  23.2 0.0 copy-start.10
  23.2 0.0 copy-start.11
  23.3 3.2 %collective-permute-start.6 = (bf16[10,8,256]{2,1,0:T(8,128)(2,1)S(1)}, bf16[10,8,256]{2,1,0:T(8,128)(2,1)S(1)}, u32[]{:S(2)}, u32[]{:S(2)}) collective-permute-start(bf16[10,8,256]{2,1,0:T(8,128)(2,1)S(1)} %get-tuple-element.42), channel_id=1, source_target_pairs={{0,16},{1,17},{2,18},{3,19},{4,20},{5,21},{6,22},{7,23},{8,24},{9,... | collective-permute-start | bytes 122888 | tf_op jit(solution)/shard_map/ppermute | solution.py:595
  26.4 1.3 %collective-permute-start.7 = (bf16[10,8,256]{2,1,0:T(8,128)(2,1)S(1)}, bf16[10,8,256]{2,1,0:T(8,128)(2,1)S(1)}, u32[]{:S(2)}, u32[]{:S(2)}) collective-permute-start(bf16[10,8,256]{2,1,0:T(8,128)(2,1)S(1)} %get-tuple-element.43), channel_id=1, source_target_pairs={{0,24},{1,25},{2,26},{3,27},{4,28},{5,29},{6,30},{7,31},{8,16},{9,... | collective-permute-start | bytes 122888 | tf_op jit(solution)/shard_map/ppermute | solution.py:595
  27.7 0.5 collective-permute-start.8
  28.2 0.1 copy.27
  28.3 0.1 copy.25.refs_5_
  28.4 0.1 reshape.22.factors
  28.6 0.3 collective-permute-done.6.refs_2_
  28.8 3.4 %collective-permute-done.7.refs_3_ = bf16[10,8,256]{2,1,0:T(8,128)(2,1)S(1)} collective-permute-done((bf16[10,8,256]{2,1,0:T(8,128)(2,1)S(1)}, bf16[10,8,256]{2,1,0:T(8,128)(2,1)S(1)}, u32[]{:S(2)}, u32[]{:S(2)}) %collective-permute-start.7) | collective-permute-done | bytes 40992 | tf_op jit(solution)/shard_map/ppermute | solution.py:595
  32.3 4.2 %column_attention.1 = (bf16[10,32,256]{2,1,0:T(8,128)(2,1)}, bf16[320,32]{1,0:T(8,128)(2,1)S(1)}, bf16[1,10,1024]{2,1,0:T(8,128)(2,1)S(1)}) custom-call(s32[1]{0:T(128)} %bitcast.idx, bf16[10,8,256]{2,1,0:T(8,128)(2,1)S(1)} %get-tuple-element.41.refs_0_, bf16[10,8,256]{2,1,0:T(8,128)(2,1)S(1)} %collective-permute-done.8.refs_1_, ...), custom_call_target="tpu_custom_call" | custom-call | flops 5000000000 | bytes 4000000 | tf_op jit(solution)/shard_map/column_attention/pallas_call | solution.py:380
  36.5 0.1 collective-permute-start.9
  36.6 2.0 %collective-permute-start.10 = (bf16[10,1024]{1,0:T(8,128)(2,1)S(1)}, bf16[10,1024]{1,0:T(8,128)(2,1)S(1)}, u32[]{:S(2)}, u32[]{:S(2)}) collective-permute-start(bf16[10,1024]{1,0:T(8,128)(2,1)S(1)} %bitcast.17), channel_id=1, source_target_pairs={{0,25},{1,24},{2,27},{3,26},{4,29},{5,28},{6,31},{7,30},{8,17},{9,... | collective-permute-start | bytes 61448 | tf_op jit(solution)/shard_map/ppermute | solution.py:595
  38.6 0.3 collective-permute-start.11
  38.9 1.2 %left_mix.1 = (bf16[1024,1280]{1,0:T(8,128)(2,1)S(1)}, f32[320,1280]{1,0:T(8,128)S(1)}) custom-call(s32[1]{0:T(128)} %bitcast.idx, bf16[320,32]{1,0:T(8,128)(2,1)S(1)} %get-tuple-element.49.left, bf16[32,4096]{1,0:T(8,128)(2,1)S(1)} %reshape.22.factors, s32[32,320]{1,0:T(8,128)S(1)} %copy-done.6), custom_call_target="tpu_custom_call" | custom-call | flops 2000000000 | bytes 4000000 | tf_op jit(solution)/shard_map/left_mix/pallas_call | solution.py:441
  40.2 0.8 %collective-permute-done.9 = bf16[10,1024]{1,0:T(8,128)(2,1)S(1)} collective-permute-done((bf16[10,1024]{1,0:T(8,128)(2,1)S(1)}, bf16[10,1024]{1,0:T(8,128)(2,1)S(1)}, u32[]{:S(2)}, u32[]{:S(2)}) %collective-permute-start.9) | collective-permute-done | bytes 20512 | tf_op jit(solution)/shard_map/ppermute | solution.py:595
  41.0 0.9 %collective-permute-done.10 = bf16[10,1024]{1,0:T(8,128)(2,1)S(1)} collective-permute-done((bf16[10,1024]{1,0:T(8,128)(2,1)S(1)}, bf16[10,1024]{1,0:T(8,128)(2,1)S(1)}, u32[]{:S(2)}, u32[]{:S(2)}) %collective-permute-start.10) | collective-permute-done | bytes 20512 | tf_op jit(solution)/shard_map/ppermute | solution.py:595
  41.8 0.5 collective-permute-done.11
  42.4 3.1 %collective-permute-start.12 = (bf16[40,1024]{1,0:T(8,128)(2,1)S(1)}, bf16[40,1024]{1,0:T(8,128)(2,1)S(1)}, u32[]{:S(2)}, u32[]{:S(2)}) collective-permute-start(bf16[40,1024]{1,0:T(8,128)(2,1)S(1)} %pad_maximum_fusion.1.refs_0_), channel_id=1, source_target_pairs={{0,7},{1,6},{2,5},{3,4},{4,3},{5,2},{6,1},{7,0},{8,15},{9,14},{10,... | collective-permute-start | bytes 245768 | tf_op jit(solution)/shard_map/ppermute | solution.py:595
  45.5 0.8 %collective-permute-start.14 = (bf16[40,1024]{1,0:T(8,128)(2,1)S(1)}, bf16[40,1024]{1,0:T(8,128)(2,1)S(1)}, u32[]{:S(2)}, u32[]{:S(2)}) collective-permute-start(bf16[40,1024]{1,0:T(8,128)(2,1)S(1)} %pad_maximum_fusion.1.refs_0_), channel_id=1, source_target_pairs={{0,5},{1,4},{2,7},{3,6},{4,1},{5,0},{6,3},{7,2},{8,13},{9,12},{10,... | collective-permute-start | bytes 245768 | tf_op jit(solution)/shard_map/ppermute | solution.py:595
  46.2 2.1 %collective-permute-done.12 = bf16[40,1024]{1,0:T(8,128)(2,1)S(1)} collective-permute-done((bf16[40,1024]{1,0:T(8,128)(2,1)S(1)}, bf16[40,1024]{1,0:T(8,128)(2,1)S(1)}, u32[]{:S(2)}, u32[]{:S(2)}) %collective-permute-start.12) | collective-permute-done | bytes 81952 | tf_op jit(solution)/shard_map/ppermute | solution.py:595
  48.3 1.9 %collective-permute-done.13 = bf16[40,1024]{1,0:T(8,128)(2,1)S(1)} collective-permute-done((bf16[40,1024]{1,0:T(8,128)(2,1)S(1)}, bf16[40,1024]{1,0:T(8,128)(2,1)S(1)}, u32[]{:S(2)}, u32[]{:S(2)}) %collective-permute-start.13) | collective-permute-done | bytes 81952 | tf_op jit(solution)/shard_map/ppermute | solution.py:595
  50.3 0.2 collective-permute-start.16
  50.4 0.4 collective-permute-start.15
  50.8 1.1 %collective-permute-done.15.refs_2_ = bf16[40,1024]{1,0:T(8,128)(2,1)S(1)} collective-permute-done((bf16[40,1024]{1,0:T(8,128)(2,1)S(1)}, bf16[40,1024]{1,0:T(8,128)(2,1)S(1)}, u32[]{:S(2)}, u32[]{:S(2)}) %collective-permute-start.15) | collective-permute-done | bytes 81952 | tf_op jit(solution)/shard_map/ppermute | solution.py:595
  52.0 3.9 %pair_update.1 = bf16[10,320,128]{2,1,0:T(8,128)(2,1)} custom-call(s32[1]{0:T(128)} %bitcast.idx, bf16[40,1024]{1,0:T(8,128)(2,1)S(1)} %pad_maximum_fusion.1.refs_0_, bf16[120,1024]{1,0:T(8,128)(2,1)S(1)} %constant_dynamic-update-slice_fusion.2.refs_1_, bf16[40,1024]{1,0:T(8,128)(2,1)S(1)} %collective-permute-done.15.refs_2_, ...), custom_call_target="tpu_custom_call" | custom-call | flops 4000000000 | bytes 4000000 | tf_op jit(solution)/shard_map/pair_update/pallas_call | solution.py:537
  (41 shorter events, 0.2 us)
Async XLA Ops:
  0.6 13.5 %collective-permute-start.3 = (bf16[1,320,256]{2,1,0:T(8,128)(2,1)}, bf16[1,320,256]{2,1,0:T(8,128)(2,1)S(1)}, u32[]{:S(2)}, u32[]{:S(2)}) collective-permute-start(bf16[1,320,256]{2,1,0:T(8,128)(2,1)} %param.23), channel_id=1, source_target_pairs={{0,6},{1,7},{2,4},{3,5},{4,2},{5,3},{6,0},{7,1},{8,14},{9,15},{10,... | collective-permute-start | bytes 491528 | tf_op jit(solution)/shard_map/ppermute | solution.py:595
  4.6 9.6 %collective-permute-start.2 = (bf16[1,320,256]{2,1,0:T(8,128)(2,1)}, bf16[1,320,256]{2,1,0:T(8,128)(2,1)S(1)}, u32[]{:S(2)}, u32[]{:S(2)}) collective-permute-start(bf16[1,320,256]{2,1,0:T(8,128)(2,1)} %param.23), channel_id=1, source_target_pairs={{0,4},{1,5},{2,6},{3,7},{4,0},{5,1},{6,2},{7,3},{8,12},{9,13},{10,... | collective-permute-start | bytes 491528 | tf_op jit(solution)/shard_map/ppermute | solution.py:595
  5.1 9.1 %collective-permute-start.1 = (bf16[1,320,256]{2,1,0:T(8,128)(2,1)}, bf16[1,320,256]{2,1,0:T(8,128)(2,1)S(1)}, u32[]{:S(2)}, u32[]{:S(2)}) collective-permute-start(bf16[1,320,256]{2,1,0:T(8,128)(2,1)} %param.23), channel_id=1, source_target_pairs={{0,2},{1,3},{2,0},{3,1},{4,6},{5,7},{6,4},{7,5},{8,10},{9,11},{10,... | collective-permute-start | bytes 491528 | tf_op jit(solution)/shard_map/ppermute | solution.py:595
  5.2 7.3 %copy-start.14 = (bf16[256,4,256]{2,1,0:T(4,128)(2,1)S(1)}, bf16[256,4,256]{2,1,0:T(4,128)(2,1)}, u32[]{:S(2)}) copy-start(bf16[256,4,256]{2,1,0:T(4,128)(2,1)} %param.32) | copy-start | bytes 1572868
  5.2 9.0 %copy-start.17 = (bf16[1,320,256]{2,1,0:T(8,128)(2,1)S(1)}, bf16[1,320,256]{2,1,0:T(8,128)(2,1)}, u32[]{:S(2)}) copy-start(bf16[1,320,256]{2,1,0:T(8,128)(2,1)} %param.23) | copy-start | bytes 491524
  8.7 7.8 %copy-start.8 = (f32[256]{0:T(256)S(1)}, f32[256]{0:T(256)}, u32[]{:S(2)}) copy-start(f32[256]{0:T(256)} %param.31) | copy-start | bytes 3076
  8.7 5.5 %collective-permute-start = (bf16[10,8,320]{2,1,0:T(8,128)(2,1)}, bf16[10,8,320]{2,1,0:T(8,128)(2,1)S(1)}, u32[]{:S(2)}, u32[]{:S(2)}) collective-permute-start(bf16[10,8,320]{2,1,0:T(8,128)(2,1)} %get-tuple-element.32), channel_id=1, source_target_pairs={{0,16},{1,17},{2,18},{3,19},{4,20},{5,21},{6,22},{7,23},{8,24},{9,... | collective-permute-start | bytes 153608 | tf_op jit(solution)/shard_map/ppermute | solution.py:595
  14.3 2.2 %collective-permute-start.5 = (bf16[4,320,256]{2,1,0:T(8,128)(2,1)S(1)}, bf16[4,320,256]{2,1,0:T(8,128)(2,1)S(1)}, u32[]{:S(2)}, u32[]{:S(2)}) collective-permute-start(bf16[4,320,256]{2,1,0:T(8,128)(2,1)S(1)} %pad_maximum_fusion.refs_0_), channel_id=1, source_target_pairs={{0,1},{1,0},{2,3},{3,2},{4,5},{5,4},{6,7},{7,6},{8,9},{9,8},{10,11... | collective-permute-start | bytes 1966088 | tf_op jit(solution)/shard_map/ppermute | solution.py:595
  14.4 5.9 %collective-permute-start.4 = (bf16[20,8,320]{2,1,0:T(8,128)(2,1)S(1)}, bf16[20,8,320]{2,1,0:T(8,128)(2,1)S(1)}, u32[]{:S(2)}, u32[]{:S(2)}) collective-permute-start(bf16[20,8,320]{2,1,0:T(8,128)(2,1)S(1)} %constant_dynamic-update-slice_fusion.refs_0_), channel_id=1, source_target_pairs={{0,8},{1,9},{2,10},{3,11},{4,12},{5,13},{6,14},{7,15},{8,0},{9,1},... | collective-permute-start | bytes 307208 | tf_op jit(solution)/shard_map/ppermute | solution.py:595
  16.5 3.8 %copy-start.2 = (bf16[256,256]{1,0:T(8,128)(2,1)S(1)}, bf16[256,256]{1,0:T(8,128)(2,1)}, u32[]{:S(2)}) copy-start(bf16[256,256]{1,0:T(8,128)(2,1)} %refs_9_.2) | copy-start | bytes 393220
  16.5 3.8 %copy-start.6 = (s32[32,320]{1,0:T(8,128)S(1)}, s32[32,320]{1,0:T(8,128)}, u32[]{:S(2)}) copy-start(s32[32,320]{1,0:T(8,128)} %validity.1) | copy-start | bytes 122884
  16.5 3.8 %copy-start.7 = (s32[320]{0:T(512)S(1)}, s32[320]{0:T(512)}, u32[]{:S(2)}) copy-start(s32[320]{0:T(512)} %refs_8_.3) | copy-start | bytes 3844
  20.3 7.9 %copy-start.15 = (bf16[256,4,256]{2,1,0:T(4,128)(2,1)S(1)}, bf16[256,4,256]{2,1,0:T(4,128)(2,1)}, u32[]{:S(2)}) copy-start(bf16[256,4,256]{2,1,0:T(4,128)(2,1)} %param.35) | copy-start | bytes 1572868
  20.3 8.0 %copy-start.18 = (bf16[256,64]{0,1:T(8,128)(2,1)S(1)}, bf16[256,64]{0,1:T(8,128)(2,1)}, u32[]{:S(2)}) copy-start(bf16[256,64]{0,1:T(8,128)(2,1)} %param.41) | copy-start | bytes 98308
  20.3 8.1 %copy-start.16 = (bf16[1024,128]{1,0:T(8,128)(2,1)S(1)}, bf16[1024,128]{1,0:T(8,128)(2,1)}, u32[]{:S(2)}) copy-start(bf16[1024,128]{1,0:T(8,128)(2,1)} %param.42) | copy-start | bytes 786436
  23.2 9.1 %copy-start = (bf16[256,1024]{1,0:T(8,128)(2,1)S(1)}, bf16[256,1024]{1,0:T(8,128)(2,1)}, u32[]{:S(2)}) copy-start(bf16[256,1024]{1,0:T(8,128)(2,1)} %refs_10_.1) | copy-start | bytes 1572868
  23.2 9.0 %copy-start.1 = (bf16[1024,256]{1,0:T(8,128)(2,1)S(1)}, bf16[1024,256]{1,0:T(8,128)(2,1)}, u32[]{:S(2)}) copy-start(bf16[1024,256]{1,0:T(8,128)(2,1)} %refs_11_.1) | copy-start | bytes 1572868
  23.2 9.0 %copy-start.3 = (bf16[256,256]{1,0:T(8,128)(2,1)S(1)}, bf16[256,256]{1,0:T(8,128)(2,1)}, u32[]{:S(2)}) copy-start(bf16[256,256]{1,0:T(8,128)(2,1)} %refs_8_.4) | copy-start | bytes 393220
  23.2 9.0 %copy-start.9 = (f32[256]{0:T(256)S(1)}, f32[256]{0:T(256)}, u32[]{:S(2)}) copy-start(f32[256]{0:T(256)} %param.34) | copy-start | bytes 3076
  23.2 9.0 %copy-start.10 = (f32[256]{0:T(256)S(1)}, f32[256]{0:T(256)}, u32[]{:S(2)}) copy-start(f32[256]{0:T(256)} %param.37) | copy-start | bytes 3076
  23.2 9.0 %copy-start.11 = (f32[256]{0:T(256)S(1)}, f32[256]{0:T(256)}, u32[]{:S(2)}) copy-start(f32[256]{0:T(256)} %param.40) | copy-start | bytes 3076
  23.3 5.6 %collective-permute-start.6 = (bf16[10,8,256]{2,1,0:T(8,128)(2,1)S(1)}, bf16[10,8,256]{2,1,0:T(8,128)(2,1)S(1)}, u32[]{:S(2)}, u32[]{:S(2)}) collective-permute-start(bf16[10,8,256]{2,1,0:T(8,128)(2,1)S(1)} %get-tuple-element.42), channel_id=1, source_target_pairs={{0,16},{1,17},{2,18},{3,19},{4,20},{5,21},{6,22},{7,23},{8,24},{9,... | collective-permute-start | bytes 122888 | tf_op jit(solution)/shard_map/ppermute | solution.py:595
  26.4 5.8 %collective-permute-start.7 = (bf16[10,8,256]{2,1,0:T(8,128)(2,1)S(1)}, bf16[10,8,256]{2,1,0:T(8,128)(2,1)S(1)}, u32[]{:S(2)}, u32[]{:S(2)}) collective-permute-start(bf16[10,8,256]{2,1,0:T(8,128)(2,1)S(1)} %get-tuple-element.43), channel_id=1, source_target_pairs={{0,24},{1,25},{2,26},{3,27},{4,28},{5,29},{6,30},{7,31},{8,16},{9,... | collective-permute-start | bytes 122888 | tf_op jit(solution)/shard_map/ppermute | solution.py:595
  27.7 4.5 %collective-permute-start.8 = (bf16[10,8,256]{2,1,0:T(8,128)(2,1)S(1)}, bf16[10,8,256]{2,1,0:T(8,128)(2,1)S(1)}, u32[]{:S(2)}, u32[]{:S(2)}) collective-permute-start(bf16[10,8,256]{2,1,0:T(8,128)(2,1)S(1)} %get-tuple-element.44), channel_id=1, source_target_pairs={{0,8},{1,9},{2,10},{3,11},{4,12},{5,13},{6,14},{7,15},{8,0},{9,1},... | collective-permute-start | bytes 122888 | tf_op jit(solution)/shard_map/ppermute | solution.py:595
  36.5 4.4 %collective-permute-start.9 = (bf16[10,1024]{1,0:T(8,128)(2,1)S(1)}, bf16[10,1024]{1,0:T(8,128)(2,1)S(1)}, u32[]{:S(2)}, u32[]{:S(2)}) collective-permute-start(bf16[10,1024]{1,0:T(8,128)(2,1)S(1)} %bitcast.16), channel_id=1, source_target_pairs={{0,17},{1,16},{2,19},{3,18},{4,21},{5,20},{6,23},{7,22},{8,25},{9,... | collective-permute-start | bytes 61448 | tf_op jit(solution)/shard_map/ppermute | solution.py:595
  36.6 5.2 %collective-permute-start.10 = (bf16[10,1024]{1,0:T(8,128)(2,1)S(1)}, bf16[10,1024]{1,0:T(8,128)(2,1)S(1)}, u32[]{:S(2)}, u32[]{:S(2)}) collective-permute-start(bf16[10,1024]{1,0:T(8,128)(2,1)S(1)} %bitcast.17), channel_id=1, source_target_pairs={{0,25},{1,24},{2,27},{3,26},{4,29},{5,28},{6,31},{7,30},{8,17},{9,... | collective-permute-start | bytes 61448 | tf_op jit(solution)/shard_map/ppermute | solution.py:595
  38.6 3.7 %collective-permute-start.11 = (bf16[10,1024]{1,0:T(8,128)(2,1)S(1)}, bf16[10,1024]{1,0:T(8,128)(2,1)S(1)}, u32[]{:S(2)}, u32[]{:S(2)}) collective-permute-start(bf16[10,1024]{1,0:T(8,128)(2,1)S(1)} %bitcast.18), channel_id=1, source_target_pairs={{0,9},{1,8},{2,11},{3,10},{4,13},{5,12},{6,15},{7,14},{8,1},{9,0},... | collective-permute-start | bytes 61448 | tf_op jit(solution)/shard_map/ppermute | solution.py:595
  38.9 13.0 %copy-start.4 = (bf16[128,512]{1,0:T(8,128)(2,1)S(1)}, bf16[128,512]{1,0:T(8,128)(2,1)}, u32[]{:S(2)}) copy-start(bf16[128,512]{1,0:T(8,128)(2,1)} %refs_8_.5) | copy-start | bytes 393220
  38.9 13.0 %copy-start.5 = (bf16[512,128]{1,0:T(8,128)(2,1)S(1)}, bf16[512,128]{1,0:T(8,128)(2,1)}, u32[]{:S(2)}) copy-start(bf16[512,128]{1,0:T(8,128)(2,1)} %refs_9_.3) | copy-start | bytes 393220
  38.9 13.0 %copy-start.12 = (f32[128]{0:T(128)S(1)}, f32[128]{0:T(128)}, u32[]{:S(2)}) copy-start(f32[128]{0:T(128)} %param.43) | copy-start | bytes 1540
  38.9 13.1 %copy-start.13 = (f32[10,320,128]{2,1,0:T(8,128)S(1)}, f32[10,320,128]{2,1,0:T(8,128)}, u32[]{:S(2)}) copy-start(f32[10,320,128]{2,1,0:T(8,128)} %get-tuple-element.61.refs_6_) | copy-start | bytes 4915204
  42.4 5.9 %collective-permute-start.12 = (bf16[40,1024]{1,0:T(8,128)(2,1)S(1)}, bf16[40,1024]{1,0:T(8,128)(2,1)S(1)}, u32[]{:S(2)}, u32[]{:S(2)}) collective-permute-start(bf16[40,1024]{1,0:T(8,128)(2,1)S(1)} %pad_maximum_fusion.1.refs_0_), channel_id=1, source_target_pairs={{0,7},{1,6},{2,5},{3,4},{4,3},{5,2},{6,1},{7,0},{8,15},{9,14},{10,... | collective-permute-start | bytes 245768 | tf_op jit(solution)/shard_map/ppermute | solution.py:595
  45.5 4.7 %collective-permute-start.13 = (bf16[40,1024]{1,0:T(8,128)(2,1)S(1)}, bf16[40,1024]{1,0:T(8,128)(2,1)S(1)}, u32[]{:S(2)}, u32[]{:S(2)}) collective-permute-start(bf16[40,1024]{1,0:T(8,128)(2,1)S(1)} %pad_maximum_fusion.1.refs_0_), channel_id=1, source_target_pairs={{0,3},{1,2},{2,1},{3,0},{4,7},{5,6},{6,5},{7,4},{8,11},{9,10},{10,... | collective-permute-start | bytes 245768 | tf_op jit(solution)/shard_map/ppermute | solution.py:595
  45.5 4.7 %collective-permute-start.14 = (bf16[40,1024]{1,0:T(8,128)(2,1)S(1)}, bf16[40,1024]{1,0:T(8,128)(2,1)S(1)}, u32[]{:S(2)}, u32[]{:S(2)}) collective-permute-start(bf16[40,1024]{1,0:T(8,128)(2,1)S(1)} %pad_maximum_fusion.1.refs_0_), channel_id=1, source_target_pairs={{0,5},{1,4},{2,7},{3,6},{4,1},{5,0},{6,3},{7,2},{8,13},{9,12},{10,... | collective-permute-start | bytes 245768 | tf_op jit(solution)/shard_map/ppermute | solution.py:595
  50.3 1.7 %collective-permute-start.16 = (bf16[120,1024]{1,0:T(8,128)(2,1)S(1)}, bf16[120,1024]{1,0:T(8,128)(2,1)S(1)}, u32[]{:S(2)}, u32[]{:S(2)}) collective-permute-start(bf16[120,1024]{1,0:T(8,128)(2,1)S(1)} %constant_dynamic-update-slice_fusion.2.refs_1_), channel_id=1, source_target_pairs={{0,1},{1,0},{2,3},{3,2},{4,5},{5,4},{6,7},{7,6},{8,9},{9,8},{10,11... | collective-permute-start | bytes 737288 | tf_op jit(solution)/shard_map/ppermute | solution.py:595
  50.4 1.5 %collective-permute-start.15 = (bf16[40,1024]{1,0:T(8,128)(2,1)S(1)}, bf16[40,1024]{1,0:T(8,128)(2,1)S(1)}, u32[]{:S(2)}, u32[]{:S(2)}) collective-permute-start(bf16[40,1024]{1,0:T(8,128)(2,1)S(1)} %pad_maximum_fusion.1.refs_0_), channel_id=1, source_target_pairs={{0,1},{1,0},{2,3},{3,2},{4,5},{5,4},{6,7},{7,6},{8,9},{9,8},{10,11... | collective-permute-start | bytes 245768 | tf_op jit(solution)/shard_map/ppermute | solution.py:595

commit v7 on v6

--- a/solution.py
+++ b/solution.py
@@ -83,14 +83,20 @@
 
     other = table[bins - 1 : bins, :]
     block = pair.shape[0]
-    for r in range(block):
-        i = idx[0] * rows + step * block + r
-        near = shifted[pl.ds(length - i, length), :]
-        same = chain_wide[...] == chain[i].astype(F32)
-        x = pair[r].astype(F32) + jnp.where(same, near, other)
-        pair_one[r] = x
-        normed = layer_norm(x, gain[...]).astype(BF16)
-        bias[r] = dot_nt(factors[...], normed).astype(BF16)
+    together = block
+    for start in range(0, block, together):
+        sums = []
+        for r in range(start, start + together):
+            i = idx[0] * rows + step * block + r
+            near = shifted[pl.ds(length - i, length), :]
+            same = chain_wide[...] == chain[i].astype(F32)
+            x = pair[r].astype(F32) + jnp.where(same, near, other)
+            pair_one[r] = x
+            sums.append(x)
+        normed = layer_norm(jnp.concatenate(sums, 0), gain[...]).astype(BF16)
+        both = dot_nt(factors[...], normed).astype(BF16)
+        for r in range(together):
+            bias[start + r] = both[:, r * length : (r + 1) * length]
 
 
 def pair_call(idx, chain, pair, table, gain, factors):

time: 56.3 us -> 56.2 us (level)
  no operation moved by 1% of the time
where the time goes in v7:
time: 56.2 us; the launch traced here: 56 us
  starting transfers between devices  21.3 us (38%)
  Pallas kernels  18 us (32%)
  waiting for transfers between devices  14 us (25%)
  local copies, waits for them, and re-layouts  1.41 us (3%)
  between operations  1.11 us (2%)
    ppermute x17, starting transfers between devices, swap(): return lax.ppermute(x, 'dap', [(d, d ^ distance) for d in range(devices)])  21.3 us
    ppermute x17, waiting for transfers between devices, swap(): return lax.ppermute(x, 'dap', [(d, d ^ distance) for d in range(devices)])  14 us
    pallas_call x1, Pallas kernels, column_call(): pl.pallas_call(functools.partial(column_kernel, sub=sub, far=far, rows=ro...  4.26 us
    pallas_call x1, Pallas kernels, finish_call(): pl.pallas_call(functools.partial(finish_kernel, pieces=len(near), sub=sub...  3.93 us
    pallas_call x1, Pallas kernels, pair_call(): pl.pallas_call(functools.partial(pair_kernel, rows=rows, length=length, b...  3.37 us
    pallas_call x1, Pallas kernels, row_call(): pl.pallas_call(functools.partial(row_kernel, order=order, sub=sub, far=fa...  2.87 us
    pallas_call x1, Pallas kernels, project_call(): pl.pallas_call(functools.partial(project_kernel, sub=sub, far=far, rows=r...  2.29 us
    unnamed x44, local copies, waits for them, and re-layouts  1.28 us
  transfers between devices with their start and end apart: 17, of which 11 were waited for; matrix products, arithmetic and copies ran while one was open for 2% of the time, Pallas kernels for 12%

profile of v7, /device:TPU:0, one launch (start us, length us, event | category | flops | bytes accessed | tf_op | source)
XLA Modules:
  0.0 56.0 jit_solution(4101341460321860227)
XLA Ops:
  0.6 4.0 %collective-permute-start.3 = (bf16[1,320,256]{2,1,0:T(8,128)(2,1)}, bf16[1,320,256]{2,1,0:T(8,128)(2,1)S(1)}, u32[]{:S(2)}, u32[]{:S(2)}) collective-permute-start(bf16[1,320,256]{2,1,0:T(8,128)(2,1)} %param.23), channel_id=1, source_target_pairs={{0,6},{1,7},{2,4},{3,5},{4,2},{5,3},{6,0},{7,1},{8,14},{9,15},{10,... | collective-permute-start | bytes 491528 | tf_op jit(solution)/shard_map/ppermute | solution.py:601
  4.6 0.5 collective-permute-start.2
  5.1 0.1 collective-permute-start.1
  5.2 3.4 %pair_bias.1 = (f32[10,320,128]{2,1,0:T(8,128)}, bf16[10,8,320]{2,1,0:T(8,128)(2,1)}) custom-call(s32[1]{0:T(128)} %bitcast.idx, s32[320]{0:T(512)} %chain_row.1, bf16[10,320,128]{2,1,0:T(8,128)(2,1)} %pair.1, s32[320]{0:T(512)} %chain_row.1, f32[66,128]{1,0:T(8,128)} %table.1, f32[1,128]{1,0:T(1,128)} %bitcast.28, bf16[8,128]{1,0:T(8,128)(2,1)} %bitcast.27), custom_call_target="tpu_custom_call" | custom-call | flops 4000000000 | bytes 4000000 | tf_op jit(solution)/shard_map/pair_bias/pallas_call | solution.py:108
  8.6 3.0 %collective-permute-start = (bf16[10,8,320]{2,1,0:T(8,128)(2,1)}, bf16[10,8,320]{2,1,0:T(8,128)(2,1)S(1)}, u32[]{:S(2)}, u32[]{:S(2)}) collective-permute-start(bf16[10,8,320]{2,1,0:T(8,128)(2,1)} %get-tuple-element.32), channel_id=1, source_target_pairs={{0,16},{1,17},{2,18},{3,19},{4,20},{5,21},{6,22},{7,23},{8,24},{9,... | collective-permute-start | bytes 153608 | tf_op jit(solution)/shard_map/ppermute | solution.py:601
  11.6 0.9 %constant_dynamic-update-slice_fusion.1 = bf16[20,8,320]{2,1,0:T(8,128)(2,1)S(1)} fusion(bf16[10,8,320]{2,1,0:T(8,128)(2,1)} %get-tuple-element.32), kind=kLoop, calls=%fused_computation.3 | loop fusion | bytes 112640
  12.5 0.1 copy.26
  12.6 1.5 %collective-permute-done = bf16[10,8,320]{2,1,0:T(8,128)(2,1)S(1)} collective-permute-done((bf16[10,8,320]{2,1,0:T(8,128)(2,1)}, bf16[10,8,320]{2,1,0:T(8,128)(2,1)S(1)}, u32[]{:S(2)}, u32[]{:S(2)}) %collective-permute-start) | collective-permute-done | bytes 51232 | tf_op jit(solution)/shard_map/ppermute | solution.py:601
  14.1 0.1 pad_maximum_fusion.refs_0_
  14.2 0.1 collective-permute-start.5
  14.3 2.0 %collective-permute-start.4 = (bf16[20,8,320]{2,1,0:T(8,128)(2,1)S(1)}, bf16[20,8,320]{2,1,0:T(8,128)(2,1)S(1)}, u32[]{:S(2)}, u32[]{:S(2)}) collective-permute-start(bf16[20,8,320]{2,1,0:T(8,128)(2,1)S(1)} %constant_dynamic-update-slice_fusion.refs_0_), channel_id=1, source_target_pairs={{0,8},{1,9},{2,10},{3,11},{4,12},{5,13},{6,14},{7,15},{8,0},{9,1},... | collective-permute-start | bytes 307208 | tf_op jit(solution)/shard_map/ppermute | solution.py:601
  16.3 0.1 collective-permute-done.5.refs_1_
  16.4 2.3 %row_project.1 = (bf16[8,320,256]{2,1,0:T(8,128)(2,1)S(1)}, bf16[8,320,256]{2,1,0:T(8,128)(2,1)S(1)}, f32[320,256]{1,0:T(8,128)S(1)}, f32[320,256]{1,0:T(8,128)S(1)}, f32[320,256]{1,0:T(8,128)S(1)}) custom-call(s32[1]{0:T(128)} %bitcast.idx, bf16[4,320,256]{2,1,0:T(8,128)(2,1)S(1)} %pad_maximum_fusion.refs_0_, ...), custom_call_target="tpu_custom_call" | custom-call | flops 3000000000 | bytes 4000000 | tf_op jit(solution)/shard_map/row_project/pallas_call | solution.py:190
  18.7 1.5 %collective-permute-done.4.refs_1_ = bf16[20,8,320]{2,1,0:T(8,128)(2,1)S(1)} collective-permute-done((bf16[20,8,320]{2,1,0:T(8,128)(2,1)S(1)}, bf16[20,8,320]{2,1,0:T(8,128)(2,1)S(1)}, u32[]{:S(2)}, u32[]{:S(2)}) %collective-permute-start.4) | collective-permute-done | bytes 102432 | tf_op jit(solution)/shard_map/ppermute | solution.py:601
  20.2 0.0 copy-start.15
  20.2 0.0 copy-start.18
  20.2 0.0 copy-start.16
  20.2 2.9 %row_attention.1 = (bf16[10,8,256]{2,1,0:T(8,128)(2,1)S(1)}, bf16[10,8,256]{2,1,0:T(8,128)(2,1)S(1)}, bf16[10,8,256]{2,1,0:T(8,128)(2,1)S(1)}, bf16[10,8,256]{2,1,0:T(8,128)(2,1)S(1)}) custom-call(s32[1]{0:T(128)} %bitcast.idx, bf16[20,8,320]{2,1,0:T(8,128)(2,1)S(1)} %constant_dynamic-update-slice_fusion.refs_0_, ...), custom_call_target="tpu_custom_call" | custom-call | flops 4000000000 | bytes 4000000 | tf_op jit(solution)/shard_map/row_attention/pallas_call | solution.py:263
  23.1 0.0 copy-start
  23.1 0.0 copy-start.1
  23.1 0.0 copy-start.3
  23.1 0.0 copy-start.9
  23.2 0.0 copy-start.10
  23.2 0.0 copy-start.11
  23.2 3.2 %collective-permute-start.6 = (bf16[10,8,256]{2,1,0:T(8,128)(2,1)S(1)}, bf16[10,8,256]{2,1,0:T(8,128)(2,1)S(1)}, u32[]{:S(2)}, u32[]{:S(2)}) collective-permute-start(bf16[10,8,256]{2,1,0:T(8,128)(2,1)S(1)} %get-tuple-element.42), channel_id=1, source_target_pairs={{0,16},{1,17},{2,18},{3,19},{4,20},{5,21},{6,22},{7,23},{8,24},{9,... | collective-permute-start | bytes 122888 | tf_op jit(solution)/shard_map/ppermute | solution.py:601
  26.3 1.3 %collective-permute-start.7 = (bf16[10,8,256]{2,1,0:T(8,128)(2,1)S(1)}, bf16[10,8,256]{2,1,0:T(8,128)(2,1)S(1)}, u32[]{:S(2)}, u32[]{:S(2)}) collective-permute-start(bf16[10,8,256]{2,1,0:T(8,128)(2,1)S(1)} %get-tuple-element.43), channel_id=1, source_target_pairs={{0,24},{1,25},{2,26},{3,27},{4,28},{5,29},{6,30},{7,31},{8,16},{9,... | collective-permute-start | bytes 122888 | tf_op jit(solution)/shard_map/ppermute | solution.py:601
  27.6 0.5 collective-permute-start.8
  28.1 0.1 copy.27
  28.2 0.1 copy.25.refs_5_
  28.4 0.1 reshape.22.factors
  28.5 0.3 collective-permute-done.6.refs_2_
  28.8 3.4 %collective-permute-done.7.refs_3_ = bf16[10,8,256]{2,1,0:T(8,128)(2,1)S(1)} collective-permute-done((bf16[10,8,256]{2,1,0:T(8,128)(2,1)S(1)}, bf16[10,8,256]{2,1,0:T(8,128)(2,1)S(1)}, u32[]{:S(2)}, u32[]{:S(2)}) %collective-permute-start.7) | collective-permute-done | bytes 40992 | tf_op jit(solution)/shard_map/ppermute | solution.py:601
  32.2 4.3 %column_attention.1 = (bf16[10,32,256]{2,1,0:T(8,128)(2,1)}, bf16[320,32]{1,0:T(8,128)(2,1)S(1)}, bf16[1,10,1024]{2,1,0:T(8,128)(2,1)S(1)}) custom-call(s32[1]{0:T(128)} %bitcast.idx, bf16[10,8,256]{2,1,0:T(8,128)(2,1)S(1)} %get-tuple-element.41.refs_0_, bf16[10,8,256]{2,1,0:T(8,128)(2,1)S(1)} %collective-permute-done.8.refs_1_, ...), custom_call_target="tpu_custom_call" | custom-call | flops 5000000000 | bytes 4000000 | tf_op jit(solution)/shard_map/column_attention/pallas_call | solution.py:386
  36.5 0.1 collective-permute-start.9
  36.5 2.0 %collective-permute-start.10 = (bf16[10,1024]{1,0:T(8,128)(2,1)S(1)}, bf16[10,1024]{1,0:T(8,128)(2,1)S(1)}, u32[]{:S(2)}, u32[]{:S(2)}) collective-permute-start(bf16[10,1024]{1,0:T(8,128)(2,1)S(1)} %bitcast.17), channel_id=1, source_target_pairs={{0,25},{1,24},{2,27},{3,26},{4,29},{5,28},{6,31},{7,30},{8,17},{9,... | collective-permute-start | bytes 61448 | tf_op jit(solution)/shard_map/ppermute | solution.py:601
  38.6 0.3 collective-permute-start.11
  38.8 1.2 %left_mix.1 = (bf16[1024,1280]{1,0:T(8,128)(2,1)S(1)}, f32[320,1280]{1,0:T(8,128)S(1)}) custom-call(s32[1]{0:T(128)} %bitcast.idx, bf16[320,32]{1,0:T(8,128)(2,1)S(1)} %get-tuple-element.49.left, bf16[32,4096]{1,0:T(8,128)(2,1)S(1)} %reshape.22.factors, s32[32,320]{1,0:T(8,128)S(1)} %copy-done.6), custom_call_target="tpu_custom_call" | custom-call | flops 2000000000 | bytes 4000000 | tf_op jit(solution)/shard_map/left_mix/pallas_call | solution.py:447
  40.1 0.8 %collective-permute-done.9 = bf16[10,1024]{1,0:T(8,128)(2,1)S(1)} collective-permute-done((bf16[10,1024]{1,0:T(8,128)(2,1)S(1)}, bf16[10,1024]{1,0:T(8,128)(2,1)S(1)}, u32[]{:S(2)}, u32[]{:S(2)}) %collective-permute-start.9) | collective-permute-done | bytes 20512 | tf_op jit(solution)/shard_map/ppermute | solution.py:601
  40.9 0.9 %collective-permute-done.10 = bf16[10,1024]{1,0:T(8,128)(2,1)S(1)} collective-permute-done((bf16[10,1024]{1,0:T(8,128)(2,1)S(1)}, bf16[10,1024]{1,0:T(8,128)(2,1)S(1)}, u32[]{:S(2)}, u32[]{:S(2)}) %collective-permute-start.10) | collective-permute-done | bytes 20512 | tf_op jit(solution)/shard_map/ppermute | solution.py:601
  41.8 0.5 collective-permute-done.11
  42.3 3.1 %collective-permute-start.12 = (bf16[40,1024]{1,0:T(8,128)(2,1)S(1)}, bf16[40,1024]{1,0:T(8,128)(2,1)S(1)}, u32[]{:S(2)}, u32[]{:S(2)}) collective-permute-start(bf16[40,1024]{1,0:T(8,128)(2,1)S(1)} %pad_maximum_fusion.1.refs_0_), channel_id=1, source_target_pairs={{0,7},{1,6},{2,5},{3,4},{4,3},{5,2},{6,1},{7,0},{8,15},{9,14},{10,... | collective-permute-start | bytes 245768 | tf_op jit(solution)/shard_map/ppermute | solution.py:601
  45.4 0.8 %collective-permute-start.14 = (bf16[40,1024]{1,0:T(8,128)(2,1)S(1)}, bf16[40,1024]{1,0:T(8,128)(2,1)S(1)}, u32[]{:S(2)}, u32[]{:S(2)}) collective-permute-start(bf16[40,1024]{1,0:T(8,128)(2,1)S(1)} %pad_maximum_fusion.1.refs_0_), channel_id=1, source_target_pairs={{0,5},{1,4},{2,7},{3,6},{4,1},{5,0},{6,3},{7,2},{8,13},{9,12},{10,... | collective-permute-start | bytes 245768 | tf_op jit(solution)/shard_map/ppermute | solution.py:601
  46.2 2.1 %collective-permute-done.12 = bf16[40,1024]{1,0:T(8,128)(2,1)S(1)} collective-permute-done((bf16[40,1024]{1,0:T(8,128)(2,1)S(1)}, bf16[40,1024]{1,0:T(8,128)(2,1)S(1)}, u32[]{:S(2)}, u32[]{:S(2)}) %collective-permute-start.12) | collective-permute-done | bytes 81952 | tf_op jit(solution)/shard_map/ppermute | solution.py:601
  48.2 1.9 %collective-permute-done.13 = bf16[40,1024]{1,0:T(8,128)(2,1)S(1)} collective-permute-done((bf16[40,1024]{1,0:T(8,128)(2,1)S(1)}, bf16[40,1024]{1,0:T(8,128)(2,1)S(1)}, u32[]{:S(2)}, u32[]{:S(2)}) %collective-permute-start.13) | collective-permute-done | bytes 81952 | tf_op jit(solution)/shard_map/ppermute | solution.py:601
  50.2 0.2 collective-permute-start.16
  50.3 0.4 collective-permute-start.15
  50.7 1.1 %collective-permute-done.15.refs_2_ = bf16[40,1024]{1,0:T(8,128)(2,1)S(1)} collective-permute-done((bf16[40,1024]{1,0:T(8,128)(2,1)S(1)}, bf16[40,1024]{1,0:T(8,128)(2,1)S(1)}, u32[]{:S(2)}, u32[]{:S(2)}) %collective-permute-start.15) | collective-permute-done | bytes 81952 | tf_op jit(solution)/shard_map/ppermute | solution.py:601
  51.9 3.9 %pair_update.1 = bf16[10,320,128]{2,1,0:T(8,128)(2,1)} custom-call(s32[1]{0:T(128)} %bitcast.idx, bf16[40,1024]{1,0:T(8,128)(2,1)S(1)} %pad_maximum_fusion.1.refs_0_, bf16[120,1024]{1,0:T(8,128)(2,1)S(1)} %constant_dynamic-update-slice_fusion.2.refs_1_, bf16[40,1024]{1,0:T(8,128)(2,1)S(1)} %collective-permute-done.15.refs_2_, ...), custom_call_target="tpu_custom_call" | custom-call | flops 4000000000 | bytes 4000000 | tf_op jit(solution)/shard_map/pair_update/pallas_call | solution.py:543
  (41 shorter events, 0.2 us)
Async XLA Ops:
  0.6 13.4 %collective-permute-start.3 = (bf16[1,320,256]{2,1,0:T(8,128)(2,1)}, bf16[1,320,256]{2,1,0:T(8,128)(2,1)S(1)}, u32[]{:S(2)}, u32[]{:S(2)}) collective-permute-start(bf16[1,320,256]{2,1,0:T(8,128)(2,1)} %param.23), channel_id=1, source_target_pairs={{0,6},{1,7},{2,4},{3,5},{4,2},{5,3},{6,0},{7,1},{8,14},{9,15},{10,... | collective-permute-start | bytes 491528 | tf_op jit(solution)/shard_map/ppermute | solution.py:601
  4.6 9.5 %collective-permute-start.2 = (bf16[1,320,256]{2,1,0:T(8,128)(2,1)}, bf16[1,320,256]{2,1,0:T(8,128)(2,1)S(1)}, u32[]{:S(2)}, u32[]{:S(2)}) collective-permute-start(bf16[1,320,256]{2,1,0:T(8,128)(2,1)} %param.23), channel_id=1, source_target_pairs={{0,4},{1,5},{2,6},{3,7},{4,0},{5,1},{6,2},{7,3},{8,12},{9,13},{10,... | collective-permute-start | bytes 491528 | tf_op jit(solution)/shard_map/ppermute | solution.py:601
  5.1 9.0 %collective-permute-start.1 = (bf16[1,320,256]{2,1,0:T(8,128)(2,1)}, bf16[1,320,256]{2,1,0:T(8,128)(2,1)S(1)}, u32[]{:S(2)}, u32[]{:S(2)}) collective-permute-start(bf16[1,320,256]{2,1,0:T(8,128)(2,1)} %param.23), channel_id=1, source_target_pairs={{0,2},{1,3},{2,0},{3,1},{4,6},{5,7},{6,4},{7,5},{8,10},{9,11},{10,... | collective-permute-start | bytes 491528 | tf_op jit(solution)/shard_map/ppermute | solution.py:601
  5.2 7.3 %copy-start.14 = (bf16[256,4,256]{2,1,0:T(4,128)(2,1)S(1)}, bf16[256,4,256]{2,1,0:T(4,128)(2,1)}, u32[]{:S(2)}) copy-start(bf16[256,4,256]{2,1,0:T(4,128)(2,1)} %param.32) | copy-start | bytes 1572868
  5.2 8.9 %copy-start.17 = (bf16[1,320,256]{2,1,0:T(8,128)(2,1)S(1)}, bf16[1,320,256]{2,1,0:T(8,128)(2,1)}, u32[]{:S(2)}) copy-start(bf16[1,320,256]{2,1,0:T(8,128)(2,1)} %param.23) | copy-start | bytes 491524
  8.6 7.8 %copy-start.8 = (f32[256]{0:T(256)S(1)}, f32[256]{0:T(256)}, u32[]{:S(2)}) copy-start(f32[256]{0:T(256)} %param.31) | copy-start | bytes 3076
  8.6 5.4 %collective-permute-start = (bf16[10,8,320]{2,1,0:T(8,128)(2,1)}, bf16[10,8,320]{2,1,0:T(8,128)(2,1)S(1)}, u32[]{:S(2)}, u32[]{:S(2)}) collective-permute-start(bf16[10,8,320]{2,1,0:T(8,128)(2,1)} %get-tuple-element.32), channel_id=1, source_target_pairs={{0,16},{1,17},{2,18},{3,19},{4,20},{5,21},{6,22},{7,23},{8,24},{9,... | collective-permute-start | bytes 153608 | tf_op jit(solution)/shard_map/ppermute | solution.py:601
  14.2 2.2 %collective-permute-start.5 = (bf16[4,320,256]{2,1,0:T(8,128)(2,1)S(1)}, bf16[4,320,256]{2,1,0:T(8,128)(2,1)S(1)}, u32[]{:S(2)}, u32[]{:S(2)}) collective-permute-start(bf16[4,320,256]{2,1,0:T(8,128)(2,1)S(1)} %pad_maximum_fusion.refs_0_), channel_id=1, source_target_pairs={{0,1},{1,0},{2,3},{3,2},{4,5},{5,4},{6,7},{7,6},{8,9},{9,8},{10,11... | collective-permute-start | bytes 1966088 | tf_op jit(solution)/shard_map/ppermute | solution.py:601
  14.3 5.9 %collective-permute-start.4 = (bf16[20,8,320]{2,1,0:T(8,128)(2,1)S(1)}, bf16[20,8,320]{2,1,0:T(8,128)(2,1)S(1)}, u32[]{:S(2)}, u32[]{:S(2)}) collective-permute-start(bf16[20,8,320]{2,1,0:T(8,128)(2,1)S(1)} %constant_dynamic-update-slice_fusion.refs_0_), channel_id=1, source_target_pairs={{0,8},{1,9},{2,10},{3,11},{4,12},{5,13},{6,14},{7,15},{8,0},{9,1},... | collective-permute-start | bytes 307208 | tf_op jit(solution)/shard_map/ppermute | solution.py:601
  16.4 3.8 %copy-start.2 = (bf16[256,256]{1,0:T(8,128)(2,1)S(1)}, bf16[256,256]{1,0:T(8,128)(2,1)}, u32[]{:S(2)}) copy-start(bf16[256,256]{1,0:T(8,128)(2,1)} %refs_9_.2) | copy-start | bytes 393220
  16.4 3.8 %copy-start.6 = (s32[32,320]{1,0:T(8,128)S(1)}, s32[32,320]{1,0:T(8,128)}, u32[]{:S(2)}) copy-start(s32[32,320]{1,0:T(8,128)} %validity.1) | copy-start | bytes 122884
  16.4 3.8 %copy-start.7 = (s32[320]{0:T(512)S(1)}, s32[320]{0:T(512)}, u32[]{:S(2)}) copy-start(s32[320]{0:T(512)} %refs_8_.3) | copy-start | bytes 3844
  20.2 7.9 %copy-start.15 = (bf16[256,4,256]{2,1,0:T(4,128)(2,1)S(1)}, bf16[256,4,256]{2,1,0:T(4,128)(2,1)}, u32[]{:S(2)}) copy-start(bf16[256,4,256]{2,1,0:T(4,128)(2,1)} %param.35) | copy-start | bytes 1572868
  20.2 8.0 %copy-start.18 = (bf16[256,64]{0,1:T(8,128)(2,1)S(1)}, bf16[256,64]{0,1:T(8,128)(2,1)}, u32[]{:S(2)}) copy-start(bf16[256,64]{0,1:T(8,128)(2,1)} %param.41) | copy-start | bytes 98308
  20.2 8.1 %copy-start.16 = (bf16[1024,128]{1,0:T(8,128)(2,1)S(1)}, bf16[1024,128]{1,0:T(8,128)(2,1)}, u32[]{:S(2)}) copy-start(bf16[1024,128]{1,0:T(8,128)(2,1)} %param.42) | copy-start | bytes 786436
  23.1 9.0 %copy-start = (bf16[256,1024]{1,0:T(8,128)(2,1)S(1)}, bf16[256,1024]{1,0:T(8,128)(2,1)}, u32[]{:S(2)}) copy-start(bf16[256,1024]{1,0:T(8,128)(2,1)} %refs_10_.1) | copy-start | bytes 1572868
  23.1 9.0 %copy-start.1 = (bf16[1024,256]{1,0:T(8,128)(2,1)S(1)}, bf16[1024,256]{1,0:T(8,128)(2,1)}, u32[]{:S(2)}) copy-start(bf16[1024,256]{1,0:T(8,128)(2,1)} %refs_11_.1) | copy-start | bytes 1572868
  23.1 9.0 %copy-start.3 = (bf16[256,256]{1,0:T(8,128)(2,1)S(1)}, bf16[256,256]{1,0:T(8,128)(2,1)}, u32[]{:S(2)}) copy-start(bf16[256,256]{1,0:T(8,128)(2,1)} %refs_8_.4) | copy-start | bytes 393220
  23.1 9.0 %copy-start.9 = (f32[256]{0:T(256)S(1)}, f32[256]{0:T(256)}, u32[]{:S(2)}) copy-start(f32[256]{0:T(256)} %param.34) | copy-start | bytes 3076
  23.2 9.0 %copy-start.10 = (f32[256]{0:T(256)S(1)}, f32[256]{0:T(256)}, u32[]{:S(2)}) copy-start(f32[256]{0:T(256)} %param.37) | copy-start | bytes 3076
  23.2 9.0 %copy-start.11 = (f32[256]{0:T(256)S(1)}, f32[256]{0:T(256)}, u32[]{:S(2)}) copy-start(f32[256]{0:T(256)} %param.40) | copy-start | bytes 3076
  23.2 5.6 %collective-permute-start.6 = (bf16[10,8,256]{2,1,0:T(8,128)(2,1)S(1)}, bf16[10,8,256]{2,1,0:T(8,128)(2,1)S(1)}, u32[]{:S(2)}, u32[]{:S(2)}) collective-permute-start(bf16[10,8,256]{2,1,0:T(8,128)(2,1)S(1)} %get-tuple-element.42), channel_id=1, source_target_pairs={{0,16},{1,17},{2,18},{3,19},{4,20},{5,21},{6,22},{7,23},{8,24},{9,... | collective-permute-start | bytes 122888 | tf_op jit(solution)/shard_map/ppermute | solution.py:601
  26.3 5.8 %collective-permute-start.7 = (bf16[10,8,256]{2,1,0:T(8,128)(2,1)S(1)}, bf16[10,8,256]{2,1,0:T(8,128)(2,1)S(1)}, u32[]{:S(2)}, u32[]{:S(2)}) collective-permute-start(bf16[10,8,256]{2,1,0:T(8,128)(2,1)S(1)} %get-tuple-element.43), channel_id=1, source_target_pairs={{0,24},{1,25},{2,26},{3,27},{4,28},{5,29},{6,30},{7,31},{8,16},{9,... | collective-permute-start | bytes 122888 | tf_op jit(solution)/shard_map/ppermute | solution.py:601
  27.6 4.5 %collective-permute-start.8 = (bf16[10,8,256]{2,1,0:T(8,128)(2,1)S(1)}, bf16[10,8,256]{2,1,0:T(8,128)(2,1)S(1)}, u32[]{:S(2)}, u32[]{:S(2)}) collective-permute-start(bf16[10,8,256]{2,1,0:T(8,128)(2,1)S(1)} %get-tuple-element.44), channel_id=1, source_target_pairs={{0,8},{1,9},{2,10},{3,11},{4,12},{5,13},{6,14},{7,15},{8,0},{9,1},... | collective-permute-start | bytes 122888 | tf_op jit(solution)/shard_map/ppermute | solution.py:601
  36.5 4.4 %collective-permute-start.9 = (bf16[10,1024]{1,0:T(8,128)(2,1)S(1)}, bf16[10,1024]{1,0:T(8,128)(2,1)S(1)}, u32[]{:S(2)}, u32[]{:S(2)}) collective-permute-start(bf16[10,1024]{1,0:T(8,128)(2,1)S(1)} %bitcast.16), channel_id=1, source_target_pairs={{0,17},{1,16},{2,19},{3,18},{4,21},{5,20},{6,23},{7,22},{8,25},{9,... | collective-permute-start | bytes 61448 | tf_op jit(solution)/shard_map/ppermute | solution.py:601
  36.5 5.2 %collective-permute-start.10 = (bf16[10,1024]{1,0:T(8,128)(2,1)S(1)}, bf16[10,1024]{1,0:T(8,128)(2,1)S(1)}, u32[]{:S(2)}, u32[]{:S(2)}) collective-permute-start(bf16[10,1024]{1,0:T(8,128)(2,1)S(1)} %bitcast.17), channel_id=1, source_target_pairs={{0,25},{1,24},{2,27},{3,26},{4,29},{5,28},{6,31},{7,30},{8,17},{9,... | collective-permute-start | bytes 61448 | tf_op jit(solution)/shard_map/ppermute | solution.py:601
  38.6 3.7 %collective-permute-start.11 = (bf16[10,1024]{1,0:T(8,128)(2,1)S(1)}, bf16[10,1024]{1,0:T(8,128)(2,1)S(1)}, u32[]{:S(2)}, u32[]{:S(2)}) collective-permute-start(bf16[10,1024]{1,0:T(8,128)(2,1)S(1)} %bitcast.18), channel_id=1, source_target_pairs={{0,9},{1,8},{2,11},{3,10},{4,13},{5,12},{6,15},{7,14},{8,1},{9,0},... | collective-permute-start | bytes 61448 | tf_op jit(solution)/shard_map/ppermute | solution.py:601
  38.8 13.0 %copy-start.4 = (bf16[128,512]{1,0:T(8,128)(2,1)S(1)}, bf16[128,512]{1,0:T(8,128)(2,1)}, u32[]{:S(2)}) copy-start(bf16[128,512]{1,0:T(8,128)(2,1)} %refs_8_.5) | copy-start | bytes 393220
  38.8 13.0 %copy-start.5 = (bf16[512,128]{1,0:T(8,128)(2,1)S(1)}, bf16[512,128]{1,0:T(8,128)(2,1)}, u32[]{:S(2)}) copy-start(bf16[512,128]{1,0:T(8,128)(2,1)} %refs_9_.3) | copy-start | bytes 393220
  38.8 13.0 %copy-start.12 = (f32[128]{0:T(128)S(1)}, f32[128]{0:T(128)}, u32[]{:S(2)}) copy-start(f32[128]{0:T(128)} %param.43) | copy-start | bytes 1540
  38.8 13.0 %copy-start.13 = (f32[10,320,128]{2,1,0:T(8,128)S(1)}, f32[10,320,128]{2,1,0:T(8,128)}, u32[]{:S(2)}) copy-start(f32[10,320,128]{2,1,0:T(8,128)} %get-tuple-element.61.refs_6_) | copy-start | bytes 4915204
  42.3 5.9 %collective-permute-start.12 = (bf16[40,1024]{1,0:T(8,128)(2,1)S(1)}, bf16[40,1024]{1,0:T(8,128)(2,1)S(1)}, u32[]{:S(2)}, u32[]{:S(2)}) collective-permute-start(bf16[40,1024]{1,0:T(8,128)(2,1)S(1)} %pad_maximum_fusion.1.refs_0_), channel_id=1, source_target_pairs={{0,7},{1,6},{2,5},{3,4},{4,3},{5,2},{6,1},{7,0},{8,15},{9,14},{10,... | collective-permute-start | bytes 245768 | tf_op jit(solution)/shard_map/ppermute | solution.py:601
  45.4 4.7 %collective-permute-start.13 = (bf16[40,1024]{1,0:T(8,128)(2,1)S(1)}, bf16[40,1024]{1,0:T(8,128)(2,1)S(1)}, u32[]{:S(2)}, u32[]{:S(2)}) collective-permute-start(bf16[40,1024]{1,0:T(8,128)(2,1)S(1)} %pad_maximum_fusion.1.refs_0_), channel_id=1, source_target_pairs={{0,3},{1,2},{2,1},{3,0},{4,7},{5,6},{6,5},{7,4},{8,11},{9,10},{10,... | collective-permute-start | bytes 245768 | tf_op jit(solution)/shard_map/ppermute | solution.py:601
  45.4 4.7 %collective-permute-start.14 = (bf16[40,1024]{1,0:T(8,128)(2,1)S(1)}, bf16[40,1024]{1,0:T(8,128)(2,1)S(1)}, u32[]{:S(2)}, u32[]{:S(2)}) collective-permute-start(bf16[40,1024]{1,0:T(8,128)(2,1)S(1)} %pad_maximum_fusion.1.refs_0_), channel_id=1, source_target_pairs={{0,5},{1,4},{2,7},{3,6},{4,1},{5,0},{6,3},{7,2},{8,13},{9,12},{10,... | collective-permute-start | bytes 245768 | tf_op jit(solution)/shard_map/ppermute | solution.py:601
  50.2 1.7 %collective-permute-start.16 = (bf16[120,1024]{1,0:T(8,128)(2,1)S(1)}, bf16[120,1024]{1,0:T(8,128)(2,1)S(1)}, u32[]{:S(2)}, u32[]{:S(2)}) collective-permute-start(bf16[120,1024]{1,0:T(8,128)(2,1)S(1)} %constant_dynamic-update-slice_fusion.2.refs_1_), channel_id=1, source_target_pairs={{0,1},{1,0},{2,3},{3,2},{4,5},{5,4},{6,7},{7,6},{8,9},{9,8},{10,11... | collective-permute-start | bytes 737288 | tf_op jit(solution)/shard_map/ppermute | solution.py:601
  50.3 1.5 %collective-permute-start.15 = (bf16[40,1024]{1,0:T(8,128)(2,1)S(1)}, bf16[40,1024]{1,0:T(8,128)(2,1)S(1)}, u32[]{:S(2)}, u32[]{:S(2)}) collective-permute-start(bf16[40,1024]{1,0:T(8,128)(2,1)S(1)} %pad_maximum_fusion.1.refs_0_), channel_id=1, source_target_pairs={{0,1},{1,0},{2,3},{3,2},{4,5},{5,4},{6,7},{7,6},{8,9},{9,8},{10,11... | collective-permute-start | bytes 245768 | tf_op jit(solution)/shard_map/ppermute | solution.py:601

commit v8 on v7

--- a/solution.py
+++ b/solution.py
@@ -132,6 +132,14 @@
     )(idx, chain, pair, chain, table, gain[None, :], factors.T)
 
 
+def core_of(place, far):
+    core, bit = 0, 0
+    while far >> (bit + 1):
+        core = core ^ ((place >> bit) & 1)
+        bit += 1
+    return core
+
+
 def project_kernel(idx, *refs, sub, far, rows, length, width):
     row_refs, refs = refs[:2], refs[2:]
     gain, entry, keys, values, query, gate, own_rows, own_normed = refs
@@ -142,12 +150,12 @@
 
     r = iota((own, length), 0)
     block = div_const(r, rows, own)
-    residue = ((z ^ block) * sub + p) * rows + r - block * rows
+    residue = ((z ^ block) * sub + (p ^ core_of(block, far))) * rows + r - block * rows
     pick = one_hot(residue == iota((own, length), 1))
 
     step = min(length, 320)
     for k in range(sub):
-        source, place = row_refs[k % 2], k // 2
+        source, place = row_refs[k % 2 ^ (k > 1)], k // 2
 
         def project(start, k=k, source=source, place=place):
             x = source[place, pl.ds(start, step), :]
@@ -604,18 +612,18 @@
     rows = couple_embedding.shape[0]
     depth = alignment_validity.shape[0]
 
-    near = [swap(alignment_embedding, k) for k in range(2, SUB, 2)]
+    near = [swap(alignment_embedding, k ^ 1) for k in range(2, SUB, 2)]
     pair_one, bias = pair_call(
         idx, amino_strand, couple_embedding, separation_embedding, couple_shift_scaling, couple_shift_factors
     )
     entry = horizontal_entry_factors.reshape(width, 4 * width)
     order, distance = [0], far // 2
-    mine, theirs = bias, swap(bias, SUB * distance)
+    mine, theirs = bias, swap(bias, SUB * distance ^ 1)
     order += [b ^ distance for b in order]
     while distance > 1:
         distance //= 2
         mine = jnp.concatenate([mine, theirs], 0)
-        theirs = swap(mine, SUB * distance)
+        theirs = swap(mine, SUB * distance ^ 1)
         order += [b ^ distance for b in order]
     near = jnp.concatenate([alignment_embedding, *near], 0)
     entry, mine, near = lax.optimization_barrier((entry, mine, near))
@@ -624,7 +632,7 @@
     sent = row_call(
         idx, [mine, theirs], order, projected, alignment_validity, amino_validity, horizontal_exit_factors
     )
-    pieces = [swap(sent[k], SUB * k) for k in [*range(2, far), 1]]
+    pieces = [swap(sent[k], SUB * k ^ core_of(k, far)) for k in [*range(2, far), 1]]
     pieces = lax.optimization_barrier(pieces)
     pieces = [sent[0]] + [part for _, part in sorted(zip([*range(2, far), 1], pieces), key=lambda pair: pair[0])]
     updated, left, right = column_call(
@@ -649,10 +657,11 @@
     parts = [right] + [part for _, part in sorted(zip([*range(2, far), 1], parts), key=lambda pair: pair[0])]
     column = jnp.concatenate(parts, 0)
     near = [swap(column, k ^ 1) for k in [6, 2, 4]]
-    near = lax.optimization_barrier(near)
+    beside = swap(column, 1)
+    *near, beside = lax.optimization_barrier((*near, beside))
     near = [part for _, part in sorted(zip([6, 2, 4], near), key=lambda pair: pair[0])]
     near = [column, jnp.concatenate(near, 0)]
-    across = [swap(a, 1) for a in near]
+    across = [beside, swap(near[1], 1)]
     updated_pairs = finish_call(
         idx,
         near,

time: 56.2 us -> 55.9 us (level)
  starting transfers between devices: 21.3 us -> 18.6 us
  waiting for transfers between devices: 14 us -> 16.6 us
    ppermute x17, starting transfers between devices: 21.3 us -> 18.6 us  [swap(): return lax.ppermute(x, 'dap', [(d, d ^ distance) for d in range(devices)])]
    ppermute x17, waiting for transfers between devices: 14 us -> 16.6 us  [swap(): return lax.ppermute(x, 'dap', [(d, d ^ distance) for d in range(devices)])]
  transfers between devices with their start and end apart: 17 -> 17, of which waited for: 11 -> 10; matrix products, arithmetic and copies ran while one was open for 2% -> 2% of each run, Pallas kernels for 12% -> 12%
where the time goes in v8:
time: 55.9 us; the launch traced here: 55.7 us
  starting transfers between devices  18.6 us (33%)
  Pallas kernels  17.9 us (32%)
  waiting for transfers between devices  16.6 us (30%)
  local copies, waits for them, and re-layouts  1.41 us (3%)
  between operations  1.09 us (2%)
    ppermute x17, starting transfers between devices, swap(): return lax.ppermute(x, 'dap', [(d, d ^ distance) for d in range(devices)])  18.6 us
    ppermute x17, waiting for transfers between devices, swap(): return lax.ppermute(x, 'dap', [(d, d ^ distance) for d in range(devices)])  16.6 us
    pallas_call x1, Pallas kernels, column_call(): pl.pallas_call(functools.partial(column_kernel, sub=sub, far=far, rows=ro...  4.26 us
    pallas_call x1, Pallas kernels, finish_call(): pl.pallas_call(functools.partial(finish_kernel, pieces=len(near), sub=sub...  3.93 us
    pallas_call x1, Pallas kernels, pair_call(): pl.pallas_call(functools.partial(pair_kernel, rows=rows, length=length, b...  3.37 us
    pallas_call x1, Pallas kernels, row_call(): pl.pallas_call(functools.partial(row_kernel, order=order, sub=sub, far=fa...  2.87 us
    pallas_call x1, Pallas kernels, project_call(): pl.pallas_call(functools.partial(project_kernel, sub=sub, far=far, rows=r...  2.28 us
    unnamed x44, local copies, waits for them, and re-layouts  1.28 us
  transfers between devices with their start and end apart: 17, of which 10 were waited for; matrix products, arithmetic and copies ran while one was open for 2% of the time, Pallas kernels for 12%

profile of v8, /device:TPU:0, one launch (start us, length us, event | category | flops | bytes accessed | tf_op | source)
XLA Modules:
  0.0 55.7 jit_solution(10474208544353856499)
XLA Ops:
  0.6 3.4 %collective-permute-start.3 = (bf16[1,320,256]{2,1,0:T(8,128)(2,1)}, bf16[1,320,256]{2,1,0:T(8,128)(2,1)S(1)}, u32[]{:S(2)}, u32[]{:S(2)}) collective-permute-start(bf16[1,320,256]{2,1,0:T(8,128)(2,1)} %param.23), channel_id=1, source_target_pairs={{0,7},{1,6},{2,5},{3,4},{4,3},{5,2},{6,1},{7,0},{8,15},{9,14},{10,... | collective-permute-start | bytes 491528 | tf_op jit(solution)/shard_map/ppermute | solution.py:609
  4.0 0.8 %collective-permute-start.2 = (bf16[1,320,256]{2,1,0:T(8,128)(2,1)}, bf16[1,320,256]{2,1,0:T(8,128)(2,1)S(1)}, u32[]{:S(2)}, u32[]{:S(2)}) collective-permute-start(bf16[1,320,256]{2,1,0:T(8,128)(2,1)} %param.23), channel_id=1, source_target_pairs={{0,5},{1,4},{2,7},{3,6},{4,1},{5,0},{6,3},{7,2},{8,13},{9,12},{10,... | collective-permute-start | bytes 491528 | tf_op jit(solution)/shard_map/ppermute | solution.py:609
  4.8 0.1 collective-permute-start.1
  5.0 3.4 %pair_bias.1 = (f32[10,320,128]{2,1,0:T(8,128)}, bf16[10,8,320]{2,1,0:T(8,128)(2,1)}) custom-call(s32[1]{0:T(128)} %bitcast.idx, s32[320]{0:T(512)} %chain_row.1, bf16[10,320,128]{2,1,0:T(8,128)(2,1)} %pair.1, s32[320]{0:T(512)} %chain_row.1, f32[66,128]{1,0:T(8,128)} %table.1, f32[1,128]{1,0:T(1,128)} %bitcast.28, bf16[8,128]{1,0:T(8,128)(2,1)} %bitcast.27), custom_call_target="tpu_custom_call" | custom-call | flops 4000000000 | bytes 4000000 | tf_op jit(solution)/shard_map/pair_bias/pallas_call | solution.py:108
  8.3 2.8 %collective-permute-start = (bf16[10,8,320]{2,1,0:T(8,128)(2,1)}, bf16[10,8,320]{2,1,0:T(8,128)(2,1)S(1)}, u32[]{:S(2)}, u32[]{:S(2)}) collective-permute-start(bf16[10,8,320]{2,1,0:T(8,128)(2,1)} %get-tuple-element.33), channel_id=1, source_target_pairs={{0,17},{1,16},{2,19},{3,18},{4,21},{5,20},{6,23},{7,22},{8,25},{9,... | collective-permute-start | bytes 153608 | tf_op jit(solution)/shard_map/ppermute | solution.py:609
  11.1 0.9 %constant_dynamic-update-slice_fusion.1 = bf16[20,8,320]{2,1,0:T(8,128)(2,1)S(1)} fusion(bf16[10,8,320]{2,1,0:T(8,128)(2,1)} %get-tuple-element.33), kind=kLoop, calls=%fused_computation.3 | loop fusion | bytes 112640
  12.0 0.1 copy.26
  12.1 3.0 %collective-permute-done = bf16[10,8,320]{2,1,0:T(8,128)(2,1)S(1)} collective-permute-done((bf16[10,8,320]{2,1,0:T(8,128)(2,1)}, bf16[10,8,320]{2,1,0:T(8,128)(2,1)S(1)}, u32[]{:S(2)}, u32[]{:S(2)}) %collective-permute-start) | collective-permute-done | bytes 51232 | tf_op jit(solution)/shard_map/ppermute | solution.py:609
  15.1 0.0 collective-permute-done.3
  15.1 0.1 pad_maximum_fusion.refs_0_
  15.2 0.2 collective-permute-start.5
  15.4 0.8 %collective-permute-start.4 = (bf16[20,8,320]{2,1,0:T(8,128)(2,1)S(1)}, bf16[20,8,320]{2,1,0:T(8,128)(2,1)S(1)}, u32[]{:S(2)}, u32[]{:S(2)}) collective-permute-start(bf16[20,8,320]{2,1,0:T(8,128)(2,1)S(1)} %constant_dynamic-update-slice_fusion.refs_0_), channel_id=1, source_target_pairs={{0,9},{1,8},{2,11},{3,10},{4,13},{5,12},{6,15},{7,14},{8,1},{9,0},... | collective-permute-start | bytes 307208 | tf_op jit(solution)/shard_map/ppermute | solution.py:609
  16.2 1.2 %collective-permute-done.5.refs_1_ = bf16[4,320,256]{2,1,0:T(8,128)(2,1)S(1)} collective-permute-done((bf16[4,320,256]{2,1,0:T(8,128)(2,1)S(1)}, bf16[4,320,256]{2,1,0:T(8,128)(2,1)S(1)}, u32[]{:S(2)}, u32[]{:S(2)}) %collective-permute-start.5) | collective-permute-done | bytes 655392 | tf_op jit(solution)/shard_map/ppermute | solution.py:609
  17.4 2.3 %row_project.1 = (bf16[8,320,256]{2,1,0:T(8,128)(2,1)S(1)}, bf16[8,320,256]{2,1,0:T(8,128)(2,1)S(1)}, f32[320,256]{1,0:T(8,128)S(1)}, f32[320,256]{1,0:T(8,128)S(1)}, f32[320,256]{1,0:T(8,128)S(1)}) custom-call(s32[1]{0:T(128)} %bitcast.idx, bf16[4,320,256]{2,1,0:T(8,128)(2,1)S(1)} %pad_maximum_fusion.refs_0_, ...), custom_call_target="tpu_custom_call" | custom-call | flops 3000000000 | bytes 4000000 | tf_op jit(solution)/shard_map/row_project/pallas_call | solution.py:198
  19.7 0.9 %collective-permute-done.4.refs_1_ = bf16[20,8,320]{2,1,0:T(8,128)(2,1)S(1)} collective-permute-done((bf16[20,8,320]{2,1,0:T(8,128)(2,1)S(1)}, bf16[20,8,320]{2,1,0:T(8,128)(2,1)S(1)}, u32[]{:S(2)}, u32[]{:S(2)}) %collective-permute-start.4) | collective-permute-done | bytes 102432 | tf_op jit(solution)/shard_map/ppermute | solution.py:609
  20.6 0.0 copy-start.15
  20.6 0.0 copy-start.18
  20.6 0.0 copy-start.16
  20.6 2.9 %row_attention.1 = (bf16[10,8,256]{2,1,0:T(8,128)(2,1)S(1)}, bf16[10,8,256]{2,1,0:T(8,128)(2,1)S(1)}, bf16[10,8,256]{2,1,0:T(8,128)(2,1)S(1)}, bf16[10,8,256]{2,1,0:T(8,128)(2,1)S(1)}) custom-call(s32[1]{0:T(128)} %bitcast.idx, bf16[20,8,320]{2,1,0:T(8,128)(2,1)S(1)} %constant_dynamic-update-slice_fusion.refs_0_, ...), custom_call_target="tpu_custom_call" | custom-call | flops 4000000000 | bytes 4000000 | tf_op jit(solution)/shard_map/row_attention/pallas_call | solution.py:271
  23.5 0.0 copy-start
  23.5 0.0 copy-start.1
  23.5 0.0 copy-start.3
  23.5 0.0 copy-start.9
  23.5 0.0 copy-start.10
  23.6 0.0 copy-start.11
  23.6 2.2 %collective-permute-start.6 = (bf16[10,8,256]{2,1,0:T(8,128)(2,1)S(1)}, bf16[10,8,256]{2,1,0:T(8,128)(2,1)S(1)}, u32[]{:S(2)}, u32[]{:S(2)}) collective-permute-start(bf16[10,8,256]{2,1,0:T(8,128)(2,1)S(1)} %get-tuple-element.43), channel_id=1, source_target_pairs={{0,17},{1,16},{2,19},{3,18},{4,21},{5,20},{6,23},{7,22},{8,25},{9,... | collective-permute-start | bytes 122888 | tf_op jit(solution)/shard_map/ppermute | solution.py:609
  25.8 1.4 %collective-permute-start.7 = (bf16[10,8,256]{2,1,0:T(8,128)(2,1)S(1)}, bf16[10,8,256]{2,1,0:T(8,128)(2,1)S(1)}, u32[]{:S(2)}, u32[]{:S(2)}) collective-permute-start(bf16[10,8,256]{2,1,0:T(8,128)(2,1)S(1)} %get-tuple-element.44), channel_id=1, source_target_pairs={{0,24},{1,25},{2,26},{3,27},{4,28},{5,29},{6,30},{7,31},{8,16},{9,... | collective-permute-start | bytes 122888 | tf_op jit(solution)/shard_map/ppermute | solution.py:609
  27.1 0.2 collective-permute-start.8
  27.4 0.1 copy.27
  27.5 0.1 copy.25.refs_5_
  27.6 0.1 reshape.22.factors
  27.7 0.2 collective-permute-done.6.refs_2_
  28.0 3.8 %collective-permute-done.7.refs_3_ = bf16[10,8,256]{2,1,0:T(8,128)(2,1)S(1)} collective-permute-done((bf16[10,8,256]{2,1,0:T(8,128)(2,1)S(1)}, bf16[10,8,256]{2,1,0:T(8,128)(2,1)S(1)}, u32[]{:S(2)}, u32[]{:S(2)}) %collective-permute-start.7) | collective-permute-done | bytes 40992 | tf_op jit(solution)/shard_map/ppermute | solution.py:609
  31.8 4.3 %column_attention.1 = (bf16[10,32,256]{2,1,0:T(8,128)(2,1)}, bf16[320,32]{1,0:T(8,128)(2,1)S(1)}, bf16[1,10,1024]{2,1,0:T(8,128)(2,1)S(1)}) custom-call(s32[1]{0:T(128)} %bitcast.idx, bf16[10,8,256]{2,1,0:T(8,128)(2,1)S(1)} %get-tuple-element.42.refs_0_, bf16[10,8,256]{2,1,0:T(8,128)(2,1)S(1)} %collective-permute-done.8.refs_1_, ...), custom_call_target="tpu_custom_call" | custom-call | flops 5000000000 | bytes 4000000 | tf_op jit(solution)/shard_map/column_attention/pallas_call | solution.py:394
  36.1 1.4 %collective-permute-start.9 = (bf16[10,1024]{1,0:T(8,128)(2,1)S(1)}, bf16[10,1024]{1,0:T(8,128)(2,1)S(1)}, u32[]{:S(2)}, u32[]{:S(2)}) collective-permute-start(bf16[10,1024]{1,0:T(8,128)(2,1)S(1)} %bitcast.16), channel_id=1, source_target_pairs={{0,17},{1,16},{2,19},{3,18},{4,21},{5,20},{6,23},{7,22},{8,25},{9,... | collective-permute-start | bytes 61448 | tf_op jit(solution)/shard_map/ppermute | solution.py:609
  37.5 1.4 %collective-permute-start.10 = (bf16[10,1024]{1,0:T(8,128)(2,1)S(1)}, bf16[10,1024]{1,0:T(8,128)(2,1)S(1)}, u32[]{:S(2)}, u32[]{:S(2)}) collective-permute-start(bf16[10,1024]{1,0:T(8,128)(2,1)S(1)} %bitcast.17), channel_id=1, source_target_pairs={{0,25},{1,24},{2,27},{3,26},{4,29},{5,28},{6,31},{7,30},{8,17},{9,... | collective-permute-start | bytes 61448 | tf_op jit(solution)/shard_map/ppermute | solution.py:609
  38.9 0.2 collective-permute-start.11
  39.1 1.2 %left_mix.1 = (bf16[1024,1280]{1,0:T(8,128)(2,1)S(1)}, f32[320,1280]{1,0:T(8,128)S(1)}) custom-call(s32[1]{0:T(128)} %bitcast.idx, bf16[320,32]{1,0:T(8,128)(2,1)S(1)} %get-tuple-element.50.left, bf16[32,4096]{1,0:T(8,128)(2,1)S(1)} %reshape.22.factors, s32[32,320]{1,0:T(8,128)S(1)} %copy-done.6), custom_call_target="tpu_custom_call" | custom-call | flops 2000000000 | bytes 4000000 | tf_op jit(solution)/shard_map/left_mix/pallas_call | solution.py:455
  40.3 0.9 %collective-permute-done.9 = bf16[10,1024]{1,0:T(8,128)(2,1)S(1)} collective-permute-done((bf16[10,1024]{1,0:T(8,128)(2,1)S(1)}, bf16[10,1024]{1,0:T(8,128)(2,1)S(1)}, u32[]{:S(2)}, u32[]{:S(2)}) %collective-permute-start.9) | collective-permute-done | bytes 20512 | tf_op jit(solution)/shard_map/ppermute | solution.py:609
  41.2 1.5 %collective-permute-done.10 = bf16[10,1024]{1,0:T(8,128)(2,1)S(1)} collective-permute-done((bf16[10,1024]{1,0:T(8,128)(2,1)S(1)}, bf16[10,1024]{1,0:T(8,128)(2,1)S(1)}, u32[]{:S(2)}, u32[]{:S(2)}) %collective-permute-start.10) | collective-permute-done | bytes 20512 | tf_op jit(solution)/shard_map/ppermute | solution.py:609
  42.8 2.4 %collective-permute-start.12 = (bf16[40,1024]{1,0:T(8,128)(2,1)S(1)}, bf16[40,1024]{1,0:T(8,128)(2,1)S(1)}, u32[]{:S(2)}, u32[]{:S(2)}) collective-permute-start(bf16[40,1024]{1,0:T(8,128)(2,1)S(1)} %pad_maximum_fusion.1.refs_0_), channel_id=1, source_target_pairs={{0,7},{1,6},{2,5},{3,4},{4,3},{5,2},{6,1},{7,0},{8,15},{9,14},{10,... | collective-permute-start | bytes 245768 | tf_op jit(solution)/shard_map/ppermute | solution.py:609
  45.3 0.1 collective-permute-start.13
  45.4 0.9 %collective-permute-start.14 = (bf16[40,1024]{1,0:T(8,128)(2,1)S(1)}, bf16[40,1024]{1,0:T(8,128)(2,1)S(1)}, u32[]{:S(2)}, u32[]{:S(2)}) collective-permute-start(bf16[40,1024]{1,0:T(8,128)(2,1)S(1)} %pad_maximum_fusion.1.refs_0_), channel_id=1, source_target_pairs={{0,5},{1,4},{2,7},{3,6},{4,1},{5,0},{6,3},{7,2},{8,13},{9,12},{10,... | collective-permute-start | bytes 245768 | tf_op jit(solution)/shard_map/ppermute | solution.py:609
  46.3 1.7 %collective-permute-done.12 = bf16[40,1024]{1,0:T(8,128)(2,1)S(1)} collective-permute-done((bf16[40,1024]{1,0:T(8,128)(2,1)S(1)}, bf16[40,1024]{1,0:T(8,128)(2,1)S(1)}, u32[]{:S(2)}, u32[]{:S(2)}) %collective-permute-start.12) | collective-permute-done | bytes 81952 | tf_op jit(solution)/shard_map/ppermute | solution.py:609
  48.1 1.9 %collective-permute-done.13 = bf16[40,1024]{1,0:T(8,128)(2,1)S(1)} collective-permute-done((bf16[40,1024]{1,0:T(8,128)(2,1)S(1)}, bf16[40,1024]{1,0:T(8,128)(2,1)S(1)}, u32[]{:S(2)}, u32[]{:S(2)}) %collective-permute-start.13) | collective-permute-done | bytes 81952 | tf_op jit(solution)/shard_map/ppermute | solution.py:609
  50.0 0.2 collective-permute-start.16
  50.2 1.4 %collective-permute-done.16.refs_3_ = bf16[120,1024]{1,0:T(8,128)(2,1)S(1)} collective-permute-done((bf16[120,1024]{1,0:T(8,128)(2,1)S(1)}, bf16[120,1024]{1,0:T(8,128)(2,1)S(1)}, u32[]{:S(2)}, u32[]{:S(2)}) %collective-permute-start.16) | collective-permute-done | bytes 245792 | tf_op jit(solution)/shard_map/ppermute | solution.py:609
  51.6 3.9 %pair_update.1 = bf16[10,320,128]{2,1,0:T(8,128)(2,1)} custom-call(s32[1]{0:T(128)} %bitcast.idx, bf16[40,1024]{1,0:T(8,128)(2,1)S(1)} %pad_maximum_fusion.1.refs_0_, bf16[120,1024]{1,0:T(8,128)(2,1)S(1)} %constant_dynamic-update-slice_fusion.2.refs_1_, bf16[40,1024]{1,0:T(8,128)(2,1)S(1)} %collective-permute-done.15.refs_2_, ...), custom_call_target="tpu_custom_call" | custom-call | flops 4000000000 | bytes 4000000 | tf_op jit(solution)/shard_map/pair_update/pallas_call | solution.py:551
  (41 shorter events, 0.2 us)
Async XLA Ops:
  0.6 14.4 %collective-permute-start.3 = (bf16[1,320,256]{2,1,0:T(8,128)(2,1)}, bf16[1,320,256]{2,1,0:T(8,128)(2,1)S(1)}, u32[]{:S(2)}, u32[]{:S(2)}) collective-permute-start(bf16[1,320,256]{2,1,0:T(8,128)(2,1)} %param.23), channel_id=1, source_target_pairs={{0,7},{1,6},{2,5},{3,4},{4,3},{5,2},{6,1},{7,0},{8,15},{9,14},{10,... | collective-permute-start | bytes 491528 | tf_op jit(solution)/shard_map/ppermute | solution.py:609
  4.0 11.1 %collective-permute-start.2 = (bf16[1,320,256]{2,1,0:T(8,128)(2,1)}, bf16[1,320,256]{2,1,0:T(8,128)(2,1)S(1)}, u32[]{:S(2)}, u32[]{:S(2)}) collective-permute-start(bf16[1,320,256]{2,1,0:T(8,128)(2,1)} %param.23), channel_id=1, source_target_pairs={{0,5},{1,4},{2,7},{3,6},{4,1},{5,0},{6,3},{7,2},{8,13},{9,12},{10,... | collective-permute-start | bytes 491528 | tf_op jit(solution)/shard_map/ppermute | solution.py:609
  4.8 10.3 %collective-permute-start.1 = (bf16[1,320,256]{2,1,0:T(8,128)(2,1)}, bf16[1,320,256]{2,1,0:T(8,128)(2,1)S(1)}, u32[]{:S(2)}, u32[]{:S(2)}) collective-permute-start(bf16[1,320,256]{2,1,0:T(8,128)(2,1)} %param.23), channel_id=1, source_target_pairs={{0,3},{1,2},{2,1},{3,0},{4,7},{5,6},{6,5},{7,4},{8,11},{9,10},{10,... | collective-permute-start | bytes 491528 | tf_op jit(solution)/shard_map/ppermute | solution.py:609
  5.0 7.0 %copy-start.14 = (bf16[256,4,256]{2,1,0:T(4,128)(2,1)S(1)}, bf16[256,4,256]{2,1,0:T(4,128)(2,1)}, u32[]{:S(2)}) copy-start(bf16[256,4,256]{2,1,0:T(4,128)(2,1)} %param.32) | copy-start | bytes 1572868
  5.0 10.2 %copy-start.17 = (bf16[1,320,256]{2,1,0:T(8,128)(2,1)S(1)}, bf16[1,320,256]{2,1,0:T(8,128)(2,1)}, u32[]{:S(2)}) copy-start(bf16[1,320,256]{2,1,0:T(8,128)(2,1)} %param.23) | copy-start | bytes 491524
  8.3 9.0 %copy-start.8 = (f32[256]{0:T(256)S(1)}, f32[256]{0:T(256)}, u32[]{:S(2)}) copy-start(f32[256]{0:T(256)} %param.31) | copy-start | bytes 3076
  8.3 6.7 %collective-permute-start = (bf16[10,8,320]{2,1,0:T(8,128)(2,1)}, bf16[10,8,320]{2,1,0:T(8,128)(2,1)S(1)}, u32[]{:S(2)}, u32[]{:S(2)}) collective-permute-start(bf16[10,8,320]{2,1,0:T(8,128)(2,1)} %get-tuple-element.33), channel_id=1, source_target_pairs={{0,17},{1,16},{2,19},{3,18},{4,21},{5,20},{6,23},{7,22},{8,25},{9,... | collective-permute-start | bytes 153608 | tf_op jit(solution)/shard_map/ppermute | solution.py:609
  15.2 2.2 %collective-permute-start.5 = (bf16[4,320,256]{2,1,0:T(8,128)(2,1)S(1)}, bf16[4,320,256]{2,1,0:T(8,128)(2,1)S(1)}, u32[]{:S(2)}, u32[]{:S(2)}) collective-permute-start(bf16[4,320,256]{2,1,0:T(8,128)(2,1)S(1)} %pad_maximum_fusion.refs_0_), channel_id=1, source_target_pairs={{0,1},{1,0},{2,3},{3,2},{4,5},{5,4},{6,7},{7,6},{8,9},{9,8},{10,11... | collective-permute-start | bytes 1966088 | tf_op jit(solution)/shard_map/ppermute | solution.py:609
  15.4 5.2 %collective-permute-start.4 = (bf16[20,8,320]{2,1,0:T(8,128)(2,1)S(1)}, bf16[20,8,320]{2,1,0:T(8,128)(2,1)S(1)}, u32[]{:S(2)}, u32[]{:S(2)}) collective-permute-start(bf16[20,8,320]{2,1,0:T(8,128)(2,1)S(1)} %constant_dynamic-update-slice_fusion.refs_0_), channel_id=1, source_target_pairs={{0,9},{1,8},{2,11},{3,10},{4,13},{5,12},{6,15},{7,14},{8,1},{9,0},... | collective-permute-start | bytes 307208 | tf_op jit(solution)/shard_map/ppermute | solution.py:609
  17.4 3.2 %copy-start.2 = (bf16[256,256]{1,0:T(8,128)(2,1)S(1)}, bf16[256,256]{1,0:T(8,128)(2,1)}, u32[]{:S(2)}) copy-start(bf16[256,256]{1,0:T(8,128)(2,1)} %refs_9_.2) | copy-start | bytes 393220
  17.4 3.2 %copy-start.6 = (s32[32,320]{1,0:T(8,128)S(1)}, s32[32,320]{1,0:T(8,128)}, u32[]{:S(2)}) copy-start(s32[32,320]{1,0:T(8,128)} %validity.1) | copy-start | bytes 122884
  17.4 3.2 %copy-start.7 = (s32[320]{0:T(512)S(1)}, s32[320]{0:T(512)}, u32[]{:S(2)}) copy-start(s32[320]{0:T(512)} %refs_8_.3) | copy-start | bytes 3844
  20.6 6.8 %copy-start.15 = (bf16[256,4,256]{2,1,0:T(4,128)(2,1)S(1)}, bf16[256,4,256]{2,1,0:T(4,128)(2,1)}, u32[]{:S(2)}) copy-start(bf16[256,4,256]{2,1,0:T(4,128)(2,1)} %param.35) | copy-start | bytes 1572868
  20.6 6.9 %copy-start.18 = (bf16[256,64]{0,1:T(8,128)(2,1)S(1)}, bf16[256,64]{0,1:T(8,128)(2,1)}, u32[]{:S(2)}) copy-start(bf16[256,64]{0,1:T(8,128)(2,1)} %param.41) | copy-start | bytes 98308
  20.6 7.0 %copy-start.16 = (bf16[1024,128]{1,0:T(8,128)(2,1)S(1)}, bf16[1024,128]{1,0:T(8,128)(2,1)}, u32[]{:S(2)}) copy-start(bf16[1024,128]{1,0:T(8,128)(2,1)} %param.42) | copy-start | bytes 786436
  23.5 8.3 %copy-start = (bf16[256,1024]{1,0:T(8,128)(2,1)S(1)}, bf16[256,1024]{1,0:T(8,128)(2,1)}, u32[]{:S(2)}) copy-start(bf16[256,1024]{1,0:T(8,128)(2,1)} %refs_10_.1) | copy-start | bytes 1572868
  23.5 8.3 %copy-start.1 = (bf16[1024,256]{1,0:T(8,128)(2,1)S(1)}, bf16[1024,256]{1,0:T(8,128)(2,1)}, u32[]{:S(2)}) copy-start(bf16[1024,256]{1,0:T(8,128)(2,1)} %refs_11_.1) | copy-start | bytes 1572868
  23.5 8.3 %copy-start.3 = (bf16[256,256]{1,0:T(8,128)(2,1)S(1)}, bf16[256,256]{1,0:T(8,128)(2,1)}, u32[]{:S(2)}) copy-start(bf16[256,256]{1,0:T(8,128)(2,1)} %refs_8_.4) | copy-start | bytes 393220
  23.5 8.2 %copy-start.9 = (f32[256]{0:T(256)S(1)}, f32[256]{0:T(256)}, u32[]{:S(2)}) copy-start(f32[256]{0:T(256)} %param.34) | copy-start | bytes 3076
  23.5 8.2 %copy-start.10 = (f32[256]{0:T(256)S(1)}, f32[256]{0:T(256)}, u32[]{:S(2)}) copy-start(f32[256]{0:T(256)} %param.37) | copy-start | bytes 3076
  23.6 8.2 %copy-start.11 = (f32[256]{0:T(256)S(1)}, f32[256]{0:T(256)}, u32[]{:S(2)}) copy-start(f32[256]{0:T(256)} %param.40) | copy-start | bytes 3076
  23.6 4.4 %collective-permute-start.6 = (bf16[10,8,256]{2,1,0:T(8,128)(2,1)S(1)}, bf16[10,8,256]{2,1,0:T(8,128)(2,1)S(1)}, u32[]{:S(2)}, u32[]{:S(2)}) collective-permute-start(bf16[10,8,256]{2,1,0:T(8,128)(2,1)S(1)} %get-tuple-element.43), channel_id=1, source_target_pairs={{0,17},{1,16},{2,19},{3,18},{4,21},{5,20},{6,23},{7,22},{8,25},{9,... | collective-permute-start | bytes 122888 | tf_op jit(solution)/shard_map/ppermute | solution.py:609
  25.8 6.0 %collective-permute-start.7 = (bf16[10,8,256]{2,1,0:T(8,128)(2,1)S(1)}, bf16[10,8,256]{2,1,0:T(8,128)(2,1)S(1)}, u32[]{:S(2)}, u32[]{:S(2)}) collective-permute-start(bf16[10,8,256]{2,1,0:T(8,128)(2,1)S(1)} %get-tuple-element.44), channel_id=1, source_target_pairs={{0,24},{1,25},{2,26},{3,27},{4,28},{5,29},{6,30},{7,31},{8,16},{9,... | collective-permute-start | bytes 122888 | tf_op jit(solution)/shard_map/ppermute | solution.py:609
  27.1 4.6 %collective-permute-start.8 = (bf16[10,8,256]{2,1,0:T(8,128)(2,1)S(1)}, bf16[10,8,256]{2,1,0:T(8,128)(2,1)S(1)}, u32[]{:S(2)}, u32[]{:S(2)}) collective-permute-start(bf16[10,8,256]{2,1,0:T(8,128)(2,1)S(1)} %get-tuple-element.45), channel_id=1, source_target_pairs={{0,9},{1,8},{2,11},{3,10},{4,13},{5,12},{6,15},{7,14},{8,1},{9,0},... | collective-permute-start | bytes 122888 | tf_op jit(solution)/shard_map/ppermute | solution.py:609
  36.1 5.2 %collective-permute-start.9 = (bf16[10,1024]{1,0:T(8,128)(2,1)S(1)}, bf16[10,1024]{1,0:T(8,128)(2,1)S(1)}, u32[]{:S(2)}, u32[]{:S(2)}) collective-permute-start(bf16[10,1024]{1,0:T(8,128)(2,1)S(1)} %bitcast.16), channel_id=1, source_target_pairs={{0,17},{1,16},{2,19},{3,18},{4,21},{5,20},{6,23},{7,22},{8,25},{9,... | collective-permute-start | bytes 61448 | tf_op jit(solution)/shard_map/ppermute | solution.py:609
  37.5 5.3 %collective-permute-start.10 = (bf16[10,1024]{1,0:T(8,128)(2,1)S(1)}, bf16[10,1024]{1,0:T(8,128)(2,1)S(1)}, u32[]{:S(2)}, u32[]{:S(2)}) collective-permute-start(bf16[10,1024]{1,0:T(8,128)(2,1)S(1)} %bitcast.17), channel_id=1, source_target_pairs={{0,25},{1,24},{2,27},{3,26},{4,29},{5,28},{6,31},{7,30},{8,17},{9,... | collective-permute-start | bytes 61448 | tf_op jit(solution)/shard_map/ppermute | solution.py:609
  38.9 3.9 %collective-permute-start.11 = (bf16[10,1024]{1,0:T(8,128)(2,1)S(1)}, bf16[10,1024]{1,0:T(8,128)(2,1)S(1)}, u32[]{:S(2)}, u32[]{:S(2)}) collective-permute-start(bf16[10,1024]{1,0:T(8,128)(2,1)S(1)} %bitcast.18), channel_id=1, source_target_pairs={{0,9},{1,8},{2,11},{3,10},{4,13},{5,12},{6,15},{7,14},{8,1},{9,0},... | collective-permute-start | bytes 61448 | tf_op jit(solution)/shard_map/ppermute | solution.py:609
  39.0 12.6 %copy-start.4 = (bf16[128,512]{1,0:T(8,128)(2,1)S(1)}, bf16[128,512]{1,0:T(8,128)(2,1)}, u32[]{:S(2)}) copy-start(bf16[128,512]{1,0:T(8,128)(2,1)} %refs_8_.5) | copy-start | bytes 393220
  39.0 12.6 %copy-start.5 = (bf16[512,128]{1,0:T(8,128)(2,1)S(1)}, bf16[512,128]{1,0:T(8,128)(2,1)}, u32[]{:S(2)}) copy-start(bf16[512,128]{1,0:T(8,128)(2,1)} %refs_9_.3) | copy-start | bytes 393220
  39.0 12.6 %copy-start.12 = (f32[128]{0:T(128)S(1)}, f32[128]{0:T(128)}, u32[]{:S(2)}) copy-start(f32[128]{0:T(128)} %param.43) | copy-start | bytes 1540
  39.0 12.6 %copy-start.13 = (f32[10,320,128]{2,1,0:T(8,128)S(1)}, f32[10,320,128]{2,1,0:T(8,128)}, u32[]{:S(2)}) copy-start(f32[10,320,128]{2,1,0:T(8,128)} %get-tuple-element.63.refs_6_) | copy-start | bytes 4915204
  42.8 5.3 %collective-permute-start.12 = (bf16[40,1024]{1,0:T(8,128)(2,1)S(1)}, bf16[40,1024]{1,0:T(8,128)(2,1)S(1)}, u32[]{:S(2)}, u32[]{:S(2)}) collective-permute-start(bf16[40,1024]{1,0:T(8,128)(2,1)S(1)} %pad_maximum_fusion.1.refs_0_), channel_id=1, source_target_pairs={{0,7},{1,6},{2,5},{3,4},{4,3},{5,2},{6,1},{7,0},{8,15},{9,14},{10,... | collective-permute-start | bytes 245768 | tf_op jit(solution)/shard_map/ppermute | solution.py:609
  45.3 4.7 %collective-permute-start.13 = (bf16[40,1024]{1,0:T(8,128)(2,1)S(1)}, bf16[40,1024]{1,0:T(8,128)(2,1)S(1)}, u32[]{:S(2)}, u32[]{:S(2)}) collective-permute-start(bf16[40,1024]{1,0:T(8,128)(2,1)S(1)} %pad_maximum_fusion.1.refs_0_), channel_id=1, source_target_pairs={{0,3},{1,2},{2,1},{3,0},{4,7},{5,6},{6,5},{7,4},{8,11},{9,10},{10,... | collective-permute-start | bytes 245768 | tf_op jit(solution)/shard_map/ppermute | solution.py:609
  45.4 4.6 %collective-permute-start.14 = (bf16[40,1024]{1,0:T(8,128)(2,1)S(1)}, bf16[40,1024]{1,0:T(8,128)(2,1)S(1)}, u32[]{:S(2)}, u32[]{:S(2)}) collective-permute-start(bf16[40,1024]{1,0:T(8,128)(2,1)S(1)} %pad_maximum_fusion.1.refs_0_), channel_id=1, source_target_pairs={{0,5},{1,4},{2,7},{3,6},{4,1},{5,0},{6,3},{7,2},{8,13},{9,12},{10,... | collective-permute-start | bytes 245768 | tf_op jit(solution)/shard_map/ppermute | solution.py:609
  46.3 3.6 %collective-permute-start.15 = (bf16[40,1024]{1,0:T(8,128)(2,1)S(1)}, bf16[40,1024]{1,0:T(8,128)(2,1)S(1)}, u32[]{:S(2)}, u32[]{:S(2)}) collective-permute-start(bf16[40,1024]{1,0:T(8,128)(2,1)S(1)} %pad_maximum_fusion.1.refs_0_), channel_id=1, source_target_pairs={{0,1},{1,0},{2,3},{3,2},{4,5},{5,4},{6,7},{7,6},{8,9},{9,8},{10,11... | collective-permute-start | bytes 245768 | tf_op jit(solution)/shard_map/ppermute | solution.py:609
  50.0 1.6 %collective-permute-start.16 = (bf16[120,1024]{1,0:T(8,128)(2,1)S(1)}, bf16[120,1024]{1,0:T(8,128)(2,1)S(1)}, u32[]{:S(2)}, u32[]{:S(2)}) collective-permute-start(bf16[120,1024]{1,0:T(8,128)(2,1)S(1)} %constant_dynamic-update-slice_fusion.2.refs_1_), channel_id=1, source_target_pairs={{0,1},{1,0},{2,3},{3,2},{4,5},{5,4},{6,7},{7,6},{8,9},{9,8},{10,11... | collective-permute-start | bytes 737288 | tf_op jit(solution)/shard_map/ppermute | solution.py:609

commit v9 on v8

--- a/solution.py
+++ b/solution.py
@@ -287,7 +287,7 @@
 def column_kernel(idx, *refs, sub, far, rows, block, depth, width):
     piece_refs, refs = refs[:far], refs[far:]
     entry, twin, *sources = refs[:9]
-    updated, left, right, start_rows, gated, *held = refs[9:-1]
+    updated, left, right, start_rows, gated, rounded, *held = refs[9:-1]
     sems = refs[-1]
     copies = [pltpu.make_async_copy(src, dst, sems.at[n]) for n, (src, dst) in enumerate(zip(sources, held))]
     steps = rows // block
@@ -351,7 +351,10 @@
     x = x + dot(gated[...].astype(BF16), exit_)
     hidden = jnp.maximum(dot(layer_norm(x, ff_gain).astype(BF16), widen).astype(BF16), 0.0)
     x = x + dot(hidden, narrow)
-    updated[...] = x.astype(BF16).reshape(block, depth, width)
+    rounded[...] = x.astype(BF16).reshape(block, depth, width)
+    here = pl.ds(0 if steps == 1 else pl.program_id(0) * block, block)
+    leave = pltpu.make_async_copy(rounded, updated.at[here], sems.at[len(copies)])
+    leave.start()
     outer = layer_norm(x, product_gain).astype(BF16)
     both = dot(outer, twin[...])
     channels = twin.shape[1] // 2
@@ -366,6 +369,7 @@
         part = (both[here] * valid[:, i : i + 1]).astype(BF16)
         left[here, :] = part[:, :channels]
         right[0, i : i + 1, :] = jnp.sum(dot(part, repeat) * mine, axis=0, keepdims=True).astype(BF16)
+    leave.wait()
 
 
 def column_call(idx, pieces, validity, col_gain, entry, exit_, ff_gain, widen, narrow, product_gain, twin):
@@ -399,7 +403,7 @@
         + [spec(a.shape, lambda s: (0, 0)) for a in here]
         + [pl.BlockSpec(memory_space=pltpu.HBM)] * len(sources),
         out_specs=[
-            spec((block, depth, width), lambda s: (s, 0, 0)),
+            pl.BlockSpec(memory_space=pl.ANY),
             spec((block * depth, channels), lambda s: (s, 0)),
             spec((1, block, channels * depth), lambda s: (s, 0, 0)),
         ],
@@ -408,9 +412,13 @@
             jax.ShapeDtypeStruct((rows * depth, channels), BF16),
             jax.ShapeDtypeStruct((steps, block, channels * depth), BF16),
         ],
-        scratch_shapes=[pltpu.VMEM((block, depth, width), F32), pltpu.VMEM((block * depth, width), F32)]
+        scratch_shapes=[
+            pltpu.VMEM((block, depth, width), F32),
+            pltpu.VMEM((block * depth, width), F32),
+            pltpu.VMEM((block, depth, width), BF16),
+        ]
         + [pltpu.VMEM(a.shape, a.dtype) for a in sources]
-        + [pltpu.SemaphoreType.DMA((len(sources),))],
+        + [pltpu.SemaphoreType.DMA((len(sources) + 1,))],
         compiler_params=pltpu.CompilerParams(vmem_limit_bytes=vmem_limit(length)),
         cost_estimate=pl.CostEstimate(flops=5 * 10**9, bytes_accessed=4000000, transcendentals=10**5),
         name="column_attention",

time: 55.9 us -> 55.9 us (level)
  no operation moved by 1% of the time
where the time goes in v9:
time: 55.9 us; the launch traced here: 55.7 us
  starting transfers between devices  18.6 us (33%)
  Pallas kernels  17.9 us (32%)
  waiting for transfers between devices  16.5 us (30%)
  local copies, waits for them, and re-layouts  1.41 us (3%)
  between operations  1.09 us (2%)
    ppermute x17, starting transfers between devices, swap(): return lax.ppermute(x, 'dap', [(d, d ^ distance) for d in range(devices)])  18.6 us
    ppermute x17, waiting for transfers between devices, swap(): return lax.ppermute(x, 'dap', [(d, d ^ distance) for d in range(devices)])  16.5 us
    pallas_call x1, Pallas kernels, column_call(): pl.pallas_call(functools.partial(column_kernel, sub=sub, far=far, rows=ro...  4.27 us
    pallas_call x1, Pallas kernels, finish_call(): pl.pallas_call(functools.partial(finish_kernel, pieces=len(near), sub=sub...  3.94 us
    pallas_call x1, Pallas kernels, pair_call(): pl.pallas_call(functools.partial(pair_kernel, rows=rows, length=length, b...  3.37 us
    pallas_call x1, Pallas kernels, row_call(): pl.pallas_call(functools.partial(row_kernel, order=order, sub=sub, far=fa...  2.87 us
    pallas_call x1, Pallas kernels, project_call(): pl.pallas_call(functools.partial(project_kernel, sub=sub, far=far, rows=r...  2.28 us
    unnamed x44, local copies, waits for them, and re-layouts  1.28 us
  transfers between devices with their start and end apart: 17, of which 10 were waited for; matrix products, arithmetic and copies ran while one was open for 2% of the time, Pallas kernels for 12%

profile of v9, /device:TPU:0, one launch (start us, length us, event | category | flops | bytes accessed | tf_op | source)
XLA Modules:
  0.0 55.7 jit_solution(2206068831262421300)
XLA Ops:
  0.6 3.4 %collective-permute-start.3 = (bf16[1,320,256]{2,1,0:T(8,128)(2,1)}, bf16[1,320,256]{2,1,0:T(8,128)(2,1)S(1)}, u32[]{:S(2)}, u32[]{:S(2)}) collective-permute-start(bf16[1,320,256]{2,1,0:T(8,128)(2,1)} %param.23), channel_id=1, source_target_pairs={{0,7},{1,6},{2,5},{3,4},{4,3},{5,2},{6,1},{7,0},{8,15},{9,14},{10,... | collective-permute-start | bytes 491528 | tf_op jit(solution)/shard_map/ppermute | solution.py:617
  4.0 0.8 %collective-permute-start.2 = (bf16[1,320,256]{2,1,0:T(8,128)(2,1)}, bf16[1,320,256]{2,1,0:T(8,128)(2,1)S(1)}, u32[]{:S(2)}, u32[]{:S(2)}) collective-permute-start(bf16[1,320,256]{2,1,0:T(8,128)(2,1)} %param.23), channel_id=1, source_target_pairs={{0,5},{1,4},{2,7},{3,6},{4,1},{5,0},{6,3},{7,2},{8,13},{9,12},{10,... | collective-permute-start | bytes 491528 | tf_op jit(solution)/shard_map/ppermute | solution.py:617
  4.8 0.1 collective-permute-start.1
  5.0 3.4 %pair_bias.1 = (f32[10,320,128]{2,1,0:T(8,128)}, bf16[10,8,320]{2,1,0:T(8,128)(2,1)}) custom-call(s32[1]{0:T(128)} %bitcast.idx, s32[320]{0:T(512)} %chain_row.1, bf16[10,320,128]{2,1,0:T(8,128)(2,1)} %pair.1, s32[320]{0:T(512)} %chain_row.1, f32[66,128]{1,0:T(8,128)} %table.1, f32[1,128]{1,0:T(1,128)} %bitcast.28, bf16[8,128]{1,0:T(8,128)(2,1)} %bitcast.27), custom_call_target="tpu_custom_call" | custom-call | flops 4000000000 | bytes 4000000 | tf_op jit(solution)/shard_map/pair_bias/pallas_call | solution.py:108
  8.3 2.8 %collective-permute-start = (bf16[10,8,320]{2,1,0:T(8,128)(2,1)}, bf16[10,8,320]{2,1,0:T(8,128)(2,1)S(1)}, u32[]{:S(2)}, u32[]{:S(2)}) collective-permute-start(bf16[10,8,320]{2,1,0:T(8,128)(2,1)} %get-tuple-element.33), channel_id=1, source_target_pairs={{0,17},{1,16},{2,19},{3,18},{4,21},{5,20},{6,23},{7,22},{8,25},{9,... | collective-permute-start | bytes 153608 | tf_op jit(solution)/shard_map/ppermute | solution.py:617
  11.1 0.9 %constant_dynamic-update-slice_fusion.1 = bf16[20,8,320]{2,1,0:T(8,128)(2,1)S(1)} fusion(bf16[10,8,320]{2,1,0:T(8,128)(2,1)} %get-tuple-element.33), kind=kLoop, calls=%fused_computation.3 | loop fusion | bytes 112640
  12.0 0.1 copy.26
  12.1 3.0 %collective-permute-done = bf16[10,8,320]{2,1,0:T(8,128)(2,1)S(1)} collective-permute-done((bf16[10,8,320]{2,1,0:T(8,128)(2,1)}, bf16[10,8,320]{2,1,0:T(8,128)(2,1)S(1)}, u32[]{:S(2)}, u32[]{:S(2)}) %collective-permute-start) | collective-permute-done | bytes 51232 | tf_op jit(solution)/shard_map/ppermute | solution.py:617
  15.1 0.0 collective-permute-done.3
  15.1 0.1 pad_maximum_fusion.refs_0_
  15.2 0.2 collective-permute-start.5
  15.4 0.8 %collective-permute-start.4 = (bf16[20,8,320]{2,1,0:T(8,128)(2,1)S(1)}, bf16[20,8,320]{2,1,0:T(8,128)(2,1)S(1)}, u32[]{:S(2)}, u32[]{:S(2)}) collective-permute-start(bf16[20,8,320]{2,1,0:T(8,128)(2,1)S(1)} %constant_dynamic-update-slice_fusion.refs_0_), channel_id=1, source_target_pairs={{0,9},{1,8},{2,11},{3,10},{4,13},{5,12},{6,15},{7,14},{8,1},{9,0},... | collective-permute-start | bytes 307208 | tf_op jit(solution)/shard_map/ppermute | solution.py:617
  16.2 1.2 %collective-permute-done.5.refs_1_ = bf16[4,320,256]{2,1,0:T(8,128)(2,1)S(1)} collective-permute-done((bf16[4,320,256]{2,1,0:T(8,128)(2,1)S(1)}, bf16[4,320,256]{2,1,0:T(8,128)(2,1)S(1)}, u32[]{:S(2)}, u32[]{:S(2)}) %collective-permute-start.5) | collective-permute-done | bytes 655392 | tf_op jit(solution)/shard_map/ppermute | solution.py:617
  17.4 2.3 %row_project.1 = (bf16[8,320,256]{2,1,0:T(8,128)(2,1)S(1)}, bf16[8,320,256]{2,1,0:T(8,128)(2,1)S(1)}, f32[320,256]{1,0:T(8,128)S(1)}, f32[320,256]{1,0:T(8,128)S(1)}, f32[320,256]{1,0:T(8,128)S(1)}) custom-call(s32[1]{0:T(128)} %bitcast.idx, bf16[4,320,256]{2,1,0:T(8,128)(2,1)S(1)} %pad_maximum_fusion.refs_0_, ...), custom_call_target="tpu_custom_call" | custom-call | flops 3000000000 | bytes 4000000 | tf_op jit(solution)/shard_map/row_project/pallas_call | solution.py:198
  19.7 0.9 %collective-permute-done.4.refs_1_ = bf16[20,8,320]{2,1,0:T(8,128)(2,1)S(1)} collective-permute-done((bf16[20,8,320]{2,1,0:T(8,128)(2,1)S(1)}, bf16[20,8,320]{2,1,0:T(8,128)(2,1)S(1)}, u32[]{:S(2)}, u32[]{:S(2)}) %collective-permute-start.4) | collective-permute-done | bytes 102432 | tf_op jit(solution)/shard_map/ppermute | solution.py:617
  20.6 0.0 copy-start.15
  20.6 0.0 copy-start.18
  20.6 0.0 copy-start.16
  20.6 2.9 %row_attention.1 = (bf16[10,8,256]{2,1,0:T(8,128)(2,1)S(1)}, bf16[10,8,256]{2,1,0:T(8,128)(2,1)S(1)}, bf16[10,8,256]{2,1,0:T(8,128)(2,1)S(1)}, bf16[10,8,256]{2,1,0:T(8,128)(2,1)S(1)}) custom-call(s32[1]{0:T(128)} %bitcast.idx, bf16[20,8,320]{2,1,0:T(8,128)(2,1)S(1)} %constant_dynamic-update-slice_fusion.refs_0_, ...), custom_call_target="tpu_custom_call" | custom-call | flops 4000000000 | bytes 4000000 | tf_op jit(solution)/shard_map/row_attention/pallas_call | solution.py:271
  23.5 0.0 copy-start
  23.5 0.0 copy-start.1
  23.5 0.0 copy-start.3
  23.5 0.0 copy-start.9
  23.5 0.0 copy-start.10
  23.6 0.0 copy-start.11
  23.6 2.2 %collective-permute-start.6 = (bf16[10,8,256]{2,1,0:T(8,128)(2,1)S(1)}, bf16[10,8,256]{2,1,0:T(8,128)(2,1)S(1)}, u32[]{:S(2)}, u32[]{:S(2)}) collective-permute-start(bf16[10,8,256]{2,1,0:T(8,128)(2,1)S(1)} %get-tuple-element.43), channel_id=1, source_target_pairs={{0,17},{1,16},{2,19},{3,18},{4,21},{5,20},{6,23},{7,22},{8,25},{9,... | collective-permute-start | bytes 122888 | tf_op jit(solution)/shard_map/ppermute | solution.py:617
  25.8 1.4 %collective-permute-start.7 = (bf16[10,8,256]{2,1,0:T(8,128)(2,1)S(1)}, bf16[10,8,256]{2,1,0:T(8,128)(2,1)S(1)}, u32[]{:S(2)}, u32[]{:S(2)}) collective-permute-start(bf16[10,8,256]{2,1,0:T(8,128)(2,1)S(1)} %get-tuple-element.44), channel_id=1, source_target_pairs={{0,24},{1,25},{2,26},{3,27},{4,28},{5,29},{6,30},{7,31},{8,16},{9,... | collective-permute-start | bytes 122888 | tf_op jit(solution)/shard_map/ppermute | solution.py:617
  27.1 0.2 collective-permute-start.8
  27.4 0.1 copy.27
  27.5 0.1 copy.25.refs_5_
  27.6 0.1 reshape.22.factors
  27.7 0.2 collective-permute-done.6.refs_2_
  28.0 3.8 %collective-permute-done.7.refs_3_ = bf16[10,8,256]{2,1,0:T(8,128)(2,1)S(1)} collective-permute-done((bf16[10,8,256]{2,1,0:T(8,128)(2,1)S(1)}, bf16[10,8,256]{2,1,0:T(8,128)(2,1)S(1)}, u32[]{:S(2)}, u32[]{:S(2)}) %collective-permute-start.7) | collective-permute-done | bytes 40992 | tf_op jit(solution)/shard_map/ppermute | solution.py:617
  31.8 4.3 %column_attention.1 = (bf16[10,32,256]{2,1,0:T(8,128)(2,1)}, bf16[320,32]{1,0:T(8,128)(2,1)S(1)}, bf16[1,10,1024]{2,1,0:T(8,128)(2,1)S(1)}) custom-call(s32[1]{0:T(128)} %bitcast.idx, bf16[10,8,256]{2,1,0:T(8,128)(2,1)S(1)} %get-tuple-element.42.refs_0_, bf16[10,8,256]{2,1,0:T(8,128)(2,1)S(1)} %collective-permute-done.8.refs_1_, ...), custom_call_target="tpu_custom_call" | custom-call | flops 5000000000 | bytes 4000000 | tf_op jit(solution)/shard_map/column_attention/pallas_call | solution.py:398
  36.1 1.4 %collective-permute-start.9 = (bf16[10,1024]{1,0:T(8,128)(2,1)S(1)}, bf16[10,1024]{1,0:T(8,128)(2,1)S(1)}, u32[]{:S(2)}, u32[]{:S(2)}) collective-permute-start(bf16[10,1024]{1,0:T(8,128)(2,1)S(1)} %bitcast.16), channel_id=1, source_target_pairs={{0,17},{1,16},{2,19},{3,18},{4,21},{5,20},{6,23},{7,22},{8,25},{9,... | collective-permute-start | bytes 61448 | tf_op jit(solution)/shard_map/ppermute | solution.py:617
  37.5 1.4 %collective-permute-start.10 = (bf16[10,1024]{1,0:T(8,128)(2,1)S(1)}, bf16[10,1024]{1,0:T(8,128)(2,1)S(1)}, u32[]{:S(2)}, u32[]{:S(2)}) collective-permute-start(bf16[10,1024]{1,0:T(8,128)(2,1)S(1)} %bitcast.17), channel_id=1, source_target_pairs={{0,25},{1,24},{2,27},{3,26},{4,29},{5,28},{6,31},{7,30},{8,17},{9,... | collective-permute-start | bytes 61448 | tf_op jit(solution)/shard_map/ppermute | solution.py:617
  38.9 0.2 collective-permute-start.11
  39.1 1.2 %left_mix.1 = (bf16[1024,1280]{1,0:T(8,128)(2,1)S(1)}, f32[320,1280]{1,0:T(8,128)S(1)}) custom-call(s32[1]{0:T(128)} %bitcast.idx, bf16[320,32]{1,0:T(8,128)(2,1)S(1)} %get-tuple-element.50.left, bf16[32,4096]{1,0:T(8,128)(2,1)S(1)} %reshape.22.factors, s32[32,320]{1,0:T(8,128)S(1)} %copy-done.6), custom_call_target="tpu_custom_call" | custom-call | flops 2000000000 | bytes 4000000 | tf_op jit(solution)/shard_map/left_mix/pallas_call | solution.py:463
  40.3 0.9 %collective-permute-done.9 = bf16[10,1024]{1,0:T(8,128)(2,1)S(1)} collective-permute-done((bf16[10,1024]{1,0:T(8,128)(2,1)S(1)}, bf16[10,1024]{1,0:T(8,128)(2,1)S(1)}, u32[]{:S(2)}, u32[]{:S(2)}) %collective-permute-start.9) | collective-permute-done | bytes 20512 | tf_op jit(solution)/shard_map/ppermute | solution.py:617
  41.3 1.5 %collective-permute-done.10 = bf16[10,1024]{1,0:T(8,128)(2,1)S(1)} collective-permute-done((bf16[10,1024]{1,0:T(8,128)(2,1)S(1)}, bf16[10,1024]{1,0:T(8,128)(2,1)S(1)}, u32[]{:S(2)}, u32[]{:S(2)}) %collective-permute-start.10) | collective-permute-done | bytes 20512 | tf_op jit(solution)/shard_map/ppermute | solution.py:617
  42.8 2.4 %collective-permute-start.12 = (bf16[40,1024]{1,0:T(8,128)(2,1)S(1)}, bf16[40,1024]{1,0:T(8,128)(2,1)S(1)}, u32[]{:S(2)}, u32[]{:S(2)}) collective-permute-start(bf16[40,1024]{1,0:T(8,128)(2,1)S(1)} %pad_maximum_fusion.1.refs_0_), channel_id=1, source_target_pairs={{0,7},{1,6},{2,5},{3,4},{4,3},{5,2},{6,1},{7,0},{8,15},{9,14},{10,... | collective-permute-start | bytes 245768 | tf_op jit(solution)/shard_map/ppermute | solution.py:617
  45.2 0.2 collective-permute-start.13
  45.4 0.9 %collective-permute-start.14 = (bf16[40,1024]{1,0:T(8,128)(2,1)S(1)}, bf16[40,1024]{1,0:T(8,128)(2,1)S(1)}, u32[]{:S(2)}, u32[]{:S(2)}) collective-permute-start(bf16[40,1024]{1,0:T(8,128)(2,1)S(1)} %pad_maximum_fusion.1.refs_0_), channel_id=1, source_target_pairs={{0,5},{1,4},{2,7},{3,6},{4,1},{5,0},{6,3},{7,2},{8,13},{9,12},{10,... | collective-permute-start | bytes 245768 | tf_op jit(solution)/shard_map/ppermute | solution.py:617
  46.3 1.7 %collective-permute-done.12 = bf16[40,1024]{1,0:T(8,128)(2,1)S(1)} collective-permute-done((bf16[40,1024]{1,0:T(8,128)(2,1)S(1)}, bf16[40,1024]{1,0:T(8,128)(2,1)S(1)}, u32[]{:S(2)}, u32[]{:S(2)}) %collective-permute-start.12) | collective-permute-done | bytes 81952 | tf_op jit(solution)/shard_map/ppermute | solution.py:617
  48.0 1.9 %collective-permute-done.13 = bf16[40,1024]{1,0:T(8,128)(2,1)S(1)} collective-permute-done((bf16[40,1024]{1,0:T(8,128)(2,1)S(1)}, bf16[40,1024]{1,0:T(8,128)(2,1)S(1)}, u32[]{:S(2)}, u32[]{:S(2)}) %collective-permute-start.13) | collective-permute-done | bytes 81952 | tf_op jit(solution)/shard_map/ppermute | solution.py:617
  50.0 0.2 collective-permute-start.16
  50.2 1.4 %collective-permute-done.16.refs_3_ = bf16[120,1024]{1,0:T(8,128)(2,1)S(1)} collective-permute-done((bf16[120,1024]{1,0:T(8,128)(2,1)S(1)}, bf16[120,1024]{1,0:T(8,128)(2,1)S(1)}, u32[]{:S(2)}, u32[]{:S(2)}) %collective-permute-start.16) | collective-permute-done | bytes 245792 | tf_op jit(solution)/shard_map/ppermute | solution.py:617
  51.6 3.9 %pair_update.1 = bf16[10,320,128]{2,1,0:T(8,128)(2,1)} custom-call(s32[1]{0:T(128)} %bitcast.idx, bf16[40,1024]{1,0:T(8,128)(2,1)S(1)} %pad_maximum_fusion.1.refs_0_, bf16[120,1024]{1,0:T(8,128)(2,1)S(1)} %constant_dynamic-update-slice_fusion.2.refs_1_, bf16[40,1024]{1,0:T(8,128)(2,1)S(1)} %collective-permute-done.15.refs_2_, ...), custom_call_target="tpu_custom_call" | custom-call | flops 4000000000 | bytes 4000000 | tf_op jit(solution)/shard_map/pair_update/pallas_call | solution.py:559
  (41 shorter events, 0.2 us)
Async XLA Ops:
  0.6 14.4 %collective-permute-start.3 = (bf16[1,320,256]{2,1,0:T(8,128)(2,1)}, bf16[1,320,256]{2,1,0:T(8,128)(2,1)S(1)}, u32[]{:S(2)}, u32[]{:S(2)}) collective-permute-start(bf16[1,320,256]{2,1,0:T(8,128)(2,1)} %param.23), channel_id=1, source_target_pairs={{0,7},{1,6},{2,5},{3,4},{4,3},{5,2},{6,1},{7,0},{8,15},{9,14},{10,... | collective-permute-start | bytes 491528 | tf_op jit(solution)/shard_map/ppermute | solution.py:617
  4.0 11.1 %collective-permute-start.2 = (bf16[1,320,256]{2,1,0:T(8,128)(2,1)}, bf16[1,320,256]{2,1,0:T(8,128)(2,1)S(1)}, u32[]{:S(2)}, u32[]{:S(2)}) collective-permute-start(bf16[1,320,256]{2,1,0:T(8,128)(2,1)} %param.23), channel_id=1, source_target_pairs={{0,5},{1,4},{2,7},{3,6},{4,1},{5,0},{6,3},{7,2},{8,13},{9,12},{10,... | collective-permute-start | bytes 491528 | tf_op jit(solution)/shard_map/ppermute | solution.py:617
  4.8 10.3 %collective-permute-start.1 = (bf16[1,320,256]{2,1,0:T(8,128)(2,1)}, bf16[1,320,256]{2,1,0:T(8,128)(2,1)S(1)}, u32[]{:S(2)}, u32[]{:S(2)}) collective-permute-start(bf16[1,320,256]{2,1,0:T(8,128)(2,1)} %param.23), channel_id=1, source_target_pairs={{0,3},{1,2},{2,1},{3,0},{4,7},{5,6},{6,5},{7,4},{8,11},{9,10},{10,... | collective-permute-start | bytes 491528 | tf_op jit(solution)/shard_map/ppermute | solution.py:617
  5.0 7.0 %copy-start.14 = (bf16[256,4,256]{2,1,0:T(4,128)(2,1)S(1)}, bf16[256,4,256]{2,1,0:T(4,128)(2,1)}, u32[]{:S(2)}) copy-start(bf16[256,4,256]{2,1,0:T(4,128)(2,1)} %param.32) | copy-start | bytes 1572868
  5.0 10.2 %copy-start.17 = (bf16[1,320,256]{2,1,0:T(8,128)(2,1)S(1)}, bf16[1,320,256]{2,1,0:T(8,128)(2,1)}, u32[]{:S(2)}) copy-start(bf16[1,320,256]{2,1,0:T(8,128)(2,1)} %param.23) | copy-start | bytes 491524
  8.3 9.0 %copy-start.8 = (f32[256]{0:T(256)S(1)}, f32[256]{0:T(256)}, u32[]{:S(2)}) copy-start(f32[256]{0:T(256)} %param.31) | copy-start | bytes 3076
  8.3 6.7 %collective-permute-start = (bf16[10,8,320]{2,1,0:T(8,128)(2,1)}, bf16[10,8,320]{2,1,0:T(8,128)(2,1)S(1)}, u32[]{:S(2)}, u32[]{:S(2)}) collective-permute-start(bf16[10,8,320]{2,1,0:T(8,128)(2,1)} %get-tuple-element.33), channel_id=1, source_target_pairs={{0,17},{1,16},{2,19},{3,18},{4,21},{5,20},{6,23},{7,22},{8,25},{9,... | collective-permute-start | bytes 153608 | tf_op jit(solution)/shard_map/ppermute | solution.py:617
  15.2 2.2 %collective-permute-start.5 = (bf16[4,320,256]{2,1,0:T(8,128)(2,1)S(1)}, bf16[4,320,256]{2,1,0:T(8,128)(2,1)S(1)}, u32[]{:S(2)}, u32[]{:S(2)}) collective-permute-start(bf16[4,320,256]{2,1,0:T(8,128)(2,1)S(1)} %pad_maximum_fusion.refs_0_), channel_id=1, source_target_pairs={{0,1},{1,0},{2,3},{3,2},{4,5},{5,4},{6,7},{7,6},{8,9},{9,8},{10,11... | collective-permute-start | bytes 1966088 | tf_op jit(solution)/shard_map/ppermute | solution.py:617
  15.4 5.2 %collective-permute-start.4 = (bf16[20,8,320]{2,1,0:T(8,128)(2,1)S(1)}, bf16[20,8,320]{2,1,0:T(8,128)(2,1)S(1)}, u32[]{:S(2)}, u32[]{:S(2)}) collective-permute-start(bf16[20,8,320]{2,1,0:T(8,128)(2,1)S(1)} %constant_dynamic-update-slice_fusion.refs_0_), channel_id=1, source_target_pairs={{0,9},{1,8},{2,11},{3,10},{4,13},{5,12},{6,15},{7,14},{8,1},{9,0},... | collective-permute-start | bytes 307208 | tf_op jit(solution)/shard_map/ppermute | solution.py:617
  17.4 3.2 %copy-start.2 = (bf16[256,256]{1,0:T(8,128)(2,1)S(1)}, bf16[256,256]{1,0:T(8,128)(2,1)}, u32[]{:S(2)}) copy-start(bf16[256,256]{1,0:T(8,128)(2,1)} %refs_9_.2) | copy-start | bytes 393220
  17.4 3.2 %copy-start.6 = (s32[32,320]{1,0:T(8,128)S(1)}, s32[32,320]{1,0:T(8,128)}, u32[]{:S(2)}) copy-start(s32[32,320]{1,0:T(8,128)} %validity.1) | copy-start | bytes 122884
  17.4 3.2 %copy-start.7 = (s32[320]{0:T(512)S(1)}, s32[320]{0:T(512)}, u32[]{:S(2)}) copy-start(s32[320]{0:T(512)} %refs_8_.3) | copy-start | bytes 3844
  20.6 6.8 %copy-start.15 = (bf16[256,4,256]{2,1,0:T(4,128)(2,1)S(1)}, bf16[256,4,256]{2,1,0:T(4,128)(2,1)}, u32[]{:S(2)}) copy-start(bf16[256,4,256]{2,1,0:T(4,128)(2,1)} %param.35) | copy-start | bytes 1572868
  20.6 6.9 %copy-start.18 = (bf16[256,64]{0,1:T(8,128)(2,1)S(1)}, bf16[256,64]{0,1:T(8,128)(2,1)}, u32[]{:S(2)}) copy-start(bf16[256,64]{0,1:T(8,128)(2,1)} %param.41) | copy-start | bytes 98308
  20.6 7.0 %copy-start.16 = (bf16[1024,128]{1,0:T(8,128)(2,1)S(1)}, bf16[1024,128]{1,0:T(8,128)(2,1)}, u32[]{:S(2)}) copy-start(bf16[1024,128]{1,0:T(8,128)(2,1)} %param.42) | copy-start | bytes 786436
  23.5 8.3 %copy-start = (bf16[256,1024]{1,0:T(8,128)(2,1)S(1)}, bf16[256,1024]{1,0:T(8,128)(2,1)}, u32[]{:S(2)}) copy-start(bf16[256,1024]{1,0:T(8,128)(2,1)} %refs_10_.1) | copy-start | bytes 1572868
  23.5 8.3 %copy-start.1 = (bf16[1024,256]{1,0:T(8,128)(2,1)S(1)}, bf16[1024,256]{1,0:T(8,128)(2,1)}, u32[]{:S(2)}) copy-start(bf16[1024,256]{1,0:T(8,128)(2,1)} %refs_11_.1) | copy-start | bytes 1572868
  23.5 8.3 %copy-start.3 = (bf16[256,256]{1,0:T(8,128)(2,1)S(1)}, bf16[256,256]{1,0:T(8,128)(2,1)}, u32[]{:S(2)}) copy-start(bf16[256,256]{1,0:T(8,128)(2,1)} %refs_8_.4) | copy-start | bytes 393220
  23.5 8.2 %copy-start.9 = (f32[256]{0:T(256)S(1)}, f32[256]{0:T(256)}, u32[]{:S(2)}) copy-start(f32[256]{0:T(256)} %param.34) | copy-start | bytes 3076
  23.5 8.2 %copy-start.10 = (f32[256]{0:T(256)S(1)}, f32[256]{0:T(256)}, u32[]{:S(2)}) copy-start(f32[256]{0:T(256)} %param.37) | copy-start | bytes 3076
  23.6 8.2 %copy-start.11 = (f32[256]{0:T(256)S(1)}, f32[256]{0:T(256)}, u32[]{:S(2)}) copy-start(f32[256]{0:T(256)} %param.40) | copy-start | bytes 3076
  23.6 4.4 %collective-permute-start.6 = (bf16[10,8,256]{2,1,0:T(8,128)(2,1)S(1)}, bf16[10,8,256]{2,1,0:T(8,128)(2,1)S(1)}, u32[]{:S(2)}, u32[]{:S(2)}) collective-permute-start(bf16[10,8,256]{2,1,0:T(8,128)(2,1)S(1)} %get-tuple-element.43), channel_id=1, source_target_pairs={{0,17},{1,16},{2,19},{3,18},{4,21},{5,20},{6,23},{7,22},{8,25},{9,... | collective-permute-start | bytes 122888 | tf_op jit(solution)/shard_map/ppermute | solution.py:617
  25.8 6.0 %collective-permute-start.7 = (bf16[10,8,256]{2,1,0:T(8,128)(2,1)S(1)}, bf16[10,8,256]{2,1,0:T(8,128)(2,1)S(1)}, u32[]{:S(2)}, u32[]{:S(2)}) collective-permute-start(bf16[10,8,256]{2,1,0:T(8,128)(2,1)S(1)} %get-tuple-element.44), channel_id=1, source_target_pairs={{0,24},{1,25},{2,26},{3,27},{4,28},{5,29},{6,30},{7,31},{8,16},{9,... | collective-permute-start | bytes 122888 | tf_op jit(solution)/shard_map/ppermute | solution.py:617
  27.1 4.6 %collective-permute-start.8 = (bf16[10,8,256]{2,1,0:T(8,128)(2,1)S(1)}, bf16[10,8,256]{2,1,0:T(8,128)(2,1)S(1)}, u32[]{:S(2)}, u32[]{:S(2)}) collective-permute-start(bf16[10,8,256]{2,1,0:T(8,128)(2,1)S(1)} %get-tuple-element.45), channel_id=1, source_target_pairs={{0,9},{1,8},{2,11},{3,10},{4,13},{5,12},{6,15},{7,14},{8,1},{9,0},... | collective-permute-start | bytes 122888 | tf_op jit(solution)/shard_map/ppermute | solution.py:617
  36.1 5.2 %collective-permute-start.9 = (bf16[10,1024]{1,0:T(8,128)(2,1)S(1)}, bf16[10,1024]{1,0:T(8,128)(2,1)S(1)}, u32[]{:S(2)}, u32[]{:S(2)}) collective-permute-start(bf16[10,1024]{1,0:T(8,128)(2,1)S(1)} %bitcast.16), channel_id=1, source_target_pairs={{0,17},{1,16},{2,19},{3,18},{4,21},{5,20},{6,23},{7,22},{8,25},{9,... | collective-permute-start | bytes 61448 | tf_op jit(solution)/shard_map/ppermute | solution.py:617
  37.5 5.2 %collective-permute-start.10 = (bf16[10,1024]{1,0:T(8,128)(2,1)S(1)}, bf16[10,1024]{1,0:T(8,128)(2,1)S(1)}, u32[]{:S(2)}, u32[]{:S(2)}) collective-permute-start(bf16[10,1024]{1,0:T(8,128)(2,1)S(1)} %bitcast.17), channel_id=1, source_target_pairs={{0,25},{1,24},{2,27},{3,26},{4,29},{5,28},{6,31},{7,30},{8,17},{9,... | collective-permute-start | bytes 61448 | tf_op jit(solution)/shard_map/ppermute | solution.py:617
  38.9 3.9 %collective-permute-start.11 = (bf16[10,1024]{1,0:T(8,128)(2,1)S(1)}, bf16[10,1024]{1,0:T(8,128)(2,1)S(1)}, u32[]{:S(2)}, u32[]{:S(2)}) collective-permute-start(bf16[10,1024]{1,0:T(8,128)(2,1)S(1)} %bitcast.18), channel_id=1, source_target_pairs={{0,9},{1,8},{2,11},{3,10},{4,13},{5,12},{6,15},{7,14},{8,1},{9,0},... | collective-permute-start | bytes 61448 | tf_op jit(solution)/shard_map/ppermute | solution.py:617
  39.1 12.5 %copy-start.4 = (bf16[128,512]{1,0:T(8,128)(2,1)S(1)}, bf16[128,512]{1,0:T(8,128)(2,1)}, u32[]{:S(2)}) copy-start(bf16[128,512]{1,0:T(8,128)(2,1)} %refs_8_.5) | copy-start | bytes 393220
  39.1 12.5 %copy-start.5 = (bf16[512,128]{1,0:T(8,128)(2,1)S(1)}, bf16[512,128]{1,0:T(8,128)(2,1)}, u32[]{:S(2)}) copy-start(bf16[512,128]{1,0:T(8,128)(2,1)} %refs_9_.3) | copy-start | bytes 393220
  39.1 12.5 %copy-start.12 = (f32[128]{0:T(128)S(1)}, f32[128]{0:T(128)}, u32[]{:S(2)}) copy-start(f32[128]{0:T(128)} %param.43) | copy-start | bytes 1540
  39.1 12.5 %copy-start.13 = (f32[10,320,128]{2,1,0:T(8,128)S(1)}, f32[10,320,128]{2,1,0:T(8,128)}, u32[]{:S(2)}) copy-start(f32[10,320,128]{2,1,0:T(8,128)} %get-tuple-element.63.refs_6_) | copy-start | bytes 4915204
  42.8 5.2 %collective-permute-start.12 = (bf16[40,1024]{1,0:T(8,128)(2,1)S(1)}, bf16[40,1024]{1,0:T(8,128)(2,1)S(1)}, u32[]{:S(2)}, u32[]{:S(2)}) collective-permute-start(bf16[40,1024]{1,0:T(8,128)(2,1)S(1)} %pad_maximum_fusion.1.refs_0_), channel_id=1, source_target_pairs={{0,7},{1,6},{2,5},{3,4},{4,3},{5,2},{6,1},{7,0},{8,15},{9,14},{10,... | collective-permute-start | bytes 245768 | tf_op jit(solution)/shard_map/ppermute | solution.py:617
  45.2 4.7 %collective-permute-start.13 = (bf16[40,1024]{1,0:T(8,128)(2,1)S(1)}, bf16[40,1024]{1,0:T(8,128)(2,1)S(1)}, u32[]{:S(2)}, u32[]{:S(2)}) collective-permute-start(bf16[40,1024]{1,0:T(8,128)(2,1)S(1)} %pad_maximum_fusion.1.refs_0_), channel_id=1, source_target_pairs={{0,3},{1,2},{2,1},{3,0},{4,7},{5,6},{6,5},{7,4},{8,11},{9,10},{10,... | collective-permute-start | bytes 245768 | tf_op jit(solution)/shard_map/ppermute | solution.py:617
  45.4 4.5 %collective-permute-start.14 = (bf16[40,1024]{1,0:T(8,128)(2,1)S(1)}, bf16[40,1024]{1,0:T(8,128)(2,1)S(1)}, u32[]{:S(2)}, u32[]{:S(2)}) collective-permute-start(bf16[40,1024]{1,0:T(8,128)(2,1)S(1)} %pad_maximum_fusion.1.refs_0_), channel_id=1, source_target_pairs={{0,5},{1,4},{2,7},{3,6},{4,1},{5,0},{6,3},{7,2},{8,13},{9,12},{10,... | collective-permute-start | bytes 245768 | tf_op jit(solution)/shard_map/ppermute | solution.py:617
  46.3 3.6 %collective-permute-start.15 = (bf16[40,1024]{1,0:T(8,128)(2,1)S(1)}, bf16[40,1024]{1,0:T(8,128)(2,1)S(1)}, u32[]{:S(2)}, u32[]{:S(2)}) collective-permute-start(bf16[40,1024]{1,0:T(8,128)(2,1)S(1)} %pad_maximum_fusion.1.refs_0_), channel_id=1, source_target_pairs={{0,1},{1,0},{2,3},{3,2},{4,5},{5,4},{6,7},{7,6},{8,9},{9,8},{10,11... | collective-permute-start | bytes 245768 | tf_op jit(solution)/shard_map/ppermute | solution.py:617
  50.0 1.6 %collective-permute-start.16 = (bf16[120,1024]{1,0:T(8,128)(2,1)S(1)}, bf16[120,1024]{1,0:T(8,128)(2,1)S(1)}, u32[]{:S(2)}, u32[]{:S(2)}) collective-permute-start(bf16[120,1024]{1,0:T(8,128)(2,1)S(1)} %constant_dynamic-update-slice_fusion.2.refs_1_), channel_id=1, source_target_pairs={{0,1},{1,0},{2,3},{3,2},{4,5},{5,4},{6,7},{7,6},{8,9},{9,8},{10,11... | collective-permute-start | bytes 737288 | tf_op jit(solution)/shard_map/ppermute | solution.py:617
